TPU v7x, 32 devices: a whole 2x2x4 slice. The times are simulated.
32 devices in a mesh: seq: 4 (over y, x), fsdp: 8 (over z, core).
Axes of the slice: x: 2, y: 2, z: 4, core: 2. Of those that a mesh axis runs over, the one named last changes fastest.
Arguments:
- tokens: bfloat16 [8, 1536, 2048], P('fsdp', 'seq'), may hold values from -6 to 6
- lengths: int32 [8, 3], P('fsdp'), may hold values from 1 to 1536, as said below
- routes: int32 [8, 1536, 8], P('fsdp', 'seq'), may hold values from 0 to 31, all different within a row; in each aligned block of 384 rows (0 to 383, 384 to 767, ..., all dimensions but the last counted through in order) at most 130 rows name the same one
- gates: float32 [8, 1536, 8], P('fsdp', 'seq'), may hold values from 0.06 to 0.25
- gain_attn: bfloat16 [2048], P('fsdp'), may hold values from 0.5 to 1.5
- gain_moe: bfloat16 [2048], P('fsdp'), may hold values from 0.5 to 1.5
- w_qkv: bfloat16 [2048, 6144], P('fsdp'), may hold values from -0.1875 to 0.1875
- w_out: bfloat16 [2048, 2048], P('fsdp'), may hold values from -0.5 to 0.5
- w_gate_up: bfloat16 [32, 2048, 2, 1024], P('seq', 'fsdp'), may hold values from -0.125 to 0.125
- w_down: bfloat16 [32, 1024, 2048], P('seq', None, 'fsdp'), may hold values from -0.75 to 0.75
- cotangent: bfloat16 [8, 1536, 2048], P('fsdp', 'seq'), may hold values from -6 to 6
Outputs:
- mixed: bfloat16 [8, 1536, 2048], P('fsdp', 'seq')
- grad_tokens: bfloat16 [8, 1536, 2048], P('fsdp', 'seq')
- grad_gain_attn: float32 [2048], P('fsdp')
- grad_gain_moe: float32 [2048], P('fsdp')
- grad_qkv: float32 [2048, 6144], P('fsdp')
- grad_out: float32 [2048, 2048], P('fsdp')
- grad_gate_up: float32 [32, 2048, 2, 1024], P('seq', 'fsdp')
- grad_down: float32 [32, 1024, 2048], P('seq', None, 'fsdp')
Inputs may be any that keep to these rules, and one draw needn't show every extreme that they name: `routes`: in the positions of one device no expert is named by more than 130 rows; the 8 experts of a position differ. Each group's lengths sum to 1536 or less; the first sequence of each group is packed first and has at least 1392 positions; the rest of the group is padding.
All inputs are finite; a program needn't handle non-finite values.
Results may differ from a plain program's by a relative error of at most 0.022.
Values may be sent and summed in bfloat16 or wider, within the bound.
A program may use at most 448 MiB of HBM per device.

v0:
```python
import jax
import jax.numpy as jnp
from jax import lax
from jax.sharding import PartitionSpec as P

D = 2048
HEADS = 16
HEAD = 128
FFE = 1024
TOP = 8


epsilon = 1e-06


def to_heads(packed):
    return lax.all_to_all(packed, "seq", split_axis=2, concat_axis=0, tiled=True)


def to_rows(packed):
    return lax.all_to_all(packed, "seq", split_axis=0, concat_axis=2, tiled=True)


def to_experts(slots):
    return lax.all_to_all(slots, "seq", split_axis=0, concat_axis=1, tiled=True)


def from_experts(slots):
    return lax.all_to_all(slots, "seq", split_axis=1, concat_axis=0, tiled=True)


def fetch_expert(gate_part, down_part):
    return (
        lax.all_gather(gate_part, "fsdp", axis=0, tiled=True),
        lax.all_gather(down_part, "fsdp", axis=1, tiled=True),
    )


def segment_ids(length_row, span_len):
    ends = jnp.cumsum(length_row)
    places = lax.iota(jnp.int32, span_len)
    return jnp.sum((places[:, None] >= ends[None, :]).astype(jnp.int32), axis=1)


def attend_forward(queries, key_rows, values, segment, block_len):
    span_len, heads_now, head_dim = queries.shape
    score_scale = head_dim ** (-0.5)

    def one_block(row_start):
        q_block = lax.dynamic_slice_in_dim(queries, row_start, block_len, 0)
        seg_block = lax.dynamic_slice_in_dim(segment, row_start, block_len, 0)
        scores = (
            jnp.einsum("qhd,khd->hqk", q_block, key_rows, preferred_element_type=jnp.float32)
            * score_scale
        )
        scores = jnp.where(seg_block[None, :, None] == segment[None, None, :], scores, -1e30)
        row_max = jnp.max(scores, axis=2, keepdims=True)
        exp_part = jnp.exp(scores - row_max)
        row_sum = jnp.sum(exp_part, axis=2, keepdims=True)
        prob_b = (exp_part / row_sum).astype(jnp.bfloat16)
        out_block = jnp.einsum("hqk,khd->qhd", prob_b, values, preferred_element_type=jnp.float32)
        return (out_block.astype(jnp.bfloat16), (row_max + jnp.log(row_sum))[:, :, 0])

    starts = jnp.arange(span_len // block_len, dtype=jnp.int32) * block_len
    outputs, log_total = lax.map(one_block, starts)
    log_total = jnp.transpose(log_total, (1, 0, 2)).reshape(heads_now, span_len)
    return (outputs.reshape(span_len, heads_now, head_dim), log_total)


def attend_backward(queries, key_rows, values, segment, log_total, grad_heads, block_len):
    span_len, heads_now, head_dim = queries.shape
    score_scale = head_dim ** (-0.5)

    def one_block(carried, row_start):
        grad_k, grad_v = carried
        q_block = lax.dynamic_slice_in_dim(queries, row_start, block_len, 0)
        seg_block = lax.dynamic_slice_in_dim(segment, row_start, block_len, 0)
        g_block = lax.dynamic_slice_in_dim(grad_heads, row_start, block_len, 0)
        lse_block = lax.dynamic_slice_in_dim(log_total, row_start, block_len, 1)
        scores = (
            jnp.einsum("qhd,khd->hqk", q_block, key_rows, preferred_element_type=jnp.float32)
            * score_scale
        )
        scores = jnp.where(seg_block[None, :, None] == segment[None, None, :], scores, -1e30)
        prob_f = jnp.exp(scores - lse_block[:, :, None])
        grad_v = grad_v + jnp.einsum(
            "hqk,qhd->khd", prob_f.astype(jnp.bfloat16), g_block, preferred_element_type=jnp.float32
        )
        grad_p = jnp.einsum("qhd,khd->hqk", g_block, values, preferred_element_type=jnp.float32)
        inner_sum = jnp.sum(prob_f * grad_p, axis=2, keepdims=True)
        dscore = (prob_f * (grad_p - inner_sum)).astype(jnp.bfloat16)
        grad_q = (
            jnp.einsum("hqk,khd->qhd", dscore, key_rows, preferred_element_type=jnp.float32)
            * score_scale
        )
        grad_k = (
            grad_k
            + jnp.einsum("hqk,qhd->khd", dscore, q_block, preferred_element_type=jnp.float32)
            * score_scale
        )
        return ((grad_k, grad_v), grad_q)

    zeros_kv = jnp.zeros((span_len, heads_now, head_dim), jnp.float32)
    starts = jnp.arange(span_len // block_len, dtype=jnp.int32) * block_len
    (grad_k, grad_v), grad_q = lax.scan(one_block, (zeros_kv, zeros_kv), starts)
    return (grad_q.reshape(span_len, heads_now, head_dim), grad_k, grad_v)


def expert_core(x_slots, gate_full, down_full):
    proj = jnp.dot(
        x_slots, gate_full.reshape(D, 2 * FFE), preferred_element_type=jnp.float32
    ).reshape(-1, 2, FFE)
    act = (jax.nn.silu(proj[:, 0]) * proj[:, 1]).astype(jnp.bfloat16)
    produced = jnp.dot(act, down_full, preferred_element_type=jnp.float32).astype(jnp.bfloat16)
    return (produced, proj)


def expert_back(x_slots, grad_slots, proj, gate_full, down_full):
    gate_v = proj[:, 0]
    up_v = proj[:, 1]
    sigma = jax.nn.sigmoid(gate_v)
    silu_v = gate_v * sigma
    act = (silu_v * up_v).astype(jnp.bfloat16)
    grad_act = jnp.einsum("rd,fd->rf", grad_slots, down_full, preferred_element_type=jnp.float32)
    grad_dn = jnp.einsum("rf,rd->fd", act, grad_slots, preferred_element_type=jnp.float32)
    grad_gate = grad_act * up_v * (sigma * (1.0 + gate_v * (1.0 - sigma)))
    grad_up = grad_act * silu_v
    grad_proj = jnp.stack([grad_gate, grad_up], axis=1).astype(jnp.bfloat16).reshape(-1, 2 * FFE)
    grad_x = jnp.einsum(
        "re,de->rd", grad_proj, gate_full.reshape(D, 2 * FFE), preferred_element_type=jnp.float32
    )
    grad_gu = jnp.einsum(
        "rd,re->de", x_slots, grad_proj, preferred_element_type=jnp.float32
    ).reshape(-1, 2, FFE)
    shard_gu, shard_dn = (
        lax.psum_scatter(
            grad_gu.astype(jnp.bfloat16), "fsdp", scatter_dimension=0, tiled=True
        ).astype(jnp.float32),
        lax.psum_scatter(
            grad_dn.astype(jnp.bfloat16), "fsdp", scatter_dimension=1, tiled=True
        ).astype(jnp.float32),
    )
    return (grad_x.astype(jnp.bfloat16), shard_gu, shard_dn)


def body(
    tokens, lengths, routes, gates, gain_attn, gain_moe, w_qkv, w_out, w_gate_up, w_down, cotangent
):
    row_count = tokens.shape[1]
    x_float = tokens[0].astype(jnp.float32)
    qkv_full, out_full, gain_a_full, gain_m_full = (
        lax.all_gather(w_qkv, "fsdp", axis=0, tiled=True),
        lax.all_gather(w_out, "fsdp", axis=0, tiled=True),
        lax.all_gather(gain_attn, "fsdp", axis=0, tiled=True),
        lax.all_gather(gain_moe, "fsdp", axis=0, tiled=True),
    )
    gain_a = gain_a_full.astype(jnp.float32)
    gain_m = gain_m_full.astype(jnp.float32)
    inv_a = lax.rsqrt(jnp.mean(x_float * x_float, axis=1, keepdims=True) + epsilon)
    normed_a = (x_float * inv_a * gain_a).astype(jnp.bfloat16)
    qkv = jnp.dot(normed_a, qkv_full, preferred_element_type=jnp.float32).astype(jnp.bfloat16)
    spread = to_heads(qkv.reshape(row_count, 3, HEADS, HEAD))
    span_len = spread.shape[0]
    segment = segment_ids(lengths[0], span_len)
    block_len = 512
    queries = spread[:, 0]
    key_rows = spread[:, 1]
    values = spread[:, 2]
    attended, log_total = attend_forward(queries, key_rows, values, segment, block_len)
    heads_rows = to_rows(attended[:, None]).reshape(row_count, D)
    resid = x_float + jnp.dot(heads_rows, out_full, preferred_element_type=jnp.float32)
    inv_m = lax.rsqrt(jnp.mean(resid * resid, axis=1, keepdims=True) + epsilon)
    normed_m = (resid * inv_m * gain_m).astype(jnp.bfloat16)
    local_count = w_gate_up.shape[0]
    experts_all = local_count * lax.axis_size("seq")
    capacity = row_count * TOP * 4 // (3 * experts_all) + 2
    flat_route = routes[0].reshape(-1)
    onehot = (flat_route[:, None] == lax.iota(jnp.int32, experts_all)[None, :]).astype(jnp.int32)
    slot_rank = jnp.sum((jnp.cumsum(onehot, axis=0) - onehot) * onehot, axis=1)
    slot_index = flat_route * capacity + slot_rank
    weight = gates[0]
    outgoing = jnp.repeat(normed_m, TOP, axis=0)
    slots = jnp.zeros((experts_all * capacity, D), jnp.bfloat16).at[slot_index].set(outgoing)
    inbound = to_experts(slots.reshape(experts_all, capacity, D))

    def forward_again(inputs_e):
        gate_full, down_full = fetch_expert(inputs_e[1], inputs_e[2])
        return expert_core(inputs_e[0], gate_full, down_full)

    produced_all, proj_all = lax.map(forward_again, (inbound, w_gate_up, w_down))
    returned = from_experts(produced_all).reshape(experts_all * capacity, D)
    picked = returned[slot_index].astype(jnp.float32).reshape(row_count, TOP, D)
    mixed = (resid + jnp.sum(weight[:, :, None] * picked, axis=1)).astype(jnp.bfloat16)
    grad_out_rows = cotangent[0].astype(jnp.float32)
    sending = (
        (weight[:, :, None] * grad_out_rows[:, None, :])
        .astype(jnp.bfloat16)
        .reshape(row_count * TOP, D)
    )
    grad_slots = jnp.zeros((experts_all * capacity, D), jnp.bfloat16).at[slot_index].set(sending)
    grad_inbound = to_experts(grad_slots.reshape(experts_all, capacity, D))

    def backward_again(inputs_e):
        gate_full, down_full = fetch_expert(inputs_e[3], inputs_e[4])
        return expert_back(inputs_e[0], inputs_e[1], inputs_e[2], gate_full, down_full)

    grad_x_slots, grad_gate_up, grad_down = lax.map(
        backward_again, (inbound, grad_inbound, proj_all, w_gate_up, w_down)
    )
    grad_back = from_experts(grad_x_slots).reshape(experts_all * capacity, D)
    grad_normed_m = jnp.sum(
        grad_back[slot_index].astype(jnp.float32).reshape(row_count, TOP, D), axis=1
    )
    scaled_m = grad_normed_m * gain_m
    grad_resid = (
        grad_out_rows
        + inv_m * scaled_m
        - inv_m * inv_m * inv_m * resid * jnp.mean(scaled_m * resid, axis=1, keepdims=True)
    )
    grad_gain_m = jnp.sum(grad_normed_m * resid * inv_m, axis=0)
    grad_attn = grad_resid.astype(jnp.bfloat16)
    grad_out_w = jnp.einsum("rd,re->de", heads_rows, grad_attn, preferred_element_type=jnp.float32)
    grad_heads_rows = jnp.einsum(
        "re,de->rd", grad_attn, out_full, preferred_element_type=jnp.float32
    ).astype(jnp.bfloat16)
    grad_heads = to_heads(grad_heads_rows.reshape(row_count, 1, HEADS, HEAD))[:, 0]
    grad_q, grad_k, grad_v = attend_backward(
        queries, key_rows, values, segment, log_total, grad_heads, block_len
    )
    grad_packed = jnp.stack([grad_q, grad_k, grad_v], axis=1).astype(jnp.bfloat16)
    grad_qkv_rows = to_rows(grad_packed).reshape(row_count, 3 * D)
    grad_qkv_w = jnp.einsum(
        "rd,re->de", normed_a, grad_qkv_rows, preferred_element_type=jnp.float32
    )
    grad_normed_a = jnp.einsum(
        "re,de->rd", grad_qkv_rows, qkv_full, preferred_element_type=jnp.float32
    )
    scaled_a = grad_normed_a * gain_a
    grad_x = (
        grad_resid
        + inv_a * scaled_a
        - inv_a * inv_a * inv_a * x_float * jnp.mean(scaled_a * x_float, axis=1, keepdims=True)
    )
    grad_gain_a = jnp.sum(grad_normed_a * x_float * inv_a, axis=0)
    shards = (
        lax.psum_scatter(
            grad_qkv_w.astype(jnp.bfloat16), "fsdp", scatter_dimension=0, tiled=True
        ).astype(jnp.float32),
        lax.psum_scatter(
            grad_out_w.astype(jnp.bfloat16), "fsdp", scatter_dimension=0, tiled=True
        ).astype(jnp.float32),
        lax.psum_scatter(
            grad_gain_a.astype(jnp.bfloat16), "fsdp", scatter_dimension=0, tiled=True
        ).astype(jnp.float32),
        lax.psum_scatter(
            grad_gain_m.astype(jnp.bfloat16), "fsdp", scatter_dimension=0, tiled=True
        ).astype(jnp.float32),
    )
    qkv_sum, out_sum, gain_a_sum, gain_m_sum = (
        lax.psum(shards[0].astype(jnp.bfloat16), "seq").astype(jnp.float32),
        lax.psum(shards[1].astype(jnp.bfloat16), "seq").astype(jnp.float32),
        lax.psum(shards[2].astype(jnp.bfloat16), "seq").astype(jnp.float32),
        lax.psum(shards[3].astype(jnp.bfloat16), "seq").astype(jnp.float32),
    )
    return (
        mixed[None],
        grad_x.astype(jnp.bfloat16)[None],
        gain_a_sum,
        gain_m_sum,
        qkv_sum,
        out_sum,
        grad_gate_up,
        grad_down,
    )


def solution(mesh):
    placed = (
        P("fsdp", "seq", None),
        P("fsdp", None),
        P("fsdp", "seq", None),
        P("fsdp", "seq", None),
        P("fsdp"),
        P("fsdp"),
        P("fsdp", None),
        P("fsdp", None),
        P("seq", "fsdp", None, None),
        P("seq", None, "fsdp"),
        P("fsdp", "seq", None),
    )
    return jax.shard_map(
        body,
        mesh=mesh,
        in_specs=placed,
        out_specs=(
            P("fsdp", "seq", None),
            P("fsdp", "seq", None),
            P("fsdp"),
            P("fsdp"),
            P("fsdp", None),
            P("fsdp", None),
            P("seq", "fsdp", None, None),
            P("seq", None, "fsdp"),
        ),
        check_vma=False,
    )
```

profile of v0, /device:TPU:0, one launch (start us, length us, event | category | flops | bytes accessed | tf_op | source)
XLA Modules:
  0.0 5364.3 jit_solution(17995221010864267221)
XLA Ops:
  22.4 209.9 %all-gather.21.cloned.1.call-done = bf16[2048,6144]{1,0:T(8,128)(2,1)} async-done(((bf16[256,6144]{1,0:T(8,128)(2,1)}), bf16[2048,6144]{1,0:T(8,128)(2,1)}) %all-gather.21.cloned.1.call-update) | async-done | bytes 25165840 | tf_op jit(solution)/shard_map/all_gather | solution.py:152
  497.2 128.0 %all-to-all-done.4 = bf16[32,130,2048]{2,1,0:T(8,128)(2,1)} async-done(((bf16[32,130,2048]{2,1,0:T(8,128)(2,1)}), bf16[32,130,2048]{2,1,0:T(8,128)(2,1)}, u32[]{:S(2)}, u32[]{:S(2)}) %all-to-all-start.4) | async-done | bytes 17039392 | tf_op jit(solution)/shard_map/all_to_all | solution.py:25
  669.6 155.8 %all-to-all-done.2 = bf16[32,130,2048]{2,1,0:T(8,128)(2,1)} async-done(((bf16[32,130,2048]{2,1,0:T(8,128)(2,1)}), bf16[32,130,2048]{2,1,0:T(8,128)(2,1)}, u32[]{:S(2)}, u32[]{:S(2)}) %all-to-all-start.2) | async-done | bytes 17039392 | tf_op jit(solution)/shard_map/all_to_all | solution.py:25
  868.7 1109.8 %while.54 = (s32[]{:T(128)}, bf16[8,520,2048]{2,1,0:T(8,128)(2,1)}, f32[8,520,2,1024]{3,2,1,0:T(2,128)}, bf16[8,520,2048]{2,1,0:T(8,128)(2,1)}, bf16[8,256,2,102...) while((s32[]{:T(128)}, bf16[8,520,2048]{2,1,0:T(8,128)(2,1)}, ...), condition=%wide.region_13.14_spmd, body=%wide.region_12.13_spmd.sunk | while | flops 6547374080 | bytes 134611184 | solution.py:190
  1011.6 78.5 %all-gather.27.cloned.1.call-done = bf16[1,2048,2,1024]{3,2,0,1:T(2,128)(2,1)} async-done(((bf16[1,256,2,1024]{3,2,0,1:T(2,128)(2,1)}), bf16[1,2048,2,1024]{3,2,0,1:T(2,128)(2,1)}) %all-gather.27.cloned.1.call-update) | async-done | bytes 8388624 | tf_op jit(solution)/shard_map/while/body/eval_jaxpr/all_gather | solution.py:34
  1150.4 78.5 %all-gather.27.cloned.1.call-done = bf16[1,2048,2,1024]{3,2,0,1:T(2,128)(2,1)} async-done(((bf16[1,256,2,1024]{3,2,0,1:T(2,128)(2,1)}), bf16[1,2048,2,1024]{3,2,0,1:T(2,128)(2,1)}) %all-gather.27.cloned.1.call-update) | async-done | bytes 8388624 | tf_op jit(solution)/shard_map/while/body/eval_jaxpr/all_gather | solution.py:34
  1289.2 78.5 %all-gather.27.cloned.1.call-done = bf16[1,2048,2,1024]{3,2,0,1:T(2,128)(2,1)} async-done(((bf16[1,256,2,1024]{3,2,0,1:T(2,128)(2,1)}), bf16[1,2048,2,1024]{3,2,0,1:T(2,128)(2,1)}) %all-gather.27.cloned.1.call-update) | async-done | bytes 8388624 | tf_op jit(solution)/shard_map/while/body/eval_jaxpr/all_gather | solution.py:34
  1428.0 78.5 %all-gather.27.cloned.1.call-done = bf16[1,2048,2,1024]{3,2,0,1:T(2,128)(2,1)} async-done(((bf16[1,256,2,1024]{3,2,0,1:T(2,128)(2,1)}), bf16[1,2048,2,1024]{3,2,0,1:T(2,128)(2,1)}) %all-gather.27.cloned.1.call-update) | async-done | bytes 8388624 | tf_op jit(solution)/shard_map/while/body/eval_jaxpr/all_gather | solution.py:34
  1566.7 78.5 %all-gather.27.cloned.1.call-done = bf16[1,2048,2,1024]{3,2,0,1:T(2,128)(2,1)} async-done(((bf16[1,256,2,1024]{3,2,0,1:T(2,128)(2,1)}), bf16[1,2048,2,1024]{3,2,0,1:T(2,128)(2,1)}) %all-gather.27.cloned.1.call-update) | async-done | bytes 8388624 | tf_op jit(solution)/shard_map/while/body/eval_jaxpr/all_gather | solution.py:34
  1705.5 78.5 %all-gather.27.cloned.1.call-done = bf16[1,2048,2,1024]{3,2,0,1:T(2,128)(2,1)} async-done(((bf16[1,256,2,1024]{3,2,0,1:T(2,128)(2,1)}), bf16[1,2048,2,1024]{3,2,0,1:T(2,128)(2,1)}) %all-gather.27.cloned.1.call-update) | async-done | bytes 8388624 | tf_op jit(solution)/shard_map/while/body/eval_jaxpr/all_gather | solution.py:34
  1844.3 78.5 %all-gather.27.cloned.1.call-done = bf16[1,2048,2,1024]{3,2,0,1:T(2,128)(2,1)} async-done(((bf16[1,256,2,1024]{3,2,0,1:T(2,128)(2,1)}), bf16[1,2048,2,1024]{3,2,0,1:T(2,128)(2,1)}) %all-gather.27.cloned.1.call-update) | async-done | bytes 8388624 | tf_op jit(solution)/shard_map/while/body/eval_jaxpr/all_gather | solution.py:34
  1984.7 2216.5 %while.55 = (s32[]{:T(128)}, bf16[8,520,2048]{2,1,0:T(8,128)(2,1)}, f32[8,256,2,1024]{3,2,1,0:T(2,128)}, f32[8,1024,256]{2,1,0:T(8,128)}, bf16[8,520,2048]{2,1,0...) while((s32[]{:T(128)}, bf16[8,520,2048]{2,1,0:T(8,128)(2,1)}, ...), condition=%wide.region_19.20_spmd, body=%wide.region_16.19_spmd.sunk | while | flops 13106618368 | bytes 181764400 | solution.py:207
  2086.5 80.4 %all-gather.29.cloned.1.call-done = bf16[1,2048,2,1024]{3,1,2,0:T(8,128)(2,1)} async-done(((bf16[1,256,2,1024]{3,1,2,0:T(8,128)(2,1)}), bf16[1,2048,2,1024]{3,1,2,0:T(8,128)(2,1)}) %all-gather.29.cloned.1.call-update) | async-done | bytes 8388624 | tf_op jit(solution)/shard_map/while/body/eval_jaxpr/all_gather | solution.py:34
  2176.2 81.3 %reduce-scatter.9.cloned.1.call-done = bf16[256,2,1024]{2,0,1:T(8,128)(2,1)} async-done(((bf16[2048,2,1024]{2,0,1:T(8,128)(2,1)}), bf16[256,2,1024]{2,0,1:T(8,128)(2,1)}) %reduce-scatter.9.cloned.1.call-update) | async-done | bytes 1048592 | tf_op jit(solution)/shard_map/while/body/eval_jaxpr/reduce_scatter | solution.py:136
  2363.8 80.4 %all-gather.29.cloned.1.call-done = bf16[1,2048,2,1024]{3,1,2,0:T(8,128)(2,1)} async-done(((bf16[1,256,2,1024]{3,1,2,0:T(8,128)(2,1)}), bf16[1,2048,2,1024]{3,1,2,0:T(8,128)(2,1)}) %all-gather.29.cloned.1.call-update) | async-done | bytes 8388624 | tf_op jit(solution)/shard_map/while/body/eval_jaxpr/all_gather | solution.py:34
  2453.4 81.2 %reduce-scatter.9.cloned.1.call-done = bf16[256,2,1024]{2,0,1:T(8,128)(2,1)} async-done(((bf16[2048,2,1024]{2,0,1:T(8,128)(2,1)}), bf16[256,2,1024]{2,0,1:T(8,128)(2,1)}) %reduce-scatter.9.cloned.1.call-update) | async-done | bytes 1048592 | tf_op jit(solution)/shard_map/while/body/eval_jaxpr/reduce_scatter | solution.py:136
  2640.7 80.4 %all-gather.29.cloned.1.call-done = bf16[1,2048,2,1024]{3,1,2,0:T(8,128)(2,1)} async-done(((bf16[1,256,2,1024]{3,1,2,0:T(8,128)(2,1)}), bf16[1,2048,2,1024]{3,1,2,0:T(8,128)(2,1)}) %all-gather.29.cloned.1.call-update) | async-done | bytes 8388624 | tf_op jit(solution)/shard_map/while/body/eval_jaxpr/all_gather | solution.py:34
  2730.4 81.2 %reduce-scatter.9.cloned.1.call-done = bf16[256,2,1024]{2,0,1:T(8,128)(2,1)} async-done(((bf16[2048,2,1024]{2,0,1:T(8,128)(2,1)}), bf16[256,2,1024]{2,0,1:T(8,128)(2,1)}) %reduce-scatter.9.cloned.1.call-update) | async-done | bytes 1048592 | tf_op jit(solution)/shard_map/while/body/eval_jaxpr/reduce_scatter | solution.py:136
  2918.0 80.3 %all-gather.29.cloned.1.call-done = bf16[1,2048,2,1024]{3,1,2,0:T(8,128)(2,1)} async-done(((bf16[1,256,2,1024]{3,1,2,0:T(8,128)(2,1)}), bf16[1,2048,2,1024]{3,1,2,0:T(8,128)(2,1)}) %all-gather.29.cloned.1.call-update) | async-done | bytes 8388624 | tf_op jit(solution)/shard_map/while/body/eval_jaxpr/all_gather | solution.py:34
  3007.5 81.3 %reduce-scatter.9.cloned.1.call-done = bf16[256,2,1024]{2,0,1:T(8,128)(2,1)} async-done(((bf16[2048,2,1024]{2,0,1:T(8,128)(2,1)}), bf16[256,2,1024]{2,0,1:T(8,128)(2,1)}) %reduce-scatter.9.cloned.1.call-update) | async-done | bytes 1048592 | tf_op jit(solution)/shard_map/while/body/eval_jaxpr/reduce_scatter | solution.py:136
  3195.1 80.3 %all-gather.29.cloned.1.call-done = bf16[1,2048,2,1024]{3,1,2,0:T(8,128)(2,1)} async-done(((bf16[1,256,2,1024]{3,1,2,0:T(8,128)(2,1)}), bf16[1,2048,2,1024]{3,1,2,0:T(8,128)(2,1)}) %all-gather.29.cloned.1.call-update) | async-done | bytes 8388624 | tf_op jit(solution)/shard_map/while/body/eval_jaxpr/all_gather | solution.py:34
  3284.7 81.3 %reduce-scatter.9.cloned.1.call-done = bf16[256,2,1024]{2,0,1:T(8,128)(2,1)} async-done(((bf16[2048,2,1024]{2,0,1:T(8,128)(2,1)}), bf16[256,2,1024]{2,0,1:T(8,128)(2,1)}) %reduce-scatter.9.cloned.1.call-update) | async-done | bytes 1048592 | tf_op jit(solution)/shard_map/while/body/eval_jaxpr/reduce_scatter | solution.py:136
  3472.1 80.4 %all-gather.29.cloned.1.call-done = bf16[1,2048,2,1024]{3,1,2,0:T(8,128)(2,1)} async-done(((bf16[1,256,2,1024]{3,1,2,0:T(8,128)(2,1)}), bf16[1,2048,2,1024]{3,1,2,0:T(8,128)(2,1)}) %all-gather.29.cloned.1.call-update) | async-done | bytes 8388624 | tf_op jit(solution)/shard_map/while/body/eval_jaxpr/all_gather | solution.py:34
  3561.8 81.3 %reduce-scatter.9.cloned.1.call-done = bf16[256,2,1024]{2,0,1:T(8,128)(2,1)} async-done(((bf16[2048,2,1024]{2,0,1:T(8,128)(2,1)}), bf16[256,2,1024]{2,0,1:T(8,128)(2,1)}) %reduce-scatter.9.cloned.1.call-update) | async-done | bytes 1048592 | tf_op jit(solution)/shard_map/while/body/eval_jaxpr/reduce_scatter | solution.py:136
  3749.2 80.3 %all-gather.29.cloned.1.call-done = bf16[1,2048,2,1024]{3,1,2,0:T(8,128)(2,1)} async-done(((bf16[1,256,2,1024]{3,1,2,0:T(8,128)(2,1)}), bf16[1,2048,2,1024]{3,1,2,0:T(8,128)(2,1)}) %all-gather.29.cloned.1.call-update) | async-done | bytes 8388624 | tf_op jit(solution)/shard_map/while/body/eval_jaxpr/all_gather | solution.py:34
  3838.8 81.1 %reduce-scatter.9.cloned.1.call-done = bf16[256,2,1024]{2,0,1:T(8,128)(2,1)} async-done(((bf16[2048,2,1024]{2,0,1:T(8,128)(2,1)}), bf16[256,2,1024]{2,0,1:T(8,128)(2,1)}) %reduce-scatter.9.cloned.1.call-update) | async-done | bytes 1048592 | tf_op jit(solution)/shard_map/while/body/eval_jaxpr/reduce_scatter | solution.py:136
  4025.9 80.3 %all-gather.29.cloned.1.call-done = bf16[1,2048,2,1024]{3,1,2,0:T(8,128)(2,1)} async-done(((bf16[1,256,2,1024]{3,1,2,0:T(8,128)(2,1)}), bf16[1,2048,2,1024]{3,1,2,0:T(8,128)(2,1)}) %all-gather.29.cloned.1.call-update) | async-done | bytes 8388624 | tf_op jit(solution)/shard_map/while/body/eval_jaxpr/all_gather | solution.py:34
  4115.4 81.3 %reduce-scatter.9.cloned.1.call-done = bf16[256,2,1024]{2,0,1:T(8,128)(2,1)} async-done(((bf16[2048,2,1024]{2,0,1:T(8,128)(2,1)}), bf16[256,2,1024]{2,0,1:T(8,128)(2,1)}) %reduce-scatter.9.cloned.1.call-update) | async-done | bytes 1048592 | tf_op jit(solution)/shard_map/while/body/eval_jaxpr/reduce_scatter | solution.py:136
  4240.4 167.2 %all-to-all-done.5 = bf16[8,520,2048]{2,0,1:T(8,128)(2,1)} async-done(((bf16[8,520,2048]{2,0,1:T(8,128)(2,1)}), bf16[8,520,2048]{2,0,1:T(8,128)(2,1)}, u32[]{:S(2)}, u32[]{:S(2)}) %all-to-all-start.5) | async-done | bytes 17039392 | tf_op jit(solution)/shard_map/all_to_all | solution.py:29
  4449.7 149.6 %all-to-all-done.3 = bf16[8,520,2048]{2,0,1:T(8,128)(2,1)} async-done(((bf16[8,520,2048]{2,0,1:T(8,128)(2,1)}), bf16[8,520,2048]{2,0,1:T(8,128)(2,1)}, u32[]{:S(2)}, u32[]{:S(2)}) %all-to-all-start.3) | async-done | bytes 17039392 | tf_op jit(solution)/shard_map/all_to_all | solution.py:29
  4755.6 123.7 %while.56 = (s32[]{:T(128)}, f32[1536,4,128]{0,2,1:T(8,128)}, f32[1536,4,128]{0,2,1:T(8,128)}, bf16[3,512,4,128]{3,1,0,2:T(8,128)(2,1)}, s32[3]{0:T(128)S(1)}, /...) while((s32[]{:T(128)}, f32[1536,4,128]{0,2,1:T(8,128)}, ...), condition=%wide.region_24.25_spmd.clone, body=%wide.region_22.24_spmd.clone.sunk | while | flops 4059822080 | bytes 154194720 | solution.py:105
  4996.8 247.5 %reduce-scatter.5.cloned.1.call-done = bf16[256,6144]{1,0:T(8,128)(2,1)} async-done(((bf16[2048,6144]{1,0:T(8,128)(2,1)}), bf16[256,6144]{1,0:T(8,128)(2,1)}) %reduce-scatter.5.cloned.1.call-update) | async-done | bytes 3145744 | tf_op jit(solution)/shard_map/reduce_scatter | solution.py:246
  (624 shorter events, 2484.7 us)
Async XLA Ops:
  7.2 225.1 %all-gather.21.cloned.1.call-start = ((), (), s32[]{:S(2)}) async-start(), calls=%async_computation.12 | async-start | bytes 28311552 | tf_op jit(solution)/shard_map/all_gather | solution.py:152
  257.1 188.5 %all-gather.23.cloned.1.call-start = ((), (), s32[]{:S(2)}) async-start(), calls=%async_computation.13 | async-start | bytes 9437184 | tf_op jit(solution)/shard_map/all_gather | solution.py:153
  424.5 200.7 %all-to-all-start.4 = ((bf16[32,130,2048]{2,1,0:T(8,128)(2,1)}), bf16[32,130,2048]{2,1,0:T(8,128)(2,1)}, u32[]{:S(2)}, u32[]{:S(2)}) async-start(bf16[32,130,2048]{2,1,0:T(8,128)(2,1)} %reshape.304), calls=%async_computation.6 | async-start | bytes 35651584 | tf_op jit(solution)/shard_map/all_to_all | solution.py:25
  625.2 200.2 %all-to-all-start.2 = ((bf16[32,130,2048]{2,1,0:T(8,128)(2,1)}), bf16[32,130,2048]{2,1,0:T(8,128)(2,1)}, u32[]{:S(2)}, u32[]{:S(2)}) async-start(bf16[32,130,2048]{2,1,0:T(8,128)(2,1)} %reshape.302), calls=%async_computation.4 | async-start | bytes 35651584 | tf_op jit(solution)/shard_map/all_to_all | solution.py:25
  1009.6 128.9 %all-gather.25.cloned.1.call-start = ((), (), s32[]{:S(2)}) async-start(), calls=%async_computation.17 | async-start | bytes 4718592 | tf_op jit(solution)/shard_map/while/body/eval_jaxpr/all_gather | solution.py:35
  1148.4 129.1 %all-gather.25.cloned.1.call-start = ((), (), s32[]{:S(2)}) async-start(), calls=%async_computation.17 | async-start | bytes 4718592 | tf_op jit(solution)/shard_map/while/body/eval_jaxpr/all_gather | solution.py:35
  1287.3 128.9 %all-gather.25.cloned.1.call-start = ((), (), s32[]{:S(2)}) async-start(), calls=%async_computation.17 | async-start | bytes 4718592 | tf_op jit(solution)/shard_map/while/body/eval_jaxpr/all_gather | solution.py:35
  1426.0 128.9 %all-gather.25.cloned.1.call-start = ((), (), s32[]{:S(2)}) async-start(), calls=%async_computation.17 | async-start | bytes 4718592 | tf_op jit(solution)/shard_map/while/body/eval_jaxpr/all_gather | solution.py:35
  1564.8 128.9 %all-gather.25.cloned.1.call-start = ((), (), s32[]{:S(2)}) async-start(), calls=%async_computation.17 | async-start | bytes 4718592 | tf_op jit(solution)/shard_map/while/body/eval_jaxpr/all_gather | solution.py:35
  1703.5 128.9 %all-gather.25.cloned.1.call-start = ((), (), s32[]{:S(2)}) async-start(), calls=%async_computation.17 | async-start | bytes 4718592 | tf_op jit(solution)/shard_map/while/body/eval_jaxpr/all_gather | solution.py:35
  1842.3 128.9 %all-gather.25.cloned.1.call-start = ((), (), s32[]{:S(2)}) async-start(), calls=%async_computation.17 | async-start | bytes 4718592 | tf_op jit(solution)/shard_map/while/body/eval_jaxpr/all_gather | solution.py:35
  2000.9 166.0 %all-gather.29.cloned.1.call-start = ((), (), s32[]{:S(2)}) async-start(), calls=%async_computation.19 | async-start | bytes 9437184 | tf_op jit(solution)/shard_map/while/body/eval_jaxpr/all_gather | solution.py:34
  2004.2 253.3 %reduce-scatter.9.cloned.1.call-start = ((), (), s32[]{:S(2)}) async-start(), calls=%async_computation.21 | async-start | bytes 9437184 | tf_op jit(solution)/shard_map/while/body/eval_jaxpr/reduce_scatter | solution.py:136
  2278.0 166.1 %all-gather.29.cloned.1.call-start = ((), (), s32[]{:S(2)}) async-start(), calls=%async_computation.19 | async-start | bytes 9437184 | tf_op jit(solution)/shard_map/while/body/eval_jaxpr/all_gather | solution.py:34
  2281.3 253.3 %reduce-scatter.9.cloned.1.call-start = ((), (), s32[]{:S(2)}) async-start(), calls=%async_computation.21 | async-start | bytes 9437184 | tf_op jit(solution)/shard_map/while/body/eval_jaxpr/reduce_scatter | solution.py:136
  2555.1 166.0 %all-gather.29.cloned.1.call-start = ((), (), s32[]{:S(2)}) async-start(), calls=%async_computation.19 | async-start | bytes 9437184 | tf_op jit(solution)/shard_map/while/body/eval_jaxpr/all_gather | solution.py:34
  2558.4 253.2 %reduce-scatter.9.cloned.1.call-start = ((), (), s32[]{:S(2)}) async-start(), calls=%async_computation.21 | async-start | bytes 9437184 | tf_op jit(solution)/shard_map/while/body/eval_jaxpr/reduce_scatter | solution.py:136
  2832.1 166.2 %all-gather.29.cloned.1.call-start = ((), (), s32[]{:S(2)}) async-start(), calls=%async_computation.19 | async-start | bytes 9437184 | tf_op jit(solution)/shard_map/while/body/eval_jaxpr/all_gather | solution.py:34
  2835.4 253.5 %reduce-scatter.9.cloned.1.call-start = ((), (), s32[]{:S(2)}) async-start(), calls=%async_computation.21 | async-start | bytes 9437184 | tf_op jit(solution)/shard_map/while/body/eval_jaxpr/reduce_scatter | solution.py:136
  3109.4 166.0 %all-gather.29.cloned.1.call-start = ((), (), s32[]{:S(2)}) async-start(), calls=%async_computation.19 | async-start | bytes 9437184 | tf_op jit(solution)/shard_map/while/body/eval_jaxpr/all_gather | solution.py:34
  3112.7 253.3 %reduce-scatter.9.cloned.1.call-start = ((), (), s32[]{:S(2)}) async-start(), calls=%async_computation.21 | async-start | bytes 9437184 | tf_op jit(solution)/shard_map/while/body/eval_jaxpr/reduce_scatter | solution.py:136
  3386.5 166.0 %all-gather.29.cloned.1.call-start = ((), (), s32[]{:S(2)}) async-start(), calls=%async_computation.19 | async-start | bytes 9437184 | tf_op jit(solution)/shard_map/while/body/eval_jaxpr/all_gather | solution.py:34
  3389.8 253.3 %reduce-scatter.9.cloned.1.call-start = ((), (), s32[]{:S(2)}) async-start(), calls=%async_computation.21 | async-start | bytes 9437184 | tf_op jit(solution)/shard_map/while/body/eval_jaxpr/reduce_scatter | solution.py:136
  3663.6 165.9 %all-gather.29.cloned.1.call-start = ((), (), s32[]{:S(2)}) async-start(), calls=%async_computation.19 | async-start | bytes 9437184 | tf_op jit(solution)/shard_map/while/body/eval_jaxpr/all_gather | solution.py:34
  3666.9 253.0 %reduce-scatter.9.cloned.1.call-start = ((), (), s32[]{:S(2)}) async-start(), calls=%async_computation.21 | async-start | bytes 9437184 | tf_op jit(solution)/shard_map/while/body/eval_jaxpr/reduce_scatter | solution.py:136
  3940.4 165.7 %all-gather.29.cloned.1.call-start = ((), (), s32[]{:S(2)}) async-start(), calls=%async_computation.19 | async-start | bytes 9437184 | tf_op jit(solution)/shard_map/while/body/eval_jaxpr/all_gather | solution.py:34
  3943.7 253.0 %reduce-scatter.9.cloned.1.call-start = ((), (), s32[]{:S(2)}) async-start(), calls=%async_computation.21 | async-start | bytes 9437184 | tf_op jit(solution)/shard_map/while/body/eval_jaxpr/reduce_scatter | solution.py:136
  4217.2 190.4 %all-to-all-start.5 = ((bf16[8,520,2048]{2,0,1:T(8,128)(2,1)}), bf16[8,520,2048]{2,0,1:T(8,128)(2,1)}, u32[]{:S(2)}, u32[]{:S(2)}) async-start(bf16[8,520,2048]{2,0,1:T(8,128)(2,1)} %copy.213), calls=%async_computation.7 | async-start | bytes 34078720 | tf_op jit(solution)/shard_map/all_to_all | solution.py:29
  4407.6 191.7 %all-to-all-start.3 = ((bf16[8,520,2048]{2,0,1:T(8,128)(2,1)}), bf16[8,520,2048]{2,0,1:T(8,128)(2,1)}, u32[]{:S(2)}, u32[]{:S(2)}) async-start(bf16[8,520,2048]{2,0,1:T(8,128)(2,1)} %copy.204), calls=%async_computation.5 | async-start | bytes 34078720 | tf_op jit(solution)/shard_map/all_to_all | solution.py:29
  4734.1 262.7 %reduce-scatter.7.cloned.1.call-start = ((), (), s32[]{:S(2)}) async-start(), calls=%async_computation.15 | async-start | bytes 9437184 | tf_op jit(solution)/shard_map/reduce_scatter | solution.py:249
  4742.4 501.9 %reduce-scatter.5.cloned.1.call-start = ((), (), s32[]{:S(2)}) async-start(), calls=%async_computation.14 | async-start | bytes 28311552 | tf_op jit(solution)/shard_map/reduce_scatter | solution.py:246
  4996.7 353.5 %all-reduce.7.cloned.1.call-start = ((), (), s32[]{:S(2)}) async-start(), calls=%async_computation.16 | async-start | bytes 8388608 | tf_op jit(solution)/shard_map/psum | solution.py:260
  (104 other events, 3845.7 us)
Sparse Core Ops, SparseCore 0:
  9.7 222.5 all-gather.20
  259.6 80.7 all-gather.22
  872.0 79.3 all-gather.26
  1009.8 80.2 all-gather.26
  1148.6 80.2 all-gather.26
  1287.4 80.2 all-gather.26
  1426.2 80.2 all-gather.26
  1564.9 80.2 all-gather.26
  1703.6 80.2 all-gather.26
  1842.4 80.2 all-gather.26
  2086.7 80.1 all-gather.28
  2169.3 88.1 reduce-scatter.8
  2363.9 80.1 all-gather.28
  2446.4 88.1 reduce-scatter.8
  2640.9 80.1 all-gather.28
  2723.4 88.1 reduce-scatter.8
  2867.6 48.2 reduce-scatter.10
  2918.0 80.2 all-gather.28
  3000.7 88.1 reduce-scatter.8
  3144.8 48.2 reduce-scatter.10
  3195.2 80.1 all-gather.28
  3277.8 88.1 reduce-scatter.8
  3421.7 48.2 reduce-scatter.10
  3472.3 80.1 all-gather.28
  3554.9 88.1 reduce-scatter.8
  3749.2 80.1 all-gather.28
  3831.7 88.1 reduce-scatter.8
  4025.9 80.1 all-gather.28
  4108.5 88.1 reduce-scatter.8
  4742.5 91.4 reduce-scatter.6
  4996.8 247.4 reduce-scatter.4
  5247.7 102.5 all-reduce.6
  (21 shorter events, 979.8 us)
where the time goes:
time: 5380 us; the launch traced here: 5360 us
  waiting for transfers between devices  3620 us (67%)
  local copies, waits for them, and re-layouts  822 us (15%)
  matrix products  597 us (11%)
  other arithmetic  154 us (3%)
  blocking collectives  102 us (2%)
    all_gather x16, waiting for transfers between devices, fetch_expert(): lax.all_gather(gate_part, 'fsdp', axis=0, tiled=True)  1270 us
    reduce_scatter x8, waiting for transfers between devices, expert_back(): lax.psum_scatter(grad_gu.astype(jnp.bfloat16), 'fsdp', scatter_dimension=...  650 us
    all_to_all x2, waiting for transfers between devices, from_experts(): return lax.all_to_all(slots, 'seq', split_axis=1, concat_axis=0, tiled=True)  317 us
    all_to_all x2, waiting for transfers between devices, to_experts(): return lax.all_to_all(slots, 'seq', split_axis=0, concat_axis=1, tiled=True)  284 us
    all_gather x16, waiting for transfers between devices, fetch_expert(): lax.all_gather(down_part, 'fsdp', axis=1, tiled=True)  267 us
    reduce_scatter x8, waiting for transfers between devices, expert_back(): lax.psum_scatter(grad_dn.astype(jnp.bfloat16), 'fsdp', scatter_dimension=...  262 us
    reduce_scatter x1, waiting for transfers between devices, body(): lax.psum_scatter(grad_qkv_w.astype(jnp.bfloat16), 'fsdp', scatter_dimensi...  248 us
    all_gather x1, waiting for transfers between devices, body(): lax.all_gather(w_qkv, 'fsdp', axis=0, tiled=True)  210 us
  transfers between devices with their start and end apart: 60, of which 57 were waited for; matrix products, arithmetic and copies ran while one was open for 22% of the time, Pallas kernels for 0%

commit v1 on v0

v1 whole, which is shorter than its diff:
```python
import jax
import jax.numpy as jnp
from jax import lax
from jax.sharding import PartitionSpec as P

D = 2048
HEADS = 16
HEAD = 128
FFE = 1024
TOP = 8

epsilon = 1e-06
f32 = jnp.float32
bf16 = jnp.bfloat16


def swap(value, axis, bit):
    size = lax.axis_size(axis)
    return lax.ppermute(value, axis, [(i, i ^ bit) for i in range(size)])


def dot(a, b, contract, batch=((), ())):
    return lax.dot_general(a, b, (contract, batch), preferred_element_type=f32)


def segment_ids(length_row, span_len):
    ends = jnp.cumsum(length_row)
    places = lax.iota(jnp.int32, span_len)
    return jnp.sum((places[:, None] >= ends[None, :]).astype(jnp.int32), axis=1)


def attend_forward(queries, key_rows, values, segment, block_len):
    span_len, heads_now, head_dim = queries.shape
    score_scale = head_dim ** (-0.5)

    def one_block(row_start):
        q_block = lax.dynamic_slice_in_dim(queries, row_start, block_len, 0)
        seg_block = lax.dynamic_slice_in_dim(segment, row_start, block_len, 0)
        scores = (
            jnp.einsum("qhd,khd->hqk", q_block, key_rows, preferred_element_type=f32)
            * score_scale
        )
        scores = jnp.where(seg_block[None, :, None] == segment[None, None, :], scores, -1e30)
        row_max = jnp.max(scores, axis=2, keepdims=True)
        exp_part = jnp.exp(scores - row_max)
        row_sum = jnp.sum(exp_part, axis=2, keepdims=True)
        prob_b = (exp_part / row_sum).astype(bf16)
        out_block = jnp.einsum("hqk,khd->qhd", prob_b, values, preferred_element_type=f32)
        return (out_block.astype(bf16), (row_max + jnp.log(row_sum))[:, :, 0])

    starts = jnp.arange(span_len // block_len, dtype=jnp.int32) * block_len
    outputs, log_total = lax.map(one_block, starts)
    log_total = jnp.transpose(log_total, (1, 0, 2)).reshape(heads_now, span_len)
    return (outputs.reshape(span_len, heads_now, head_dim), log_total)


def attend_backward(queries, key_rows, values, segment, log_total, grad_heads, block_len):
    span_len, heads_now, head_dim = queries.shape
    score_scale = head_dim ** (-0.5)

    def one_block(carried, row_start):
        grad_k, grad_v = carried
        q_block = lax.dynamic_slice_in_dim(queries, row_start, block_len, 0)
        seg_block = lax.dynamic_slice_in_dim(segment, row_start, block_len, 0)
        g_block = lax.dynamic_slice_in_dim(grad_heads, row_start, block_len, 0)
        lse_block = lax.dynamic_slice_in_dim(log_total, row_start, block_len, 1)
        scores = (
            jnp.einsum("qhd,khd->hqk", q_block, key_rows, preferred_element_type=f32)
            * score_scale
        )
        scores = jnp.where(seg_block[None, :, None] == segment[None, None, :], scores, -1e30)
        prob_f = jnp.exp(scores - lse_block[:, :, None])
        grad_v = grad_v + jnp.einsum(
            "hqk,qhd->khd", prob_f.astype(bf16), g_block, preferred_element_type=f32
        )
        grad_p = jnp.einsum("qhd,khd->hqk", g_block, values, preferred_element_type=f32)
        inner_sum = jnp.sum(prob_f * grad_p, axis=2, keepdims=True)
        dscore = (prob_f * (grad_p - inner_sum)).astype(bf16)
        grad_q = (
            jnp.einsum("hqk,khd->qhd", dscore, key_rows, preferred_element_type=f32)
            * score_scale
        )
        grad_k = (
            grad_k
            + jnp.einsum("hqk,qhd->khd", dscore, q_block, preferred_element_type=f32)
            * score_scale
        )
        return ((grad_k, grad_v), grad_q)

    zeros_kv = jnp.zeros((span_len, heads_now, head_dim), f32)
    starts = jnp.arange(span_len // block_len, dtype=jnp.int32) * block_len
    (grad_k, grad_v), grad_q = lax.scan(one_block, (zeros_kv, zeros_kv), starts)
    return (grad_q.reshape(span_len, heads_now, head_dim), grad_k, grad_v)


def gather_expert(own, other):
    size = lax.axis_size("fsdp")
    place = lax.axis_index("fsdp")
    rows, columns = own.shape
    bit = size // 2
    piece, sent = own[None], other[None]
    while bit:
        received = swap(sent, "fsdp", bit)
        low = ((place // bit) % 2) == 0
        piece = jnp.stack(
            [jnp.where(low, piece, received), jnp.where(low, received, piece)], axis=1
        ).reshape(-1, rows, columns)
        sent = piece
        bit //= 2
    return piece.reshape(-1, columns)


def scatter_expert(grad):
    size = lax.axis_size("fsdp")
    place = lax.axis_index("fsdp")
    columns = grad.shape[1]
    rows = grad.shape[0] // size
    bit, many = 1, size // 2
    piece = grad.reshape(size, rows, columns)
    while bit < size:
        mine = (place // bit) % 2
        piece = piece.reshape(many, 2, rows, columns)
        kept = lax.dynamic_index_in_dim(piece, mine, 1, keepdims=False)
        received = swap(lax.dynamic_index_in_dim(piece, 1 - mine, 1, keepdims=False), "fsdp", bit)
        if many == 1:
            return kept[0], received[0]
        piece = (kept.astype(f32) + received.astype(f32)).astype(bf16)
        bit *= 2
        many //= 2


def to_group(rows):
    pair = jnp.stack([rows, swap(rows, "fsdp", lax.axis_size("fsdp") // 2)])
    return lax.all_gather(pair, "seq", axis=0, tiled=False)


def from_group(sums):
    rows, width = sums.shape[2:]
    mine = lax.psum_scatter(
        sums.astype(bf16).reshape(-1, width), "seq", scatter_dimension=0, tiled=True
    )
    other = swap(mine[rows:], "fsdp", lax.axis_size("fsdp") // 2)
    return mine[:rows].astype(f32) + other.astype(f32)


def body(
    tokens, lengths, routes, gates, gain_attn, gain_moe, w_qkv, w_out, w_gate_up, w_down, cotangent
):
    n_seq, n_fsdp = lax.axis_size("seq"), lax.axis_size("fsdp")
    at_seq, at_fsdp = lax.axis_index("seq"), lax.axis_index("fsdp")
    rows = tokens.shape[1]
    shard = D // n_fsdp
    local_count = w_gate_up.shape[0]
    per_half = local_count // 2
    half = at_fsdp // (n_fsdp // 2)
    heads_here = HEADS // n_seq
    width = heads_here * HEAD
    span_len = rows * n_seq

    packed = jnp.concatenate(
        [w_gate_up.reshape(local_count, shard, 2 * FFE), jnp.swapaxes(w_down, 1, 2)], axis=2
    )
    own_part = lax.dynamic_slice_in_dim(packed, half * per_half, per_half, 0)
    other_part = lax.dynamic_slice_in_dim(packed, (1 - half) * per_half, per_half, 0)
    experts = [gather_expert(own_part[i], other_part[i]) for i in range(per_half)]

    x_all = lax.all_gather(tokens[0], "seq", axis=0, tiled=True)
    part = lax.dynamic_slice_in_dim(
        w_qkv.reshape(shard, 3, HEADS, HEAD), at_seq * heads_here, heads_here, 2
    ).reshape(shard, 3 * width)
    gains = jnp.zeros((shard, 128), bf16).at[:, 0].set(gain_attn).at[:, 1].set(gain_moe)
    gathered = lax.all_gather(
        jnp.concatenate([part, gains], axis=1), "fsdp", axis=0, tiled=True
    )
    qkv_own = gathered[:, : 3 * width]
    gain_a = gathered[:, 3 * width].astype(f32)
    gain_m = gathered[:, 3 * width + 1].astype(f32)
    out_full = lax.all_gather(w_out, "fsdp", axis=0, tiled=True)

    routing = jnp.concatenate([routes[0].astype(f32), gates[0]], axis=1)
    routing = to_group(routing).reshape(2 * n_seq, rows, 2 * TOP)
    capacity = rows * TOP * 4 // (3 * local_count * n_seq) + 2
    capacity = -(-capacity // 8) * 8
    named = at_seq * local_count + half * per_half + lax.iota(jnp.int32, per_half)
    hits = routing[:, :, :TOP, None].astype(jnp.int32) == named
    mask = jnp.any(hits, axis=2)
    weight = jnp.sum(jnp.where(hits, routing[:, :, TOP:, None], 0.0), axis=2)
    below = (lax.iota(jnp.int32, rows)[:, None] > lax.iota(jnp.int32, rows)[None, :]).astype(bf16)
    rank = jnp.einsum("rq,bqe->bre", below, mask.astype(bf16), preferred_element_type=f32)
    rank = jnp.where(mask, rank.astype(jnp.int32), -1)
    picks = jnp.swapaxes(rank, 1, 2)[:, :, None, :] == lax.iota(jnp.int32, capacity)[:, None]
    share = jnp.sum(
        jnp.where(picks, jnp.swapaxes(weight, 1, 2)[:, :, None, :], 0.0), axis=3
    )
    picks = picks.astype(bf16)
    cot_all = to_group(cotangent[0]).reshape(2 * n_seq, rows, D)

    def normed_rows(values, gain):
        inverse = lax.rsqrt(jnp.mean(values * values, axis=1, keepdims=True) + epsilon)
        return (values * inverse * gain).astype(bf16), inverse

    normed_a, _ = normed_rows(x_all.astype(f32), gain_a)
    qkv = dot(normed_a, qkv_own, ((1,), (0,))).astype(bf16)
    spread = qkv.reshape(span_len, 3, heads_here, HEAD)
    segment = segment_ids(lengths[0], span_len)
    block_len = span_len // 3
    queries, key_rows, values = spread[:, 0], spread[:, 1], spread[:, 2]
    attended, log_total = attend_forward(queries, key_rows, values, segment, block_len)
    heads_rows = lax.all_to_all(
        attended.reshape(span_len, width), "seq", split_axis=0, concat_axis=1, tiled=True
    )
    x_float = tokens[0].astype(f32)
    resid = x_float + dot(heads_rows, out_full, ((1,), (0,)))
    normed_m, inv_m = normed_rows(resid, gain_m)
    moe_all = to_group(normed_m).reshape(2 * n_seq, rows, D)

    forward_parts, backward_parts, grads_own, grads_other = [], [], [], []
    for i in range(per_half):
        expert = experts[i]
        gate_up, down_t = expert[:, : 2 * FFE], expert[:, 2 * FFE :]
        pick = picks[:, i]
        share_i = share[:, i].reshape(-1, 1)
        slots = dot(pick, moe_all, ((2,), (1,)), ((0,), (0,))).astype(bf16).reshape(-1, D)
        grad_slots = dot(pick, cot_all, ((2,), (1,)), ((0,), (0,))).reshape(-1, D)
        grad_slots = (share_i * grad_slots).astype(bf16)
        proj = dot(slots, gate_up, ((1,), (0,)))
        gate_v, up_v = proj[:, :FFE], proj[:, FFE:]
        sigma = jax.nn.sigmoid(gate_v)
        silu_v = gate_v * sigma
        act = (silu_v * up_v).astype(bf16)
        produced = (share_i * dot(act, down_t, ((1,), (1,)))).astype(bf16)
        grad_act = dot(grad_slots, down_t, ((1,), (0,)))
        grad_gate = grad_act * up_v * (sigma * (1.0 + gate_v * (1.0 - sigma)))
        grad_up = grad_act * silu_v
        grad_proj = jnp.concatenate([grad_gate.astype(bf16), grad_up.astype(bf16)], axis=1)
        grad_in = dot(grad_proj, gate_up, ((1,), (1,))).astype(bf16)
        grad_expert = jnp.concatenate(
            [
                dot(slots, grad_proj, ((0,), (0,))).astype(bf16),
                dot(grad_slots, act, ((0,), (0,))).astype(bf16),
            ],
            axis=1,
        )
        forward_parts.append(produced.reshape(2 * n_seq, capacity, D))
        backward_parts.append(grad_in.reshape(2 * n_seq, capacity, D))
        mine, theirs = scatter_expert(grad_expert)
        grads_own.append(mine)
        grads_other.append(theirs)

    every_pick = picks.reshape(2 * n_seq, per_half * capacity, rows)

    def combine(parts):
        together = jnp.concatenate(parts, axis=1)
        sums = dot(every_pick, together, ((1,), (1,)), ((0,), (0,)))
        return from_group(sums.reshape(n_seq, 2, rows, D))

    grad_normed_m = combine(backward_parts)
    mixed = (resid + combine(forward_parts)).astype(bf16)

    scaled_m = grad_normed_m * gain_m
    grad_resid = (
        cotangent[0].astype(f32)
        + inv_m * scaled_m
        - inv_m * inv_m * inv_m * resid * jnp.mean(scaled_m * resid, axis=1, keepdims=True)
    )
    grad_gain_m = jnp.sum(grad_normed_m * resid * inv_m, axis=0)
    grad_attn = grad_resid.astype(bf16)
    grad_heads_rows = dot(grad_attn, out_full, ((1,), (1,))).astype(bf16)
    grad_heads = lax.all_to_all(
        grad_heads_rows, "seq", split_axis=1, concat_axis=0, tiled=True
    ).reshape(span_len, heads_here, HEAD)
    grad_out_w = dot(heads_rows, grad_attn, ((0,), (0,))).astype(bf16)
    out_sum = lax.psum_scatter(grad_out_w, "fsdp", scatter_dimension=0, tiled=True)
    out_sum = lax.psum(out_sum, "seq").astype(f32)

    grad_q, grad_k, grad_v = attend_backward(
        queries, key_rows, values, segment, log_total, grad_heads, block_len
    )
    grad_qkv = jnp.stack([grad_q, grad_k, grad_v], axis=1).astype(bf16)
    grad_qkv = grad_qkv.reshape(span_len, 3 * width)
    grad_normed_a = dot(grad_qkv, qkv_own, ((1,), (1,))).astype(bf16)
    grad_normed_a = lax.psum_scatter(
        grad_normed_a, "seq", scatter_dimension=0, tiled=True
    ).astype(f32)
    grad_qkv_w = dot(normed_a, grad_qkv, ((0,), (0,))).astype(bf16)
    qkv_sum = lax.psum_scatter(grad_qkv_w, "fsdp", scatter_dimension=0, tiled=True)
    qkv_sum = lax.all_gather(
        qkv_sum.reshape(shard, 3, width), "seq", axis=2, tiled=True
    ).reshape(shard, 3 * D)
    inv_a = lax.rsqrt(jnp.mean(x_float * x_float, axis=1, keepdims=True) + epsilon)
    scaled_a = grad_normed_a * gain_a
    grad_x = (
        grad_resid
        + inv_a * scaled_a
        - inv_a * inv_a * inv_a * x_float * jnp.mean(scaled_a * x_float, axis=1, keepdims=True)
    )
    grad_gain_a = jnp.sum(grad_normed_a * x_float * inv_a, axis=0)
    gain_sums = lax.psum(jnp.stack([grad_gain_a, grad_gain_m]), ("seq", "fsdp"))
    gain_sums = lax.dynamic_slice_in_dim(gain_sums, at_fsdp * shard, shard, 1)

    own_grads, other_grads = jnp.stack(grads_own), jnp.stack(grads_other)
    first = half == 0
    grad_all = jnp.concatenate(
        [jnp.where(first, own_grads, other_grads), jnp.where(first, other_grads, own_grads)]
    ).astype(f32)
    return (
        mixed[None],
        grad_x.astype(bf16)[None],
        gain_sums[0],
        gain_sums[1],
        qkv_sum.astype(f32),
        out_sum,
        grad_all[:, :, : 2 * FFE].reshape(local_count, shard, 2, FFE),
        jnp.swapaxes(grad_all[:, :, 2 * FFE :], 1, 2),
    )


def solution(mesh):
    placed = (
        P("fsdp", "seq", None),
        P("fsdp", None),
        P("fsdp", "seq", None),
        P("fsdp", "seq", None),
        P("fsdp"),
        P("fsdp"),
        P("fsdp", None),
        P("fsdp", None),
        P("seq", "fsdp", None, None),
        P("seq", None, "fsdp"),
        P("fsdp", "seq", None),
    )
    return jax.shard_map(
        body,
        mesh=mesh,
        in_specs=placed,
        out_specs=(
            P("fsdp", "seq", None),
            P("fsdp", "seq", None),
            P("fsdp"),
            P("fsdp"),
            P("fsdp", None),
            P("fsdp", None),
            P("seq", "fsdp", None, None),
            P("seq", None, "fsdp"),
        ),
        check_vma=False,
    )
```

time: 5380 us -> 2730 us (0.51)
  waiting for transfers between devices: 3620 us -> 1160 us
  local copies, waits for them, and re-layouts: 822 us -> 631 us
  other arithmetic: 154 us -> 287 us
  matrix products: 597 us -> 519 us
  blocking collectives: 102 us -> 47.7 us
    all_gather x34 -> x6, waiting for transfers between devices: 1750 us -> 17.6 us  [the longest x2 17.6 us: to_group(): return lax.all_gather(pair, 'seq', axis=0, tiled=False)]
    reduce_scatter x18 -> x5, waiting for transfers between devices: 1160 us -> 40 us  [the longest x2 40 us: from_group(): lax.psum_scatter(sums.astype(bf16).reshape(-1, width), 'seq', scatter_dim...]
    ppermute x0 -> x29, waiting for transfers between devices: none -> 1100 us  [swap(): return lax.ppermute(value, axis, [(i, i ^ bit) for i in range(size)])]
    all_to_all x7 -> x2, waiting for transfers between devices: 651 us -> 0.01 us  [the longest x1 0.01 us: body(): lax.all_to_all(attended.reshape(span_len, width), 'seq', split_axis=0, co...]
    unnamed x95 -> x250, local copies, waits for them, and re-layouts: 5.06 us -> 290 us
    while x78 -> x42, local copies, waits for them, and re-layouts: 173 us -> 8.55 us
    reshape x14 -> x2, local copies, waits for them, and re-layouts: 121 us -> 18.5 us  [the longest x1 14.4 us: body(): w_gate_up.reshape(local_count, shard, 2 * FFE)]
    all_to_all x10 -> x3, local copies, waits for them, and re-layouts: 89.7 us -> 7.07 us  [the longest x2 5.8 us: body(): lax.all_to_all(attended.reshape(span_len, width), 'seq', split_axis=0, co...]
  transfers between devices with their start and end apart: 60 -> 43, of which waited for: 57 -> 17; matrix products, arithmetic and copies ran while one was open for 22% -> 44% of each run, Pallas kernels for 0% -> 0%
where the time goes in v1:
time: 2730 us; the launch traced here: 2710 us
  waiting for transfers between devices  1160 us (42%)
  local copies, waits for them, and re-layouts  631 us (23%)
  matrix products  519 us (19%)
  other arithmetic  287 us (11%)
  blocking collectives  47.7 us (2%)
  starting transfers between devices  43.7 us (2%)
    ppermute x29, waiting for transfers between devices, swap(): return lax.ppermute(value, axis, [(i, i ^ bit) for i in range(size)])  1100 us
    dot_general x40, matrix products, dot(): return lax.dot_general(a, b, (contract, batch), preferred_element_type=f32)  432 us
    unnamed x250, local copies, waits for them, and re-layouts  290 us
    dynamic_slice x2, local copies, waits for them, and re-layouts, scatter_expert(): kept = lax.dynamic_index_in_dim(piece, mine, 1, keepdims=False)  112 us
    another operation x4, local copies, waits for them, and re-layouts, scatter_expert(): piece = piece.reshape(many, 2, rows, columns)  85 us
    concatenate x4, other arithmetic, body(): jnp.concatenate([dot(slots, grad_proj, ((0,), (0,))).astype(bf16), dot(gr...  57.8 us
  transfers between devices with their start and end apart: 43, of which 17 were waited for; matrix products, arithmetic and copies ran while one was open for 44% of the time, Pallas kernels for 0%

profile of v1, /device:TPU:0, one launch (start us, length us, event | category | flops | bytes accessed | tf_op | source)
XLA Modules:
  0.0 2713.0 jit_solution(1832570662352118285)
XLA Ops:
  57.7 222.0 %collective-permute-done.2 = bf16[1,256,3072]{2,1,0:T(8,128)(2,1)} collective-permute-done((bf16[1,256,3072]{2,1,0:T(8,128)(2,1)}, bf16[1,256,3072]{2,1,0:T(8,128)(2,1)}, u32[]{:S(2)}, u32[]{:S(2)}) %collective-permute-start.2) | collective-permute-done | bytes 1572896 | tf_op jit(solution)/shard_map/ppermute | solution.py:19
  279.7 91.5 %collective-permute-done.8 = bf16[1,256,3072]{2,1,0:T(8,128)(2,1)} collective-permute-done((bf16[1,256,3072]{2,1,0:T(8,128)(2,1)}, bf16[1,256,3072]{2,1,0:T(8,128)(2,1)}, u32[]{:S(2)}, u32[]{:S(2)}) %collective-permute-start.8) | collective-permute-done | bytes 1572896 | tf_op jit(solution)/shard_map/ppermute | solution.py:19
  371.2 43.8 %collective-permute-done.5 = bf16[1,256,3072]{2,1,0:T(8,128)(2,1)} collective-permute-done((bf16[1,256,3072]{2,1,0:T(8,128)(2,1)S(1)}, bf16[1,256,3072]{2,1,0:T(8,128)(2,1)}, u32[]{:S(2)}, u32[]{:S(2)}) %collective-permute-start.5) | collective-permute-done | bytes 1572896 | tf_op jit(solution)/shard_map/ppermute | solution.py:19
  415.0 32.4 %collective-permute-done.11 = bf16[1,256,3072]{2,1,0:T(8,128)(2,1)} collective-permute-done((bf16[1,256,3072]{2,1,0:T(8,128)(2,1)S(1)}, bf16[1,256,3072]{2,1,0:T(8,128)(2,1)}, u32[]{:S(2)}, u32[]{:S(2)}) %collective-permute-start.11) | collective-permute-done | bytes 1572896 | tf_op jit(solution)/shard_map/ppermute | solution.py:19
  464.0 64.5 %collective-permute-done = f32[384,16]{0,1:T(8,128)S(1)} collective-permute-done((f32[384,16]{0,1:T(8,128)S(1)}, f32[384,16]{0,1:T(8,128)S(1)}, u32[]{:S(2)}, u32[]{:S(2)}) %collective-permute-start) | collective-permute-done | bytes 24608 | tf_op jit(solution)/shard_map/ppermute | solution.py:19
  600.9 51.9 %while.29 = (s32[]{:T(128)}, bf16[3,512,4,128]{3,2,1,0:T(4,128)(2,1)}, f32[3,4,512]{2,1,0:T(4,128)}, s32[3]{0:T(128)S(1)}, s32[1536]{0:T(1024)S(1)}, /*index=5*/...) while((s32[]{:T(128)}, ...), condition=%wide.region_8.9_spmd, body=%wide.region_5.8_spmd.sunk | while | flops 1649408000 | bytes 46215344 | solution.py:52
  661.1 103.3 %collective-permute-done.6 = bf16[2,256,3072]{2,1,0:T(8,128)(2,1)} collective-permute-done((bf16[2,256,3072]{2,1,0:T(8,128)(2,1)}, bf16[2,256,3072]{2,1,0:T(8,128)(2,1)}, u32[]{:S(2)}, u32[]{:S(2)}) %collective-permute-start.6) | collective-permute-done | bytes 3145760 | tf_op jit(solution)/shard_map/ppermute | solution.py:19
  791.0 62.3 %collective-permute-done.1 = bf16[384,2048]{1,0:T(8,128)(2,1)S(1)} collective-permute-done((bf16[384,2048]{1,0:T(8,128)(2,1)S(1)}, bf16[384,2048]{1,0:T(8,128)(2,1)S(1)}, u32[]{:S(2)}, u32[]{:S(2)}) %collective-permute-start.1) | collective-permute-done | bytes 1572896 | tf_op jit(solution)/shard_map/ppermute | solution.py:19
  1343.9 21.4 reshape_reshape.31
  1365.4 21.2 reshape_reshape.30
  1386.6 40.0 %reduce-scatter.6.cloned.1.call-done = bf16[768,2048]{1,0:T(8,128)(2,1)} async-done(((bf16[3072,2048]{1,0:T(8,128)(2,1)}), bf16[768,2048]{1,0:T(8,128)(2,1)}) %reduce-scatter.6.cloned.1.call-update) | async-done | bytes 3145744 | tf_op jit(solution)/shard_map/reduce_scatter | solution.py:139
  1442.0 56.9 %collective-permute-done.14 = bf16[384,2048]{1,0:T(8,128)(2,1)S(1)} collective-permute-done((bf16[384,2048]{1,0:T(8,128)(2,1)S(1)}, bf16[384,2048]{1,0:T(8,128)(2,1)S(1)}, u32[]{:S(2)}, u32[]{:S(2)}) %collective-permute-start.14) | collective-permute-done | bytes 1572896 | tf_op jit(solution)/shard_map/ppermute | solution.py:19
  1560.5 104.9 %while.30 = (s32[]{:T(128)}, f32[1536,4,128]{0,2,1:T(8,128)}, f32[1536,4,128]{0,2,1:T(8,128)}, bf16[3,512,4,128]{3,1,0,2:T(8,128)(2,1)}, s32[3]{0:T(128)S(1)}, /...) while((s32[]{:T(128)}, f32[1536,4,128]{0,2,1:T(8,128)}, ...), condition=%wide.region_19.20_spmd.clone, body=%wide.region_17.19_spmd.clone.sunk | while | flops 4059822080 | bytes 186700224 | solution.py:92
  1722.7 21.3 reshape_reshape.32
  1744.0 56.0 %constant_dynamic-slice_fusion.8 = (bf16[4,1,256,3072]{2,1,0,3:T(2,128)(2,1)}, bf16[4,1,256,3072]{2,1,0,3:T(2,128)(2,1)}, bf16[4,1,256,3072]{2,1,0,3:T(2,128)(2,1)}, bf16[4,1,256,3072]{2,1,0,3:T(2,128)(2,1)}) fusion(bf16[4,2,256,3072]{2,1,0,3:T(2,128)(2,1)} %reshape_reshape.32, s32[]{:T(128)S(6)} %select_n.326, s32[]{:T(128)S(6)} %select_n.327, ...), kind=kLoop, calls=%fused_computation.294 | loop fusion | bytes 50331656 | tf_op jit(solution)/shard_map/jit(dynamic_index_in_dim)/dynamic_slice | solution.py:123
  1800.0 25.9 copy.211
  1825.8 56.0 %constant_dynamic-slice_fusion.14 = (bf16[4,1,256,3072]{2,1,0,3:T(2,128)(2,1)}, bf16[4,1,256,3072]{2,1,0,3:T(2,128)(2,1)}, bf16[4,1,256,3072]{2,1,0,3:T(2,128)(2,1)}, bf16[4,1,256,3072]{2,1,0,3:T(2,128)(2,1)}) fusion(bf16[4,2,256,3072]{2,1,0,3:T(2,128)(2,1)} %reshape_reshape.30, s32[]{:T(128)S(6)} %select_n.326, s32[]{:T(128)S(6)} %select_n.327, ...), kind=kLoop, calls=%fused_computation.300 | loop fusion | bytes 50331656 | tf_op jit(solution)/shard_map/jit(dynamic_index_in_dim)/dynamic_slice | solution.py:123
  1881.9 25.9 copy.206
  1908.3 25.9 copy.214
  1934.2 26.0 copy.208
  1976.3 26.2 copy.213
  2002.5 26.1 copy.210
  2028.7 26.0 copy.207
  2054.7 25.8 copy.205
  2122.0 39.2 %collective-permute-done.22 = bf16[2,256,3072]{2,1,0:T(8,128)(2,1)} collective-permute-done((bf16[2,256,3072]{2,1,0:T(8,128)(2,1)}, bf16[2,256,3072]{2,1,0:T(8,128)(2,1)}, u32[]{:S(2)}, u32[]{:S(2)}) %collective-permute-start.22) | collective-permute-done | bytes 3145760 | tf_op jit(solution)/shard_map/ppermute | solution.py:19
  2168.5 93.8 %collective-permute-done.18 = bf16[2,256,3072]{2,1,0:T(8,128)(2,1)} collective-permute-done((bf16[2,256,3072]{2,1,0:T(8,128)(2,1)}, bf16[2,256,3072]{2,1,0:T(8,128)(2,1)}, u32[]{:S(2)}, u32[]{:S(2)}) %collective-permute-start.18) | collective-permute-done | bytes 3145760 | tf_op jit(solution)/shard_map/ppermute | solution.py:19
  2268.3 95.1 %collective-permute-done.20 = bf16[2,256,3072]{2,1,0:T(8,128)(2,1)} collective-permute-done((bf16[2,256,3072]{2,1,0:T(8,128)(2,1)}, bf16[2,256,3072]{2,1,0:T(8,128)(2,1)}, u32[]{:S(2)}, u32[]{:S(2)}) %collective-permute-start.20) | collective-permute-done | bytes 3145760 | tf_op jit(solution)/shard_map/ppermute | solution.py:19
  2369.4 60.4 %collective-permute-done.24 = bf16[2,256,3072]{2,1,0:T(8,128)(2,1)S(1)} collective-permute-done((bf16[2,256,3072]{2,1,0:T(8,128)(2,1)S(1)}, bf16[2,256,3072]{2,1,0:T(8,128)(2,1)S(1)}, u32[]{:S(2)}, u32[]{:S(2)}) %collective-permute-start.24) | collective-permute-done | bytes 3145760 | tf_op jit(solution)/shard_map/ppermute | solution.py:19
  2437.3 95.1 %collective-permute-done.26 = bf16[1,256,3072]{2,1,0:T(8,128)(2,1)} collective-permute-done((bf16[1,256,3072]{2,1,0:T(8,128)(2,1)}, bf16[1,256,3072]{2,1,0:T(8,128)(2,1)}, u32[]{:S(2)}, u32[]{:S(2)}) %collective-permute-start.26) | collective-permute-done | bytes 1572896 | tf_op jit(solution)/shard_map/ppermute | solution.py:19
  2540.4 25.6 collective-permute-done.28
  2620.1 25.3 copy.193
  2647.8 38.6 %psum.14 = f32[2,2048]{1,0:T(2,128)S(1)} all-reduce(f32[2,2048]{1,0:T(2,128)S(1)} %pad_maximum_fusion.31), channel_id=1, replica_groups=mesh['seq'=4,'fsdp'=8] {'seq','fsdp'}, use_global_device_ids=true, to_apply=%region_24.25 | all-reduce | flops 4096 | bytes 32768 | tf_op jit(solution)/shard_map/psum | solution.py:298
  (608 shorter events, 1110.9 us)
Async XLA Ops:
  7.2 564.5 %all-gather.17.cloned.1.call-start = ((), (), s32[]{:S(2)}) async-start(), calls=%async_computation.16 | async-start | bytes 7864320 | tf_op jit(solution)/shard_map/all_gather | solution.py:167
  7.9 567.9 %all-gather.11.cloned.1.call-start = ((), (), s32[]{:S(2)}) async-start(), calls=%async_computation.7 | async-start | bytes 7667712 | tf_op jit(solution)/shard_map/all_gather | solution.py:172
  18.4 755.1 %all-gather.13.cloned.1.call-start = ((), (), s32[]{:S(2)}) async-start(), calls=%async_computation.8 | async-start | bytes 9437184 | tf_op jit(solution)/shard_map/all_gather | solution.py:178
  19.1 899.2 %all-gather.21.cloned.1.call-start = ((), (), s32[]{:S(2)}) async-start(), calls=%async_computation.18 | async-start | bytes 15728640 | tf_op jit(solution)/shard_map/all_gather | solution.py:134
  49.8 229.9 %collective-permute-start.2 = (bf16[1,256,3072]{2,1,0:T(8,128)(2,1)}, bf16[1,256,3072]{2,1,0:T(8,128)(2,1)}, u32[]{:S(2)}, u32[]{:S(2)}) collective-permute-start(bf16[1,256,3072]{2,1,0:T(8,128)(2,1)} %get-tuple-element.347), channel_id=1, source_target_pairs={{0,4},{1,5},{2,6},{3,7},{4,0},{5,1},{6,2},{7,3},{8,12},{9,13},{10,... | collective-permute-start | bytes 4718600 | tf_op jit(solution)/shard_map/ppermute | solution.py:19
  54.8 316.5 %collective-permute-start.8 = (bf16[1,256,3072]{2,1,0:T(8,128)(2,1)}, bf16[1,256,3072]{2,1,0:T(8,128)(2,1)}, u32[]{:S(2)}, u32[]{:S(2)}) collective-permute-start(bf16[1,256,3072]{2,1,0:T(8,128)(2,1)} %get-tuple-element.348), channel_id=1, source_target_pairs={{0,4},{1,5},{2,6},{3,7},{4,0},{5,1},{6,2},{7,3},{8,12},{9,13},{10,... | collective-permute-start | bytes 4718600 | tf_op jit(solution)/shard_map/ppermute | solution.py:19
  54.8 360.3 %collective-permute-start.5 = (bf16[1,256,3072]{2,1,0:T(8,128)(2,1)S(1)}, bf16[1,256,3072]{2,1,0:T(8,128)(2,1)}, u32[]{:S(2)}, u32[]{:S(2)}) collective-permute-start(bf16[1,256,3072]{2,1,0:T(8,128)(2,1)S(1)} %get-tuple-element.349), channel_id=1, source_target_pairs={{0,4},{1,5},{2,6},{3,7},{4,0},{5,1},{6,2},{7,3},{8,12},{9,13},{10,... | collective-permute-start | bytes 4718600 | tf_op jit(solution)/shard_map/ppermute | solution.py:19
  57.7 389.8 %collective-permute-start.11 = (bf16[1,256,3072]{2,1,0:T(8,128)(2,1)S(1)}, bf16[1,256,3072]{2,1,0:T(8,128)(2,1)}, u32[]{:S(2)}, u32[]{:S(2)}) collective-permute-start(bf16[1,256,3072]{2,1,0:T(8,128)(2,1)S(1)} %get-tuple-element.350), channel_id=1, source_target_pairs={{0,4},{1,5},{2,6},{3,7},{4,0},{5,1},{6,2},{7,3},{8,12},{9,13},{10,... | collective-permute-start | bytes 4718600 | tf_op jit(solution)/shard_map/ppermute | solution.py:19
  542.4 315.6 %collective-permute-start.12 = (bf16[2,256,3072]{2,1,0:T(8,128)(2,1)}, bf16[2,256,3072]{2,1,0:T(8,128)(2,1)}, u32[]{:S(2)}, u32[]{:S(2)}) collective-permute-start(bf16[2,256,3072]{2,1,0:T(8,128)(2,1)} %maximum_bitcast_fusion.3), channel_id=1, source_target_pairs={{0,2},{1,3},{2,0},{3,1},{4,6},{5,7},{6,4},{7,5},{8,10},{9,11},{10,... | collective-permute-start | bytes 9437192 | tf_op jit(solution)/shard_map/ppermute | solution.py:19
  548.2 236.4 %collective-permute-start.9 = (bf16[2,256,3072]{2,1,0:T(8,128)(2,1)}, bf16[2,256,3072]{2,1,0:T(8,128)(2,1)}, u32[]{:S(2)}, u32[]{:S(2)}) collective-permute-start(bf16[2,256,3072]{2,1,0:T(8,128)(2,1)} %maximum_bitcast_fusion.2), channel_id=1, source_target_pairs={{0,2},{1,3},{2,0},{3,1},{4,6},{5,7},{6,4},{7,5},{8,10},{9,11},{10,... | collective-permute-start | bytes 9437192 | tf_op jit(solution)/shard_map/ppermute | solution.py:19
  550.1 214.2 %collective-permute-start.6 = (bf16[2,256,3072]{2,1,0:T(8,128)(2,1)}, bf16[2,256,3072]{2,1,0:T(8,128)(2,1)}, u32[]{:S(2)}, u32[]{:S(2)}) collective-permute-start(bf16[2,256,3072]{2,1,0:T(8,128)(2,1)} %maximum_bitcast_fusion.1), channel_id=1, source_target_pairs={{0,2},{1,3},{2,0},{3,1},{4,6},{5,7},{6,4},{7,5},{8,10},{9,11},{10,... | collective-permute-start | bytes 9437192 | tf_op jit(solution)/shard_map/ppermute | solution.py:19
  571.7 296.4 %collective-permute-start.4 = (bf16[4,256,3072]{2,1,0:T(8,128)(2,1)}, bf16[4,256,3072]{2,1,0:T(8,128)(2,1)}, u32[]{:S(2)}, u32[]{:S(2)}) collective-permute-start(bf16[4,256,3072]{2,1,0:T(8,128)(2,1)} %bitcast.37), channel_id=1, source_target_pairs={{0,1},{1,0},{2,3},{3,2},{4,5},{5,4},{6,7},{7,6},{8,9},{9,8},{10,11... | collective-permute-start | bytes 18874376 | tf_op jit(solution)/shard_map/ppermute | solution.py:19
  656.7 114.8 %all-to-all-start = ((bf16[4,384,512]{2,1,0:T(8,128)(2,1)}), bf16[4,384,512]{2,1,0:T(8,128)(2,1)}, u32[]{:S(2)}, u32[]{:S(2)}) async-start(bf16[4,384,512]{2,1,0:T(8,128)(2,1)} %all_to_all.26), calls=%async_computation | async-start | bytes 3145728 | tf_op jit(solution)/shard_map/all_to_all | solution.py:209
  661.0 320.9 %all-gather.19.cloned.1.call-start = ((), (), s32[]{:S(2)}) async-start(), calls=%async_computation.17 | async-start | bytes 15728640 | tf_op jit(solution)/shard_map/all_gather | solution.py:134
  858.0 467.4 %reduce-scatter.8.cloned.1.call-start = ((), (), s32[]{:S(2)}) async-start(), calls=%async_computation.10 | async-start | bytes 15728640 | tf_op jit(solution)/shard_map/reduce_scatter | solution.py:139
  1181.3 245.3 %reduce-scatter.6.cloned.1.call-start = ((), (), s32[]{:S(2)}) async-start(), calls=%async_computation.9 | async-start | bytes 15728640 | tf_op jit(solution)/shard_map/reduce_scatter | solution.py:139
  1512.4 921.7 %reduce-scatter.14.cloned.1.call-start = ((), (), s32[]{:S(2)}) async-start(), calls=%async_computation.14 | async-start | bytes 9437184 | tf_op jit(solution)/shard_map/reduce_scatter | solution.py:273
  1556.3 978.8 %reduce-scatter.12.cloned.1.call-start = ((), (), s32[]{:S(2)}) async-start(), calls=%async_computation.12 | async-start | bytes 7077888 | tf_op jit(solution)/shard_map/reduce_scatter | solution.py:286
  1698.1 947.4 %reduce-scatter.10.cloned.1.call-start = ((), (), s32[]{:S(2)}) async-start(), calls=%async_computation.11 | async-start | bytes 7864320 | tf_op jit(solution)/shard_map/reduce_scatter | solution.py:282
  1825.8 254.6 %collective-permute-start.21 = (bf16[4,256,3072]{2,1,0:T(8,128)(2,1)}, bf16[4,256,3072]{2,1,0:T(8,128)(2,1)}, u32[]{:S(2)}, u32[]{:S(2)}) collective-permute-start(bf16[4,256,3072]{2,1,0:T(8,128)(2,1)} %bitcast.441), channel_id=1, source_target_pairs={{0,1},{1,0},{2,3},{3,2},{4,5},{5,4},{6,7},{7,6},{8,9},{9,8},{10,11... | collective-permute-start | bytes 18874376 | tf_op jit(solution)/shard_map/ppermute | solution.py:19
  1907.8 183.6 %collective-permute-start.17 = (bf16[4,256,3072]{2,1,0:T(8,128)(2,1)}, bf16[4,256,3072]{2,1,0:T(8,128)(2,1)}, u32[]{:S(2)}, u32[]{:S(2)}) collective-permute-start(bf16[4,256,3072]{2,1,0:T(8,128)(2,1)} %bitcast.442), channel_id=1, source_target_pairs={{0,1},{1,0},{2,3},{3,2},{4,5},{5,4},{6,7},{7,6},{8,9},{9,8},{10,11... | collective-permute-start | bytes 18874376 | tf_op jit(solution)/shard_map/ppermute | solution.py:19
  1934.2 179.3 %collective-permute-start.23 = (bf16[4,256,3072]{2,1,0:T(8,128)(2,1)}, bf16[4,256,3072]{2,1,0:T(8,128)(2,1)}, u32[]{:S(2)}, u32[]{:S(2)}) collective-permute-start(bf16[4,256,3072]{2,1,0:T(8,128)(2,1)} %bitcast.440), channel_id=1, source_target_pairs={{0,1},{1,0},{2,3},{3,2},{4,5},{5,4},{6,7},{7,6},{8,9},{9,8},{10,11... | collective-permute-start | bytes 18874376 | tf_op jit(solution)/shard_map/ppermute | solution.py:19
  1960.1 142.3 %collective-permute-start.19 = (bf16[4,256,3072]{2,1,0:T(8,128)(2,1)}, bf16[4,256,3072]{2,1,0:T(8,128)(2,1)}, u32[]{:S(2)}, u32[]{:S(2)}) collective-permute-start(bf16[4,256,3072]{2,1,0:T(8,128)(2,1)} %bitcast.443), channel_id=1, source_target_pairs={{0,1},{1,0},{2,3},{3,2},{4,5},{5,4},{6,7},{7,6},{8,9},{9,8},{10,11... | collective-permute-start | bytes 18874376 | tf_op jit(solution)/shard_map/ppermute | solution.py:19
  1976.3 715.2 %all-reduce.3.cloned.1.call-start = ((), (), s32[]{:S(2)}) async-start(), calls=%async_computation.15 | async-start | bytes 2097152 | tf_op jit(solution)/shard_map/psum | solution.py:274
  2100.9 161.4 %collective-permute-start.18 = (bf16[2,256,3072]{2,1,0:T(8,128)(2,1)}, bf16[2,256,3072]{2,1,0:T(8,128)(2,1)}, u32[]{:S(2)}, u32[]{:S(2)}) collective-permute-start(bf16[2,256,3072]{2,1,0:T(8,128)(2,1)} %dynamic-slice_bitcast_fusion.3), channel_id=1, source_target_pairs={{0,2},{1,3},{2,0},{3,1},{4,6},{5,7},{6,4},{7,5},{8,10},{9,11},{10,... | collective-permute-start | bytes 9437192 | tf_op jit(solution)/shard_map/ppermute | solution.py:19
  2112.0 251.4 %collective-permute-start.20 = (bf16[2,256,3072]{2,1,0:T(8,128)(2,1)}, bf16[2,256,3072]{2,1,0:T(8,128)(2,1)}, u32[]{:S(2)}, u32[]{:S(2)}) collective-permute-start(bf16[2,256,3072]{2,1,0:T(8,128)(2,1)} %dynamic-slice_bitcast_fusion.2), channel_id=1, source_target_pairs={{0,2},{1,3},{2,0},{3,1},{4,6},{5,7},{6,4},{7,5},{8,10},{9,11},{10,... | collective-permute-start | bytes 9437192 | tf_op jit(solution)/shard_map/ppermute | solution.py:19
  2121.3 308.5 %collective-permute-start.24 = (bf16[2,256,3072]{2,1,0:T(8,128)(2,1)S(1)}, bf16[2,256,3072]{2,1,0:T(8,128)(2,1)S(1)}, u32[]{:S(2)}, u32[]{:S(2)}) collective-permute-start(bf16[2,256,3072]{2,1,0:T(8,128)(2,1)S(1)} %dynamic-slice_bitcast_fusion), channel_id=1, source_target_pairs={{0,2},{1,3},{2,0},{3,1},{4,6},{5,7},{6,4},{7,5},{8,10},{9,11},{10,... | collective-permute-start | bytes 9437192 | tf_op jit(solution)/shard_map/ppermute | solution.py:19
  2167.0 370.6 %collective-permute-start.27 = (bf16[1,256,3072]{2,1,0:T(8,128)(2,1)}, bf16[1,256,3072]{2,1,0:T(8,128)(2,1)}, u32[]{:S(2)}, u32[]{:S(2)}) collective-permute-start(bf16[1,256,3072]{2,1,0:T(8,128)(2,1)} %get-tuple-element.365), channel_id=1, source_target_pairs={{0,4},{1,5},{2,6},{3,7},{4,0},{5,1},{6,2},{7,3},{8,12},{9,13},{10,... | collective-permute-start | bytes 4718600 | tf_op jit(solution)/shard_map/ppermute | solution.py:19
  2267.2 167.4 %collective-permute-start.25 = (bf16[1,256,3072]{2,1,0:T(8,128)(2,1)}, bf16[1,256,3072]{2,1,0:T(8,128)(2,1)}, u32[]{:S(2)}, u32[]{:S(2)}) collective-permute-start(bf16[1,256,3072]{2,1,0:T(8,128)(2,1)} %get-tuple-element.361), channel_id=1, source_target_pairs={{0,4},{1,5},{2,6},{3,7},{4,0},{5,1},{6,2},{7,3},{8,12},{9,13},{10,... | collective-permute-start | bytes 4718600 | tf_op jit(solution)/shard_map/ppermute | solution.py:19
  2368.3 164.1 %collective-permute-start.26 = (bf16[1,256,3072]{2,1,0:T(8,128)(2,1)}, bf16[1,256,3072]{2,1,0:T(8,128)(2,1)}, u32[]{:S(2)}, u32[]{:S(2)}) collective-permute-start(bf16[1,256,3072]{2,1,0:T(8,128)(2,1)} %get-tuple-element.363), channel_id=1, source_target_pairs={{0,4},{1,5},{2,6},{3,7},{4,0},{5,1},{6,2},{7,3},{8,12},{9,13},{10,... | collective-permute-start | bytes 4718600 | tf_op jit(solution)/shard_map/ppermute | solution.py:19
  2432.9 133.1 %collective-permute-start.28 = (bf16[1,256,3072]{2,1,0:T(8,128)(2,1)}, bf16[1,256,3072]{2,1,0:T(8,128)(2,1)}, u32[]{:S(2)}, u32[]{:S(2)}) collective-permute-start(bf16[1,256,3072]{2,1,0:T(8,128)(2,1)} %get-tuple-element.367), channel_id=1, source_target_pairs={{0,4},{1,5},{2,6},{3,7},{4,0},{5,1},{6,2},{7,3},{8,12},{9,13},{10,... | collective-permute-start | bytes 4718600 | tf_op jit(solution)/shard_map/ppermute | solution.py:19
  2434.2 260.1 %all-gather.15.cloned.1.call-start = ((), (), s32[]{:S(2)}) async-start(), calls=%async_computation.13 | async-start | bytes 3932160 | tf_op jit(solution)/shard_map/all_gather | solution.py:287
  (147 other events, 4171.8 us)
Sparse Core Ops, SparseCore 0:
  9.8 72.8 all-gather.16
  84.3 190.9 all-gather.10
  276.9 116.0 all-gather.12
  566.4 140.9 all-gather.20
  858.1 123.7 all-gather.18
  1181.4 120.7 reduce-scatter.7
  1305.8 120.7 reduce-scatter.5
  1556.4 90.9 reduce-scatter.13
  1698.2 70.9 reduce-scatter.11
  1976.4 71.3 reduce-scatter.9
  2434.3 53.0 all-reduce.2
  2537.6 42.8 all-gather.14

commit v2 on v1

--- a/solution.py
+++ b/solution.py
@@ -1,6 +1,8 @@
 import jax
 import jax.numpy as jnp
 from jax import lax
+from jax.experimental import pallas as pl
+from jax.experimental.pallas import tpu as pltpu
 from jax.sharding import PartitionSpec as P
 
 D = 2048
@@ -93,54 +95,238 @@
     return (grad_q.reshape(span_len, heads_now, head_dim), grad_k, grad_v)
 
 
-def gather_expert(own, other):
+def after(value, *others):
+    return lax.optimization_barrier((value, *others))[0]
+
+
+def reversed_bits(index, size):
+    count, total = size.bit_length() - 1, 0
+    for bit in range(count):
+        total = total + (((index >> bit) & 1) << (count - 1 - bit))
+    return total
+
+
+def start_expert(mine, sent, start):
     size = lax.axis_size("fsdp")
-    place = lax.axis_index("fsdp")
-    rows, columns = own.shape
+    mine = after(mine, start)
+    pieces = {0: mine, size // 2: swap(after(sent, start), "fsdp", size // 2)}
+    bit = size // 4
+    while bit:
+        pieces[bit] = swap(mine, "fsdp", bit)
+        bit //= 2
+    return pieces
+
+
+def finish_expert(pieces, middle):
+    size = lax.axis_size("fsdp")
+    pieces = dict(pieces)
+    for j in sorted(range(size), key=lambda j: (j & 1, j.bit_count())):
+        if j not in pieces:
+            low = j & -j
+            pieces[j] = swap(after(pieces[j ^ low], middle), "fsdp", low)
+    return [pieces[j] for j in range(size)]
+
+
+def gather_rows(piece, axis):
+    place, rows = lax.axis_index(axis), piece.shape[0]
+    whole = jnp.zeros((lax.axis_size(axis) * rows, *piece.shape[1:]), piece.dtype)
+    for k in range(lax.axis_size(axis)):
+        part = swap(piece, axis, k) if k else piece
+        whole = lax.dynamic_update_slice_in_dim(whole, part, (place ^ k) * rows, 0)
+    return whole
+
+
+def scatter_rows(sums, axis):
+    place, rows = lax.axis_index(axis), sums.shape[0] // lax.axis_size(axis)
+    parts = [
+        lax.dynamic_slice_in_dim(sums, (place ^ k) * rows, rows, 0)
+        for k in range(lax.axis_size(axis))
+    ]
+    return sum((swap(part, axis, k) if k else part).astype(f32) for k, part in enumerate(parts))
+
+
+def gather_doubling(piece, axis, start):
+    size, place = lax.axis_size(axis), lax.axis_index(axis)
+    rows = piece.shape[0]
+    whole = after(piece, start)[None]
     bit = size // 2
-    piece, sent = own[None], other[None]
     while bit:
-        received = swap(sent, "fsdp", bit)
-        low = ((place // bit) % 2) == 0
-        piece = jnp.stack(
-            [jnp.where(low, piece, received), jnp.where(low, received, piece)], axis=1
-        ).reshape(-1, rows, columns)
-        sent = piece
+        received = swap(whole, axis, bit)
+        low = (place // bit) % 2 == 0
+        whole = jnp.stack(
+            [jnp.where(low, whole, received), jnp.where(low, received, whole)], axis=1
+        ).reshape(-1, *piece.shape)
         bit //= 2
-    return piece.reshape(-1, columns)
-
-
-def scatter_expert(grad):
-    size = lax.axis_size("fsdp")
-    place = lax.axis_index("fsdp")
-    columns = grad.shape[1]
-    rows = grad.shape[0] // size
-    bit, many = 1, size // 2
-    piece = grad.reshape(size, rows, columns)
-    while bit < size:
-        mine = (place // bit) % 2
-        piece = piece.reshape(many, 2, rows, columns)
-        kept = lax.dynamic_index_in_dim(piece, mine, 1, keepdims=False)
-        received = swap(lax.dynamic_index_in_dim(piece, 1 - mine, 1, keepdims=False), "fsdp", bit)
-        if many == 1:
-            return kept[0], received[0]
-        piece = (kept.astype(f32) + received.astype(f32)).astype(bf16)
-        bit *= 2
-        many //= 2
-
-
-def to_group(rows):
-    pair = jnp.stack([rows, swap(rows, "fsdp", lax.axis_size("fsdp") // 2)])
-    return lax.all_gather(pair, "seq", axis=0, tiled=False)
-
-
-def from_group(sums):
-    rows, width = sums.shape[2:]
-    mine = lax.psum_scatter(
-        sums.astype(bf16).reshape(-1, width), "seq", scatter_dimension=0, tiled=True
-    )
-    other = swap(mine[rows:], "fsdp", lax.axis_size("fsdp") // 2)
-    return mine[:rows].astype(f32) + other.astype(f32)
+    return whole.reshape(-1, *piece.shape[1:])
+
+
+def expert_kernel(size, tiles, part, place_ref, share_ref, *rest):
+    slots, pieces, rest = rest[:4], rest[4 : 4 + size], rest[4 + size :]
+    made_ref, back_ref, send_ref, keep_ref, weights, x_ref, g_ref, act, grad_proj, sems = rest
+    step = pl.program_id(0)
+    place = place_ref[0]
+    rows = weights.shape[0] // size
+    ffe = act.shape[1]
+    wide = ffe // tiles
+    nn, nt, tn = ((1,), (0,)), ((1,), (1,)), ((0,), (0,))
+
+    @pl.when(step == 0)
+    def _():
+        copies = [
+            pltpu.make_async_copy(
+                pieces[j].at[part],
+                weights.at[pl.ds(pl.multiple_of((place ^ j) * rows, rows), rows)],
+                sems.at[j],
+            )
+            for j in range(size)
+        ]
+        count = slots[0].shape[0]
+        for k, slot in enumerate(slots):
+            copies.append(
+                pltpu.make_async_copy(
+                    slot,
+                    (x_ref, g_ref)[k // 2].at[pl.ds(k % 2 * count, count)],
+                    sems.at[size + k],
+                )
+            )
+        for copy in copies:
+            copy.start()
+        for copy in copies:
+            copy.wait()
+
+    @pl.when(step < tiles)
+    def _():
+        first = pl.multiple_of(step * wide, wide)
+        gate = dot(x_ref[...], weights[:, pl.ds(first, wide)], nn)
+        up = dot(x_ref[...], weights[:, pl.ds(pl.multiple_of(ffe + first, wide), wide)], nn)
+        grad_act = dot(
+            g_ref[...], weights[:, pl.ds(pl.multiple_of(2 * ffe + first, wide), wide)], nn
+        )
+        sigma = 1.0 / (1.0 + jnp.exp(-gate))
+        silu = gate * sigma
+        act[:, pl.ds(first, wide)] = (silu * up).astype(bf16)
+        grad_proj[:, pl.ds(first, wide)] = (
+            grad_act * up * (sigma * (1.0 + gate * (1.0 - sigma)))
+        ).astype(bf16)
+        grad_proj[:, pl.ds(pl.multiple_of(ffe + first, wide), wide)] = (grad_act * silu).astype(
+            bf16
+        )
+
+    @pl.when(step >= tiles)
+    def _():
+        turn = step - tiles
+        whose = place ^ reversed_bits((turn + size // 2) % size, size)
+        at = pl.ds(pl.multiple_of(whose * rows, rows), rows)
+        made_ref[...] = (
+            share_ref[...] * dot(act[...], weights[at, 2 * ffe :], nt)
+        ).astype(bf16)
+        back_ref[...] = dot(grad_proj[...], weights[at, : 2 * ffe], nt).astype(bf16)
+
+        def grads(out_ref):
+            out_ref[0, :, : 2 * ffe] = dot(x_ref[:, at], grad_proj[...], tn).astype(bf16)
+            out_ref[0, :, 2 * ffe :] = dot(g_ref[:, at], act[...], tn).astype(bf16)
+
+        @pl.when(turn < size // 2)
+        def _():
+            grads(send_ref)
+
+        @pl.when(turn >= size // 2)
+        def _():
+            grads(keep_ref)
+
+
+def run_expert(place, share, slots, grad_slots, pieces, part):
+    size, (_, rows, columns) = len(pieces), pieces[0].shape
+    count = 2 * slots[0].shape[0]
+    ffe = columns // 3
+    tiles = 4
+    half = size // 2
+
+    def whose(step, place):
+        turn = jnp.maximum(step - tiles, 0)
+        return 0, place[0] ^ reversed_bits((turn + half) % size, size)
+
+    flops = 2 * count * D * ffe * 9
+    return pl.pallas_call(
+        lambda *refs: expert_kernel(size, tiles, part, *refs),
+        out_shape=[
+            jax.ShapeDtypeStruct((count, D), bf16),
+            jax.ShapeDtypeStruct((count, D), bf16),
+            jax.ShapeDtypeStruct((half, rows, columns), bf16),
+            jax.ShapeDtypeStruct((half, rows, columns), bf16),
+        ],
+        grid_spec=pltpu.PrefetchScalarGridSpec(
+            num_scalar_prefetch=1,
+            grid=(tiles + size,),
+            in_specs=[
+                pl.BlockSpec((count, 1), lambda step, place: (0, 0)),
+                *[pl.BlockSpec(memory_space=pl.ANY)] * (size + 4),
+            ],
+            out_specs=[
+                pl.BlockSpec((count, rows), whose),
+                pl.BlockSpec((count, rows), whose),
+                pl.BlockSpec(
+                    (1, rows, columns), lambda t, place: (jnp.clip(t - tiles, 0, half - 1), 0, 0)
+                ),
+                pl.BlockSpec(
+                    (1, rows, columns),
+                    lambda t, place: (jnp.clip(t - tiles - half, 0, half - 1), 0, 0),
+                ),
+            ],
+            scratch_shapes=[
+                pltpu.VMEM((size * rows, columns), bf16),
+                pltpu.VMEM((count, D), bf16),
+                pltpu.VMEM((count, D), bf16),
+                pltpu.VMEM((count, ffe), bf16),
+                pltpu.VMEM((count, 2 * ffe), bf16),
+                pltpu.SemaphoreType.DMA((size + 4,)),
+            ],
+        ),
+        compiler_params=pltpu.CompilerParams(
+            dimension_semantics=("arbitrary",), vmem_limit_bytes=60 * 2**20
+        ),
+        cost_estimate=pl.CostEstimate(
+            flops=flops, bytes_accessed=8 * count * D + 8 * size * rows * columns, transcendentals=0
+        ),
+        name="expert",
+    )(place, share, *slots, *grad_slots, *pieces)
+
+
+class GradChain:
+    def __init__(self, send, keep):
+        self.bit, self.size = 1, lax.axis_size("fsdp")
+        self.terms, self.send = [keep], send
+
+    def sums(self):
+        if self.bit == self.size:
+            return self.terms[-1]
+        received = swap(self.send, "fsdp", self.bit)
+        self.terms.append(received)
+        self.bit *= 2
+        many = self.terms[0].shape[0] // 2
+        if many:
+            total = sum(t[many:].astype(f32) for t in self.terms)
+            self.send = total.astype(bf16)
+            self.terms = [t[:many] for t in self.terms]
+            return self.send
+        return received
+
+    def ended(self):
+        other = self.terms.pop()[0]
+        return sum(t[0].astype(f32) for t in self.terms).astype(bf16), other
+
+
+def to_group(rows, *others):
+    own = lax.all_gather(rows, "seq", axis=0, tiled=False)
+    swapped = swap(after(rows, *others) if others else rows, "fsdp", lax.axis_size("fsdp") // 2)
+    return own, lax.all_gather(swapped, "seq", axis=0, tiled=False), swapped
+
+
+def from_group(sums_own, sums_other):
+    mine = lax.psum_scatter(sums_other, "seq", scatter_dimension=0, tiled=True)
+    other = swap(mine, "fsdp", lax.axis_size("fsdp") // 2)
+    mine = lax.psum_scatter(sums_own, "seq", scatter_dimension=0, tiled=True)
+    return mine.astype(f32) + other.astype(f32)
 
 
 def body(
@@ -162,9 +348,7 @@
     )
     own_part = lax.dynamic_slice_in_dim(packed, half * per_half, per_half, 0)
     other_part = lax.dynamic_slice_in_dim(packed, (1 - half) * per_half, per_half, 0)
-    experts = [gather_expert(own_part[i], other_part[i]) for i in range(per_half)]
-
-    x_all = lax.all_gather(tokens[0], "seq", axis=0, tiled=True)
+    x_all = gather_rows(tokens[0], "seq")
     part = lax.dynamic_slice_in_dim(
         w_qkv.reshape(shard, 3, HEADS, HEAD), at_seq * heads_here, heads_here, 2
     ).reshape(shard, 3 * width)
@@ -175,10 +359,11 @@
     qkv_own = gathered[:, : 3 * width]
     gain_a = gathered[:, 3 * width].astype(f32)
     gain_m = gathered[:, 3 * width + 1].astype(f32)
-    out_full = lax.all_gather(w_out, "fsdp", axis=0, tiled=True)
-
+    out_full = gather_doubling(w_out, "fsdp", gathered)
+
+    parts = per_half // 2
     routing = jnp.concatenate([routes[0].astype(f32), gates[0]], axis=1)
-    routing = to_group(routing).reshape(2 * n_seq, rows, 2 * TOP)
+    routing = jnp.stack(to_group(routing)[:2]).reshape(2 * n_seq, rows, 2 * TOP)
     capacity = rows * TOP * 4 // (3 * local_count * n_seq) + 2
     capacity = -(-capacity // 8) * 8
     named = at_seq * local_count + half * per_half + lax.iota(jnp.int32, per_half)
@@ -193,13 +378,13 @@
         jnp.where(picks, jnp.swapaxes(weight, 1, 2)[:, :, None, :], 0.0), axis=3
     )
     picks = picks.astype(bf16)
-    cot_all = to_group(cotangent[0]).reshape(2 * n_seq, rows, D)
+    cot_all = to_group(after(cotangent[0], x_all, gathered))
 
     def normed_rows(values, gain):
         inverse = lax.rsqrt(jnp.mean(values * values, axis=1, keepdims=True) + epsilon)
         return (values * inverse * gain).astype(bf16), inverse
 
-    normed_a, _ = normed_rows(x_all.astype(f32), gain_a)
+    normed_a, inv_all = normed_rows(x_all.astype(f32), gain_a)
     qkv = dot(normed_a, qkv_own, ((1,), (0,))).astype(bf16)
     spread = qkv.reshape(span_len, 3, heads_here, HEAD)
     segment = segment_ids(lengths[0], span_len)
@@ -209,53 +394,65 @@
     heads_rows = lax.all_to_all(
         attended.reshape(span_len, width), "seq", split_axis=0, concat_axis=1, tiled=True
     )
+    first_part = start_expert(own_part[:2], other_part[:2], gathered)
+    heads_rows = after(heads_rows, *first_part.values())
     x_float = tokens[0].astype(f32)
     resid = x_float + dot(heads_rows, out_full, ((1,), (0,)))
     normed_m, inv_m = normed_rows(resid, gain_m)
-    moe_all = to_group(normed_m).reshape(2 * n_seq, rows, D)
-
-    forward_parts, backward_parts, grads_own, grads_other = [], [], [], []
+    moe_all = to_group(normed_m)
+
+    begun = [first_part]
+    for c in range(1, parts):
+        begun.append(
+            start_expert(
+                own_part[2 * c : 2 * c + 2], other_part[2 * c : 2 * c + 2], moe_all[2]
+            )
+        )
+    experts = [
+        finish_expert(begun[c], heads_rows if c == 0 else moe_all[1]) for c in range(parts)
+    ]
+
+    place = jnp.full((1,), at_fsdp, jnp.int32)
+    forward_parts, backward_parts, chains = [], [], []
+    slots_of, grad_slots_of = [], []
     for i in range(per_half):
-        expert = experts[i]
-        gate_up, down_t = expert[:, : 2 * FFE], expert[:, 2 * FFE :]
-        pick = picks[:, i]
-        share_i = share[:, i].reshape(-1, 1)
-        slots = dot(pick, moe_all, ((2,), (1,)), ((0,), (0,))).astype(bf16).reshape(-1, D)
-        grad_slots = dot(pick, cot_all, ((2,), (1,)), ((0,), (0,))).reshape(-1, D)
-        grad_slots = (share_i * grad_slots).astype(bf16)
-        proj = dot(slots, gate_up, ((1,), (0,)))
-        gate_v, up_v = proj[:, :FFE], proj[:, FFE:]
-        sigma = jax.nn.sigmoid(gate_v)
-        silu_v = gate_v * sigma
-        act = (silu_v * up_v).astype(bf16)
-        produced = (share_i * dot(act, down_t, ((1,), (1,)))).astype(bf16)
-        grad_act = dot(grad_slots, down_t, ((1,), (0,)))
-        grad_gate = grad_act * up_v * (sigma * (1.0 + gate_v * (1.0 - sigma)))
-        grad_up = grad_act * silu_v
-        grad_proj = jnp.concatenate([grad_gate.astype(bf16), grad_up.astype(bf16)], axis=1)
-        grad_in = dot(grad_proj, gate_up, ((1,), (1,))).astype(bf16)
-        grad_expert = jnp.concatenate(
-            [
-                dot(slots, grad_proj, ((0,), (0,))).astype(bf16),
-                dot(grad_slots, act, ((0,), (0,))).astype(bf16),
-            ],
-            axis=1,
-        )
-        forward_parts.append(produced.reshape(2 * n_seq, capacity, D))
-        backward_parts.append(grad_in.reshape(2 * n_seq, capacity, D))
-        mine, theirs = scatter_expert(grad_expert)
-        grads_own.append(mine)
-        grads_other.append(theirs)
-
-    every_pick = picks.reshape(2 * n_seq, per_half * capacity, rows)
-
-    def combine(parts):
-        together = jnp.concatenate(parts, axis=1)
-        sums = dot(every_pick, together, ((1,), (1,)), ((0,), (0,)))
-        return from_group(sums.reshape(n_seq, 2, rows, D))
-
-    grad_normed_m = combine(backward_parts)
-    mixed = (resid + combine(forward_parts)).astype(bf16)
+        for g in range(2):
+            pick = picks[g * n_seq : (g + 1) * n_seq, i]
+            share_i = share[g * n_seq : (g + 1) * n_seq, i].reshape(-1, 1)
+            slots = dot(pick, moe_all[g], ((2,), (1,)), ((0,), (0,))).astype(bf16)
+            slots_of.append(slots.reshape(-1, D))
+            grad_slots = dot(pick, cot_all[g], ((2,), (1,)), ((0,), (0,))).reshape(-1, D)
+            grad_slots_of.append((share_i * grad_slots).astype(bf16))
+    for i in range(per_half):
+        slots = slots_of[2 * i : 2 * i + 2]
+        if i >= 2:
+            slots = [after(slots[0], chains[i - 2].sums()), slots[1]]
+        elif i < 1 and parts > 1:
+            slots = [after(slots[0], begun[1][n_fsdp // 2]), slots[1]]
+        made, back, send, keep = run_expert(
+            place,
+            share[:, i].reshape(-1, 1),
+            slots,
+            grad_slots_of[2 * i : 2 * i + 2],
+            experts[i // 2],
+            i % 2,
+        )
+        forward_parts.append(made.reshape(2, n_seq, capacity, D))
+        backward_parts.append(back.reshape(2, n_seq, capacity, D))
+        chains.append(GradChain(send, keep))
+
+    every_pick = picks.reshape(2, n_seq, per_half * capacity, rows)
+
+    def combine(parts, *others):
+        sums = []
+        for g in range(2):
+            together = after(jnp.concatenate([part[g] for part in parts], axis=1), *others)
+            total = dot(every_pick[g], together, ((1,), (1,)), ((0,), (0,)))
+            sums.append(total.astype(bf16).reshape(span_len, D))
+        return from_group(*sums)
+
+    grad_normed_m = combine(backward_parts, chains[0].sums())
+    grad_normed_m = after(grad_normed_m, *[chain.sums() for chain in chains[1:]])
 
     scaled_m = grad_normed_m * gain_m
     grad_resid = (
@@ -265,6 +462,7 @@
     )
     grad_gain_m = jnp.sum(grad_normed_m * resid * inv_m, axis=0)
     grad_attn = grad_resid.astype(bf16)
+    mixed = (resid + combine(forward_parts, grad_attn)).astype(bf16)
     grad_heads_rows = dot(grad_attn, out_full, ((1,), (1,))).astype(bf16)
     grad_heads = lax.all_to_all(
         grad_heads_rows, "seq", split_axis=1, concat_axis=0, tiled=True
@@ -273,19 +471,27 @@
     out_sum = lax.psum_scatter(grad_out_w, "fsdp", scatter_dimension=0, tiled=True)
     out_sum = lax.psum(out_sum, "seq").astype(f32)
 
+    grad_heads = after(grad_heads, *[chain.sums() for chain in chains])
+
     grad_q, grad_k, grad_v = attend_backward(
         queries, key_rows, values, segment, log_total, grad_heads, block_len
     )
     grad_qkv = jnp.stack([grad_q, grad_k, grad_v], axis=1).astype(bf16)
-    grad_qkv = grad_qkv.reshape(span_len, 3 * width)
-    grad_normed_a = dot(grad_qkv, qkv_own, ((1,), (1,))).astype(bf16)
-    grad_normed_a = lax.psum_scatter(
-        grad_normed_a, "seq", scatter_dimension=0, tiled=True
-    ).astype(f32)
+    grad_qkv = after(grad_qkv.reshape(span_len, 3 * width), mixed)
+    part_normed_a = dot(grad_qkv, qkv_own, ((1,), (1,)))
+    grad_normed_a = scatter_rows(part_normed_a.astype(bf16), "seq")
+    part_gain_a = jnp.sum(part_normed_a * x_all.astype(f32) * inv_all, axis=0)
+    gain_columns = jnp.zeros((D, 128), bf16)
+    gain_columns = gain_columns.at[:, 0].set(part_gain_a.astype(bf16))
+    gain_columns = gain_columns.at[:, 1].set(grad_gain_m.astype(bf16))
     grad_qkv_w = dot(normed_a, grad_qkv, ((0,), (0,))).astype(bf16)
-    qkv_sum = lax.psum_scatter(grad_qkv_w, "fsdp", scatter_dimension=0, tiled=True)
-    qkv_sum = lax.all_gather(
-        qkv_sum.reshape(shard, 3, width), "seq", axis=2, tiled=True
+    qkv_sum = lax.psum_scatter(
+        jnp.concatenate([grad_qkv_w, gain_columns], axis=1), "fsdp", scatter_dimension=0, tiled=True
+    )
+    qkv_sum = lax.all_gather(qkv_sum, "seq", axis=0, tiled=False)
+    gain_sums = jnp.sum(qkv_sum[:, :, 3 * width : 3 * width + 2].astype(f32), axis=0)
+    qkv_sum = jnp.transpose(
+        qkv_sum[:, :, : 3 * width].reshape(n_seq, shard, 3, width), (1, 2, 0, 3)
     ).reshape(shard, 3 * D)
     inv_a = lax.rsqrt(jnp.mean(x_float * x_float, axis=1, keepdims=True) + epsilon)
     scaled_a = grad_normed_a * gain_a
@@ -294,11 +500,12 @@
         + inv_a * scaled_a
         - inv_a * inv_a * inv_a * x_float * jnp.mean(scaled_a * x_float, axis=1, keepdims=True)
     )
-    grad_gain_a = jnp.sum(grad_normed_a * x_float * inv_a, axis=0)
-    gain_sums = lax.psum(jnp.stack([grad_gain_a, grad_gain_m]), ("seq", "fsdp"))
-    gain_sums = lax.dynamic_slice_in_dim(gain_sums, at_fsdp * shard, shard, 1)
-
-    own_grads, other_grads = jnp.stack(grads_own), jnp.stack(grads_other)
+
+    for chain in chains:
+        while chain.bit < n_fsdp:
+            chain.sums()
+    ended = [chain.ended() for chain in chains]
+    own_grads, other_grads = jnp.stack([e[0] for e in ended]), jnp.stack([e[1] for e in ended])
     first = half == 0
     grad_all = jnp.concatenate(
         [jnp.where(first, own_grads, other_grads), jnp.where(first, other_grads, own_grads)]
@@ -306,8 +513,8 @@
     return (
         mixed[None],
         grad_x.astype(bf16)[None],
-        gain_sums[0],
-        gain_sums[1],
+        gain_sums[:, 0],
+        gain_sums[:, 1],
         qkv_sum.astype(f32),
         out_sum,
         grad_all[:, :, : 2 * FFE].reshape(local_count, shard, 2, FFE),

time: 2730 us -> 2130 us (0.78)
  local copies, waits for them, and re-layouts: 631 us -> 220 us
  matrix products: 519 us -> 265 us
  Pallas kernels: 0 us -> 244 us
  other arithmetic: 287 us -> 203 us
  waiting for transfers between devices: 1160 us -> 1090 us
  blocking collectives: 47.7 us -> 17.5 us
    dot_general x40 -> x26, matrix products: 432 us -> 155 us  [dot(): return lax.dot_general(a, b, (contract, batch), preferred_element_type=f32)]
    ppermute x29 -> x40, waiting for transfers between devices: 1100 us -> 840 us  [swap(): return lax.ppermute(value, axis, [(i, i ^ bit) for i in range(size)])]
    pallas_call x0 -> x4, Pallas kernels: none -> 244 us  [run_expert(): pl.pallas_call(lambda *refs: expert_kernel(size, tiles, part, *refs), out...]
    unnamed x250 -> x201, local copies, waits for them, and re-layouts: 290 us -> 50.8 us
    reduce_scatter x4 -> x5, waiting for transfers between devices: 40 us -> 198 us  [the longest x1 158 us: body(): lax.psum_scatter(jnp.concatenate([grad_qkv_w, gain_columns], axis=1), 'fs...]
    dynamic_slice x2 -> x1, local copies, waits for them, and re-layouts: 112 us -> 5.32 us  [scatter_rows(): lax.dynamic_slice_in_dim(sums, (place ^ k) * rows, rows, 0)]
    another operation x14 -> x13, local copies, waits for them, and re-layouts: 120 us -> 16.1 us  [the longest x1 8.58 us: gather_doubling(): jnp.stack([jnp.where(low, whole, received), jnp.where(low, received, whol...]
    another operation x28 -> x13, other arithmetic: 62.4 us -> 20.8 us  [the longest x5 16.9 us: gather_doubling(): jnp.stack([jnp.where(low, whole, received), jnp.where(low, received, whol...]
  transfers between devices with their start and end apart: 43 -> 55, of which waited for: 17 -> 19; matrix products, arithmetic and copies ran while one was open for 44% -> 28% of each run, Pallas kernels for 0% -> 11%
where the time goes in v2:
time: 2130 us; the launch traced here: 2120 us
  waiting for transfers between devices  1090 us (51%)
  matrix products  265 us (12%)
  Pallas kernels  244 us (11%)
  local copies, waits for them, and re-layouts  220 us (10%)
  other arithmetic  203 us (10%)
  starting transfers between devices  50.2 us (2%)
    ppermute x40, waiting for transfers between devices, swap(): return lax.ppermute(value, axis, [(i, i ^ bit) for i in range(size)])  840 us
    pallas_call x4, Pallas kernels, run_expert(): pl.pallas_call(lambda *refs: expert_kernel(size, tiles, part, *refs), out...  244 us
    reduce_scatter x1, waiting for transfers between devices, body(): lax.psum_scatter(jnp.concatenate([grad_qkv_w, gain_columns], axis=1), 'fs...  158 us
    dot_general x26, matrix products, dot(): return lax.dot_general(a, b, (contract, batch), preferred_element_type=f32)  155 us
    unnamed x201, local copies, waits for them, and re-layouts  50.8 us
  transfers between devices with their start and end apart: 55, of which 19 were waited for; matrix products, arithmetic and copies ran while one was open for 28% of the time, Pallas kernels for 11%

profile of v2, /device:TPU:0, one launch (start us, length us, event | category | flops | bytes accessed | tf_op | source)
XLA Modules:
  0.0 2119.7 jit_solution(4328887899934262419)
XLA Ops:
  27.0 29.0 %collective-permute-done = bf16[384,2048]{1,0:T(8,128)(2,1)} collective-permute-done((bf16[384,2048]{1,0:T(8,128)(2,1)S(1)}, bf16[384,2048]{1,0:T(8,128)(2,1)}, u32[]{:S(2)}, u32[]{:S(2)}) %collective-permute-start) | collective-permute-done | bytes 1572896 | tf_op jit(solution)/shard_map/ppermute | solution.py:21
  58.8 31.6 %collective-permute-done.1 = bf16[384,2048]{1,0:T(8,128)(2,1)} collective-permute-done((bf16[384,2048]{1,0:T(8,128)(2,1)S(1)}, bf16[384,2048]{1,0:T(8,128)(2,1)}, u32[]{:S(2)}, u32[]{:S(2)}) %collective-permute-start.1) | collective-permute-done | bytes 1572896 | tf_op jit(solution)/shard_map/ppermute | solution.py:21
  95.0 14.7 reshape.488
  139.4 33.3 %collective-permute-done.6 = bf16[1,256,2048]{2,1,0:T(8,128)(2,1)S(1)} collective-permute-done((bf16[1,256,2048]{2,1,0:T(8,128)(2,1)S(1)}, bf16[1,256,2048]{2,1,0:T(8,128)(2,1)S(1)}, u32[]{:S(2)}, u32[]{:S(2)}) %collective-permute-start.6) | collective-permute-done | bytes 1048608 | tf_op jit(solution)/shard_map/ppermute | solution.py:21
  175.4 13.6 convolution_convert_fusion.2
  195.0 59.6 %collective-permute-done.12 = bf16[384,2048]{1,0:T(8,128)(2,1)} collective-permute-done((bf16[384,2048]{1,0:T(8,128)(2,1)}, bf16[384,2048]{1,0:T(8,128)(2,1)}, u32[]{:S(2)}, u32[]{:S(2)}) %collective-permute-start.12) | collective-permute-done | bytes 1572896 | tf_op jit(solution)/shard_map/ppermute | solution.py:21
  254.6 107.2 %collective-permute-done.7 = bf16[2,256,2048]{2,1,0:T(8,128)(2,1)} collective-permute-done((bf16[2,256,2048]{2,1,0:T(8,128)(2,1)}, bf16[2,256,2048]{2,1,0:T(8,128)(2,1)}, u32[]{:S(2)}, u32[]{:S(2)}) %collective-permute-start.7) | collective-permute-done | bytes 2097184 | tf_op jit(solution)/shard_map/ppermute | solution.py:21
  366.7 51.6 %while.31 = (s32[]{:T(128)}, bf16[3,512,4,128]{3,2,1,0:T(4,128)(2,1)}, f32[3,4,512]{2,1,0:T(4,128)}, s32[3]{0:T(128)S(1)}, s32[1536]{0:T(1024)S(1)}, /*index=5*/...) while((s32[]{:T(128)}, ...), condition=%wide.region_8.9_spmd, body=%wide.region_5.8_spmd.sunk | while | flops 1649408000 | bytes 46216352 | solution.py:54
  426.7 20.2 all-to-all-done
  481.1 68.5 %collective-permute-done.10 = bf16[384,2048]{1,0:T(8,128)(2,1)S(1)} collective-permute-done((bf16[384,2048]{1,0:T(8,128)(2,1)}, bf16[384,2048]{1,0:T(8,128)(2,1)S(1)}, u32[]{:S(2)}, u32[]{:S(2)}) %collective-permute-start.10) | collective-permute-done | bytes 1572896 | tf_op jit(solution)/shard_map/ppermute | solution.py:21
  562.6 55.6 %collective-permute-done.9 = f32[384,16]{0,1:T(8,128)S(1)} collective-permute-done((f32[384,16]{0,1:T(8,128)S(1)}, f32[384,16]{0,1:T(8,128)S(1)}, u32[]{:S(2)}, u32[]{:S(2)}) %collective-permute-start.9) | collective-permute-done | bytes 24608 | tf_op jit(solution)/shard_map/ppermute | solution.py:21
  677.6 99.9 %collective-permute-done.11.refs_10_ = bf16[2,256,3072]{2,1,0:T(8,128)(2,1)} collective-permute-done((bf16[2,256,3072]{2,1,0:T(8,128)(2,1)}, bf16[2,256,3072]{2,1,0:T(8,128)(2,1)}, u32[]{:S(2)}, u32[]{:S(2)}) %collective-permute-start.11) | collective-permute-done | bytes 3145760 | tf_op jit(solution)/shard_map/ppermute | solution.py:21
  788.6 60.8 %expert.4 = (bf16[1088,2048]{1,0:T(8,128)(2,1)}, bf16[1088,2048]{1,0:T(8,128)(2,1)}, bf16[4,256,3072]{2,1,0:T(8,128)(2,1)}, bf16[4,256,3072]{2,1,0:T(8,128)(2,1)}) custom-call(s32[1]{0:T(128)} %bitcast.33.refs_0_, f32[1088,1]{1,0:T(8,128)} %reshape_squeeze.24.refs_1_, bf16[544,2048]{1,0:T(8,128)(2,1)} %bitcast.405, bf16[544,2048]{1,0:T(8,128)(2,1)} %bitcast.406, ...), custom_call_target="tpu_custom_call" | custom-call | flops 41070624768 | bytes 68157440 | tf_op jit(solution)/shard_map/expert/pallas_call | solution.py:250
  850.1 61.3 %expert.5 = (bf16[1088,2048]{1,0:T(8,128)(2,1)}, bf16[1088,2048]{1,0:T(8,128)(2,1)}, bf16[4,256,3072]{2,1,0:T(8,128)(2,1)}, bf16[4,256,3072]{2,1,0:T(8,128)(2,1)}) custom-call(s32[1]{0:T(128)} %bitcast.33.refs_0_, f32[1088,1]{1,0:T(8,128)} %reshape_squeeze.25.refs_1_, bf16[544,2048]{1,0:T(8,128)(2,1)} %bitcast.403, bf16[544,2048]{1,0:T(8,128)(2,1)} %bitcast.404, ...), custom_call_target="tpu_custom_call" | custom-call | flops 41070624768 | bytes 68157440 | tf_op jit(solution)/shard_map/expert/pallas_call | solution.py:250
  938.5 50.2 %collective-permute-done.22.refs_12_ = bf16[2,256,3072]{2,1,0:T(8,128)(2,1)} collective-permute-done((bf16[2,256,3072]{2,1,0:T(8,128)(2,1)}, bf16[2,256,3072]{2,1,0:T(8,128)(2,1)}, u32[]{:S(2)}, u32[]{:S(2)}) %collective-permute-start.22) | collective-permute-done | bytes 3145760 | tf_op jit(solution)/shard_map/ppermute | solution.py:21
  1006.3 60.7 %expert.6 = (bf16[1088,2048]{1,0:T(8,128)(2,1)}, bf16[1088,2048]{1,0:T(8,128)(2,1)}, bf16[4,256,3072]{2,1,0:T(8,128)(2,1)}, bf16[4,256,3072]{2,1,0:T(8,128)(2,1)}) custom-call(s32[1]{0:T(128)} %bitcast.33.refs_0_, f32[1088,1]{1,0:T(8,128)} %reshape_squeeze.26.refs_1_, bf16[544,2048]{1,0:T(8,128)(2,1)} %bitcast.400, bf16[544,2048]{1,0:T(8,128)(2,1)} %bitcast.402, ...), custom_call_target="tpu_custom_call" | custom-call | flops 41070624768 | bytes 68157440 | tf_op jit(solution)/shard_map/expert/pallas_call | solution.py:250
  1067.0 60.9 %expert.7 = (bf16[1088,2048]{1,0:T(8,128)(2,1)}, bf16[1088,2048]{1,0:T(8,128)(2,1)}, bf16[4,256,3072]{2,1,0:T(8,128)(2,1)}, bf16[4,256,3072]{2,1,0:T(8,128)(2,1)}) custom-call(s32[1]{0:T(128)} %bitcast.33.refs_0_, f32[1088,1]{1,0:T(8,128)} %reshape_squeeze.27.refs_1_, bf16[544,2048]{1,0:T(8,128)(2,1)} %bitcast.399, bf16[544,2048]{1,0:T(8,128)(2,1)} %bitcast.401, ...), custom_call_target="tpu_custom_call" | custom-call | flops 41070624768 | bytes 68157440 | tf_op jit(solution)/shard_map/expert/pallas_call | solution.py:250
  1180.7 53.1 %collective-permute-done.27 = bf16[2,256,3072]{2,1,0:T(8,128)(2,1)S(1)} collective-permute-done((bf16[2,256,3072]{2,1,0:T(8,128)(2,1)S(1)}, bf16[2,256,3072]{2,1,0:T(8,128)(2,1)S(1)}, u32[]{:S(2)}, u32[]{:S(2)}) %collective-permute-start.27) | collective-permute-done | bytes 3145760 | tf_op jit(solution)/shard_map/ppermute | solution.py:21
  1252.4 39.9 %reduce-scatter.7.cloned.1.call-done = bf16[384,2048]{1,0:T(8,128)(2,1)} async-done(((bf16[1536,2048]{1,0:T(8,128)(2,1)}), bf16[384,2048]{1,0:T(8,128)(2,1)}) %reduce-scatter.7.cloned.1.call-update) | async-done | bytes 1572880 | tf_op jit(solution)/shard_map/reduce_scatter | solution.py:328
  1292.3 16.3 collective-permute-done.26
  1344.0 133.6 %collective-permute-done.33 = bf16[2,256,3072]{2,1,0:T(8,128)(2,1)} collective-permute-done((bf16[2,256,3072]{2,1,0:T(8,128)(2,1)S(1)}, bf16[2,256,3072]{2,1,0:T(8,128)(2,1)}, u32[]{:S(2)}, u32[]{:S(2)}) %collective-permute-start.33) | collective-permute-done | bytes 3145760 | tf_op jit(solution)/shard_map/ppermute | solution.py:21
  1495.2 47.9 %collective-permute-done.34 = bf16[2,256,3072]{2,1,0:T(8,128)(2,1)} collective-permute-done((bf16[2,256,3072]{2,1,0:T(8,128)(2,1)}, bf16[2,256,3072]{2,1,0:T(8,128)(2,1)}, u32[]{:S(2)}, u32[]{:S(2)}) %collective-permute-start.34) | collective-permute-done | bytes 3145760 | tf_op jit(solution)/shard_map/ppermute | solution.py:21
  1559.0 127.6 %while.32 = (s32[]{:T(128)}, f32[1536,4,128]{0,2,1:T(8,128)}, f32[1536,4,128]{0,2,1:T(8,128)}, bf16[3,512,4,128]{3,1,0,2:T(8,128)(2,1)}, s32[3]{0:T(128)S(1)}, /...) while((s32[]{:T(128)}, f32[1536,4,128]{0,2,1:T(8,128)}, ...), condition=%wide.region_21.22_spmd.clone, body=%wide.region_19.21_spmd.clone.sunk | while | flops 4059822080 | bytes 155243296 | solution.py:94
  1616.5 9.1 multiply_convert_fusion.3
  1707.2 16.9 fusion.33
  1725.0 15.6 convolution_convert_fusion
  1758.3 157.9 %reduce-scatter.15.cloned.1.call-done = bf16[256,1664]{0,1:T(8,128)(2,1)} async-done(((bf16[2048,1664]{0,1:T(8,128)(2,1)}), bf16[256,1664]{0,1:T(8,128)(2,1)}) %reduce-scatter.15.cloned.1.call-update) | async-done | bytes 851984 | tf_op jit(solution)/shard_map/reduce_scatter | solution.py:488
  1918.8 31.0 %collective-permute-done.39 = bf16[1,256,3072]{2,1,0:T(8,128)(2,1)} collective-permute-done((bf16[1,256,3072]{2,1,0:T(8,128)(2,1)S(1)}, bf16[1,256,3072]{2,1,0:T(8,128)(2,1)}, u32[]{:S(2)}, u32[]{:S(2)}) %collective-permute-start.39) | collective-permute-done | bytes 1572896 | tf_op jit(solution)/shard_map/ppermute | solution.py:21
  1974.9 9.1 copy.109
  1996.6 22.2 %reshape.516 = f32[8,256,2,1024]{3,2,1,0:T(2,128)} reshape(f32[8,256,2048]{2,1,0:T(8,128)} %slice.512) | data formatting | bytes 33554432 | tf_op jit(solution)/shard_map/reshape | solution.py:520
  2018.8 22.5 %collective-permute-done.37 = bf16[384,2048]{1,0:T(8,128)(2,1)} collective-permute-done((bf16[384,2048]{1,0:T(8,128)(2,1)}, bf16[384,2048]{1,0:T(8,128)(2,1)}, u32[]{:S(2)}, u32[]{:S(2)}) %collective-permute-start.37) | collective-permute-done | bytes 1572896 | tf_op jit(solution)/shard_map/ppermute | solution.py:21
  2053.0 34.5 %all-gather.24.cloned.1.call-done = bf16[1024,1664]{0,1:T(8,128)(2,1)} async-done(((bf16[256,1664]{0,1:T(8,128)(2,1)}), bf16[1024,1664]{0,1:T(8,128)(2,1)}) %all-gather.24.cloned.1.call-update) | async-done | bytes 3407888 | tf_op jit(solution)/shard_map/all_gather | solution.py:491
  (554 shorter events, 655.5 us)
Async XLA Ops:
  17.6 623.6 %all-gather.20.cloned.1.call-start = ((), (), s32[]{:S(2)}) async-start(), calls=%async_computation.18 | async-start | bytes 7864320 | tf_op jit(solution)/shard_map/all_gather | solution.py:320
  94.4 563.5 %all-gather.22.cloned.1.call-start = ((), (), s32[]{:S(2)}) async-start(), calls=%async_computation.19 | async-start | bytes 7864320 | tf_op jit(solution)/shard_map/all_gather | solution.py:322
  134.1 314.7 %collective-permute-start.4 = (bf16[2,256,3072]{2,1,0:T(8,128)(2,1)}, bf16[2,256,3072]{2,1,0:T(8,128)(2,1)}, u32[]{:S(2)}, u32[]{:S(2)}) collective-permute-start(bf16[2,256,3072]{2,1,0:T(8,128)(2,1)} %get-tuple-element.198.refs_6_), channel_id=1, source_target_pairs={{0,2},{1,3},{2,0},{3,1},{4,6},{5,7},{6,4},{7,5},{8,10},{9,11},{10,... | collective-permute-start | bytes 9437192 | tf_op jit(solution)/shard_map/ppermute | solution.py:21
  135.9 312.9 %collective-permute-start.5 = (bf16[2,256,3072]{2,1,0:T(8,128)(2,1)}, bf16[2,256,3072]{2,1,0:T(8,128)(2,1)}, u32[]{:S(2)}, u32[]{:S(2)}) collective-permute-start(bf16[2,256,3072]{2,1,0:T(8,128)(2,1)} %get-tuple-element.198.refs_6_), channel_id=1, source_target_pairs={{0,1},{1,0},{2,3},{3,2},{4,5},{5,4},{6,7},{7,6},{8,9},{9,8},{10,11... | collective-permute-start | bytes 9437192 | tf_op jit(solution)/shard_map/ppermute | solution.py:21
  135.9 118.7 %collective-permute-start.12 = (bf16[384,2048]{1,0:T(8,128)(2,1)}, bf16[384,2048]{1,0:T(8,128)(2,1)}, u32[]{:S(2)}, u32[]{:S(2)}) collective-permute-start(bf16[384,2048]{1,0:T(8,128)(2,1)} %bitcast.42), channel_id=1, source_target_pairs={{0,4},{1,5},{2,6},{3,7},{4,0},{5,1},{6,2},{7,3},{8,12},{9,13},{10,... | collective-permute-start | bytes 4718600 | tf_op jit(solution)/shard_map/ppermute | solution.py:21
  136.8 311.9 %collective-permute-start.3 = (bf16[2,256,3072]{2,1,0:T(8,128)(2,1)}, bf16[2,256,3072]{2,1,0:T(8,128)(2,1)}, u32[]{:S(2)}, u32[]{:S(2)}) collective-permute-start(bf16[2,256,3072]{2,1,0:T(8,128)(2,1)} %get-tuple-element.199), channel_id=1, source_target_pairs={{0,4},{1,5},{2,6},{3,7},{4,0},{5,1},{6,2},{7,3},{8,12},{9,13},{10,... | collective-permute-start | bytes 9437192 | tf_op jit(solution)/shard_map/ppermute | solution.py:21
  175.4 186.4 %collective-permute-start.7 = (bf16[2,256,2048]{2,1,0:T(8,128)(2,1)}, bf16[2,256,2048]{2,1,0:T(8,128)(2,1)}, u32[]{:S(2)}, u32[]{:S(2)}) collective-permute-start(bf16[2,256,2048]{2,1,0:T(8,128)(2,1)} %maximum_bitcast_fusion), channel_id=1, source_target_pairs={{0,2},{1,3},{2,0},{3,1},{4,6},{5,7},{6,4},{7,5},{8,10},{9,11},{10,... | collective-permute-start | bytes 6291464 | tf_op jit(solution)/shard_map/ppermute | solution.py:21
  426.6 245.4 %all-gather.16.cloned.1.call-start = ((), (), s32[]{:S(2)}) async-start(), calls=%async_computation.16 | async-start | bytes 7864320 | tf_op jit(solution)/shard_map/all_gather | solution.py:320
  478.5 301.7 %all-gather.18.cloned.1.call-start = ((), (), s32[]{:S(2)}) async-start(), calls=%async_computation.17 | async-start | bytes 7864320 | tf_op jit(solution)/shard_map/all_gather | solution.py:322
  550.7 687.4 %reduce-scatter.9.cloned.1.call-start = ((), (), s32[]{:S(2)}) async-start(), calls=%async_computation.10 | async-start | bytes 7864320 | tf_op jit(solution)/shard_map/reduce_scatter | solution.py:326
  637.1 151.5 %collective-permute-start.14 = (bf16[2,256,3072]{2,1,0:T(8,128)(2,1)}, bf16[2,256,3072]{2,1,0:T(8,128)(2,1)}, u32[]{:S(2)}, u32[]{:S(2)}) collective-permute-start(bf16[2,256,3072]{2,1,0:T(8,128)(2,1)} %collective-permute-done.3.refs_10_), channel_id=1, source_target_pairs={{0,1},{1,0},{2,3},{3,2},{4,5},{5,4},{6,7},{7,6},{8,9},{9,8},{10,11... | collective-permute-start | bytes 9437192 | tf_op jit(solution)/shard_map/ppermute | solution.py:21
  637.2 151.5 %collective-permute-start.13 = (bf16[2,256,3072]{2,1,0:T(8,128)(2,1)}, bf16[2,256,3072]{2,1,0:T(8,128)(2,1)}, u32[]{:S(2)}, u32[]{:S(2)}) collective-permute-start(bf16[2,256,3072]{2,1,0:T(8,128)(2,1)} %collective-permute-done.4.refs_8_), channel_id=1, source_target_pairs={{0,1},{1,0},{2,3},{3,2},{4,5},{5,4},{6,7},{7,6},{8,9},{9,8},{10,11... | collective-permute-start | bytes 9437192 | tf_op jit(solution)/shard_map/ppermute | solution.py:21
  637.7 151.0 %collective-permute-start.16 = (bf16[2,256,3072]{2,1,0:T(8,128)(2,1)}, bf16[2,256,3072]{2,1,0:T(8,128)(2,1)}, u32[]{:S(2)}, u32[]{:S(2)}) collective-permute-start(bf16[2,256,3072]{2,1,0:T(8,128)(2,1)} %collective-permute-done.15.refs_12_), channel_id=1, source_target_pairs={{0,1},{1,0},{2,3},{3,2},{4,5},{5,4},{6,7},{7,6},{8,9},{9,8},{10,11... | collective-permute-start | bytes 9437192 | tf_op jit(solution)/shard_map/ppermute | solution.py:21
  637.7 139.9 %collective-permute-start.11 = (bf16[2,256,3072]{2,1,0:T(8,128)(2,1)}, bf16[2,256,3072]{2,1,0:T(8,128)(2,1)}, u32[]{:S(2)}, u32[]{:S(2)}) collective-permute-start(bf16[2,256,3072]{2,1,0:T(8,128)(2,1)} %get-tuple-element.202), channel_id=1, source_target_pairs={{0,4},{1,5},{2,6},{3,7},{4,0},{5,1},{6,2},{7,3},{8,12},{9,13},{10,... | collective-permute-start | bytes 9437192 | tf_op jit(solution)/shard_map/ppermute | solution.py:21
  641.0 294.2 %collective-permute-start.19 = (bf16[2,256,3072]{2,1,0:T(8,128)(2,1)}, bf16[2,256,3072]{2,1,0:T(8,128)(2,1)}, u32[]{:S(2)}, u32[]{:S(2)}) collective-permute-start(bf16[2,256,3072]{2,1,0:T(8,128)(2,1)} %get-tuple-element.213.refs_6_), channel_id=1, source_target_pairs={{0,2},{1,3},{2,0},{3,1},{4,6},{5,7},{6,4},{7,5},{8,10},{9,11},{10,... | collective-permute-start | bytes 9437192 | tf_op jit(solution)/shard_map/ppermute | solution.py:21
  777.5 228.7 %collective-permute-start.18 = (bf16[2,256,3072]{2,1,0:T(8,128)(2,1)}, bf16[2,256,3072]{2,1,0:T(8,128)(2,1)}, u32[]{:S(2)}, u32[]{:S(2)}) collective-permute-start(bf16[2,256,3072]{2,1,0:T(8,128)(2,1)} %get-tuple-element.213.refs_6_), channel_id=1, source_target_pairs={{0,1},{1,0},{2,3},{3,2},{4,5},{5,4},{6,7},{7,6},{8,9},{9,8},{10,11... | collective-permute-start | bytes 9437192 | tf_op jit(solution)/shard_map/ppermute | solution.py:21
  849.5 139.2 %collective-permute-start.17 = (bf16[4,256,3072]{2,1,0:T(8,128)(2,1)}, bf16[4,256,3072]{2,1,0:T(8,128)(2,1)}, u32[]{:S(2)}, u32[]{:S(2)}) collective-permute-start(bf16[4,256,3072]{2,1,0:T(8,128)(2,1)} %get-tuple-element.211), channel_id=1, source_target_pairs={{0,1},{1,0},{2,3},{3,2},{4,5},{5,4},{6,7},{7,6},{8,9},{9,8},{10,11... | collective-permute-start | bytes 18874376 | tf_op jit(solution)/shard_map/ppermute | solution.py:21
  1001.1 135.3 %collective-permute-start.25 = (bf16[2,256,3072]{2,1,0:T(8,128)(2,1)}, bf16[2,256,3072]{2,1,0:T(8,128)(2,1)}, u32[]{:S(2)}, u32[]{:S(2)}) collective-permute-start(bf16[2,256,3072]{2,1,0:T(8,128)(2,1)} %add_convert_fusion.3), channel_id=1, source_target_pairs={{0,2},{1,3},{2,0},{3,1},{4,6},{5,7},{6,4},{7,5},{8,10},{9,11},{10,... | collective-permute-start | bytes 9437192 | tf_op jit(solution)/shard_map/ppermute | solution.py:21
  1149.3 143.1 %reduce-scatter.7.cloned.1.call-start = ((), (), s32[]{:S(2)}) async-start(), calls=%async_computation.9 | async-start | bytes 7864320 | tf_op jit(solution)/shard_map/reduce_scatter | solution.py:328
  1161.9 396.9 %reduce-scatter.13.cloned.1.call-start = ((), (), s32[]{:S(2)}) async-start(), calls=%async_computation.12 | async-start | bytes 7864320 | tf_op jit(solution)/shard_map/reduce_scatter | solution.py:326
  1324.2 379.1 %reduce-scatter.11.cloned.1.call-start = ((), (), s32[]{:S(2)}) async-start(), calls=%async_computation.11 | async-start | bytes 7864320 | tf_op jit(solution)/shard_map/reduce_scatter | solution.py:328
  1339.0 138.6 %collective-permute-start.33 = (bf16[2,256,3072]{2,1,0:T(8,128)(2,1)S(1)}, bf16[2,256,3072]{2,1,0:T(8,128)(2,1)}, u32[]{:S(2)}, u32[]{:S(2)}) collective-permute-start(bf16[2,256,3072]{2,1,0:T(8,128)(2,1)S(1)} %copy-done.31), channel_id=1, source_target_pairs={{0,2},{1,3},{2,0},{3,1},{4,6},{5,7},{6,4},{7,5},{8,10},{9,11},{10,... | collective-permute-start | bytes 9437192 | tf_op jit(solution)/shard_map/ppermute | solution.py:21
  1339.0 204.1 %collective-permute-start.34 = (bf16[2,256,3072]{2,1,0:T(8,128)(2,1)}, bf16[2,256,3072]{2,1,0:T(8,128)(2,1)}, u32[]{:S(2)}, u32[]{:S(2)}) collective-permute-start(bf16[2,256,3072]{2,1,0:T(8,128)(2,1)} %add_convert_fusion), channel_id=1, source_target_pairs={{0,2},{1,3},{2,0},{3,1},{4,6},{5,7},{6,4},{7,5},{8,10},{9,11},{10,... | collective-permute-start | bytes 9437192 | tf_op jit(solution)/shard_map/ppermute | solution.py:21
  1341.1 217.8 %collective-permute-start.32 = (bf16[1,256,3072]{2,1,0:T(8,128)(2,1)}, bf16[1,256,3072]{2,1,0:T(8,128)(2,1)}, u32[]{:S(2)}, u32[]{:S(2)}) collective-permute-start(bf16[1,256,3072]{2,1,0:T(8,128)(2,1)} %get-tuple-element.393), channel_id=1, source_target_pairs={{0,4},{1,5},{2,6},{3,7},{4,0},{5,1},{6,2},{7,3},{8,12},{9,13},{10,... | collective-permute-start | bytes 4718600 | tf_op jit(solution)/shard_map/ppermute | solution.py:21
  1341.6 217.2 %collective-permute-start.31 = (bf16[1,256,3072]{2,1,0:T(8,128)(2,1)}, bf16[1,256,3072]{2,1,0:T(8,128)(2,1)}, u32[]{:S(2)}, u32[]{:S(2)}) collective-permute-start(bf16[1,256,3072]{2,1,0:T(8,128)(2,1)} %get-tuple-element.391), channel_id=1, source_target_pairs={{0,4},{1,5},{2,6},{3,7},{4,0},{5,1},{6,2},{7,3},{8,12},{9,13},{10,... | collective-permute-start | bytes 4718600 | tf_op jit(solution)/shard_map/ppermute | solution.py:21
  1495.1 257.3 %reduce-scatter.17.cloned.1.call-start = ((), (), s32[]{:S(2)}) async-start(), calls=%async_computation.14 | async-start | bytes 9437184 | tf_op jit(solution)/shard_map/reduce_scatter | solution.py:471
  1556.7 359.4 %reduce-scatter.15.cloned.1.call-start = ((), (), s32[]{:S(2)}) async-start(), calls=%async_computation.13 | async-start | bytes 7667712 | tf_op jit(solution)/shard_map/reduce_scatter | solution.py:488
  1558.9 144.4 %collective-permute-start.30 = (bf16[384,2048]{1,0:T(8,128)(2,1)}, bf16[384,2048]{1,0:T(8,128)(2,1)}, u32[]{:S(2)}, u32[]{:S(2)}) collective-permute-start(bf16[384,2048]{1,0:T(8,128)(2,1)} %reduce-scatter.13.cloned.1.call-done), channel_id=1, source_target_pairs={{0,4},{1,5},{2,6},{3,7},{4,0},{5,1},{6,2},{7,3},{8,12},{9,13},{10,... | collective-permute-start | bytes 4718600 | tf_op jit(solution)/shard_map/ppermute | solution.py:21
  1747.6 302.5 %all-reduce.4.cloned.1.call-start = ((), (), s32[]{:S(2)}) async-start(), calls=%async_computation.15 | async-start | bytes 2097152 | tf_op jit(solution)/shard_map/psum | solution.py:472
  1749.0 167.2 %collective-permute-start.38 = (bf16[1,256,3072]{2,1,0:T(8,128)(2,1)S(1)}, bf16[1,256,3072]{2,1,0:T(8,128)(2,1)}, u32[]{:S(2)}, u32[]{:S(2)}) collective-permute-start(bf16[1,256,3072]{2,1,0:T(8,128)(2,1)S(1)} %copy-done.32), channel_id=1, source_target_pairs={{0,4},{1,5},{2,6},{3,7},{4,0},{5,1},{6,2},{7,3},{8,12},{9,13},{10,... | collective-permute-start | bytes 4718600 | tf_op jit(solution)/shard_map/ppermute | solution.py:21
  1752.0 197.8 %collective-permute-start.39 = (bf16[1,256,3072]{2,1,0:T(8,128)(2,1)S(1)}, bf16[1,256,3072]{2,1,0:T(8,128)(2,1)}, u32[]{:S(2)}, u32[]{:S(2)}) collective-permute-start(bf16[1,256,3072]{2,1,0:T(8,128)(2,1)S(1)} %copy-done.33), channel_id=1, source_target_pairs={{0,4},{1,5},{2,6},{3,7},{4,0},{5,1},{6,2},{7,3},{8,12},{9,13},{10,... | collective-permute-start | bytes 4718600 | tf_op jit(solution)/shard_map/ppermute | solution.py:21
  1752.5 335.0 %all-gather.24.cloned.1.call-start = ((), (), s32[]{:S(2)}) async-start(), calls=%async_computation.20 | async-start | bytes 4259840 | tf_op jit(solution)/shard_map/all_gather | solution.py:491
  (128 other events, 3182.2 us)
Sparse Core Ops, SparseCore 0:
  17.8 72.1 all-gather.13
  94.5 70.4 all-gather.19
  254.7 70.3 all-gather.21
  478.7 69.2 all-gather.15
  550.8 69.6 all-gather.17
  1149.4 69.6 reduce-scatter.8
  1222.1 70.1 reduce-scatter.6
  1324.3 69.1 reduce-scatter.12
  1396.5 70.1 reduce-scatter.10
  1556.8 138.7 reduce-scatter.16
  1747.7 168.3 reduce-scatter.14
  1919.0 101.1 all-reduce.3
  2022.1 65.3 all-gather.23

commit v3 on v2

--- a/solution.py
+++ b/solution.py
@@ -31,71 +31,109 @@
     return jnp.sum((places[:, None] >= ends[None, :]).astype(jnp.int32), axis=1)
 
 
-def attend_forward(queries, key_rows, values, segment, block_len):
-    span_len, heads_now, head_dim = queries.shape
-    score_scale = head_dim ** (-0.5)
-
-    def one_block(row_start):
-        q_block = lax.dynamic_slice_in_dim(queries, row_start, block_len, 0)
-        seg_block = lax.dynamic_slice_in_dim(segment, row_start, block_len, 0)
-        scores = (
-            jnp.einsum("qhd,khd->hqk", q_block, key_rows, preferred_element_type=f32)
-            * score_scale
-        )
-        scores = jnp.where(seg_block[None, :, None] == segment[None, None, :], scores, -1e30)
-        row_max = jnp.max(scores, axis=2, keepdims=True)
-        exp_part = jnp.exp(scores - row_max)
-        row_sum = jnp.sum(exp_part, axis=2, keepdims=True)
-        prob_b = (exp_part / row_sum).astype(bf16)
-        out_block = jnp.einsum("hqk,khd->qhd", prob_b, values, preferred_element_type=f32)
-        return (out_block.astype(bf16), (row_max + jnp.log(row_sum))[:, :, 0])
-
-    starts = jnp.arange(span_len // block_len, dtype=jnp.int32) * block_len
-    outputs, log_total = lax.map(one_block, starts)
-    log_total = jnp.transpose(log_total, (1, 0, 2)).reshape(heads_now, span_len)
-    return (outputs.reshape(span_len, heads_now, head_dim), log_total)
-
-
-def attend_backward(queries, key_rows, values, segment, log_total, grad_heads, block_len):
-    span_len, heads_now, head_dim = queries.shape
-    score_scale = head_dim ** (-0.5)
-
-    def one_block(carried, row_start):
-        grad_k, grad_v = carried
-        q_block = lax.dynamic_slice_in_dim(queries, row_start, block_len, 0)
-        seg_block = lax.dynamic_slice_in_dim(segment, row_start, block_len, 0)
-        g_block = lax.dynamic_slice_in_dim(grad_heads, row_start, block_len, 0)
-        lse_block = lax.dynamic_slice_in_dim(log_total, row_start, block_len, 1)
-        scores = (
-            jnp.einsum("qhd,khd->hqk", q_block, key_rows, preferred_element_type=f32)
-            * score_scale
-        )
-        scores = jnp.where(seg_block[None, :, None] == segment[None, None, :], scores, -1e30)
-        prob_f = jnp.exp(scores - lse_block[:, :, None])
-        grad_v = grad_v + jnp.einsum(
-            "hqk,qhd->khd", prob_f.astype(bf16), g_block, preferred_element_type=f32
-        )
-        grad_p = jnp.einsum("qhd,khd->hqk", g_block, values, preferred_element_type=f32)
-        inner_sum = jnp.sum(prob_f * grad_p, axis=2, keepdims=True)
-        dscore = (prob_f * (grad_p - inner_sum)).astype(bf16)
-        grad_q = (
-            jnp.einsum("hqk,khd->qhd", dscore, key_rows, preferred_element_type=f32)
-            * score_scale
-        )
-        grad_k = (
-            grad_k
-            + jnp.einsum("hqk,qhd->khd", dscore, q_block, preferred_element_type=f32)
-            * score_scale
-        )
-        return ((grad_k, grad_v), grad_q)
-
-    zeros_kv = jnp.zeros((span_len, heads_now, head_dim), f32)
-    starts = jnp.arange(span_len // block_len, dtype=jnp.int32) * block_len
-    (grad_k, grad_v), grad_q = lax.scan(one_block, (zeros_kv, zeros_kv), starts)
-    return (grad_q.reshape(span_len, heads_now, head_dim), grad_k, grad_v)
+def score_probs(keys, queries, seg_column, seg_row):
+    raw = dot(keys, queries, ((1,), (1,)))
+    raw = jnp.where(seg_column == seg_row, raw, -1e30)
+    top = jnp.max(raw, axis=0, keepdims=True)
+    part = jnp.exp((raw - top) * HEAD ** (-0.5))
+    return part * (1.0 / jnp.sum(part, axis=0, keepdims=True))
+
+
+def head_columns(heads_here, head):
+    return [
+        pl.ds(pl.multiple_of((third * heads_here + head) * HEAD, HEAD), HEAD) for third in range(3)
+    ]
+
+
+def attend_forward_kernel(heads_here, qkv_ref, seg_column, seg_row, out_ref):
+    block = out_ref.shape[0]
+    at = pl.ds(pl.multiple_of(pl.program_id(1) * block, block), block)
+    q_at, k_at, v_at = head_columns(heads_here, pl.program_id(0))
+    probs = score_probs(qkv_ref[:, k_at], qkv_ref[at, q_at], seg_column[...], seg_row[...])
+    out_ref[...] = dot(qkv_ref[:, v_at], probs.astype(bf16), ((0,), (0,))).T.astype(bf16)
+
+
+def attend_backward_kernel(
+    heads_here, qkv_ref, grad_ref, seg_column, seg_row, out_ref, grad_k, grad_v
+):
+    block = grad_ref.shape[0]
+    turn = pl.program_id(1)
+    at = pl.ds(pl.multiple_of(turn * block, block), block)
+    q_at, k_at, v_at = head_columns(heads_here, pl.program_id(0))
+    queries, keys, grads = qkv_ref[at, q_at], qkv_ref[:, k_at], grad_ref[...]
+    probs = score_probs(keys, queries, seg_column[...], seg_row[...])
+    grad_probs = dot(qkv_ref[:, v_at], grads, ((1,), (1,)))
+    inner = jnp.sum(probs * grad_probs, axis=0, keepdims=True)
+    grad_scores = (probs * (grad_probs - inner)).astype(bf16)
+    scale = HEAD ** (-0.5)
+
+    @pl.when(turn == 0)
+    def _():
+        grad_k[...] = jnp.zeros_like(grad_k)
+        grad_v[...] = jnp.zeros_like(grad_v)
+
+    grad_v[...] += dot(probs.astype(bf16), grads, ((1,), (0,)))
+    grad_k[...] += dot(grad_scores, queries, ((1,), (0,)))
+    out_ref[at, q_at] = (dot(keys, grad_scores, ((0,), (0,))).T * scale).astype(bf16)
+
+    @pl.when(turn == pl.num_programs(1) - 1)
+    def _():
+        out_ref[:, k_at] = (grad_k[...] * scale).astype(bf16)
+        out_ref[:, v_at] = grad_v[...].astype(bf16)
+
+
+def attend(qkv, segment, grad=None):
+    span_len, columns = qkv.shape
+    heads_here = columns // (3 * HEAD)
+    blocks = 3
+    block = span_len // blocks
+    whole = pl.BlockSpec((span_len, columns), lambda h, i: (0, 0), pipeline_mode=pl.Buffered(1))
+    cut = pl.BlockSpec((block, HEAD), lambda h, i: (i, h))
+    segments = [
+        pl.BlockSpec((span_len, 1), lambda h, i: (0, 0)),
+        pl.BlockSpec((1, block), lambda h, i: (0, i)),
+    ]
+    backward = grad is not None
+    return pl.pallas_call(
+        lambda *refs: (attend_backward_kernel if backward else attend_forward_kernel)(
+            heads_here, *refs
+        ),
+        out_shape=jax.ShapeDtypeStruct((span_len, columns if backward else columns // 3), bf16),
+        grid=(heads_here, blocks),
+        in_specs=[whole, *[cut] * backward, *segments],
+        out_specs=pl.BlockSpec((span_len, columns), lambda h, i: (0, 0)) if backward else cut,
+        scratch_shapes=[pltpu.VMEM((span_len, HEAD), f32)] * (2 * backward),
+        compiler_params=pltpu.CompilerParams(
+            dimension_semantics=("arbitrary", "arbitrary"), vmem_limit_bytes=60 * 2**20
+        ),
+        cost_estimate=pl.CostEstimate(
+            flops=(40 if backward else 20) * span_len * span_len * HEAD * heads_here,
+            bytes_accessed=4 * span_len * columns,
+            transcendentals=span_len * span_len * heads_here,
+        ),
+        name="attend_backward" if backward else "attend_forward",
+    )(*[qkv, *[grad] * backward, segment.reshape(span_len, 1), segment.reshape(1, span_len)])
+
+
+def unpack_kernel(in_ref, out_ref):
+    out_ref[...] = in_ref[0].astype(f32)
+
+
+def unpack_columns(gathered, width, thirds):
+    n_seq, rows, _ = gathered.shape
+    return pl.pallas_call(
+        unpack_kernel,
+        out_shape=jax.ShapeDtypeStruct((rows, thirds * n_seq * width), f32),
+        grid=(n_seq, thirds),
+        in_specs=[pl.BlockSpec((1, rows, width), lambda s, p: (s, 0, p))],
+        out_specs=pl.BlockSpec((rows, width), lambda s, p: (0, p * n_seq + s)),
+        name="unpack",
+    )(gathered)
 
 
 def after(value, *others):
+    if not others:
+        return value
     return lax.optimization_barrier((value, *others))[0]
 
 
@@ -106,10 +144,10 @@
     return total
 
 
-def start_expert(mine, sent, start):
+def start_expert(mine, sent, *start):
     size = lax.axis_size("fsdp")
-    mine = after(mine, start)
-    pieces = {0: mine, size // 2: swap(after(sent, start), "fsdp", size // 2)}
+    mine, sent = after(mine, *start), after(sent, *start)
+    pieces = {0: mine, size // 2: swap(sent, "fsdp", size // 2)}
     bit = size // 4
     while bit:
         pieces[bit] = swap(mine, "fsdp", bit)
@@ -117,13 +155,13 @@
     return pieces
 
 
-def finish_expert(pieces, middle):
+def finish_expert(pieces):
     size = lax.axis_size("fsdp")
     pieces = dict(pieces)
     for j in sorted(range(size), key=lambda j: (j & 1, j.bit_count())):
         if j not in pieces:
             low = j & -j
-            pieces[j] = swap(after(pieces[j ^ low], middle), "fsdp", low)
+            pieces[j] = swap(pieces[j ^ low], "fsdp", low)
     return [pieces[j] for j in range(size)]
 
 
@@ -143,21 +181,6 @@
         for k in range(lax.axis_size(axis))
     ]
     return sum((swap(part, axis, k) if k else part).astype(f32) for k, part in enumerate(parts))
-
-
-def gather_doubling(piece, axis, start):
-    size, place = lax.axis_size(axis), lax.axis_index(axis)
-    rows = piece.shape[0]
-    whole = after(piece, start)[None]
-    bit = size // 2
-    while bit:
-        received = swap(whole, axis, bit)
-        low = (place // bit) % 2 == 0
-        whole = jnp.stack(
-            [jnp.where(low, whole, received), jnp.where(low, received, whole)], axis=1
-        ).reshape(-1, *piece.shape)
-        bit //= 2
-    return whole.reshape(-1, *piece.shape[1:])
 
 
 def expert_kernel(size, tiles, part, place_ref, share_ref, *rest):
@@ -246,7 +269,6 @@
         turn = jnp.maximum(step - tiles, 0)
         return 0, place[0] ^ reversed_bits((turn + half) % size, size)
 
-    flops = 2 * count * D * ffe * 9
     return pl.pallas_call(
         lambda *refs: expert_kernel(size, tiles, part, *refs),
         out_shape=[
@@ -286,7 +308,9 @@
             dimension_semantics=("arbitrary",), vmem_limit_bytes=60 * 2**20
         ),
         cost_estimate=pl.CostEstimate(
-            flops=flops, bytes_accessed=8 * count * D + 8 * size * rows * columns, transcendentals=0
+            flops=18 * count * D * ffe,
+            bytes_accessed=8 * count * D + 4 * size * rows * columns,
+            transcendentals=count * ffe,
         ),
         name="expert",
     )(place, share, *slots, *grad_slots, *pieces)
@@ -318,7 +342,7 @@
 
 def to_group(rows, *others):
     own = lax.all_gather(rows, "seq", axis=0, tiled=False)
-    swapped = swap(after(rows, *others) if others else rows, "fsdp", lax.axis_size("fsdp") // 2)
+    swapped = swap(after(rows, *others), "fsdp", lax.axis_size("fsdp") // 2)
     return own, lax.all_gather(swapped, "seq", axis=0, tiled=False), swapped
 
 
@@ -359,9 +383,9 @@
     qkv_own = gathered[:, : 3 * width]
     gain_a = gathered[:, 3 * width].astype(f32)
     gain_m = gathered[:, 3 * width + 1].astype(f32)
-    out_full = gather_doubling(w_out, "fsdp", gathered)
-
-    parts = per_half // 2
+    out_full = lax.all_gather(after(w_out, x_all), "fsdp", axis=0, tiled=True)
+    cot_other = swap(cotangent[0], "fsdp", n_fsdp // 2)
+
     routing = jnp.concatenate([routes[0].astype(f32), gates[0]], axis=1)
     routing = jnp.stack(to_group(routing)[:2]).reshape(2 * n_seq, rows, 2 * TOP)
     capacity = rows * TOP * 4 // (3 * local_count * n_seq) + 2
@@ -378,64 +402,54 @@
         jnp.where(picks, jnp.swapaxes(weight, 1, 2)[:, :, None, :], 0.0), axis=3
     )
     picks = picks.astype(bf16)
-    cot_all = to_group(after(cotangent[0], x_all, gathered))
 
     def normed_rows(values, gain):
         inverse = lax.rsqrt(jnp.mean(values * values, axis=1, keepdims=True) + epsilon)
         return (values * inverse * gain).astype(bf16), inverse
 
+    x_all = after(x_all, own_part, other_part, picks, share, cot_other)
     normed_a, inv_all = normed_rows(x_all.astype(f32), gain_a)
     qkv = dot(normed_a, qkv_own, ((1,), (0,))).astype(bf16)
-    spread = qkv.reshape(span_len, 3, heads_here, HEAD)
     segment = segment_ids(lengths[0], span_len)
-    block_len = span_len // 3
-    queries, key_rows, values = spread[:, 0], spread[:, 1], spread[:, 2]
-    attended, log_total = attend_forward(queries, key_rows, values, segment, block_len)
-    heads_rows = lax.all_to_all(
-        attended.reshape(span_len, width), "seq", split_axis=0, concat_axis=1, tiled=True
-    )
-    first_part = start_expert(own_part[:2], other_part[:2], gathered)
-    heads_rows = after(heads_rows, *first_part.values())
+    attended = attend(qkv, segment)
+    heads_rows = lax.all_to_all(attended, "seq", split_axis=0, concat_axis=1, tiled=True)
+    cot_own = gather_rows(after(cotangent[0], x_all), "seq")
+    cot_all = [cot_own, gather_rows(after(cot_other, x_all), "seq")]
+    cot_all = [rows_of.reshape(n_seq, rows, D) for rows_of in cot_all]
+    begun = [start_expert(own_part[:1], other_part[:1])]
+    heads_rows = after(heads_rows, cot_own, *begun[0].values())
     x_float = tokens[0].astype(f32)
     resid = x_float + dot(heads_rows, out_full, ((1,), (0,)))
     normed_m, inv_m = normed_rows(resid, gain_m)
     moe_all = to_group(normed_m)
 
-    begun = [first_part]
-    for c in range(1, parts):
-        begun.append(
-            start_expert(
-                own_part[2 * c : 2 * c + 2], other_part[2 * c : 2 * c + 2], moe_all[2]
-            )
-        )
-    experts = [
-        finish_expert(begun[c], heads_rows if c == 0 else moe_all[1]) for c in range(parts)
-    ]
+    for i in range(1, per_half):
+        begun.append(start_expert(own_part[i : i + 1], other_part[i : i + 1], attended))
+    experts = [finish_expert(pieces) for pieces in begun]
 
     place = jnp.full((1,), at_fsdp, jnp.int32)
     forward_parts, backward_parts, chains = [], [], []
-    slots_of, grad_slots_of = [], []
+    def dispatch(i, g, source, weighted):
+        at = slice(g * n_seq, (g + 1) * n_seq)
+        part = dot(picks[at, i], source, ((2,), (1,)), ((0,), (0,)))
+        if weighted:
+            part = part * share[at, i, :, None]
+        return part.astype(bf16).reshape(-1, D)
+
+    grad_slots = [[dispatch(i, g, cot_all[g], True) for g in range(2)] for i in range(per_half)]
     for i in range(per_half):
-        for g in range(2):
-            pick = picks[g * n_seq : (g + 1) * n_seq, i]
-            share_i = share[g * n_seq : (g + 1) * n_seq, i].reshape(-1, 1)
-            slots = dot(pick, moe_all[g], ((2,), (1,)), ((0,), (0,))).astype(bf16)
-            slots_of.append(slots.reshape(-1, D))
-            grad_slots = dot(pick, cot_all[g], ((2,), (1,)), ((0,), (0,))).reshape(-1, D)
-            grad_slots_of.append((share_i * grad_slots).astype(bf16))
-    for i in range(per_half):
-        slots = slots_of[2 * i : 2 * i + 2]
+        ready = list(backward_parts[-1:]) + [experts[i][j] for j in range(n_fsdp - 1)]
+        if i + 1 < per_half:
+            ready.extend(begun[i + 1].values())
         if i >= 2:
-            slots = [after(slots[0], chains[i - 2].sums()), slots[1]]
-        elif i < 1 and parts > 1:
-            slots = [after(slots[0], begun[1][n_fsdp // 2]), slots[1]]
+            ready.append(chains[i - 2].sums())
+        if i >= 3:
+            ready.append(chains[i - 3].sums())
+        slots = [dispatch(i, g, after(moe_all[g], *ready), False) for g in range(2)]
+        if i == 0:
+            slots[0] = after(slots[0], *[part for parts in grad_slots for part in parts])
         made, back, send, keep = run_expert(
-            place,
-            share[:, i].reshape(-1, 1),
-            slots,
-            grad_slots_of[2 * i : 2 * i + 2],
-            experts[i // 2],
-            i % 2,
+            place, share[:, i].reshape(-1, 1), slots, grad_slots[i], experts[i], 0
         )
         forward_parts.append(made.reshape(2, n_seq, capacity, D))
         backward_parts.append(back.reshape(2, n_seq, capacity, D))
@@ -449,10 +463,12 @@
             together = after(jnp.concatenate([part[g] for part in parts], axis=1), *others)
             total = dot(every_pick[g], together, ((1,), (1,)), ((0,), (0,)))
             sums.append(total.astype(bf16).reshape(span_len, D))
-        return from_group(*sums)
-
-    grad_normed_m = combine(backward_parts, chains[0].sums())
-    grad_normed_m = after(grad_normed_m, *[chain.sums() for chain in chains[1:]])
+        return sums
+
+    backward_sums = combine(backward_parts, *[chain.sums() for chain in chains[:-1]])
+    grad_normed_m = from_group(*backward_sums)
+    forward_sums = combine(forward_parts, *backward_sums, chains[-1].sums())
+    grad_normed_m = after(grad_normed_m, *forward_sums)
 
     scaled_m = grad_normed_m * gain_m
     grad_resid = (
@@ -462,22 +478,23 @@
     )
     grad_gain_m = jnp.sum(grad_normed_m * resid * inv_m, axis=0)
     grad_attn = grad_resid.astype(bf16)
-    mixed = (resid + combine(forward_parts, grad_attn)).astype(bf16)
+    mixed = (resid + from_group(*forward_sums)).astype(bf16)
     grad_heads_rows = dot(grad_attn, out_full, ((1,), (1,))).astype(bf16)
     grad_heads = lax.all_to_all(
         grad_heads_rows, "seq", split_axis=1, concat_axis=0, tiled=True
-    ).reshape(span_len, heads_here, HEAD)
-    grad_out_w = dot(heads_rows, grad_attn, ((0,), (0,))).astype(bf16)
-    out_sum = lax.psum_scatter(grad_out_w, "fsdp", scatter_dimension=0, tiled=True)
-    out_sum = lax.psum(out_sum, "seq").astype(f32)
-
-    grad_heads = after(grad_heads, *[chain.sums() for chain in chains])
-
-    grad_q, grad_k, grad_v = attend_backward(
-        queries, key_rows, values, segment, log_total, grad_heads, block_len
-    )
-    grad_qkv = jnp.stack([grad_q, grad_k, grad_v], axis=1).astype(bf16)
-    grad_qkv = after(grad_qkv.reshape(span_len, 3 * width), mixed)
+    )
+    grad_heads = after(grad_heads, chains[-1].sums())
+    out_sum = None
+    for k in range(n_seq):
+        columns = lax.dynamic_slice_in_dim(grad_attn, (at_seq ^ k) * width, width, 1)
+        part = dot(heads_rows, columns, ((0,), (0,))).astype(bf16)
+        part = (swap(part, "seq", k) if k else part).astype(f32)
+        out_sum = part if out_sum is None else out_sum + part
+    out_sum = lax.psum_scatter(out_sum.astype(bf16), "fsdp", scatter_dimension=0, tiled=True)
+    out_sum = unpack_columns(lax.all_gather(out_sum, "seq", axis=0, tiled=False), width, 1)
+
+    grad_qkv = attend(qkv, segment, grad_heads)
+    grad_qkv = after(grad_qkv, mixed, *[chain.sums() for chain in chains])
     part_normed_a = dot(grad_qkv, qkv_own, ((1,), (1,)))
     grad_normed_a = scatter_rows(part_normed_a.astype(bf16), "seq")
     part_gain_a = jnp.sum(part_normed_a * x_all.astype(f32) * inv_all, axis=0)
@@ -488,11 +505,10 @@
     qkv_sum = lax.psum_scatter(
         jnp.concatenate([grad_qkv_w, gain_columns], axis=1), "fsdp", scatter_dimension=0, tiled=True
     )
+    qkv_sum = after(qkv_sum, grad_normed_a, *[chain.sums() for chain in chains])
     qkv_sum = lax.all_gather(qkv_sum, "seq", axis=0, tiled=False)
     gain_sums = jnp.sum(qkv_sum[:, :, 3 * width : 3 * width + 2].astype(f32), axis=0)
-    qkv_sum = jnp.transpose(
-        qkv_sum[:, :, : 3 * width].reshape(n_seq, shard, 3, width), (1, 2, 0, 3)
-    ).reshape(shard, 3 * D)
+    qkv_sum = unpack_columns(qkv_sum, width, 3)
     inv_a = lax.rsqrt(jnp.mean(x_float * x_float, axis=1, keepdims=True) + epsilon)
     scaled_a = grad_normed_a * gain_a
     grad_x = (
@@ -515,7 +531,7 @@
         grad_x.astype(bf16)[None],
         gain_sums[:, 0],
         gain_sums[:, 1],
-        qkv_sum.astype(f32),
+        qkv_sum,
         out_sum,
         grad_all[:, :, : 2 * FFE].reshape(local_count, shard, 2, FFE),
         jnp.swapaxes(grad_all[:, :, 2 * FFE :], 1, 2),

time: 2130 us -> 1980 us (0.930)
  matrix products: 265 us -> 175 us
  Pallas kernels: 244 us -> 332 us
  other arithmetic: 203 us -> 121 us
  local copies, waits for them, and re-layouts: 220 us -> 172 us
    reduce_scatter x1, waiting for transfers between devices: 158 us -> 5.94 us  [body(): lax.psum_scatter(jnp.concatenate([grad_qkv_w, gain_columns], axis=1), 'fs...]
    ppermute x40 -> x60, waiting for transfers between devices: 840 us -> 965 us  [swap(): return lax.ppermute(value, axis, [(i, i ^ bit) for i in range(size)])]
    dot_general x21 -> x0, matrix products: 111 us -> none  [the longest x6 37.3 us: one_block(): jnp.einsum('qhd,khd->hqk', q_block, key_rows, preferred_element_type=f32)]
    pallas_call x0 -> x4, Pallas kernels: none -> 88.2 us  [the longest x2 76.3 us: attend(): pl.pallas_call(lambda *refs: (attend_backward_kernel if backward else att...]
    convert_element_type x9 -> x2, other arithmetic: 49.8 us -> 5.32 us  [the longest x1 5.31 us: body(): out_sum.astype(bf16)]
    reduce_scatter x2, waiting for transfers between devices: 0.01 us -> 31.8 us  [from_group(): mine = lax.psum_scatter(sums_other, 'seq', scatter_dimension=0, tiled=True)]
    another operation x13 -> x7, other arithmetic: 25.8 us -> 4.05 us  [the longest x5 16.9 us: gather_doubling(): jnp.stack([jnp.where(low, whole, received), jnp.where(low, received, whol...]
    all_gather x1, waiting for transfers between devices: 34.5 us -> 12.7 us  [body(): qkv_sum = lax.all_gather(qkv_sum, 'seq', axis=0, tiled=False)]
  transfers between devices with their start and end apart: 55 -> 74, of which waited for: 19 -> 30; matrix products, arithmetic and copies ran while one was open for 28% -> 21% of each run, Pallas kernels for 11% -> 16%
where the time goes in v3:
time: 1980 us; the launch traced here: 1970 us
  waiting for transfers between devices  1070 us (54%)
  Pallas kernels  332 us (17%)
  matrix products  175 us (9%)
  local copies, waits for them, and re-layouts  172 us (9%)
  other arithmetic  121 us (6%)
  starting transfers between devices  70.6 us (4%)
    ppermute x60, waiting for transfers between devices, swap(): return lax.ppermute(value, axis, [(i, i ^ bit) for i in range(size)])  965 us
    pallas_call x4, Pallas kernels, run_expert(): pl.pallas_call(lambda *refs: expert_kernel(size, tiles, part, *refs), out...  243 us
    dot_general x29, matrix products, dot(): return lax.dot_general(a, b, (contract, batch), preferred_element_type=f32)  175 us
    pallas_call x2, Pallas kernels, attend(): pl.pallas_call(lambda *refs: (attend_backward_kernel if backward else att...  76.3 us
    ppermute x60, starting transfers between devices, swap(): return lax.ppermute(value, axis, [(i, i ^ bit) for i in range(size)])  49 us
    unnamed x158, local copies, waits for them, and re-layouts  39.9 us
  transfers between devices with their start and end apart: 74, of which 30 were waited for; matrix products, arithmetic and copies ran while one was open for 21% of the time, Pallas kernels for 16%

profile of v3, /device:TPU:0, one launch (start us, length us, event | category | flops | bytes accessed | tf_op | source)
XLA Modules:
  0.0 1969.9 jit_solution(1664789084110812073)
XLA Ops:
  27.1 29.0 %collective-permute-done = bf16[384,2048]{1,0:T(8,128)(2,1)} collective-permute-done((bf16[384,2048]{1,0:T(8,128)(2,1)S(1)}, bf16[384,2048]{1,0:T(8,128)(2,1)}, u32[]{:S(2)}, u32[]{:S(2)}) %collective-permute-start) | collective-permute-done | bytes 1572896 | tf_op jit(solution)/shard_map/ppermute | solution.py:21
  58.9 31.6 %collective-permute-done.1 = bf16[384,2048]{1,0:T(8,128)(2,1)} collective-permute-done((bf16[384,2048]{1,0:T(8,128)(2,1)S(1)}, bf16[384,2048]{1,0:T(8,128)(2,1)}, u32[]{:S(2)}, u32[]{:S(2)}) %collective-permute-start.1) | collective-permute-done | bytes 1572896 | tf_op jit(solution)/shard_map/ppermute | solution.py:21
  144.4 50.8 %collective-permute-done.3 = f32[384,16]{0,1:T(8,128)S(1)} collective-permute-done((f32[384,16]{0,1:T(8,128)S(1)}, f32[384,16]{0,1:T(8,128)S(1)}, u32[]{:S(2)}, u32[]{:S(2)}) %collective-permute-start.3) | collective-permute-done | bytes 24608 | tf_op jit(solution)/shard_map/ppermute | solution.py:21
  205.8 71.6 %collective-permute-done.4 = bf16[384,2048]{1,0:T(8,128)(2,1)S(1)} collective-permute-done((bf16[384,2048]{1,0:T(8,128)(2,1)}, bf16[384,2048]{1,0:T(8,128)(2,1)S(1)}, u32[]{:S(2)}, u32[]{:S(2)}) %collective-permute-start.4) | collective-permute-done | bytes 1572896 | tf_op jit(solution)/shard_map/ppermute | solution.py:21
  285.5 15.8 convolution_convert_fusion.1.refs_0_
  315.0 25.2 %attend_forward.1 = bf16[1536,512]{1,0:T(8,128)(2,1)} custom-call(bf16[1536,1536]{1,0:T(8,128)(2,1)} %convolution_convert_fusion.1.refs_0_, s32[1536,1]{1,0:T(8,128)} %reshape.435.refs_1_.refs_2_, s32[1,1536]{1,0:T(1,128)} %reshape.395.refs_2_.refs_3_), custom_call_target="tpu_custom_call" | custom-call | flops 24159191040 | bytes 9437184 | tf_op jit(solution)/shard_map/attend_forward/pallas_call | solution.py:97
  376.8 69.2 %collective-permute-done.20 = bf16[384,2048]{1,0:T(8,128)(2,1)S(1)} collective-permute-done((bf16[384,2048]{1,0:T(8,128)(2,1)}, bf16[384,2048]{1,0:T(8,128)(2,1)S(1)}, u32[]{:S(2)}, u32[]{:S(2)}) %collective-permute-start.20) | collective-permute-done | bytes 1572896 | tf_op jit(solution)/shard_map/ppermute | solution.py:21
  455.7 47.2 %collective-permute-done.17 = bf16[384,2048]{1,0:T(8,128)(2,1)} collective-permute-done((bf16[384,2048]{1,0:T(8,128)(2,1)S(1)}, bf16[384,2048]{1,0:T(8,128)(2,1)}, u32[]{:S(2)}, u32[]{:S(2)}) %collective-permute-start.17) | collective-permute-done | bytes 1572896 | tf_op jit(solution)/shard_map/ppermute | solution.py:21
  506.2 63.3 %collective-permute-done.19 = bf16[384,2048]{1,0:T(8,128)(2,1)} collective-permute-done((bf16[384,2048]{1,0:T(8,128)(2,1)S(1)}, bf16[384,2048]{1,0:T(8,128)(2,1)}, u32[]{:S(2)}, u32[]{:S(2)}) %collective-permute-start.19) | collective-permute-done | bytes 1572896 | tf_op jit(solution)/shard_map/ppermute | solution.py:21
  597.0 51.3 %collective-permute-done.14.refs_10_ = bf16[1,256,3072]{2,1,0:T(8,128)(2,1)} collective-permute-done((bf16[1,256,3072]{2,1,0:T(8,128)(2,1)S(1)}, bf16[1,256,3072]{2,1,0:T(8,128)(2,1)}, u32[]{:S(2)}, u32[]{:S(2)}) %collective-permute-start.14) | collective-permute-done | bytes 1572896 | tf_op jit(solution)/shard_map/ppermute | solution.py:21
  674.2 38.0 %collective-permute-done.25.refs_10_ = bf16[1,256,3072]{2,1,0:T(8,128)(2,1)} collective-permute-done((bf16[1,256,3072]{2,1,0:T(8,128)(2,1)}, bf16[1,256,3072]{2,1,0:T(8,128)(2,1)}, u32[]{:S(2)}, u32[]{:S(2)}) %collective-permute-start.25) | collective-permute-done | bytes 1572896 | tf_op jit(solution)/shard_map/ppermute | solution.py:21
  719.5 60.6 %expert.4 = (bf16[1088,2048]{1,0:T(8,128)(2,1)}, bf16[1088,2048]{1,0:T(8,128)(2,1)}, bf16[4,256,3072]{2,1,0:T(8,128)(2,1)}, bf16[4,256,3072]{2,1,0:T(8,128)(2,1)}) custom-call(s32[1]{0:T(128)} %bitcast.17.refs_0_, f32[1088,1]{1,0:T(8,128)} %reshape_squeeze.16.refs_1_, bf16[544,2048]{1,0:T(8,128)(2,1)} %bitcast.256, bf16[544,2048]{1,0:T(8,128)(2,1)} %bitcast.257, ...), custom_call_target="tpu_custom_call" | custom-call | flops 41070624768 | bytes 42991616 | tf_op jit(solution)/shard_map/expert/pallas_call | solution.py:272
  791.7 61.0 %expert.5 = (bf16[1088,2048]{1,0:T(8,128)(2,1)}, bf16[1088,2048]{1,0:T(8,128)(2,1)}, bf16[4,256,3072]{2,1,0:T(8,128)(2,1)}, bf16[4,256,3072]{2,1,0:T(8,128)(2,1)}) custom-call(s32[1]{0:T(128)} %bitcast.17.refs_0_, f32[1088,1]{1,0:T(8,128)} %reshape_squeeze.17.refs_1_, bf16[544,2048]{1,0:T(8,128)(2,1)} %bitcast.263, bf16[544,2048]{1,0:T(8,128)(2,1)} %bitcast.262, ...), custom_call_target="tpu_custom_call" | custom-call | flops 41070624768 | bytes 42991616 | tf_op jit(solution)/shard_map/expert/pallas_call | solution.py:272
  867.1 57.5 %collective-permute-done.32.refs_10_ = bf16[1,256,3072]{2,1,0:T(8,128)(2,1)} collective-permute-done((bf16[1,256,3072]{2,1,0:T(8,128)(2,1)}, bf16[1,256,3072]{2,1,0:T(8,128)(2,1)}, u32[]{:S(2)}, u32[]{:S(2)}) %collective-permute-start.32) | collective-permute-done | bytes 1572896 | tf_op jit(solution)/shard_map/ppermute | solution.py:21
  936.8 25.7 %collective-permute-done.31.refs_12_ = bf16[1,256,3072]{2,1,0:T(8,128)(2,1)S(1)} collective-permute-done((bf16[1,256,3072]{2,1,0:T(8,128)(2,1)}, bf16[1,256,3072]{2,1,0:T(8,128)(2,1)S(1)}, u32[]{:S(2)}, u32[]{:S(2)}) %collective-permute-start.31) | collective-permute-done | bytes 1572896 | tf_op jit(solution)/shard_map/ppermute | solution.py:21
  962.5 33.0 %collective-permute-done.39.refs_12_ = bf16[1,256,3072]{2,1,0:T(8,128)(2,1)} collective-permute-done((bf16[1,256,3072]{2,1,0:T(8,128)(2,1)}, bf16[1,256,3072]{2,1,0:T(8,128)(2,1)}, u32[]{:S(2)}, u32[]{:S(2)}) %collective-permute-start.39) | collective-permute-done | bytes 1572896 | tf_op jit(solution)/shard_map/ppermute | solution.py:21
  1008.9 60.9 %expert.6 = (bf16[1088,2048]{1,0:T(8,128)(2,1)}, bf16[1088,2048]{1,0:T(8,128)(2,1)}, bf16[4,256,3072]{2,1,0:T(8,128)(2,1)}, bf16[4,256,3072]{2,1,0:T(8,128)(2,1)}) custom-call(s32[1]{0:T(128)} %bitcast.17.refs_0_, f32[1088,1]{1,0:T(8,128)} %reshape_squeeze.18.refs_1_, bf16[544,2048]{1,0:T(8,128)(2,1)} %bitcast.259, bf16[544,2048]{1,0:T(8,128)(2,1)} %bitcast.258, ...), custom_call_target="tpu_custom_call" | custom-call | flops 41070624768 | bytes 42991616 | tf_op jit(solution)/shard_map/expert/pallas_call | solution.py:272
  1091.0 60.9 %expert.7 = (bf16[1088,2048]{1,0:T(8,128)(2,1)}, bf16[1088,2048]{1,0:T(8,128)(2,1)}, bf16[4,256,3072]{2,1,0:T(8,128)(2,1)}, bf16[4,256,3072]{2,1,0:T(8,128)(2,1)}) custom-call(s32[1]{0:T(128)} %bitcast.17.refs_0_, f32[1088,1]{1,0:T(8,128)} %reshape_squeeze.19.refs_1_, bf16[544,2048]{1,0:T(8,128)(2,1)} %bitcast.261, bf16[544,2048]{1,0:T(8,128)(2,1)} %bitcast.260, ...), custom_call_target="tpu_custom_call" | custom-call | flops 41070624768 | bytes 42991616 | tf_op jit(solution)/shard_map/expert/pallas_call | solution.py:272
  1242.8 31.8 %reduce-scatter.13.cloned.1.call-done = bf16[384,2048]{1,0:T(8,128)(2,1)} async-done(((bf16[1536,2048]{1,0:T(8,128)(2,1)}), bf16[384,2048]{1,0:T(8,128)(2,1)}) %reduce-scatter.13.cloned.1.call-update) | async-done | bytes 1572880 | tf_op jit(solution)/shard_map/reduce_scatter | solution.py:350
  1277.0 101.6 %collective-permute-done.51 = bf16[2,256,3072]{2,1,0:T(8,128)(2,1)} collective-permute-done((bf16[2,256,3072]{2,1,0:T(8,128)(2,1)S(1)}, bf16[2,256,3072]{2,1,0:T(8,128)(2,1)}, u32[]{:S(2)}, u32[]{:S(2)}) %collective-permute-start.51) | collective-permute-done | bytes 3145760 | tf_op jit(solution)/shard_map/ppermute | solution.py:21
  1384.9 60.0 %collective-permute-done.49 = bf16[2,256,3072]{2,1,0:T(8,128)(2,1)} collective-permute-done((bf16[2,256,3072]{2,1,0:T(8,128)(2,1)}, bf16[2,256,3072]{2,1,0:T(8,128)(2,1)}, u32[]{:S(2)}, u32[]{:S(2)}) %collective-permute-start.49) | collective-permute-done | bytes 3145760 | tf_op jit(solution)/shard_map/ppermute | solution.py:21
  1456.4 38.9 %reduce-scatter.7.cloned.1.call-done = bf16[384,2048]{1,0:T(8,128)(2,1)} async-done(((bf16[1536,2048]{1,0:T(8,128)(2,1)}), bf16[384,2048]{1,0:T(8,128)(2,1)}) %reduce-scatter.7.cloned.1.call-update) | async-done | bytes 1572880 | tf_op jit(solution)/shard_map/reduce_scatter | solution.py:352
  1495.3 50.7 %collective-permute-done.47 = bf16[384,2048]{1,0:T(8,128)(2,1)} collective-permute-done((bf16[384,2048]{1,0:T(8,128)(2,1)}, bf16[384,2048]{1,0:T(8,128)(2,1)}, u32[]{:S(2)}, u32[]{:S(2)}) %collective-permute-start.47) | collective-permute-done | bytes 1572896 | tf_op jit(solution)/shard_map/ppermute | solution.py:21
  1560.2 16.3 all-to-all-start.1
  1597.3 51.1 %attend_backward.1 = bf16[1536,1536]{1,0:T(8,128)(2,1)} custom-call(bf16[1536,1536]{1,0:T(8,128)(2,1)} %convolution_convert_fusion.1.refs_0_, bf16[1536,512]{1,0:T(8,128)(2,1)} %bitcast.81.refs_1_, s32[1536,1]{1,0:T(8,128)} %reshape.435.refs_1_.refs_2_, s32[1,1536]{1,0:T(1,128)} %reshape.395.refs_2_.refs_3_), custom_call_target="tpu_custom_call" | custom-call | flops 48318382080 | bytes 9437184 | tf_op jit(solution)/shard_map/attend_backward/pallas_call | solution.py:97
  1648.5 38.7 %collective-permute-done.59 = bf16[2048,512]{1,0:T(8,128)(2,1)} collective-permute-done((bf16[2048,512]{1,0:T(8,128)(2,1)}, bf16[2048,512]{1,0:T(8,128)(2,1)}, u32[]{:S(2)}, u32[]{:S(2)}) %collective-permute-start.59) | collective-permute-done | bytes 2097184 | tf_op jit(solution)/shard_map/ppermute | solution.py:21
  1693.0 16.8 fusion.4
  1710.7 16.0 convolution_convert_fusion
  1742.3 33.9 %collective-permute-done.53 = bf16[384,2048]{1,0:T(8,128)(2,1)} collective-permute-done((bf16[384,2048]{1,0:T(8,128)(2,1)}, bf16[384,2048]{1,0:T(8,128)(2,1)}, u32[]{:S(2)}, u32[]{:S(2)}) %collective-permute-start.53) | collective-permute-done | bytes 1572896 | tf_op jit(solution)/shard_map/ppermute | solution.py:21
  1776.2 33.4 %collective-permute-done.54 = bf16[384,2048]{1,0:T(8,128)(2,1)} collective-permute-done((bf16[384,2048]{1,0:T(8,128)(2,1)}, bf16[384,2048]{1,0:T(8,128)(2,1)}, u32[]{:S(2)}, u32[]{:S(2)}) %collective-permute-start.54) | collective-permute-done | bytes 1572896 | tf_op jit(solution)/shard_map/ppermute | solution.py:21
  1815.4 43.1 %collective-permute-done.56 = bf16[1,256,3072]{2,1,0:T(8,128)(2,1)} collective-permute-done((bf16[1,256,3072]{2,1,0:T(8,128)(2,1)S(1)}, bf16[1,256,3072]{2,1,0:T(8,128)(2,1)}, u32[]{:S(2)}, u32[]{:S(2)}) %collective-permute-start.56) | collective-permute-done | bytes 1572896 | tf_op jit(solution)/shard_map/ppermute | solution.py:21
  1903.5 22.1 %reshape.423 = f32[8,256,2,1024]{3,2,1,0:T(2,128)} reshape(f32[8,256,2048]{2,1,0:T(8,128)} %slice.520) | data formatting | bytes 33554432 | tf_op jit(solution)/shard_map/reshape | solution.py:536
  (439 shorter events, 547.1 us)
Async XLA Ops:
  7.2 277.5 %all-gather.13.cloned.1.call-start = ((), (), s32[]{:S(2)}) async-start(), calls=%async_computation.8 | async-start | bytes 7667712 | tf_op jit(solution)/shard_map/all_gather | solution.py:380
  17.7 349.2 %all-gather.15.cloned.1.call-start = ((), (), s32[]{:S(2)}) async-start(), calls=%async_computation.9 | async-start | bytes 9437184 | tf_op jit(solution)/shard_map/all_gather | solution.py:386
  123.8 237.0 %collective-permute-start.10 = (bf16[1,256,3072]{2,1,0:T(8,128)(2,1)}, bf16[1,256,3072]{2,1,0:T(8,128)(2,1)}, u32[]{:S(2)}, u32[]{:S(2)}) collective-permute-start(bf16[1,256,3072]{2,1,0:T(8,128)(2,1)} %get-tuple-element.219.refs_6_), channel_id=1, source_target_pairs={{0,1},{1,0},{2,3},{3,2},{4,5},{5,4},{6,7},{7,6},{8,9},{9,8},{10,11... | collective-permute-start | bytes 4718600 | tf_op jit(solution)/shard_map/ppermute | solution.py:21
  123.8 237.0 %collective-permute-start.9 = (bf16[1,256,3072]{2,1,0:T(8,128)(2,1)}, bf16[1,256,3072]{2,1,0:T(8,128)(2,1)}, u32[]{:S(2)}, u32[]{:S(2)}) collective-permute-start(bf16[1,256,3072]{2,1,0:T(8,128)(2,1)} %get-tuple-element.219.refs_6_), channel_id=1, source_target_pairs={{0,2},{1,3},{2,0},{3,1},{4,6},{5,7},{6,4},{7,5},{8,10},{9,11},{10,... | collective-permute-start | bytes 4718600 | tf_op jit(solution)/shard_map/ppermute | solution.py:21
  128.2 149.3 %collective-permute-start.4 = (bf16[384,2048]{1,0:T(8,128)(2,1)}, bf16[384,2048]{1,0:T(8,128)(2,1)S(1)}, u32[]{:S(2)}, u32[]{:S(2)}) collective-permute-start(bf16[384,2048]{1,0:T(8,128)(2,1)} %bitcast.8), channel_id=1, source_target_pairs={{0,4},{1,5},{2,6},{3,7},{4,0},{5,1},{6,2},{7,3},{8,12},{9,13},{10,... | collective-permute-start | bytes 4718600 | tf_op jit(solution)/shard_map/ppermute | solution.py:21
  131.4 229.4 %collective-permute-start.8 = (bf16[1,256,3072]{2,1,0:T(8,128)(2,1)}, bf16[1,256,3072]{2,1,0:T(8,128)(2,1)}, u32[]{:S(2)}, u32[]{:S(2)}) collective-permute-start(bf16[1,256,3072]{2,1,0:T(8,128)(2,1)} %get-tuple-element.215), channel_id=1, source_target_pairs={{0,4},{1,5},{2,6},{3,7},{4,0},{5,1},{6,2},{7,3},{8,12},{9,13},{10,... | collective-permute-start | bytes 4718600 | tf_op jit(solution)/shard_map/ppermute | solution.py:21
  346.3 316.5 %all-gather.17.cloned.1.call-start = ((), (), s32[]{:S(2)}) async-start(), calls=%async_computation.16 | async-start | bytes 7864320 | tf_op jit(solution)/shard_map/all_gather | solution.py:344
  376.7 291.5 %all-gather.19.cloned.1.call-start = ((), (), s32[]{:S(2)}) async-start(), calls=%async_computation.17 | async-start | bytes 7864320 | tf_op jit(solution)/shard_map/all_gather | solution.py:346
  447.2 827.5 %reduce-scatter.13.cloned.1.call-start = ((), (), s32[]{:S(2)}) async-start(), calls=%async_computation.13 | async-start | bytes 7864320 | tf_op jit(solution)/shard_map/reduce_scatter | solution.py:350
  449.5 120.0 %collective-permute-start.19 = (bf16[384,2048]{1,0:T(8,128)(2,1)S(1)}, bf16[384,2048]{1,0:T(8,128)(2,1)}, u32[]{:S(2)}, u32[]{:S(2)}) collective-permute-start(bf16[384,2048]{1,0:T(8,128)(2,1)S(1)} %copy-done.34), channel_id=1, source_target_pairs={{0,24},{8,16},{16,8},{24,0},{1,25},{9,17},{17,9},{25,1},{2,26},{10... | collective-permute-start | bytes 4718600 | tf_op jit(solution)/shard_map/ppermute | solution.py:21
  454.2 131.1 %collective-permute-start.11 = (bf16[1,256,3072]{2,1,0:T(8,128)(2,1)}, bf16[1,256,3072]{2,1,0:T(8,128)(2,1)S(1)}, u32[]{:S(2)}, u32[]{:S(2)}) collective-permute-start(bf16[1,256,3072]{2,1,0:T(8,128)(2,1)} %collective-permute-done.9.refs_8_), channel_id=1, source_target_pairs={{0,1},{1,0},{2,3},{3,2},{4,5},{5,4},{6,7},{7,6},{8,9},{9,8},{10,11... | collective-permute-start | bytes 4718600 | tf_op jit(solution)/shard_map/ppermute | solution.py:21
  454.2 142.6 %collective-permute-start.12 = (bf16[1,256,3072]{2,1,0:T(8,128)(2,1)}, bf16[1,256,3072]{2,1,0:T(8,128)(2,1)S(1)}, u32[]{:S(2)}, u32[]{:S(2)}) collective-permute-start(bf16[1,256,3072]{2,1,0:T(8,128)(2,1)} %collective-permute-done.8.refs_10_), channel_id=1, source_target_pairs={{0,1},{1,0},{2,3},{3,2},{4,5},{5,4},{6,7},{7,6},{8,9},{9,8},{10,11... | collective-permute-start | bytes 4718600 | tf_op jit(solution)/shard_map/ppermute | solution.py:21
  659.6 120.5 %collective-permute-start.26 = (bf16[1,256,3072]{2,1,0:T(8,128)(2,1)S(1)}, bf16[1,256,3072]{2,1,0:T(8,128)(2,1)}, u32[]{:S(2)}, u32[]{:S(2)}) collective-permute-start(bf16[1,256,3072]{2,1,0:T(8,128)(2,1)S(1)} %copy-done.26), channel_id=1, source_target_pairs={{0,2},{1,3},{2,0},{3,1},{4,6},{5,7},{6,4},{7,5},{8,10},{9,11},{10,... | collective-permute-start | bytes 4718600 | tf_op jit(solution)/shard_map/ppermute | solution.py:21
  662.8 117.4 %collective-permute-start.27 = (bf16[1,256,3072]{2,1,0:T(8,128)(2,1)S(1)}, bf16[1,256,3072]{2,1,0:T(8,128)(2,1)}, u32[]{:S(2)}, u32[]{:S(2)}) collective-permute-start(bf16[1,256,3072]{2,1,0:T(8,128)(2,1)S(1)} %copy-done.26), channel_id=1, source_target_pairs={{0,1},{1,0},{2,3},{3,2},{4,5},{5,4},{6,7},{7,6},{8,9},{9,8},{10,11... | collective-permute-start | bytes 4718600 | tf_op jit(solution)/shard_map/ppermute | solution.py:21
  780.2 144.9 %collective-permute-start.35 = (bf16[4,256,3072]{2,1,0:T(8,128)(2,1)}, bf16[4,256,3072]{2,1,0:T(8,128)(2,1)}, u32[]{:S(2)}, u32[]{:S(2)}) collective-permute-start(bf16[4,256,3072]{2,1,0:T(8,128)(2,1)} %get-tuple-element.121), channel_id=1, source_target_pairs={{0,1},{1,0},{2,3},{3,2},{4,5},{5,4},{6,7},{7,6},{8,9},{9,8},{10,11... | collective-permute-start | bytes 18874376 | tf_op jit(solution)/shard_map/ppermute | solution.py:21
  852.8 148.2 %collective-permute-start.40 = (bf16[4,256,3072]{2,1,0:T(8,128)(2,1)}, bf16[4,256,3072]{2,1,0:T(8,128)(2,1)}, u32[]{:S(2)}, u32[]{:S(2)}) collective-permute-start(bf16[4,256,3072]{2,1,0:T(8,128)(2,1)} %get-tuple-element.127), channel_id=1, source_target_pairs={{0,1},{1,0},{2,3},{3,2},{4,5},{5,4},{6,7},{7,6},{8,9},{9,8},{10,11... | collective-permute-start | bytes 18874376 | tf_op jit(solution)/shard_map/ppermute | solution.py:21
  936.3 146.4 %collective-permute-start.38 = (bf16[1,256,3072]{2,1,0:T(8,128)(2,1)}, bf16[1,256,3072]{2,1,0:T(8,128)(2,1)}, u32[]{:S(2)}, u32[]{:S(2)}) collective-permute-start(bf16[1,256,3072]{2,1,0:T(8,128)(2,1)} %collective-permute-done.32.refs_10_), channel_id=1, source_target_pairs={{0,1},{1,0},{2,3},{3,2},{4,5},{5,4},{6,7},{7,6},{8,9},{9,8},{10,11... | collective-permute-start | bytes 4718600 | tf_op jit(solution)/shard_map/ppermute | solution.py:21
  936.3 145.9 %collective-permute-start.37 = (bf16[1,256,3072]{2,1,0:T(8,128)(2,1)}, bf16[1,256,3072]{2,1,0:T(8,128)(2,1)}, u32[]{:S(2)}, u32[]{:S(2)}) collective-permute-start(bf16[1,256,3072]{2,1,0:T(8,128)(2,1)} %collective-permute-done.33.refs_8_), channel_id=1, source_target_pairs={{0,1},{1,0},{2,3},{3,2},{4,5},{5,4},{6,7},{7,6},{8,9},{9,8},{10,11... | collective-permute-start | bytes 4718600 | tf_op jit(solution)/shard_map/ppermute | solution.py:21
  1007.2 165.8 %collective-permute-start.44 = (bf16[2,256,3072]{2,1,0:T(8,128)(2,1)}, bf16[2,256,3072]{2,1,0:T(8,128)(2,1)}, u32[]{:S(2)}, u32[]{:S(2)}) collective-permute-start(bf16[2,256,3072]{2,1,0:T(8,128)(2,1)} %add_convert_fusion.2), channel_id=1, source_target_pairs={{0,2},{1,3},{2,0},{3,1},{4,6},{5,7},{6,4},{7,5},{8,10},{9,11},{10,... | collective-permute-start | bytes 9437192 | tf_op jit(solution)/shard_map/ppermute | solution.py:21
  1192.7 191.7 %reduce-scatter.9.cloned.1.call-start = ((), (), s32[]{:S(2)}) async-start(), calls=%async_computation.11 | async-start | bytes 7864320 | tf_op jit(solution)/shard_map/reduce_scatter | solution.py:350
  1225.1 225.8 %reduce-scatter.11.cloned.1.call-start = ((), (), s32[]{:S(2)}) async-start(), calls=%async_computation.12 | async-start | bytes 7864320 | tf_op jit(solution)/shard_map/reduce_scatter | solution.py:352
  1225.9 269.4 %reduce-scatter.7.cloned.1.call-start = ((), (), s32[]{:S(2)}) async-start(), calls=%async_computation.10 | async-start | bytes 7864320 | tf_op jit(solution)/shard_map/reduce_scatter | solution.py:352
  1240.2 138.5 %collective-permute-start.51 = (bf16[2,256,3072]{2,1,0:T(8,128)(2,1)S(1)}, bf16[2,256,3072]{2,1,0:T(8,128)(2,1)}, u32[]{:S(2)}, u32[]{:S(2)}) collective-permute-start(bf16[2,256,3072]{2,1,0:T(8,128)(2,1)S(1)} %copy-done.24), channel_id=1, source_target_pairs={{0,2},{1,3},{2,0},{3,1},{4,6},{5,7},{6,4},{7,5},{8,10},{9,11},{10,... | collective-permute-start | bytes 9437192 | tf_op jit(solution)/shard_map/ppermute | solution.py:21
  1240.2 204.7 %collective-permute-start.49 = (bf16[2,256,3072]{2,1,0:T(8,128)(2,1)}, bf16[2,256,3072]{2,1,0:T(8,128)(2,1)}, u32[]{:S(2)}, u32[]{:S(2)}) collective-permute-start(bf16[2,256,3072]{2,1,0:T(8,128)(2,1)} %add_convert_fusion), channel_id=1, source_target_pairs={{0,2},{1,3},{2,0},{3,1},{4,6},{5,7},{6,4},{7,5},{8,10},{9,11},{10,... | collective-permute-start | bytes 9437192 | tf_op jit(solution)/shard_map/ppermute | solution.py:21
  1242.2 406.2 %collective-permute-start.50 = (bf16[1,256,3072]{2,1,0:T(8,128)(2,1)}, bf16[1,256,3072]{2,1,0:T(8,128)(2,1)}, u32[]{:S(2)}, u32[]{:S(2)}) collective-permute-start(bf16[1,256,3072]{2,1,0:T(8,128)(2,1)} %get-tuple-element.196), channel_id=1, source_target_pairs={{0,4},{1,5},{2,6},{3,7},{4,0},{5,1},{6,2},{7,3},{8,12},{9,13},{10,... | collective-permute-start | bytes 4718600 | tf_op jit(solution)/shard_map/ppermute | solution.py:21
  1274.6 176.3 %collective-permute-start.48 = (bf16[384,2048]{1,0:T(8,128)(2,1)}, bf16[384,2048]{1,0:T(8,128)(2,1)}, u32[]{:S(2)}, u32[]{:S(2)}) collective-permute-start(bf16[384,2048]{1,0:T(8,128)(2,1)} %reduce-scatter.13.cloned.1.call-done), channel_id=1, source_target_pairs={{0,4},{1,5},{2,6},{3,7},{4,0},{5,1},{6,2},{7,3},{8,12},{9,13},{10,... | collective-permute-start | bytes 4718600 | tf_op jit(solution)/shard_map/ppermute | solution.py:21
  1384.4 161.6 %collective-permute-start.47 = (bf16[384,2048]{1,0:T(8,128)(2,1)}, bf16[384,2048]{1,0:T(8,128)(2,1)}, u32[]{:S(2)}, u32[]{:S(2)}) collective-permute-start(bf16[384,2048]{1,0:T(8,128)(2,1)} %reduce-scatter.9.cloned.1.call-done), channel_id=1, source_target_pairs={{0,4},{1,5},{2,6},{3,7},{4,0},{5,1},{6,2},{7,3},{8,12},{9,13},{10,... | collective-permute-start | bytes 4718600 | tf_op jit(solution)/shard_map/ppermute | solution.py:21
  1450.8 197.6 %collective-permute-start.52 = (bf16[1,256,3072]{2,1,0:T(8,128)(2,1)}, bf16[1,256,3072]{2,1,0:T(8,128)(2,1)}, u32[]{:S(2)}, u32[]{:S(2)}) collective-permute-start(bf16[1,256,3072]{2,1,0:T(8,128)(2,1)} %get-tuple-element.200), channel_id=1, source_target_pairs={{0,4},{1,5},{2,6},{3,7},{4,0},{5,1},{6,2},{7,3},{8,12},{9,13},{10,... | collective-permute-start | bytes 4718600 | tf_op jit(solution)/shard_map/ppermute | solution.py:21
  1576.5 165.5 %reduce-scatter.17.cloned.1.call-start = ((), (), s32[]{:S(2)}) async-start(), calls=%async_computation.15 | async-start | bytes 2359296 | tf_op jit(solution)/shard_map/reduce_scatter | solution.py:493
  1692.5 172.0 %reduce-scatter.15.cloned.1.call-start = ((), (), s32[]{:S(2)}) async-start(), calls=%async_computation.14 | async-start | bytes 7667712 | tf_op jit(solution)/shard_map/reduce_scatter | solution.py:505
  1733.6 197.2 %all-gather.23.cloned.1.call-start = ((), (), s32[]{:S(2)}) async-start(), calls=%async_computation.19 | async-start | bytes 1310720 | tf_op jit(solution)/shard_map/all_gather | solution.py:494
  1742.1 205.0 %all-gather.21.cloned.1.call-start = ((), (), s32[]{:S(2)}) async-start(), calls=%async_computation.18 | async-start | bytes 4259840 | tf_op jit(solution)/shard_map/all_gather | solution.py:509
  (118 other events, 4470.6 us)
Sparse Core Ops, SparseCore 0:
  17.9 72.1 all-gather.12
  94.6 136.0 all-gather.14
  376.8 68.3 all-gather.16
  447.5 120.5 all-gather.18
  1192.9 81.7 reduce-scatter.12
  1278.0 70.2 reduce-scatter.8
  1351.3 70.1 reduce-scatter.10
  1425.1 70.2 reduce-scatter.6
  1692.6 33.2 reduce-scatter.16
  1733.7 130.7 reduce-scatter.14
  1866.3 32.9 all-gather.22
  1901.0 46.0 all-gather.20

commit v4 on v3

--- a/solution.py
+++ b/solution.py
@@ -147,29 +147,29 @@
 def start_expert(mine, sent, *start):
     size = lax.axis_size("fsdp")
     mine, sent = after(mine, *start), after(sent, *start)
-    pieces = {0: mine, size // 2: swap(sent, "fsdp", size // 2)}
+    pieces = {size // 2: swap(sent, "fsdp", size // 2)}
     bit = size // 4
-    while bit:
+    while bit > 1:
         pieces[bit] = swap(mine, "fsdp", bit)
         bit //= 2
     return pieces
 
 
-def finish_expert(pieces):
+def finish_expert(pieces, *start):
     size = lax.axis_size("fsdp")
     pieces = dict(pieces)
-    for j in sorted(range(size), key=lambda j: (j & 1, j.bit_count())):
+    for j in sorted(range(2, size, 2), key=lambda j: j.bit_count()):
         if j not in pieces:
             low = j & -j
-            pieces[j] = swap(pieces[j ^ low], "fsdp", low)
-    return [pieces[j] for j in range(size)]
-
-
-def gather_rows(piece, axis):
+            pieces[j] = swap(after(pieces[j ^ low], *start), "fsdp", low)
+    return [pieces[j] for j in range(2, size, 2)]
+
+
+def gather_rows(piece, axis, *others):
     place, rows = lax.axis_index(axis), piece.shape[0]
     whole = jnp.zeros((lax.axis_size(axis) * rows, *piece.shape[1:]), piece.dtype)
     for k in range(lax.axis_size(axis)):
-        part = swap(piece, axis, k) if k else piece
+        part = swap(piece, axis, k) if k else after(piece, *others)
         whole = lax.dynamic_update_slice_in_dim(whole, part, (place ^ k) * rows, 0)
     return whole
 
@@ -183,9 +183,11 @@
     return sum((swap(part, axis, k) if k else part).astype(f32) for k, part in enumerate(parts))
 
 
-def expert_kernel(size, tiles, part, place_ref, share_ref, *rest):
-    slots, pieces, rest = rest[:4], rest[4 : 4 + size], rest[4 + size :]
-    made_ref, back_ref, send_ref, keep_ref, weights, x_ref, g_ref, act, grad_proj, sems = rest
+def expert_kernel(size, tiles, parts, place_ref, share_ref, *rest):
+    arrays = 1 + max(array for array, _ in parts)
+    slots, pieces, rest = rest[:4], rest[4 : 4 + arrays], rest[4 + arrays :]
+    made_refs, back_refs, rest = rest[:2], rest[2:4], rest[4:]
+    send_ref, keep_ref, weights, x_ref, g_ref, act, grad_proj, sems = rest
     step = pl.program_id(0)
     place = place_ref[0]
     rows = weights.shape[0] // size
@@ -197,7 +199,7 @@
     def _():
         copies = [
             pltpu.make_async_copy(
-                pieces[j].at[part],
+                pieces[parts[j][0]].at[parts[j][1]],
                 weights.at[pl.ds(pl.multiple_of((place ^ j) * rows, rows), rows)],
                 sems.at[j],
             )
@@ -240,10 +242,12 @@
         turn = step - tiles
         whose = place ^ reversed_bits((turn + size // 2) % size, size)
         at = pl.ds(pl.multiple_of(whose * rows, rows), rows)
-        made_ref[...] = (
-            share_ref[...] * dot(act[...], weights[at, 2 * ffe :], nt)
-        ).astype(bf16)
-        back_ref[...] = dot(grad_proj[...], weights[at, : 2 * ffe], nt).astype(bf16)
+        count = act.shape[0] // 2
+        made = (share_ref[...] * dot(act[...], weights[at, 2 * ffe :], nt)).astype(bf16)
+        back = dot(grad_proj[...], weights[at, : 2 * ffe], nt).astype(bf16)
+        for g in range(2):
+            made_refs[g][...] = made[g * count : (g + 1) * count]
+            back_refs[g][...] = back[g * count : (g + 1) * count]
 
         def grads(out_ref):
             out_ref[0, :, : 2 * ffe] = dot(x_ref[:, at], grad_proj[...], tn).astype(bf16)
@@ -258,8 +262,8 @@
             grads(keep_ref)
 
 
-def run_expert(place, share, slots, grad_slots, pieces, part):
-    size, (_, rows, columns) = len(pieces), pieces[0].shape
+def run_expert(place, share, slots, grad_slots, pieces, parts):
+    size, (_, rows, columns) = len(parts), pieces[0].shape
     count = 2 * slots[0].shape[0]
     ffe = columns // 3
     tiles = 4
@@ -270,10 +274,9 @@
         return 0, place[0] ^ reversed_bits((turn + half) % size, size)
 
     return pl.pallas_call(
-        lambda *refs: expert_kernel(size, tiles, part, *refs),
+        lambda *refs: expert_kernel(size, tiles, parts, *refs),
         out_shape=[
-            jax.ShapeDtypeStruct((count, D), bf16),
-            jax.ShapeDtypeStruct((count, D), bf16),
+            *[jax.ShapeDtypeStruct((count // 2, D), bf16)] * 4,
             jax.ShapeDtypeStruct((half, rows, columns), bf16),
             jax.ShapeDtypeStruct((half, rows, columns), bf16),
         ],
@@ -282,11 +285,10 @@
             grid=(tiles + size,),
             in_specs=[
                 pl.BlockSpec((count, 1), lambda step, place: (0, 0)),
-                *[pl.BlockSpec(memory_space=pl.ANY)] * (size + 4),
+                *[pl.BlockSpec(memory_space=pl.ANY)] * (len(pieces) + 4),
             ],
             out_specs=[
-                pl.BlockSpec((count, rows), whose),
-                pl.BlockSpec((count, rows), whose),
+                *[pl.BlockSpec((count // 2, rows), whose)] * 4,
                 pl.BlockSpec(
                     (1, rows, columns), lambda t, place: (jnp.clip(t - tiles, 0, half - 1), 0, 0)
                 ),
@@ -321,36 +323,27 @@
         self.bit, self.size = 1, lax.axis_size("fsdp")
         self.terms, self.send = [keep], send
 
-    def sums(self):
-        if self.bit == self.size:
-            return self.terms[-1]
-        received = swap(self.send, "fsdp", self.bit)
-        self.terms.append(received)
-        self.bit *= 2
+    def arrive(self):
+        if self.bit < self.size:
+            self.terms.append(swap(self.send, "fsdp", self.bit))
+            self.bit *= 2
+        return self.terms[-1]
+
+    def add(self, *others):
         many = self.terms[0].shape[0] // 2
         if many:
-            total = sum(t[many:].astype(f32) for t in self.terms)
-            self.send = total.astype(bf16)
+            self.terms[0] = after(self.terms[0], *others)
+            self.send = sum(t[many:].astype(f32) for t in self.terms).astype(bf16)
             self.terms = [t[:many] for t in self.terms]
-            return self.send
-        return received
+        return self.send
+
+    def sums(self):
+        self.arrive()
+        return self.add()
 
     def ended(self):
         other = self.terms.pop()[0]
         return sum(t[0].astype(f32) for t in self.terms).astype(bf16), other
-
-
-def to_group(rows, *others):
-    own = lax.all_gather(rows, "seq", axis=0, tiled=False)
-    swapped = swap(after(rows, *others), "fsdp", lax.axis_size("fsdp") // 2)
-    return own, lax.all_gather(swapped, "seq", axis=0, tiled=False), swapped
-
-
-def from_group(sums_own, sums_other):
-    mine = lax.psum_scatter(sums_other, "seq", scatter_dimension=0, tiled=True)
-    other = swap(mine, "fsdp", lax.axis_size("fsdp") // 2)
-    mine = lax.psum_scatter(sums_own, "seq", scatter_dimension=0, tiled=True)
-    return mine.astype(f32) + other.astype(f32)
 
 
 def body(
@@ -372,7 +365,8 @@
     )
     own_part = lax.dynamic_slice_in_dim(packed, half * per_half, per_half, 0)
     other_part = lax.dynamic_slice_in_dim(packed, (1 - half) * per_half, per_half, 0)
-    x_all = gather_rows(tokens[0], "seq")
+    cot_other = swap(cotangent[0], "fsdp", n_fsdp // 2)
+
     part = lax.dynamic_slice_in_dim(
         w_qkv.reshape(shard, 3, HEADS, HEAD), at_seq * heads_here, heads_here, 2
     ).reshape(shard, 3 * width)
@@ -383,11 +377,11 @@
     qkv_own = gathered[:, : 3 * width]
     gain_a = gathered[:, 3 * width].astype(f32)
     gain_m = gathered[:, 3 * width + 1].astype(f32)
-    out_full = lax.all_gather(after(w_out, x_all), "fsdp", axis=0, tiled=True)
-    cot_other = swap(cotangent[0], "fsdp", n_fsdp // 2)
 
     routing = jnp.concatenate([routes[0].astype(f32), gates[0]], axis=1)
-    routing = jnp.stack(to_group(routing)[:2]).reshape(2 * n_seq, rows, 2 * TOP)
+    routing = jnp.stack([routing, swap(routing, "fsdp", n_fsdp // 2)])
+    routing = jnp.swapaxes(lax.all_gather(routing, "seq", axis=0, tiled=False), 0, 1)
+    routing = routing.reshape(2 * n_seq, rows, 2 * TOP)
     capacity = rows * TOP * 4 // (3 * local_count * n_seq) + 2
     capacity = -(-capacity // 8) * 8
     named = at_seq * local_count + half * per_half + lax.iota(jnp.int32, per_half)
@@ -407,7 +401,8 @@
         inverse = lax.rsqrt(jnp.mean(values * values, axis=1, keepdims=True) + epsilon)
         return (values * inverse * gain).astype(bf16), inverse
 
-    x_all = after(x_all, own_part, other_part, picks, share, cot_other)
+    x_all = gather_rows(tokens[0], "seq", own_part, other_part, picks, share, cot_other)
+    out_full = lax.all_gather(after(w_out, x_all), "fsdp", axis=0, tiled=True)
     normed_a, inv_all = normed_rows(x_all.astype(f32), gain_a)
     qkv = dot(normed_a, qkv_own, ((1,), (0,))).astype(bf16)
     segment = segment_ids(lengths[0], span_len)
@@ -416,19 +411,21 @@
     cot_own = gather_rows(after(cotangent[0], x_all), "seq")
     cot_all = [cot_own, gather_rows(after(cot_other, x_all), "seq")]
     cot_all = [rows_of.reshape(n_seq, rows, D) for rows_of in cot_all]
-    begun = [start_expert(own_part[:1], other_part[:1])]
-    heads_rows = after(heads_rows, cot_own, *begun[0].values())
+    beside = swap(after(own_part, x_all), "fsdp", 1)
+    heads_rows = after(heads_rows, cot_own, beside)
+    begun = [start_expert(own_part[:1], other_part[:1], out_full)]
     x_float = tokens[0].astype(f32)
     resid = x_float + dot(heads_rows, out_full, ((1,), (0,)))
     normed_m, inv_m = normed_rows(resid, gain_m)
-    moe_all = to_group(normed_m)
-
-    for i in range(1, per_half):
-        begun.append(start_expert(own_part[i : i + 1], other_part[i : i + 1], attended))
-    experts = [finish_expert(pieces) for pieces in begun]
+    moe_own = lax.all_gather(normed_m, "seq", axis=0, tiled=False)
+    moe_other = swap(after(normed_m, *begun[0].values()), "fsdp", n_fsdp // 2)
+    experts = [finish_expert(begun[0], heads_rows)]
+    moe_other = after(moe_other, moe_own, cot_all[1], *experts[0])
+    moe_all = [moe_own, lax.all_gather(moe_other, "seq", axis=0, tiled=False), moe_other]
 
     place = jnp.full((1,), at_fsdp, jnp.int32)
     forward_parts, backward_parts, chains = [], [], []
+
     def dispatch(i, g, source, weighted):
         at = slice(g * n_seq, (g + 1) * n_seq)
         part = dot(picks[at, i], source, ((2,), (1,)), ((0,), (0,)))
@@ -436,9 +433,20 @@
             part = part * share[at, i, :, None]
         return part.astype(bf16).reshape(-1, D)
 
+    def begin(i, *start):
+        if i < per_half:
+            begun.append(start_expert(own_part[i : i + 1], other_part[i : i + 1], *start))
+
     grad_slots = [[dispatch(i, g, cot_all[g], True) for g in range(2)] for i in range(per_half)]
+    begin(1, moe_all[2])
+    begin(2, moe_all[1])
+    experts.append(finish_expert(begun[1], moe_all[1]))
     for i in range(per_half):
-        ready = list(backward_parts[-1:]) + [experts[i][j] for j in range(n_fsdp - 1)]
+        ready = list(experts[i])
+        near = jnp.concatenate(experts[i])
+        near = swap(after(near, *(backward_parts[-1][:1] if i else [])), "fsdp", 1)
+        if i:
+            ready.extend(backward_parts[-1])
         if i + 1 < per_half:
             ready.extend(begun[i + 1].values())
         if i >= 2:
@@ -448,27 +456,39 @@
         slots = [dispatch(i, g, after(moe_all[g], *ready), False) for g in range(2)]
         if i == 0:
             slots[0] = after(slots[0], *[part for parts in grad_slots for part in parts])
-        made, back, send, keep = run_expert(
-            place, share[:, i].reshape(-1, 1), slots, grad_slots[i], experts[i], 0
+        pieces = [own_part, beside, *experts[i], near]
+        parts = [(0, i), (1, i)]
+        for j in range(1, n_fsdp // 2):
+            parts.extend([(j + 1, 0), (n_fsdp // 2 + 1, j - 1)])
+        *made, send, keep = run_expert(
+            place, share[:, i].reshape(-1, 1), slots, grad_slots[i], pieces, parts
         )
-        forward_parts.append(made.reshape(2, n_seq, capacity, D))
-        backward_parts.append(back.reshape(2, n_seq, capacity, D))
+        forward_parts.append([part.reshape(n_seq, capacity, D) for part in made[:2]])
+        backward_parts.append([part.reshape(n_seq, capacity, D) for part in made[2:]])
         chains.append(GradChain(send, keep))
+        begin(i + 3, backward_parts[-1][0])
+        if i + 2 < per_half:
+            experts.append(finish_expert(begun[i + 2], backward_parts[-1][0]))
 
     every_pick = picks.reshape(2, n_seq, per_half * capacity, rows)
 
-    def combine(parts, *others):
-        sums = []
-        for g in range(2):
-            together = after(jnp.concatenate([part[g] for part in parts], axis=1), *others)
-            total = dot(every_pick[g], together, ((1,), (1,)), ((0,), (0,)))
-            sums.append(total.astype(bf16).reshape(span_len, D))
-        return sums
-
-    backward_sums = combine(backward_parts, *[chain.sums() for chain in chains[:-1]])
-    grad_normed_m = from_group(*backward_sums)
-    forward_sums = combine(forward_parts, *backward_sums, chains[-1].sums())
-    grad_normed_m = after(grad_normed_m, *forward_sums)
+    def combine(parts, g, *others):
+        together = after(jnp.concatenate([part[g] for part in parts], axis=1), *others)
+        total = dot(every_pick[g], together, ((1,), (1,)), ((0,), (0,)))
+        return total.astype(bf16).reshape(span_len, D)
+
+    def scatter(sums, *others):
+        return lax.psum_scatter(after(sums, *others), "seq", scatter_dimension=0, tiled=True)
+
+    back_other = combine(backward_parts, 1, *[chain.arrive() for chain in chains[:-1]])
+    back_own = combine(backward_parts, 0, back_other)
+    swapped_back = swap(scatter(back_other), "fsdp", n_fsdp // 2)
+    ready = [chains[-2].add(back_own), chains[-1].arrive()]
+    made_other = combine(forward_parts, 1, back_own)
+    made_own = combine(forward_parts, 0, made_other, *ready)
+    mixed_own = scatter_rows(made_own, "seq")
+    mixed_other = scatter(made_other, back_own)
+    grad_normed_m = after(scatter(back_own), mixed_own).astype(f32) + swapped_back.astype(f32)
 
     scaled_m = grad_normed_m * gain_m
     grad_resid = (
@@ -478,36 +498,43 @@
     )
     grad_gain_m = jnp.sum(grad_normed_m * resid * inv_m, axis=0)
     grad_attn = grad_resid.astype(bf16)
-    mixed = (resid + from_group(*forward_sums)).astype(bf16)
     grad_heads_rows = dot(grad_attn, out_full, ((1,), (1,))).astype(bf16)
     grad_heads = lax.all_to_all(
         grad_heads_rows, "seq", split_axis=1, concat_axis=0, tiled=True
     )
-    grad_heads = after(grad_heads, chains[-1].sums())
-    out_sum = None
+    ready = [chain.add(grad_heads_rows) for chain in (*chains[1:-2], chains[-1])]
+    grad_heads = after(grad_heads, chains[-2].arrive(), *ready)
+    out_sum = []
     for k in range(n_seq):
         columns = lax.dynamic_slice_in_dim(grad_attn, (at_seq ^ k) * width, width, 1)
         part = dot(heads_rows, columns, ((0,), (0,))).astype(bf16)
-        part = (swap(part, "seq", k) if k else part).astype(f32)
-        out_sum = part if out_sum is None else out_sum + part
-    out_sum = lax.psum_scatter(out_sum.astype(bf16), "fsdp", scatter_dimension=0, tiled=True)
+        out_sum.append(swap(after(part, grad_heads), "seq", k) if k else part)
+    grad_qkv = attend(qkv, segment, grad_heads)
+    ready = [chain.arrive() for chain in (*chains[1:-2], chains[-1])]
+    grad_qkv = after(grad_qkv, mixed_other, *ready)
+    mixed_other = swap(after(mixed_other, grad_qkv), "fsdp", n_fsdp // 2)
+    mixed = (resid + mixed_own + mixed_other.astype(f32)).astype(bf16)
+
+    grad_qkv_w = dot(normed_a, grad_qkv, ((0,), (0,))).astype(bf16)
+    qkv_sum = lax.psum_scatter(grad_qkv_w, "fsdp", scatter_dimension=0, tiled=True)
+    part_normed_a = dot(after(grad_qkv, grad_qkv_w), qkv_own, ((1,), (1,)))
+    part_sent = part_normed_a.astype(bf16)
+    ready = [chain.add(part_sent) for chain in chains[-2:]]
+    out_sum[0] = after(out_sum[0], part_sent)
+    grad_normed_a = scatter_rows(after(part_sent, *out_sum, *ready), "seq")
+    out_sum = sum(part.astype(f32) for part in out_sum)
+    out_sum = after(out_sum.astype(bf16), qkv_sum)
+    out_sum = lax.psum_scatter(out_sum, "fsdp", scatter_dimension=0, tiled=True)
     out_sum = unpack_columns(lax.all_gather(out_sum, "seq", axis=0, tiled=False), width, 1)
-
-    grad_qkv = attend(qkv, segment, grad_heads)
-    grad_qkv = after(grad_qkv, mixed, *[chain.sums() for chain in chains])
-    part_normed_a = dot(grad_qkv, qkv_own, ((1,), (1,)))
-    grad_normed_a = scatter_rows(part_normed_a.astype(bf16), "seq")
     part_gain_a = jnp.sum(part_normed_a * x_all.astype(f32) * inv_all, axis=0)
-    gain_columns = jnp.zeros((D, 128), bf16)
-    gain_columns = gain_columns.at[:, 0].set(part_gain_a.astype(bf16))
-    gain_columns = gain_columns.at[:, 1].set(grad_gain_m.astype(bf16))
-    grad_qkv_w = dot(normed_a, grad_qkv, ((0,), (0,))).astype(bf16)
-    qkv_sum = lax.psum_scatter(
-        jnp.concatenate([grad_qkv_w, gain_columns], axis=1), "fsdp", scatter_dimension=0, tiled=True
-    )
-    qkv_sum = after(qkv_sum, grad_normed_a, *[chain.sums() for chain in chains])
+    gain_sums = jnp.zeros((D, 128), bf16)
+    gain_sums = gain_sums.at[:, 0].set(part_gain_a.astype(bf16))
+    gain_sums = gain_sums.at[:, 1].set(grad_gain_m.astype(bf16))
+    gain_sums = lax.psum_scatter(after(gain_sums, qkv_sum), "fsdp", scatter_dimension=0, tiled=True)
+    gain_sums = lax.all_gather(gain_sums, "seq", axis=0, tiled=False)
+    gain_sums = jnp.sum(gain_sums[:, :, :2].astype(f32), axis=0)
+    qkv_sum = after(qkv_sum, grad_normed_a)
     qkv_sum = lax.all_gather(qkv_sum, "seq", axis=0, tiled=False)
-    gain_sums = jnp.sum(qkv_sum[:, :, 3 * width : 3 * width + 2].astype(f32), axis=0)
     qkv_sum = unpack_columns(qkv_sum, width, 3)
     inv_a = lax.rsqrt(jnp.mean(x_float * x_float, axis=1, keepdims=True) + epsilon)
     scaled_a = grad_normed_a * gain_a

time: 1980 us -> 1870 us (0.944)
  waiting for transfers between devices: 1070 us -> 907 us
  other arithmetic: 121 us -> 156 us
  blocking collectives: 17.1 us -> 48.9 us
    ppermute x60 -> x52, waiting for transfers between devices: 965 us -> 765 us  [swap(): return lax.ppermute(value, axis, [(i, i ^ bit) for i in range(size)])]
    reduce_scatter x6, waiting for transfers between devices: 76.7 us -> 118 us  [the longest x3 118 us: scatter(): lax.psum_scatter(after(sums, *others), 'seq', scatter_dimension=0, tiled=...]
    all_gather x2, blocking collectives: 17.1 us -> 48.9 us  [the longest x1 38.6 us: body(): lax.all_gather(routing, 'seq', axis=0, tiled=False)]
    ppermute x60 -> x52, starting transfers between devices: 49 us -> 55.8 us  [swap(): return lax.ppermute(value, axis, [(i, i ^ bit) for i in range(size)])]
    unnamed x158 -> x140, local copies, waits for them, and re-layouts: 39.9 us -> 36.9 us
  transfers between devices with their start and end apart: 74 -> 66, of which waited for: 30 -> 28; matrix products, arithmetic and copies ran while one was open for 21% -> 23% of each run, Pallas kernels for 16% -> 18%
where the time goes in v4:
time: 1870 us
  waiting for transfers between devices  907 us (49%)
  Pallas kernels  333 us (18%)
  matrix products  175 us (9%)
  local copies, waits for them, and re-layouts  166 us (9%)
  other arithmetic  156 us (8%)
  starting transfers between devices  65.4 us (3%)
  blocking collectives  48.9 us (3%)
    ppermute x52, waiting for transfers between devices, swap(): return lax.ppermute(value, axis, [(i, i ^ bit) for i in range(size)])  765 us
    pallas_call x4, Pallas kernels, run_expert(): pl.pallas_call(lambda *refs: expert_kernel(size, tiles, parts, *refs), ou...  245 us
    dot_general x29, matrix products, dot(): return lax.dot_general(a, b, (contract, batch), preferred_element_type=f32)  175 us
    reduce_scatter x3, waiting for transfers between devices, scatter(): lax.psum_scatter(after(sums, *others), 'seq', scatter_dimension=0, tiled=...  118 us
    pallas_call x2, Pallas kernels, attend(): pl.pallas_call(lambda *refs: (attend_backward_kernel if backward else att...  76.3 us
    ppermute x52, starting transfers between devices, swap(): return lax.ppermute(value, axis, [(i, i ^ bit) for i in range(size)])  55.8 us
    all_gather x1, blocking collectives, body(): lax.all_gather(routing, 'seq', axis=0, tiled=False)  38.6 us
  transfers between devices with their start and end apart: 66, of which 28 were waited for; matrix products, arithmetic and copies ran while one was open for 23% of the time, Pallas kernels for 18%

profile of v4, /device:TPU:0, one launch (start us, length us, event | category | flops | bytes accessed | tf_op | source)
XLA Modules:
  0.0 1866.8 jit_solution(5365180756380922864)
XLA Ops:
  57.2 38.6 %all-gather = f32[8,384,16]{1,2,0:T(8,128)S(1)} all-gather(f32[2,384,16]{1,2,0:T(8,128)S(1)} %pad_maximum_fusion.10), channel_id=2, replica_groups=mesh['seq'=4,'fsdp'=8] {'seq'}, dimensions={0}, use_global_device_ids=true | all-gather | bytes 245760 | tf_op jit(solution)/shard_map/all_gather | solution.py:383
  97.6 54.1 %collective-permute-done.1 = bf16[384,2048]{1,0:T(8,128)(2,1)S(1)} collective-permute-done((bf16[384,2048]{1,0:T(8,128)(2,1)}, bf16[384,2048]{1,0:T(8,128)(2,1)S(1)}, u32[]{:S(2)}, u32[]{:S(2)}) %collective-permute-start.1) | collective-permute-done | bytes 1572896 | tf_op jit(solution)/shard_map/ppermute | solution.py:21
  175.3 15.8 convolution_convert_fusion.1.refs_0_
  191.1 25.2 %attend_forward.1 = bf16[1536,512]{1,0:T(8,128)(2,1)} custom-call(bf16[1536,1536]{1,0:T(8,128)(2,1)} %convolution_convert_fusion.1.refs_0_, s32[1536,1]{1,0:T(8,128)} %reshape.448.refs_1_.refs_2_, s32[1,1536]{1,0:T(1,128)} %reshape.397.refs_2_.refs_3_), custom_call_target="tpu_custom_call" | custom-call | flops 24159191040 | bytes 9437184 | tf_op jit(solution)/shard_map/attend_forward/pallas_call | solution.py:97
  232.0 19.3 %collective-permute-done.6 = bf16[384,2048]{1,0:T(8,128)(2,1)} collective-permute-done((bf16[384,2048]{1,0:T(8,128)(2,1)}, bf16[384,2048]{1,0:T(8,128)(2,1)}, u32[]{:S(2)}, u32[]{:S(2)}) %collective-permute-start.6) | collective-permute-done | bytes 1572896 | tf_op jit(solution)/shard_map/ppermute | solution.py:21
  286.3 64.2 %collective-permute-done.10.refs_9_ = bf16[1,256,3072]{2,1,0:T(8,128)(2,1)S(1)} collective-permute-done((bf16[1,256,3072]{2,1,0:T(8,128)(2,1)S(1)}, bf16[1,256,3072]{2,1,0:T(8,128)(2,1)S(1)}, u32[]{:S(2)}, u32[]{:S(2)}) %collective-permute-start.10) | collective-permute-done | bytes 1572896 | tf_op jit(solution)/shard_map/ppermute | solution.py:21
  360.7 37.3 %collective-permute-done.15 = bf16[384,2048]{1,0:T(8,128)(2,1)S(1)} collective-permute-done((bf16[384,2048]{1,0:T(8,128)(2,1)S(1)}, bf16[384,2048]{1,0:T(8,128)(2,1)S(1)}, u32[]{:S(2)}, u32[]{:S(2)}) %collective-permute-start.15) | collective-permute-done | bytes 1572896 | tf_op jit(solution)/shard_map/ppermute | solution.py:21
  399.3 20.8 %collective-permute-done.11.refs_10_ = bf16[1,256,3072]{2,1,0:T(8,128)(2,1)S(1)} collective-permute-done((bf16[1,256,3072]{2,1,0:T(8,128)(2,1)S(1)}, bf16[1,256,3072]{2,1,0:T(8,128)(2,1)S(1)}, u32[]{:S(2)}, u32[]{:S(2)}) %collective-permute-start.11) | collective-permute-done | bytes 1572896 | tf_op jit(solution)/shard_map/ppermute | solution.py:21
  478.2 45.7 %collective-permute-done.16.refs_9_ = bf16[1,256,3072]{2,1,0:T(8,128)(2,1)S(1)} collective-permute-done((bf16[1,256,3072]{2,1,0:T(8,128)(2,1)S(1)}, bf16[1,256,3072]{2,1,0:T(8,128)(2,1)S(1)}, u32[]{:S(2)}, u32[]{:S(2)}) %collective-permute-start.16) | collective-permute-done | bytes 1572896 | tf_op jit(solution)/shard_map/ppermute | solution.py:21
  532.4 61.4 %expert.4 = (bf16[544,2048]{1,0:T(8,128)(2,1)}, bf16[544,2048]{1,0:T(8,128)(2,1)}, bf16[544,2048]{1,0:T(8,128)(2,1)}, bf16[544,2048]{1,0:T(8,128)(2,1)}, bf16[4,...) custom-call(s32[1]{0:T(128)} %bitcast.21.refs_0_, f32[1088,1]{1,0:T(8,128)} %reshape_squeeze.16.refs_1_, ...), custom_call_target="tpu_custom_call" | custom-call | flops 41070624768 | bytes 42991616 | tf_op jit(solution)/shard_map/expert/pallas_call | solution.py:276
  601.4 69.2 %collective-permute-done.20.refs_9_ = bf16[1,256,3072]{2,1,0:T(8,128)(2,1)} collective-permute-done((bf16[1,256,3072]{2,1,0:T(8,128)(2,1)S(1)}, bf16[1,256,3072]{2,1,0:T(8,128)(2,1)}, u32[]{:S(2)}, u32[]{:S(2)}) %collective-permute-start.20) | collective-permute-done | bytes 1572896 | tf_op jit(solution)/shard_map/ppermute | solution.py:21
  680.1 26.8 %collective-permute-done.23.refs_10_ = bf16[1,256,3072]{2,1,0:T(8,128)(2,1)} collective-permute-done((bf16[1,256,3072]{2,1,0:T(8,128)(2,1)}, bf16[1,256,3072]{2,1,0:T(8,128)(2,1)}, u32[]{:S(2)}, u32[]{:S(2)}) %collective-permute-start.23) | collective-permute-done | bytes 1572896 | tf_op jit(solution)/shard_map/ppermute | solution.py:21
  711.8 61.1 %expert.5 = (bf16[544,2048]{1,0:T(8,128)(2,1)}, bf16[544,2048]{1,0:T(8,128)(2,1)}, bf16[544,2048]{1,0:T(8,128)(2,1)}, bf16[544,2048]{1,0:T(8,128)(2,1)}, bf16[4,...) custom-call(s32[1]{0:T(128)} %bitcast.21.refs_0_, f32[1088,1]{1,0:T(8,128)} %reshape_squeeze.17.refs_1_, ...), custom_call_target="tpu_custom_call" | custom-call | flops 41070624768 | bytes 42991616 | tf_op jit(solution)/shard_map/expert/pallas_call | solution.py:276
  776.5 68.0 %collective-permute-done.24.refs_9_ = bf16[1,256,3072]{2,1,0:T(8,128)(2,1)} collective-permute-done((bf16[1,256,3072]{2,1,0:T(8,128)(2,1)}, bf16[1,256,3072]{2,1,0:T(8,128)(2,1)}, u32[]{:S(2)}, u32[]{:S(2)}) %collective-permute-start.24) | collective-permute-done | bytes 1572896 | tf_op jit(solution)/shard_map/ppermute | solution.py:21
  863.3 18.7 collective-permute-done.28.refs_10_
  886.4 61.2 %expert.6 = (bf16[544,2048]{1,0:T(8,128)(2,1)}, bf16[544,2048]{1,0:T(8,128)(2,1)}, bf16[544,2048]{1,0:T(8,128)(2,1)}, bf16[544,2048]{1,0:T(8,128)(2,1)}, bf16[4,...) custom-call(s32[1]{0:T(128)} %bitcast.21.refs_0_, f32[1088,1]{1,0:T(8,128)} %reshape_squeeze.18.refs_1_, ...), custom_call_target="tpu_custom_call" | custom-call | flops 41070624768 | bytes 42991616 | tf_op jit(solution)/shard_map/expert/pallas_call | solution.py:276
  973.7 61.2 %expert.7 = (bf16[544,2048]{1,0:T(8,128)(2,1)}, bf16[544,2048]{1,0:T(8,128)(2,1)}, bf16[544,2048]{1,0:T(8,128)(2,1)}, bf16[544,2048]{1,0:T(8,128)(2,1)}, bf16[4,...) custom-call(s32[1]{0:T(128)} %bitcast.21.refs_0_, f32[1088,1]{1,0:T(8,128)} %reshape_squeeze.19.refs_1_, ...), custom_call_target="tpu_custom_call" | custom-call | flops 41070624768 | bytes 42991616 | tf_op jit(solution)/shard_map/expert/pallas_call | solution.py:276
  1039.2 29.8 %collective-permute-done.33 = bf16[2,256,3072]{2,1,0:T(8,128)(2,1)} collective-permute-done((bf16[2,256,3072]{2,1,0:T(8,128)(2,1)}, bf16[2,256,3072]{2,1,0:T(8,128)(2,1)}, u32[]{:S(2)}, u32[]{:S(2)}) %collective-permute-start.33) | collective-permute-done | bytes 3145760 | tf_op jit(solution)/shard_map/ppermute | solution.py:21
  1127.0 67.8 %reduce-scatter.11.cloned.1.call-done = bf16[384,2048]{1,0:T(8,128)(2,1)} async-done(((bf16[1536,2048]{1,0:T(8,128)(2,1)}), bf16[384,2048]{1,0:T(8,128)(2,1)}) %reduce-scatter.11.cloned.1.call-update) | async-done | bytes 1572880 | tf_op jit(solution)/shard_map/reduce_scatter | solution.py:481
  1221.2 50.5 %reduce-scatter.9.cloned.1.call-done = bf16[384,2048]{1,0:T(8,128)(2,1)} async-done(((bf16[1536,2048]{1,0:T(8,128)(2,1)}), bf16[384,2048]{1,0:T(8,128)(2,1)}) %reduce-scatter.9.cloned.1.call-update) | async-done | bytes 1572880 | tf_op jit(solution)/shard_map/reduce_scatter | solution.py:481
  1305.4 20.6 %all-to-all-done.1 = bf16[384,4,512]{2,0,1:T(8,128)(2,1)} async-done(((bf16[384,4,512]{2,0,1:T(8,128)(2,1)}), bf16[384,4,512]{2,0,1:T(8,128)(2,1)}, u32[]{:S(2)}, u32[]{:S(2)}) %all-to-all-start.1) | async-done | bytes 1572896 | tf_op jit(solution)/shard_map/all_to_all | solution.py:502
  1326.0 51.1 %attend_backward.1 = bf16[1536,1536]{1,0:T(8,128)(2,1)} custom-call(bf16[1536,1536]{1,0:T(8,128)(2,1)} %convolution_convert_fusion.1.refs_0_, bf16[1536,512]{1,0:T(8,128)(2,1)} %bitcast.81.refs_1_, s32[1536,1]{1,0:T(8,128)} %reshape.448.refs_1_.refs_2_, s32[1,1536]{1,0:T(1,128)} %reshape.397.refs_2_.refs_3_), custom_call_target="tpu_custom_call" | custom-call | flops 48318382080 | bytes 9437184 | tf_op jit(solution)/shard_map/attend_backward/pallas_call | solution.py:97
  1377.1 27.0 %collective-permute-done.42 = bf16[2,256,3072]{2,1,0:T(8,128)(2,1)} collective-permute-done((bf16[2,256,3072]{2,1,0:T(8,128)(2,1)}, bf16[2,256,3072]{2,1,0:T(8,128)(2,1)}, u32[]{:S(2)}, u32[]{:S(2)}) %collective-permute-start.42) | collective-permute-done | bytes 3145760 | tf_op jit(solution)/shard_map/ppermute | solution.py:21
  1404.2 15.8 convolution_convert_fusion
  1451.2 27.9 %collective-permute-done.44 = bf16[2048,512]{1,0:T(8,128)(2,1)S(1)} collective-permute-done((bf16[2048,512]{1,0:T(8,128)(2,1)}, bf16[2048,512]{1,0:T(8,128)(2,1)S(1)}, u32[]{:S(2)}, u32[]{:S(2)}) %collective-permute-start.44) | collective-permute-done | bytes 2097184 | tf_op jit(solution)/shard_map/ppermute | solution.py:21
  1479.2 44.6 %collective-permute-done.45 = bf16[2048,512]{1,0:T(8,128)(2,1)S(1)} collective-permute-done((bf16[2048,512]{1,0:T(8,128)(2,1)}, bf16[2048,512]{1,0:T(8,128)(2,1)S(1)}, u32[]{:S(2)}, u32[]{:S(2)}) %collective-permute-start.45) | collective-permute-done | bytes 2097184 | tf_op jit(solution)/shard_map/ppermute | solution.py:21
  1553.3 28.3 %collective-permute-done.49 = bf16[384,2048]{1,0:T(8,128)(2,1)} collective-permute-done((bf16[384,2048]{1,0:T(8,128)(2,1)}, bf16[384,2048]{1,0:T(8,128)(2,1)}, u32[]{:S(2)}, u32[]{:S(2)}) %collective-permute-start.49) | collective-permute-done | bytes 1572896 | tf_op jit(solution)/shard_map/ppermute | solution.py:21
  1581.5 29.9 %collective-permute-done.48 = bf16[384,2048]{1,0:T(8,128)(2,1)} collective-permute-done((bf16[384,2048]{1,0:T(8,128)(2,1)}, bf16[384,2048]{1,0:T(8,128)(2,1)}, u32[]{:S(2)}, u32[]{:S(2)}) %collective-permute-start.48) | collective-permute-done | bytes 1572896 | tf_op jit(solution)/shard_map/ppermute | solution.py:21
  1621.3 75.8 %collective-permute-done.50 = bf16[1,256,3072]{2,1,0:T(8,128)(2,1)} collective-permute-done((bf16[1,256,3072]{2,1,0:T(8,128)(2,1)}, bf16[1,256,3072]{2,1,0:T(8,128)(2,1)}, u32[]{:S(2)}, u32[]{:S(2)}) %collective-permute-start.50) | collective-permute-done | bytes 1572896 | tf_op jit(solution)/shard_map/ppermute | solution.py:21
  1698.6 32.2 %collective-permute-done.51 = bf16[1,256,3072]{2,1,0:T(8,128)(2,1)} collective-permute-done((bf16[1,256,3072]{2,1,0:T(8,128)(2,1)}, bf16[1,256,3072]{2,1,0:T(8,128)(2,1)}, u32[]{:S(2)}, u32[]{:S(2)}) %collective-permute-start.51) | collective-permute-done | bytes 1572896 | tf_op jit(solution)/shard_map/ppermute | solution.py:21
  1732.4 31.6 %collective-permute-done.43 = bf16[384,2048]{1,0:T(8,128)(2,1)} collective-permute-done((bf16[384,2048]{1,0:T(8,128)(2,1)}, bf16[384,2048]{1,0:T(8,128)(2,1)}, u32[]{:S(2)}, u32[]{:S(2)}) %collective-permute-start.43) | collective-permute-done | bytes 1572896 | tf_op jit(solution)/shard_map/ppermute | solution.py:21
  1800.5 22.0 %reshape.438 = f32[8,256,2,1024]{3,2,1,0:T(2,128)} reshape(f32[8,256,2048]{2,1,0:T(8,128)} %slice.443) | data formatting | bytes 33554432 | tf_op jit(solution)/shard_map/reshape | solution.py:563
  (405 shorter events, 548.0 us)
Async XLA Ops:
  7.2 167.3 %all-gather.13.cloned.1.call-start = ((), (), s32[]{:S(2)}) async-start(), calls=%async_computation.8 | async-start | bytes 7667712 | tf_op jit(solution)/shard_map/all_gather | solution.py:374
  19.1 240.7 %all-gather.15.cloned.1.call-start = ((), (), s32[]{:S(2)}) async-start(), calls=%async_computation.9 | async-start | bytes 9437184 | tf_op jit(solution)/shard_map/all_gather | solution.py:405
  19.1 137.3 %collective-permute-start.2 = (bf16[384,2048]{1,0:T(8,128)(2,1)S(1)}, bf16[384,2048]{1,0:T(8,128)(2,1)}, u32[]{:S(2)}, u32[]{:S(2)}) collective-permute-start(bf16[384,2048]{1,0:T(8,128)(2,1)S(1)} %bitcast.203), channel_id=1, source_target_pairs={{0,8},{8,0},{16,24},{24,16},{1,9},{9,1},{17,25},{25,17},{2,10},{10... | collective-permute-start | bytes 4718600 | tf_op jit(solution)/shard_map/ppermute | solution.py:21
  22.1 137.1 %collective-permute-start.3 = (bf16[384,2048]{1,0:T(8,128)(2,1)S(1)}, bf16[384,2048]{1,0:T(8,128)(2,1)}, u32[]{:S(2)}, u32[]{:S(2)}) collective-permute-start(bf16[384,2048]{1,0:T(8,128)(2,1)S(1)} %bitcast.204), channel_id=1, source_target_pairs={{0,16},{8,24},{16,0},{24,8},{1,17},{9,25},{17,1},{25,9},{2,18},{10... | collective-permute-start | bytes 4718600 | tf_op jit(solution)/shard_map/ppermute | solution.py:21
  23.6 138.3 %collective-permute-start.4 = (bf16[384,2048]{1,0:T(8,128)(2,1)S(1)}, bf16[384,2048]{1,0:T(8,128)(2,1)}, u32[]{:S(2)}, u32[]{:S(2)}) collective-permute-start(bf16[384,2048]{1,0:T(8,128)(2,1)S(1)} %bitcast.205), channel_id=1, source_target_pairs={{0,24},{8,16},{16,8},{24,0},{1,25},{9,17},{17,9},{25,1},{2,26},{10... | collective-permute-start | bytes 4718600 | tf_op jit(solution)/shard_map/ppermute | solution.py:21
  26.8 124.9 %collective-permute-start.1 = (bf16[384,2048]{1,0:T(8,128)(2,1)}, bf16[384,2048]{1,0:T(8,128)(2,1)S(1)}, u32[]{:S(2)}, u32[]{:S(2)}) collective-permute-start(bf16[384,2048]{1,0:T(8,128)(2,1)} %bitcast.12), channel_id=1, source_target_pairs={{0,4},{1,5},{2,6},{3,7},{4,0},{5,1},{6,2},{7,3},{8,12},{9,13},{10,... | collective-permute-start | bytes 4718600 | tf_op jit(solution)/shard_map/ppermute | solution.py:21
  222.6 199.0 %all-gather.17.cloned.1.call-start = ((), (), s32[]{:S(2)}) async-start(), calls=%async_computation.16 | async-start | bytes 7864320 | tf_op jit(solution)/shard_map/all_gather | solution.py:420
  269.4 257.4 %all-gather.19.cloned.1.call-start = ((), (), s32[]{:S(2)}) async-start(), calls=%async_computation.17 | async-start | bytes 7864320 | tf_op jit(solution)/shard_map/all_gather | solution.py:424
  284.4 113.7 %collective-permute-start.15 = (bf16[384,2048]{1,0:T(8,128)(2,1)S(1)}, bf16[384,2048]{1,0:T(8,128)(2,1)S(1)}, u32[]{:S(2)}, u32[]{:S(2)}) collective-permute-start(bf16[384,2048]{1,0:T(8,128)(2,1)S(1)} %copy-done.35), channel_id=1, source_target_pairs={{0,24},{8,16},{16,8},{24,0},{1,25},{9,17},{17,9},{25,1},{2,26},{10... | collective-permute-start | bytes 4718600 | tf_op jit(solution)/shard_map/ppermute | solution.py:21
  421.7 773.1 %reduce-scatter.11.cloned.1.call-start = ((), (), s32[]{:S(2)}) async-start(), calls=%async_computation.12 | async-start | bytes 7864320 | tf_op jit(solution)/shard_map/reduce_scatter | solution.py:481
  429.1 103.3 %collective-permute-start.18 = (bf16[3,256,3072]{2,1,0:T(8,128)(2,1)}, bf16[3,256,3072]{2,1,0:T(8,128)(2,1)}, u32[]{:S(2)}, u32[]{:S(2)}) collective-permute-start(bf16[3,256,3072]{2,1,0:T(8,128)(2,1)} %pad_maximum_fusion.5), channel_id=1, source_target_pairs={{0,1},{1,0},{2,3},{3,2},{4,5},{5,4},{6,7},{7,6},{8,9},{9,8},{10,11... | collective-permute-start | bytes 14155784 | tf_op jit(solution)/shard_map/ppermute | solution.py:21
  599.0 112.8 %collective-permute-start.22 = (bf16[3,256,3072]{2,1,0:T(8,128)(2,1)}, bf16[3,256,3072]{2,1,0:T(8,128)(2,1)}, u32[]{:S(2)}, u32[]{:S(2)}) collective-permute-start(bf16[3,256,3072]{2,1,0:T(8,128)(2,1)} %pad_maximum_fusion.6), channel_id=1, source_target_pairs={{0,1},{1,0},{2,3},{3,2},{4,5},{5,4},{6,7},{7,6},{8,9},{9,8},{10,11... | collective-permute-start | bytes 14155784 | tf_op jit(solution)/shard_map/ppermute | solution.py:21
  671.6 173.0 %collective-permute-start.26 = (bf16[4,256,3072]{2,1,0:T(8,128)(2,1)}, bf16[4,256,3072]{2,1,0:T(8,128)(2,1)}, u32[]{:S(2)}, u32[]{:S(2)}) collective-permute-start(bf16[4,256,3072]{2,1,0:T(8,128)(2,1)} %get-tuple-element.167), channel_id=1, source_target_pairs={{0,1},{1,0},{2,3},{3,2},{4,5},{5,4},{6,7},{7,6},{8,9},{9,8},{10,11... | collective-permute-start | bytes 18874376 | tf_op jit(solution)/shard_map/ppermute | solution.py:21
  773.0 113.4 %collective-permute-start.27 = (bf16[3,256,3072]{2,1,0:T(8,128)(2,1)}, bf16[3,256,3072]{2,1,0:T(8,128)(2,1)}, u32[]{:S(2)}, u32[]{:S(2)}) collective-permute-start(bf16[3,256,3072]{2,1,0:T(8,128)(2,1)} %pad_maximum_fusion.7), channel_id=1, source_target_pairs={{0,1},{1,0},{2,3},{3,2},{4,5},{5,4},{6,7},{7,6},{8,9},{9,8},{10,11... | collective-permute-start | bytes 14155784 | tf_op jit(solution)/shard_map/ppermute | solution.py:21
  850.4 101.7 %collective-permute-start.30 = (bf16[2,256,3072]{2,1,0:T(8,128)(2,1)}, bf16[2,256,3072]{2,1,0:T(8,128)(2,1)}, u32[]{:S(2)}, u32[]{:S(2)}) collective-permute-start(bf16[2,256,3072]{2,1,0:T(8,128)(2,1)} %add_convert_fusion.3), channel_id=1, source_target_pairs={{0,2},{1,3},{2,0},{3,1},{4,6},{5,7},{6,4},{7,5},{8,10},{9,11},{10,... | collective-permute-start | bytes 9437192 | tf_op jit(solution)/shard_map/ppermute | solution.py:21
  852.4 106.3 %collective-permute-start.29 = (bf16[4,256,3072]{2,1,0:T(8,128)(2,1)}, bf16[4,256,3072]{2,1,0:T(8,128)(2,1)}, u32[]{:S(2)}, u32[]{:S(2)}) collective-permute-start(bf16[4,256,3072]{2,1,0:T(8,128)(2,1)} %get-tuple-element.176), channel_id=1, source_target_pairs={{0,1},{1,0},{2,3},{3,2},{4,5},{5,4},{6,7},{7,6},{8,9},{9,8},{10,11... | collective-permute-start | bytes 18874376 | tf_op jit(solution)/shard_map/ppermute | solution.py:21
  958.4 110.5 %collective-permute-start.34 = (bf16[4,256,3072]{2,1,0:T(8,128)(2,1)}, bf16[4,256,3072]{2,1,0:T(8,128)(2,1)}, u32[]{:S(2)}, u32[]{:S(2)}) collective-permute-start(bf16[4,256,3072]{2,1,0:T(8,128)(2,1)} %get-tuple-element.187), channel_id=1, source_target_pairs={{0,1},{1,0},{2,3},{3,2},{4,5},{5,4},{6,7},{7,6},{8,9},{9,8},{10,11... | collective-permute-start | bytes 18874376 | tf_op jit(solution)/shard_map/ppermute | solution.py:21
  964.4 104.5 %collective-permute-start.33 = (bf16[2,256,3072]{2,1,0:T(8,128)(2,1)}, bf16[2,256,3072]{2,1,0:T(8,128)(2,1)}, u32[]{:S(2)}, u32[]{:S(2)}) collective-permute-start(bf16[2,256,3072]{2,1,0:T(8,128)(2,1)} %add_convert_fusion.2), channel_id=1, source_target_pairs={{0,2},{1,3},{2,0},{3,1},{4,6},{5,7},{6,4},{7,5},{8,10},{9,11},{10,... | collective-permute-start | bytes 9437192 | tf_op jit(solution)/shard_map/ppermute | solution.py:21
  1076.1 195.6 %reduce-scatter.9.cloned.1.call-start = ((), (), s32[]{:S(2)}) async-start(), calls=%async_computation.11 | async-start | bytes 7864320 | tf_op jit(solution)/shard_map/reduce_scatter | solution.py:481
  1088.2 288.9 %reduce-scatter.7.cloned.1.call-start = ((), (), s32[]{:S(2)}) async-start(), calls=%async_computation.10 | async-start | bytes 7864320 | tf_op jit(solution)/shard_map/reduce_scatter | solution.py:481
  1124.8 90.3 %collective-permute-start.37 = (bf16[384,2048]{1,0:T(8,128)(2,1)}, bf16[384,2048]{1,0:T(8,128)(2,1)}, u32[]{:S(2)}, u32[]{:S(2)}) collective-permute-start(bf16[384,2048]{1,0:T(8,128)(2,1)} %get-tuple-element.282), channel_id=1, source_target_pairs={{0,16},{8,24},{16,0},{24,8},{1,17},{9,25},{17,1},{25,9},{2,18},{10... | collective-permute-start | bytes 4718600 | tf_op jit(solution)/shard_map/ppermute | solution.py:21
  1200.0 105.4 %collective-permute-start.40 = (bf16[2,256,3072]{2,1,0:T(8,128)(2,1)}, bf16[2,256,3072]{2,1,0:T(8,128)(2,1)}, u32[]{:S(2)}, u32[]{:S(2)}) collective-permute-start(bf16[2,256,3072]{2,1,0:T(8,128)(2,1)} %add_convert_fusion.1), channel_id=1, source_target_pairs={{0,2},{1,3},{2,0},{3,1},{4,6},{5,7},{6,4},{7,5},{8,10},{9,11},{10,... | collective-permute-start | bytes 9437192 | tf_op jit(solution)/shard_map/ppermute | solution.py:21
  1288.9 237.3 %reduce-scatter.13.cloned.1.call-start = ((), (), s32[]{:S(2)}) async-start(), calls=%async_computation.13 | async-start | bytes 7077888 | tf_op jit(solution)/shard_map/reduce_scatter | solution.py:519
  1303.0 101.1 %collective-permute-start.42 = (bf16[2,256,3072]{2,1,0:T(8,128)(2,1)}, bf16[2,256,3072]{2,1,0:T(8,128)(2,1)}, u32[]{:S(2)}, u32[]{:S(2)}) collective-permute-start(bf16[2,256,3072]{2,1,0:T(8,128)(2,1)} %add_convert_fusion), channel_id=1, source_target_pairs={{0,2},{1,3},{2,0},{3,1},{4,6},{5,7},{6,4},{7,5},{8,10},{9,11},{10,... | collective-permute-start | bytes 9437192 | tf_op jit(solution)/shard_map/ppermute | solution.py:21
  1419.9 362.0 %reduce-scatter.17.cloned.1.call-start = ((), (), s32[]{:S(2)}) async-start(), calls=%async_computation.15 | async-start | bytes 2359296 | tf_op jit(solution)/shard_map/reduce_scatter | solution.py:527
  1432.4 91.3 %collective-permute-start.45 = (bf16[2048,512]{1,0:T(8,128)(2,1)}, bf16[2048,512]{1,0:T(8,128)(2,1)S(1)}, u32[]{:S(2)}, u32[]{:S(2)}) collective-permute-start(bf16[2048,512]{1,0:T(8,128)(2,1)} %convolution_convert_fusion.15), channel_id=1, source_target_pairs={{0,16},{8,24},{16,0},{24,8},{1,17},{9,25},{17,1},{25,9},{2,18},{10... | collective-permute-start | bytes 6291464 | tf_op jit(solution)/shard_map/ppermute | solution.py:21
  1526.2 310.4 %reduce-scatter.15.cloned.1.call-start = ((), (), s32[]{:S(2)}) async-start(), calls=%async_computation.14 | async-start | bytes 589824 | tf_op jit(solution)/shard_map/reduce_scatter | solution.py:533
  1550.0 297.7 %all-gather.21.cloned.1.call-start = ((), (), s32[]{:S(2)}) async-start(), calls=%async_computation.18 | async-start | bytes 3932160 | tf_op jit(solution)/shard_map/all_gather | solution.py:537
  1550.3 146.8 %collective-permute-start.50 = (bf16[1,256,3072]{2,1,0:T(8,128)(2,1)}, bf16[1,256,3072]{2,1,0:T(8,128)(2,1)}, u32[]{:S(2)}, u32[]{:S(2)}) collective-permute-start(bf16[1,256,3072]{2,1,0:T(8,128)(2,1)} %get-tuple-element.268), channel_id=1, source_target_pairs={{0,4},{1,5},{2,6},{3,7},{4,0},{5,1},{6,2},{7,3},{8,12},{9,13},{10,... | collective-permute-start | bytes 4718600 | tf_op jit(solution)/shard_map/ppermute | solution.py:21
  1550.6 180.3 %collective-permute-start.51 = (bf16[1,256,3072]{2,1,0:T(8,128)(2,1)}, bf16[1,256,3072]{2,1,0:T(8,128)(2,1)}, u32[]{:S(2)}, u32[]{:S(2)}) collective-permute-start(bf16[1,256,3072]{2,1,0:T(8,128)(2,1)} %get-tuple-element.270), channel_id=1, source_target_pairs={{0,4},{1,5},{2,6},{3,7},{4,0},{5,1},{6,2},{7,3},{8,12},{9,13},{10,... | collective-permute-start | bytes 4718600 | tf_op jit(solution)/shard_map/ppermute | solution.py:21
  1617.8 238.4 %all-gather.23.cloned.1.call-start = ((), (), s32[]{:S(2)}) async-start(), calls=%async_computation.19 | async-start | bytes 1310720 | tf_op jit(solution)/shard_map/all_gather | solution.py:528
  1617.8 146.1 %collective-permute-start.43 = (bf16[384,2048]{1,0:T(8,128)(2,1)}, bf16[384,2048]{1,0:T(8,128)(2,1)}, u32[]{:S(2)}, u32[]{:S(2)}) collective-permute-start(bf16[384,2048]{1,0:T(8,128)(2,1)} %reduce-scatter.7.cloned.1.call-done), channel_id=1, source_target_pairs={{0,4},{1,5},{2,6},{3,7},{4,0},{5,1},{6,2},{7,3},{8,12},{9,13},{10,... | collective-permute-start | bytes 4718600 | tf_op jit(solution)/shard_map/ppermute | solution.py:21
  (101 other events, 4034.9 us)
Sparse Core Ops, SparseCore 0:
  19.2 129.0 all-gather.12
  164.8 81.4 all-gather.14
  269.6 114.8 all-gather.16
  421.8 68.9 all-gather.18
  1076.2 118.5 reduce-scatter.10
  1197.6 74.0 reduce-scatter.8
  1274.7 87.1 reduce-scatter.6
  1420.1 71.4 reduce-scatter.12
  1526.3 38.8 reduce-scatter.16
  1567.3 128.3 reduce-scatter.14
  1697.7 112.4 all-gather.20
  1812.1 26.6 all-gather.22

commit v5 on v4

--- a/solution.py
+++ b/solution.py
@@ -115,6 +115,34 @@
     )(*[qkv, *[grad] * backward, segment.reshape(span_len, 1), segment.reshape(1, span_len)])
 
 
+def finish_kernel(in_ref, gate_ref, down_ref):
+    ffe = down_ref.shape[1]
+    whole = in_ref[0].astype(f32)
+    gate_ref[0, :, 0, :] = whole[:, :ffe]
+    gate_ref[0, :, 1, :] = whole[:, ffe : 2 * ffe]
+    down_ref[0] = whole[:, 2 * ffe :].T
+
+
+def finish_grads(packed):
+    count, rows, columns = packed.shape
+    ffe = columns // 3
+    return pl.pallas_call(
+        finish_kernel,
+        out_shape=[
+            jax.ShapeDtypeStruct((count, rows, 2, ffe), f32),
+            jax.ShapeDtypeStruct((count, ffe, rows), f32),
+        ],
+        grid=(count,),
+        in_specs=[pl.BlockSpec((1, rows, columns), lambda e: (e, 0, 0))],
+        out_specs=[
+            pl.BlockSpec((1, rows, 2, ffe), lambda e: (e, 0, 0, 0)),
+            pl.BlockSpec((1, ffe, rows), lambda e: (e, 0, 0)),
+        ],
+        compiler_params=pltpu.CompilerParams(vmem_limit_bytes=60 * 2**20),
+        name="finish",
+    )(packed)
+
+
 def unpack_kernel(in_ref, out_ref):
     out_ref[...] = in_ref[0].astype(f32)
 
@@ -144,9 +172,9 @@
     return total
 
 
-def start_expert(mine, sent, *start):
+def start_expert(mine, sent, *start, later=()):
     size = lax.axis_size("fsdp")
-    mine, sent = after(mine, *start), after(sent, *start)
+    mine, sent = after(mine, *start, *later), after(sent, *start)
     pieces = {size // 2: swap(sent, "fsdp", size // 2)}
     bit = size // 4
     while bit > 1:
@@ -157,20 +185,36 @@
 
 def finish_expert(pieces, *start):
     size = lax.axis_size("fsdp")
-    pieces = dict(pieces)
+    pieces, brought = dict(pieces), {}
     for j in sorted(range(2, size, 2), key=lambda j: j.bit_count()):
         if j not in pieces:
             low = j & -j
-            pieces[j] = swap(after(pieces[j ^ low], *start), "fsdp", low)
-    return [pieces[j] for j in range(2, size, 2)]
-
-
-def gather_rows(piece, axis, *others):
-    place, rows = lax.axis_index(axis), piece.shape[0]
-    whole = jnp.zeros((lax.axis_size(axis) * rows, *piece.shape[1:]), piece.dtype)
-    for k in range(lax.axis_size(axis)):
-        part = swap(piece, axis, k) if k else after(piece, *others)
-        whole = lax.dynamic_update_slice_in_dim(whole, part, (place ^ k) * rows, 0)
+            pieces[j] = brought[j] = swap(after(pieces[j ^ low], *start), "fsdp", low)
+    return brought
+
+
+def both_cores(pieces, *start):
+    size = lax.axis_size("fsdp")
+    return lax.all_gather(
+        after(jnp.concatenate(pieces), *start),
+        "fsdp",
+        axis=0,
+        tiled=True,
+        axis_index_groups=[[i, i + 1] for i in range(0, size, 2)],
+    )
+
+
+def send_rows(piece, axis, *start):
+    sent = after(piece, *start)
+    return [piece, *[swap(sent, axis, k) for k in range(1, lax.axis_size(axis))]]
+
+
+def join_rows(pieces, axis, *others):
+    place, rows = lax.axis_index(axis), pieces[0].shape[0]
+    whole = jnp.zeros((len(pieces) * rows, *pieces[0].shape[1:]), pieces[0].dtype)
+    for k, piece in enumerate(pieces):
+        piece = piece if k else after(piece, *others)
+        whole = lax.dynamic_update_slice_in_dim(whole, piece, (place ^ k) * rows, 0)
     return whole
 
 
@@ -184,10 +228,10 @@
 
 
 def expert_kernel(size, tiles, parts, place_ref, share_ref, *rest):
-    arrays = 1 + max(array for array, _ in parts)
+    arrays = 1 + max(part[0] for part in parts)
     slots, pieces, rest = rest[:4], rest[4 : 4 + arrays], rest[4 + arrays :]
     made_refs, back_refs, rest = rest[:2], rest[2:4], rest[4:]
-    send_ref, keep_ref, weights, x_ref, g_ref, act, grad_proj, sems = rest
+    grad_ref, weights, x_ref, g_ref, act, grad_proj, sems = rest
     step = pl.program_id(0)
     place = place_ref[0]
     rows = weights.shape[0] // size
@@ -199,7 +243,7 @@
     def _():
         copies = [
             pltpu.make_async_copy(
-                pieces[parts[j][0]].at[parts[j][1]],
+                pieces[parts[j][0]].at[parts[j][1] + parts[j][2] * (1 - (place & 1))],
                 weights.at[pl.ds(pl.multiple_of((place ^ j) * rows, rows), rows)],
                 sems.at[j],
             )
@@ -249,17 +293,8 @@
             made_refs[g][...] = made[g * count : (g + 1) * count]
             back_refs[g][...] = back[g * count : (g + 1) * count]
 
-        def grads(out_ref):
-            out_ref[0, :, : 2 * ffe] = dot(x_ref[:, at], grad_proj[...], tn).astype(bf16)
-            out_ref[0, :, 2 * ffe :] = dot(g_ref[:, at], act[...], tn).astype(bf16)
-
-        @pl.when(turn < size // 2)
-        def _():
-            grads(send_ref)
-
-        @pl.when(turn >= size // 2)
-        def _():
-            grads(keep_ref)
+        grad_ref[0, :, : 2 * ffe] = dot(x_ref[:, at], grad_proj[...], tn).astype(bf16)
+        grad_ref[0, :, 2 * ffe :] = dot(g_ref[:, at], act[...], tn).astype(bf16)
 
 
 def run_expert(place, share, slots, grad_slots, pieces, parts):
@@ -273,12 +308,16 @@
         turn = jnp.maximum(step - tiles, 0)
         return 0, place[0] ^ reversed_bits((turn + half) % size, size)
 
+    def stands(step, place):
+        turn = jnp.maximum(step - tiles, 0)
+        core = (whose(step, place)[1]) & 1
+        return core * half + turn % half, 0, 0
+
     return pl.pallas_call(
         lambda *refs: expert_kernel(size, tiles, parts, *refs),
         out_shape=[
             *[jax.ShapeDtypeStruct((count // 2, D), bf16)] * 4,
-            jax.ShapeDtypeStruct((half, rows, columns), bf16),
-            jax.ShapeDtypeStruct((half, rows, columns), bf16),
+            jax.ShapeDtypeStruct((size, rows, columns), bf16),
         ],
         grid_spec=pltpu.PrefetchScalarGridSpec(
             num_scalar_prefetch=1,
@@ -289,13 +328,7 @@
             ],
             out_specs=[
                 *[pl.BlockSpec((count // 2, rows), whose)] * 4,
-                pl.BlockSpec(
-                    (1, rows, columns), lambda t, place: (jnp.clip(t - tiles, 0, half - 1), 0, 0)
-                ),
-                pl.BlockSpec(
-                    (1, rows, columns),
-                    lambda t, place: (jnp.clip(t - tiles - half, 0, half - 1), 0, 0),
-                ),
+                pl.BlockSpec((1, rows, columns), stands),
             ],
             scratch_shapes=[
                 pltpu.VMEM((size * rows, columns), bf16),
@@ -319,14 +352,22 @@
 
 
 class GradChain:
-    def __init__(self, send, keep):
+    def __init__(self, grad):
         self.bit, self.size = 1, lax.axis_size("fsdp")
-        self.terms, self.send = [keep], send
+        rows, columns = grad.shape[1:]
+        core_sums = lax.psum_scatter(
+            grad.reshape(-1, columns),
+            "fsdp",
+            scatter_dimension=0,
+            tiled=True,
+            axis_index_groups=[[i, i + 1] for i in range(0, self.size, 2)],
+        )
+        self.terms = [core_sums.reshape(-1, rows, columns)]
 
     def arrive(self):
-        if self.bit < self.size:
+        if 1 < self.bit < self.size:
             self.terms.append(swap(self.send, "fsdp", self.bit))
-            self.bit *= 2
+        self.bit = min(2 * self.bit, self.size)
         return self.terms[-1]
 
     def add(self, *others):
@@ -366,6 +407,9 @@
     own_part = lax.dynamic_slice_in_dim(packed, half * per_half, per_half, 0)
     other_part = lax.dynamic_slice_in_dim(packed, (1 - half) * per_half, per_half, 0)
     cot_other = swap(cotangent[0], "fsdp", n_fsdp // 2)
+    begun = [start_expert(own_part[:1], other_part[:1], later=(cot_other,))]
+    x_parts = send_rows(tokens[0], "seq")
+    cot_own = join_rows(send_rows(cotangent[0], "seq", *x_parts), "seq")
 
     part = lax.dynamic_slice_in_dim(
         w_qkv.reshape(shard, 3, HEADS, HEAD), at_seq * heads_here, heads_here, 2
@@ -401,26 +445,24 @@
         inverse = lax.rsqrt(jnp.mean(values * values, axis=1, keepdims=True) + epsilon)
         return (values * inverse * gain).astype(bf16), inverse
 
-    x_all = gather_rows(tokens[0], "seq", own_part, other_part, picks, share, cot_other)
+    x_all = join_rows(
+        x_parts, "seq", own_part, other_part, picks, share, cot_own, begun[0][n_fsdp // 2]
+    )
     out_full = lax.all_gather(after(w_out, x_all), "fsdp", axis=0, tiled=True)
-    normed_a, inv_all = normed_rows(x_all.astype(f32), gain_a)
+    normed_a, _ = normed_rows(x_all.astype(f32), gain_a)
     qkv = dot(normed_a, qkv_own, ((1,), (0,))).astype(bf16)
     segment = segment_ids(lengths[0], span_len)
     attended = attend(qkv, segment)
     heads_rows = lax.all_to_all(attended, "seq", split_axis=0, concat_axis=1, tiled=True)
-    cot_own = gather_rows(after(cotangent[0], x_all), "seq")
-    cot_all = [cot_own, gather_rows(after(cot_other, x_all), "seq")]
+    cot_all = [cot_own, join_rows(send_rows(cot_other, "seq", cot_own), "seq")]
     cot_all = [rows_of.reshape(n_seq, rows, D) for rows_of in cot_all]
-    beside = swap(after(own_part, x_all), "fsdp", 1)
-    heads_rows = after(heads_rows, cot_own, beside)
-    begun = [start_expert(own_part[:1], other_part[:1], out_full)]
+    experts = [finish_expert(begun[0], x_all)]
+    heads_rows = after(heads_rows, *cot_all, *experts[0].values(), *begun[0].values())
     x_float = tokens[0].astype(f32)
     resid = x_float + dot(heads_rows, out_full, ((1,), (0,)))
     normed_m, inv_m = normed_rows(resid, gain_m)
     moe_own = lax.all_gather(normed_m, "seq", axis=0, tiled=False)
-    moe_other = swap(after(normed_m, *begun[0].values()), "fsdp", n_fsdp // 2)
-    experts = [finish_expert(begun[0], heads_rows)]
-    moe_other = after(moe_other, moe_own, cot_all[1], *experts[0])
+    moe_other = after(swap(normed_m, "fsdp", n_fsdp // 2), moe_own)
     moe_all = [moe_own, lax.all_gather(moe_other, "seq", axis=0, tiled=False), moe_other]
 
     place = jnp.full((1,), at_fsdp, jnp.int32)
@@ -437,16 +479,18 @@
         if i < per_half:
             begun.append(start_expert(own_part[i : i + 1], other_part[i : i + 1], *start))
 
-    grad_slots = [[dispatch(i, g, cot_all[g], True) for g in range(2)] for i in range(per_half)]
     begin(1, moe_all[2])
     begin(2, moe_all[1])
-    experts.append(finish_expert(begun[1], moe_all[1]))
+    beside = swap(after(own_part, normed_m), "fsdp", 1)
+    near = [both_cores(list(begun[0].values()))]
     for i in range(per_half):
-        ready = list(experts[i])
-        near = jnp.concatenate(experts[i])
-        near = swap(after(near, *(backward_parts[-1][:1] if i else [])), "fsdp", 1)
+        first, later = begun[i], experts[i]
+        ready = [near[i], *later.values()]
+        last = jnp.concatenate(list(later.values()))
+        last = swap(after(last, *(backward_parts[-1][:1] if i else [])), "fsdp", 1)
         if i:
             ready.extend(backward_parts[-1])
+        cots = [after(cot_all[g], *ready) for g in range(2)]
         if i + 1 < per_half:
             ready.extend(begun[i + 1].values())
         if i >= 2:
@@ -454,21 +498,24 @@
         if i >= 3:
             ready.append(chains[i - 3].sums())
         slots = [dispatch(i, g, after(moe_all[g], *ready), False) for g in range(2)]
-        if i == 0:
-            slots[0] = after(slots[0], *[part for parts in grad_slots for part in parts])
-        pieces = [own_part, beside, *experts[i], near]
-        parts = [(0, i), (1, i)]
-        for j in range(1, n_fsdp // 2):
-            parts.extend([(j + 1, 0), (n_fsdp // 2 + 1, j - 1)])
-        *made, send, keep = run_expert(
-            place, share[:, i].reshape(-1, 1), slots, grad_slots[i], pieces, parts
+        grad_slots = [dispatch(i, g, cots[g], True) for g in range(2)]
+        if i + 1 < per_half:
+            experts.append(finish_expert(begun[i + 1], slots[1]))
+            near.append(both_cores(list(begun[i + 1].values()), slots[1]))
+        even = [*first, *later]
+        pieces = [own_part, beside, near[i], last, *first.values(), *later.values()]
+        parts = {0: (0, i, 0), 1: (1, i, 0)}
+        for n, j in enumerate(even):
+            parts[j] = (4 + n, 0, 0)
+            parts[j + 1] = (2, n, len(first)) if j in first else (3, n - len(first), 0)
+        parts = [parts[j] for j in range(n_fsdp)]
+        *made, grad = run_expert(
+            place, share[:, i].reshape(-1, 1), slots, grad_slots, pieces, parts
         )
         forward_parts.append([part.reshape(n_seq, capacity, D) for part in made[:2]])
         backward_parts.append([part.reshape(n_seq, capacity, D) for part in made[2:]])
-        chains.append(GradChain(send, keep))
+        chains.append(GradChain(grad))
         begin(i + 3, backward_parts[-1][0])
-        if i + 2 < per_half:
-            experts.append(finish_expert(begun[i + 2], backward_parts[-1][0]))
 
     every_pick = picks.reshape(2, n_seq, per_half * capacity, rows)
 
@@ -480,15 +527,16 @@
     def scatter(sums, *others):
         return lax.psum_scatter(after(sums, *others), "seq", scatter_dimension=0, tiled=True)
 
-    back_other = combine(backward_parts, 1, *[chain.arrive() for chain in chains[:-1]])
+    back_other = combine(backward_parts, 1)
     back_own = combine(backward_parts, 0, back_other)
-    swapped_back = swap(scatter(back_other), "fsdp", n_fsdp // 2)
-    ready = [chains[-2].add(back_own), chains[-1].arrive()]
+    swapped_back = scatter(back_other)
+    grad_normed_m = scatter(back_own, swapped_back)
+    swapped_back = swap(swapped_back, "fsdp", n_fsdp // 2)
+    ready = [chain.arrive() for chain in chains]
+    ready.extend(chain.add(back_own) for chain in chains[1:-1])
     made_other = combine(forward_parts, 1, back_own)
     made_own = combine(forward_parts, 0, made_other, *ready)
-    mixed_own = scatter_rows(made_own, "seq")
-    mixed_other = scatter(made_other, back_own)
-    grad_normed_m = after(scatter(back_own), mixed_own).astype(f32) + swapped_back.astype(f32)
+    grad_normed_m = after(grad_normed_m, made_own).astype(f32) + swapped_back.astype(f32)
 
     scaled_m = grad_normed_m * gain_m
     grad_resid = (
@@ -499,43 +547,46 @@
     grad_gain_m = jnp.sum(grad_normed_m * resid * inv_m, axis=0)
     grad_attn = grad_resid.astype(bf16)
     grad_heads_rows = dot(grad_attn, out_full, ((1,), (1,))).astype(bf16)
+    mixed_other = scatter(made_other, grad_heads_rows)
+    mixed_own = scatter(made_own, grad_heads_rows)
     grad_heads = lax.all_to_all(
         grad_heads_rows, "seq", split_axis=1, concat_axis=0, tiled=True
     )
-    ready = [chain.add(grad_heads_rows) for chain in (*chains[1:-2], chains[-1])]
-    grad_heads = after(grad_heads, chains[-2].arrive(), *ready)
+    ready = [chains[-1].add(grad_heads_rows)]
+    chains[-2].arrive()
+    ready.append(chains[-2].add(grad_heads_rows))
+    grad_heads = after(grad_heads, *ready)
     out_sum = []
     for k in range(n_seq):
         columns = lax.dynamic_slice_in_dim(grad_attn, (at_seq ^ k) * width, width, 1)
         part = dot(heads_rows, columns, ((0,), (0,))).astype(bf16)
-        out_sum.append(swap(after(part, grad_heads), "seq", k) if k else part)
+        out_sum.append(part)
     grad_qkv = attend(qkv, segment, grad_heads)
-    ready = [chain.arrive() for chain in (*chains[1:-2], chains[-1])]
+    ready = [chain.arrive() for chain in chains[1:-2]]
     grad_qkv = after(grad_qkv, mixed_other, *ready)
-    mixed_other = swap(after(mixed_other, grad_qkv), "fsdp", n_fsdp // 2)
-    mixed = (resid + mixed_own + mixed_other.astype(f32)).astype(bf16)
+    mixed_other = swap(mixed_other, "fsdp", n_fsdp // 2)
+    mixed = (resid + mixed_own.astype(f32) + mixed_other.astype(f32)).astype(bf16)
 
     grad_qkv_w = dot(normed_a, grad_qkv, ((0,), (0,))).astype(bf16)
-    qkv_sum = lax.psum_scatter(grad_qkv_w, "fsdp", scatter_dimension=0, tiled=True)
+    reduced_qkv = lax.psum_scatter(grad_qkv_w, "fsdp", scatter_dimension=0, tiled=True)
     part_normed_a = dot(after(grad_qkv, grad_qkv_w), qkv_own, ((1,), (1,)))
     part_sent = part_normed_a.astype(bf16)
-    ready = [chain.add(part_sent) for chain in chains[-2:]]
-    out_sum[0] = after(out_sum[0], part_sent)
-    grad_normed_a = scatter_rows(after(part_sent, *out_sum, *ready), "seq")
-    out_sum = sum(part.astype(f32) for part in out_sum)
-    out_sum = after(out_sum.astype(bf16), qkv_sum)
+    chains[-1].arrive()
+    ready = [chains[-1].add(part_sent)]
+    out_sum = [swap(after(p, grad_qkv_w), "seq", k) if k else p for k, p in enumerate(out_sum)]
+    grad_normed_a = scatter_rows(after(part_sent, *out_sum), "seq")
+    qkv_sum = after(reduced_qkv, mixed_other, *ready, *out_sum[1:])
+    qkv_sum = lax.all_gather(qkv_sum, "seq", axis=0, tiled=False)
+    out_sum[0] = after(out_sum[0], qkv_sum)
+    out_sum = sum(part.astype(f32) for part in out_sum).astype(bf16)
+    gain_column = jnp.zeros((D, 128), bf16).at[:, 0].set(grad_gain_m.astype(bf16))
+    out_sum = jnp.concatenate([out_sum, gain_column], axis=1)
     out_sum = lax.psum_scatter(out_sum, "fsdp", scatter_dimension=0, tiled=True)
-    out_sum = unpack_columns(lax.all_gather(out_sum, "seq", axis=0, tiled=False), width, 1)
-    part_gain_a = jnp.sum(part_normed_a * x_all.astype(f32) * inv_all, axis=0)
-    gain_sums = jnp.zeros((D, 128), bf16)
-    gain_sums = gain_sums.at[:, 0].set(part_gain_a.astype(bf16))
-    gain_sums = gain_sums.at[:, 1].set(grad_gain_m.astype(bf16))
-    gain_sums = lax.psum_scatter(after(gain_sums, qkv_sum), "fsdp", scatter_dimension=0, tiled=True)
-    gain_sums = lax.all_gather(gain_sums, "seq", axis=0, tiled=False)
-    gain_sums = jnp.sum(gain_sums[:, :, :2].astype(f32), axis=0)
-    qkv_sum = after(qkv_sum, grad_normed_a)
-    qkv_sum = lax.all_gather(qkv_sum, "seq", axis=0, tiled=False)
+    out_sum = lax.all_gather(out_sum, "seq", axis=0, tiled=False)
     qkv_sum = unpack_columns(qkv_sum, width, 3)
+    gain_m_sum = jnp.sum(out_sum[:, :, width].astype(f32), axis=0)
+    out_sum = unpack_columns(out_sum, width, 1)
+    gain_a_sum = jnp.sum(w_qkv.astype(f32) * qkv_sum, axis=1) / gain_attn.astype(f32)
     inv_a = lax.rsqrt(jnp.mean(x_float * x_float, axis=1, keepdims=True) + epsilon)
     scaled_a = grad_normed_a * gain_a
     grad_x = (
@@ -552,16 +603,17 @@
     first = half == 0
     grad_all = jnp.concatenate(
         [jnp.where(first, own_grads, other_grads), jnp.where(first, other_grads, own_grads)]
-    ).astype(f32)
+    )
+    grad_gate_up, grad_down = finish_grads(grad_all)
     return (
         mixed[None],
         grad_x.astype(bf16)[None],
-        gain_sums[:, 0],
-        gain_sums[:, 1],
+        gain_a_sum,
+        gain_m_sum,
         qkv_sum,
         out_sum,
-        grad_all[:, :, : 2 * FFE].reshape(local_count, shard, 2, FFE),
-        jnp.swapaxes(grad_all[:, :, 2 * FFE :], 1, 2),
+        grad_gate_up,
+        grad_down,
     )
 
 

time: 1870 us -> 2080 us (1.11)
  waiting for transfers between devices: 907 us -> 1210 us
  other arithmetic: 156 us -> 113 us
  blocking collectives: 48.9 us -> 8.68 us
  local copies, waits for them, and re-layouts: 166 us -> 136 us
    ppermute x52 -> x45, waiting for transfers between devices: 765 us -> 1100 us  [swap(): return lax.ppermute(value, axis, [(i, i ^ bit) for i in range(size)])]
    reduce_scatter x3 -> x4, waiting for transfers between devices: 118 us -> 54.7 us  [scatter(): lax.psum_scatter(after(sums, *others), 'seq', scatter_dimension=0, tiled=...]
    all_gather x1, waiting for transfers between devices: 0.01 us -> 38.3 us  [body(): qkv_sum = lax.all_gather(qkv_sum, 'seq', axis=0, tiled=False)]
    all_gather x1, blocking collectives: 38.6 us -> 8.68 us  [body(): lax.all_gather(routing, 'seq', axis=0, tiled=False)]
    convert_element_type x6 -> x1, other arithmetic: 34.3 us -> 4.64 us  [body(): out_sum = sum((part.astype(f32) for part in out_sum)).astype(bf16)]
    reshape x1 -> x0, local copies, waits for them, and re-layouts: 22 us -> none  [body(): grad_all[:, :, :2 * FFE].reshape(local_count, shard, 2, FFE)]
    ppermute x52 -> x45, starting transfers between devices: 55.8 us -> 56.2 us  [swap(): return lax.ppermute(value, axis, [(i, i ^ bit) for i in range(size)])]
  transfers between devices with their start and end apart: 66 -> 67, of which waited for: 28 -> 26; matrix products, arithmetic and copies ran while one was open for 23% -> 17% of each run, Pallas kernels for 18% -> 13%
where the time goes in v5:
time: 2080 us
  waiting for transfers between devices  1210 us (58%)
  Pallas kernels  343 us (16%)
  matrix products  187 us (9%)
  local copies, waits for them, and re-layouts  136 us (7%)
  other arithmetic  113 us (5%)
  starting transfers between devices  66.5 us (3%)
    ppermute x45, waiting for transfers between devices, swap(): return lax.ppermute(value, axis, [(i, i ^ bit) for i in range(size)])  1100 us
    pallas_call x4, Pallas kernels, run_expert(): pl.pallas_call(lambda *refs: expert_kernel(size, tiles, parts, *refs), ou...  240 us
    dot_general x29, matrix products, dot(): return lax.dot_general(a, b, (contract, batch), preferred_element_type=f32)  187 us
    pallas_call x2, Pallas kernels, attend(): pl.pallas_call(lambda *refs: (attend_backward_kernel if backward else att...  76.2 us
    ppermute x45, starting transfers between devices, swap(): return lax.ppermute(value, axis, [(i, i ^ bit) for i in range(size)])  56.2 us
    reduce_scatter x4, waiting for transfers between devices, scatter(): lax.psum_scatter(after(sums, *others), 'seq', scatter_dimension=0, tiled=...  54.7 us
  transfers between devices with their start and end apart: 67, of which 26 were waited for; matrix products, arithmetic and copies ran while one was open for 17% of the time, Pallas kernels for 13%

profile of v5, /device:TPU:0, one launch (start us, length us, event | category | flops | bytes accessed | tf_op | source)
XLA Modules:
  0.0 2075.2 jit_solution(11235193299045705241)
XLA Ops:
  22.3 14.6 reshape.383
  56.8 33.6 %collective-permute-done.2 = bf16[384,2048]{1,0:T(8,128)(2,1)} collective-permute-done((bf16[384,2048]{1,0:T(8,128)(2,1)S(1)}, bf16[384,2048]{1,0:T(8,128)(2,1)}, u32[]{:S(2)}, u32[]{:S(2)}) %collective-permute-start.2) | collective-permute-done | bytes 1572896 | tf_op jit(solution)/shard_map/ppermute | solution.py:21
  98.7 57.8 %collective-permute-done = f32[384,16]{0,1:T(8,128)S(1)} collective-permute-done((f32[384,16]{0,1:T(8,128)S(1)}, f32[384,16]{0,1:T(8,128)S(1)}, u32[]{:S(2)}, u32[]{:S(2)}) %collective-permute-start) | collective-permute-done | bytes 24608 | tf_op jit(solution)/shard_map/ppermute | solution.py:21
  196.0 127.3 %collective-permute-done.8 = bf16[384,2048]{1,0:T(8,128)(2,1)} collective-permute-done((bf16[384,2048]{1,0:T(8,128)(2,1)S(1)}, bf16[384,2048]{1,0:T(8,128)(2,1)}, u32[]{:S(2)}, u32[]{:S(2)}) %collective-permute-start.8) | collective-permute-done | bytes 1572896 | tf_op jit(solution)/shard_map/ppermute | solution.py:21
  333.8 15.9 convolution_convert_fusion.2.refs_0_
  349.7 25.2 %attend_forward.1 = bf16[1536,512]{1,0:T(8,128)(2,1)} custom-call(bf16[1536,1536]{1,0:T(8,128)(2,1)} %convolution_convert_fusion.2.refs_0_, s32[1536,1]{1,0:T(8,128)} %reshape.449.refs_1_.refs_2_, s32[1,1536]{1,0:T(1,128)} %reshape.392.refs_2_.refs_3_), custom_call_target="tpu_custom_call" | custom-call | flops 24159191040 | bytes 9437184 | tf_op jit(solution)/shard_map/attend_forward/pallas_call | solution.py:97
  390.0 11.7 collective-permute-done.10
  428.9 68.4 %collective-permute-done.14 = bf16[384,2048]{1,0:T(8,128)(2,1)} collective-permute-done((bf16[384,2048]{1,0:T(8,128)(2,1)S(1)}, bf16[384,2048]{1,0:T(8,128)(2,1)}, u32[]{:S(2)}, u32[]{:S(2)}) %collective-permute-start.14) | collective-permute-done | bytes 1572896 | tf_op jit(solution)/shard_map/ppermute | solution.py:21
  501.5 66.8 %collective-permute-done.16.refs_11_ = bf16[1,256,3072]{2,1,0:T(8,128)(2,1)S(1)} collective-permute-done((bf16[1,256,3072]{2,1,0:T(8,128)(2,1)}, bf16[1,256,3072]{2,1,0:T(8,128)(2,1)S(1)}, u32[]{:S(2)}, u32[]{:S(2)}) %collective-permute-start.16) | collective-permute-done | bytes 1572896 | tf_op jit(solution)/shard_map/ppermute | solution.py:21
  572.8 10.5 all-gather.30.cloned.1.call-done
  610.1 60.1 %expert.4 = (bf16[544,2048]{1,0:T(8,128)(2,1)}, bf16[544,2048]{1,0:T(8,128)(2,1)}, bf16[544,2048]{1,0:T(8,128)(2,1)}, bf16[544,2048]{1,0:T(8,128)(2,1)}, bf16[8,256,3072]{2,1,0:T(8,128)(2,1)}) custom-call(s32[1]{0:T(128)} %bitcast.23.refs_0_, f32[1088,1]{1,0:T(8,128)} %reshape_squeeze.16.refs_1_, bf16[544,2048]{1,0:T(8,128)(2,1)} %bitcast.263, ...), custom_call_target="tpu_custom_call" | custom-call | flops 41070624768 | bytes 42991616 | tf_op jit(solution)/shard_map/expert/pallas_call | solution.py:316
  675.8 34.4 %collective-permute-done.21.refs_11_ = bf16[1,256,3072]{2,1,0:T(8,128)(2,1)} collective-permute-done((bf16[1,256,3072]{2,1,0:T(8,128)(2,1)}, bf16[1,256,3072]{2,1,0:T(8,128)(2,1)}, u32[]{:S(2)}, u32[]{:S(2)}) %collective-permute-start.21) | collective-permute-done | bytes 1572896 | tf_op jit(solution)/shard_map/ppermute | solution.py:21
  740.3 60.8 %expert.5 = (bf16[544,2048]{1,0:T(8,128)(2,1)}, bf16[544,2048]{1,0:T(8,128)(2,1)}, bf16[544,2048]{1,0:T(8,128)(2,1)}, bf16[544,2048]{1,0:T(8,128)(2,1)}, bf16[8,256,3072]{2,1,0:T(8,128)(2,1)}) custom-call(s32[1]{0:T(128)} %bitcast.23.refs_0_, f32[1088,1]{1,0:T(8,128)} %reshape_squeeze.17.refs_1_, bf16[544,2048]{1,0:T(8,128)(2,1)} %bitcast.269, ...), custom_call_target="tpu_custom_call" | custom-call | flops 41070624768 | bytes 42991616 | tf_op jit(solution)/shard_map/expert/pallas_call | solution.py:316
  811.5 63.0 %collective-permute-done.24.refs_10_ = bf16[1,256,3072]{2,1,0:T(8,128)(2,1)} collective-permute-done((bf16[1,256,3072]{2,1,0:T(8,128)(2,1)S(1)}, bf16[1,256,3072]{2,1,0:T(8,128)(2,1)}, u32[]{:S(2)}, u32[]{:S(2)}) %collective-permute-start.24) | collective-permute-done | bytes 1572896 | tf_op jit(solution)/shard_map/ppermute | solution.py:21
  879.3 29.3 %collective-permute-done.23.refs_12_ = bf16[1,256,3072]{2,1,0:T(8,128)(2,1)} collective-permute-done((bf16[1,256,3072]{2,1,0:T(8,128)(2,1)}, bf16[1,256,3072]{2,1,0:T(8,128)(2,1)}, u32[]{:S(2)}, u32[]{:S(2)}) %collective-permute-start.23) | collective-permute-done | bytes 1572896 | tf_op jit(solution)/shard_map/ppermute | solution.py:21
  937.4 59.5 %expert.6 = (bf16[544,2048]{1,0:T(8,128)(2,1)}, bf16[544,2048]{1,0:T(8,128)(2,1)}, bf16[544,2048]{1,0:T(8,128)(2,1)}, bf16[544,2048]{1,0:T(8,128)(2,1)}, bf16[8,256,3072]{2,1,0:T(8,128)(2,1)}) custom-call(s32[1]{0:T(128)} %bitcast.23.refs_0_, f32[1088,1]{1,0:T(8,128)} %reshape_squeeze.18.refs_1_, bf16[544,2048]{1,0:T(8,128)(2,1)} %bitcast.272, ...), custom_call_target="tpu_custom_call" | custom-call | flops 41070624768 | bytes 42991616 | tf_op jit(solution)/shard_map/expert/pallas_call | solution.py:316
  996.9 36.4 %collective-permute-done.27.refs_12_ = bf16[1,256,3072]{2,1,0:T(8,128)(2,1)S(1)} collective-permute-done((bf16[1,256,3072]{2,1,0:T(8,128)(2,1)}, bf16[1,256,3072]{2,1,0:T(8,128)(2,1)S(1)}, u32[]{:S(2)}, u32[]{:S(2)}) %collective-permute-start.27) | collective-permute-done | bytes 1572896 | tf_op jit(solution)/shard_map/ppermute | solution.py:21
  1067.5 59.6 %expert.7 = (bf16[544,2048]{1,0:T(8,128)(2,1)}, bf16[544,2048]{1,0:T(8,128)(2,1)}, bf16[544,2048]{1,0:T(8,128)(2,1)}, bf16[544,2048]{1,0:T(8,128)(2,1)}, bf16[8,256,3072]{2,1,0:T(8,128)(2,1)}) custom-call(s32[1]{0:T(128)} %bitcast.23.refs_0_, f32[1088,1]{1,0:T(8,128)} %reshape_squeeze.19.refs_1_, bf16[544,2048]{1,0:T(8,128)(2,1)} %bitcast.265, ...), custom_call_target="tpu_custom_call" | custom-call | flops 41070624768 | bytes 42991616 | tf_op jit(solution)/shard_map/expert/pallas_call | solution.py:316
  1150.3 54.7 %reduce-scatter.19.cloned.1.call-done = bf16[384,2048]{1,0:T(8,128)(2,1)} async-done(((bf16[1536,2048]{1,0:T(8,128)(2,1)}), bf16[384,2048]{1,0:T(8,128)(2,1)}) %reduce-scatter.19.cloned.1.call-update) | async-done | bytes 1572880 | tf_op jit(solution)/shard_map/reduce_scatter | solution.py:528
  1232.3 78.1 %collective-permute-done.31 = bf16[2,256,3072]{2,1,0:T(8,128)(2,1)S(1)} collective-permute-done((bf16[2,256,3072]{2,1,0:T(8,128)(2,1)S(1)}, bf16[2,256,3072]{2,1,0:T(8,128)(2,1)S(1)}, u32[]{:S(2)}, u32[]{:S(2)}) %collective-permute-start.31) | collective-permute-done | bytes 3145760 | tf_op jit(solution)/shard_map/ppermute | solution.py:21
  1320.9 9.7 convolution_convert_fusion.3
  1330.6 52.8 %collective-permute-done.32 = bf16[384,2048]{1,0:T(8,128)(2,1)} collective-permute-done((bf16[384,2048]{1,0:T(8,128)(2,1)}, bf16[384,2048]{1,0:T(8,128)(2,1)}, u32[]{:S(2)}, u32[]{:S(2)}) %collective-permute-start.32) | collective-permute-done | bytes 1572896 | tf_op jit(solution)/shard_map/ppermute | solution.py:21
  1407.3 92.8 %collective-permute-done.34 = bf16[2,256,3072]{2,1,0:T(8,128)(2,1)} collective-permute-done((bf16[2,256,3072]{2,1,0:T(8,128)(2,1)}, bf16[2,256,3072]{2,1,0:T(8,128)(2,1)}, u32[]{:S(2)}, u32[]{:S(2)}) %collective-permute-start.34) | collective-permute-done | bytes 3145760 | tf_op jit(solution)/shard_map/ppermute | solution.py:21
  1511.7 51.0 %attend_backward.1 = bf16[1536,1536]{1,0:T(8,128)(2,1)} custom-call(bf16[1536,1536]{1,0:T(8,128)(2,1)} %convolution_convert_fusion.2.refs_0_, bf16[1536,512]{1,0:T(8,128)(2,1)} %bitcast.92.refs_1_, s32[1536,1]{1,0:T(8,128)} %reshape.449.refs_1_.refs_2_, s32[1,1536]{1,0:T(1,128)} %reshape.392.refs_2_.refs_3_), custom_call_target="tpu_custom_call" | custom-call | flops 48318382080 | bytes 9437184 | tf_op jit(solution)/shard_map/attend_backward/pallas_call | solution.py:97
  1562.7 15.8 convolution_convert_fusion.1
  1591.5 13.6 convolution_convert_fusion
  1605.1 135.0 %collective-permute-done.42 = bf16[2,256,3072]{2,1,0:T(8,128)(2,1)} collective-permute-done((bf16[2,256,3072]{2,1,0:T(8,128)(2,1)}, bf16[2,256,3072]{2,1,0:T(8,128)(2,1)}, u32[]{:S(2)}, u32[]{:S(2)}) %collective-permute-start.42) | collective-permute-done | bytes 3145760 | tf_op jit(solution)/shard_map/ppermute | solution.py:21
  1751.3 38.3 %all-gather.32.cloned.1.call-done = bf16[1024,1536]{1,0:T(8,128)(2,1)} async-done(((bf16[256,1536]{1,0:T(8,128)(2,1)}), bf16[1024,1536]{1,0:T(8,128)(2,1)}) %all-gather.32.cloned.1.call-update) | async-done | bytes 3145744 | tf_op jit(solution)/shard_map/all_gather | solution.py:579
  1802.4 124.3 %collective-permute-done.43 = bf16[1,256,3072]{2,1,0:T(8,128)(2,1)} collective-permute-done((bf16[1,256,3072]{2,1,0:T(8,128)(2,1)}, bf16[1,256,3072]{2,1,0:T(8,128)(2,1)}, u32[]{:S(2)}, u32[]{:S(2)}) %collective-permute-start.43) | collective-permute-done | bytes 1572896 | tf_op jit(solution)/shard_map/ppermute | solution.py:21
  1928.2 31.2 %collective-permute-done.44 = bf16[1,256,3072]{2,1,0:T(8,128)(2,1)} collective-permute-done((bf16[1,256,3072]{2,1,0:T(8,128)(2,1)}, bf16[1,256,3072]{2,1,0:T(8,128)(2,1)}, u32[]{:S(2)}, u32[]{:S(2)}) %collective-permute-start.44) | collective-permute-done | bytes 1572896 | tf_op jit(solution)/shard_map/ppermute | solution.py:21
  1976.0 14.6 finish.1
  2006.8 33.0 %collective-permute-done.41 = bf16[384,2048]{1,0:T(8,128)(2,1)} collective-permute-done((bf16[384,2048]{1,0:T(8,128)(2,1)}, bf16[384,2048]{1,0:T(8,128)(2,1)}, u32[]{:S(2)}, u32[]{:S(2)}) %collective-permute-start.41) | collective-permute-done | bytes 1572896 | tf_op jit(solution)/shard_map/ppermute | solution.py:21
  (389 shorter events, 480.0 us)
Async XLA Ops:
  7.2 325.8 %all-gather.16.cloned.1.call-start = ((), (), s32[]{:S(2)}) async-start(), calls=%async_computation.12 | async-start | bytes 7667712 | tf_op jit(solution)/shard_map/all_gather | solution.py:418
  17.7 393.3 %all-gather.18.cloned.1.call-start = ((), (), s32[]{:S(2)}) async-start(), calls=%async_computation.13 | async-start | bytes 9437184 | tf_op jit(solution)/shard_map/all_gather | solution.py:451
  53.7 120.0 %collective-permute-start.7 = (bf16[1,256,3072]{2,1,0:T(8,128)(2,1)}, bf16[1,256,3072]{2,1,0:T(8,128)(2,1)}, u32[]{:S(2)}, u32[]{:S(2)}) collective-permute-start(bf16[1,256,3072]{2,1,0:T(8,128)(2,1)} %get-tuple-element.241), channel_id=1, source_target_pairs={{0,4},{1,5},{2,6},{3,7},{4,0},{5,1},{6,2},{7,3},{8,12},{9,13},{10,... | collective-permute-start | bytes 4718600 | tf_op jit(solution)/shard_map/ppermute | solution.py:21
  186.7 136.6 %collective-permute-start.8 = (bf16[384,2048]{1,0:T(8,128)(2,1)S(1)}, bf16[384,2048]{1,0:T(8,128)(2,1)}, u32[]{:S(2)}, u32[]{:S(2)}) collective-permute-start(bf16[384,2048]{1,0:T(8,128)(2,1)S(1)} %bitcast.240), channel_id=1, source_target_pairs={{0,4},{1,5},{2,6},{3,7},{4,0},{5,1},{6,2},{7,3},{8,12},{9,13},{10,... | collective-permute-start | bytes 4718600 | tf_op jit(solution)/shard_map/ppermute | solution.py:21
  381.1 116.2 %all-gather.28.cloned.1.call-start = ((), (), s32[]{:S(2)}) async-start(), calls=%async_computation.28 | async-start | bytes 7864320 | tf_op jit(solution)/shard_map/all_gather | solution.py:464
  420.9 151.9 %all-gather.20.cloned.1.call-start = ((), (), s32[]{:S(2)}) async-start(), calls=%async_computation.14 | async-start | bytes 9437184 | tf_op jit(solution)/shard_map/all_gather | solution.py:198
  424.8 158.5 %all-gather.30.cloned.1.call-start = ((), (), s32[]{:S(2)}) async-start(), calls=%async_computation.29 | async-start | bytes 7864320 | tf_op jit(solution)/shard_map/all_gather | solution.py:466
  497.3 216.8 %all-gather.22.cloned.1.call-start = ((), (), s32[]{:S(2)}) async-start(), calls=%async_computation.15 | async-start | bytes 9437184 | tf_op jit(solution)/shard_map/all_gather | solution.py:198
  497.5 112.6 %collective-permute-start.17 = (bf16[4,256,3072]{2,1,0:T(8,128)(2,1)}, bf16[4,256,3072]{2,1,0:T(8,128)(2,1)}, u32[]{:S(2)}, u32[]{:S(2)}) collective-permute-start(bf16[4,256,3072]{2,1,0:T(8,128)(2,1)} %get-tuple-element.141.refs_6_), channel_id=1, source_target_pairs={{0,1},{1,0},{2,3},{3,2},{4,5},{5,4},{6,7},{7,6},{8,9},{9,8},{10,11... | collective-permute-start | bytes 18874376 | tf_op jit(solution)/shard_map/ppermute | solution.py:21
  588.9 319.7 %all-gather.24.cloned.1.call-start = ((), (), s32[]{:S(2)}) async-start(), calls=%async_computation.16 | async-start | bytes 9437184 | tf_op jit(solution)/shard_map/all_gather | solution.py:198
  719.7 194.4 %reduce-scatter.11.cloned.1.call-start = ((), (), s32[]{:S(2)}) async-start(), calls=%async_computation.17 | async-start | bytes 18874368 | tf_op jit(solution)/shard_map/reduce_scatter | solution.py:358
  720.5 319.2 %reduce-scatter.13.cloned.1.call-start = ((), (), s32[]{:S(2)}) async-start(), calls=%async_computation.19 | async-start | bytes 18874368 | tf_op jit(solution)/shard_map/reduce_scatter | solution.py:358
  801.2 244.4 %all-gather.26.cloned.1.call-start = ((), (), s32[]{:S(2)}) async-start(), calls=%async_computation.18 | async-start | bytes 9437184 | tf_op jit(solution)/shard_map/all_gather | solution.py:198
  923.4 281.5 %reduce-scatter.19.cloned.1.call-start = ((), (), s32[]{:S(2)}) async-start(), calls=%async_computation.22 | async-start | bytes 7864320 | tf_op jit(solution)/shard_map/reduce_scatter | solution.py:528
  1136.1 178.6 %reduce-scatter.15.cloned.1.call-start = ((), (), s32[]{:S(2)}) async-start(), calls=%async_computation.20 | async-start | bytes 18874368 | tf_op jit(solution)/shard_map/reduce_scatter | solution.py:358
  1136.7 184.2 %reduce-scatter.17.cloned.1.call-start = ((), (), s32[]{:S(2)}) async-start(), calls=%async_computation.21 | async-start | bytes 18874368 | tf_op jit(solution)/shard_map/reduce_scatter | solution.py:358
  1137.4 193.2 %reduce-scatter.21.cloned.1.call-start = ((), (), s32[]{:S(2)}) async-start(), calls=%async_computation.23 | async-start | bytes 7864320 | tf_op jit(solution)/shard_map/reduce_scatter | solution.py:528
  1205.0 357.7 %reduce-scatter.25.cloned.1.call-start = ((), (), s32[]{:S(2)}) async-start(), calls=%async_computation.25 | async-start | bytes 7864320 | tf_op jit(solution)/shard_map/reduce_scatter | solution.py:528
  1208.3 112.5 %collective-permute-start.30 = (bf16[1,256,3072]{2,1,0:T(8,128)(2,1)}, bf16[1,256,3072]{2,1,0:T(8,128)(2,1)}, u32[]{:S(2)}, u32[]{:S(2)}) collective-permute-start(bf16[1,256,3072]{2,1,0:T(8,128)(2,1)} %get-tuple-element.221), channel_id=1, source_target_pairs={{0,4},{1,5},{2,6},{3,7},{4,0},{5,1},{6,2},{7,3},{8,12},{9,13},{10,... | collective-permute-start | bytes 4718600 | tf_op jit(solution)/shard_map/ppermute | solution.py:21
  1396.9 165.8 %collective-permute-start.35 = (bf16[1,256,3072]{2,1,0:T(8,128)(2,1)}, bf16[1,256,3072]{2,1,0:T(8,128)(2,1)}, u32[]{:S(2)}, u32[]{:S(2)}) collective-permute-start(bf16[1,256,3072]{2,1,0:T(8,128)(2,1)} %get-tuple-element.225), channel_id=1, source_target_pairs={{0,4},{1,5},{2,6},{3,7},{4,0},{5,1},{6,2},{7,3},{8,12},{9,13},{10,... | collective-permute-start | bytes 4718600 | tf_op jit(solution)/shard_map/ppermute | solution.py:21
  1406.8 338.0 %reduce-scatter.27.cloned.1.call-start = ((), (), s32[]{:S(2)}) async-start(), calls=%async_computation.26 | async-start | bytes 7077888 | tf_op jit(solution)/shard_map/reduce_scatter | solution.py:571
  1578.5 211.1 %all-gather.32.cloned.1.call-start = ((), (), s32[]{:S(2)}) async-start(), calls=%async_computation.30 | async-start | bytes 3932160 | tf_op jit(solution)/shard_map/all_gather | solution.py:579
  1578.7 161.4 %collective-permute-start.42 = (bf16[2,256,3072]{2,1,0:T(8,128)(2,1)}, bf16[2,256,3072]{2,1,0:T(8,128)(2,1)}, u32[]{:S(2)}, u32[]{:S(2)}) collective-permute-start(bf16[2,256,3072]{2,1,0:T(8,128)(2,1)} %get-tuple-element.231), channel_id=1, source_target_pairs={{0,2},{1,3},{2,0},{3,1},{4,6},{5,7},{6,4},{7,5},{8,10},{9,11},{10,... | collective-permute-start | bytes 9437192 | tf_op jit(solution)/shard_map/ppermute | solution.py:21
  1584.3 160.5 %collective-permute-start.38 = (bf16[2048,512]{1,0:T(8,128)(2,1)S(1)}, bf16[2048,512]{1,0:T(8,128)(2,1)}, u32[]{:S(2)}, u32[]{:S(2)}) collective-permute-start(bf16[2048,512]{1,0:T(8,128)(2,1)S(1)} %convolution_convert_fusion.14), channel_id=1, source_target_pairs={{0,24},{8,16},{16,8},{24,0},{1,25},{9,17},{17,9},{25,1},{2,26},{10... | collective-permute-start | bytes 6291464 | tf_op jit(solution)/shard_map/ppermute | solution.py:21
  1585.9 158.9 %collective-permute-start.37 = (bf16[2048,512]{1,0:T(8,128)(2,1)S(1)}, bf16[2048,512]{1,0:T(8,128)(2,1)}, u32[]{:S(2)}, u32[]{:S(2)}) collective-permute-start(bf16[2048,512]{1,0:T(8,128)(2,1)S(1)} %convolution_convert_fusion.15), channel_id=1, source_target_pairs={{0,16},{8,24},{16,0},{24,8},{1,17},{9,25},{17,1},{25,9},{2,18},{10... | collective-permute-start | bytes 6291464 | tf_op jit(solution)/shard_map/ppermute | solution.py:21
  1587.4 157.4 %collective-permute-start.36 = (bf16[2048,512]{1,0:T(8,128)(2,1)S(1)}, bf16[2048,512]{1,0:T(8,128)(2,1)}, u32[]{:S(2)}, u32[]{:S(2)}) collective-permute-start(bf16[2048,512]{1,0:T(8,128)(2,1)S(1)} %convolution_convert_fusion.16), channel_id=1, source_target_pairs={{0,8},{8,0},{16,24},{24,16},{1,9},{9,1},{17,25},{25,17},{2,10},{10... | collective-permute-start | bytes 6291464 | tf_op jit(solution)/shard_map/ppermute | solution.py:21
  1587.9 156.9 %collective-permute-start.33 = (bf16[384,2048]{1,0:T(8,128)(2,1)S(1)}, bf16[384,2048]{1,0:T(8,128)(2,1)}, u32[]{:S(2)}, u32[]{:S(2)}) collective-permute-start(bf16[384,2048]{1,0:T(8,128)(2,1)S(1)} %copy-done.50), channel_id=1, source_target_pairs={{0,4},{1,5},{2,6},{3,7},{4,0},{5,1},{6,2},{7,3},{8,12},{9,13},{10,... | collective-permute-start | bytes 4718600 | tf_op jit(solution)/shard_map/ppermute | solution.py:21
  1744.9 245.8 %reduce-scatter.23.cloned.1.call-start = ((), (), s32[]{:S(2)}) async-start(), calls=%async_computation.24 | async-start | bytes 7864320 | tf_op jit(solution)/shard_map/reduce_scatter | solution.py:528
  1745.4 249.0 %reduce-scatter.29.cloned.1.call-start = ((), (), s32[]{:S(2)}) async-start(), calls=%async_computation.27 | async-start | bytes 2949120 | tf_op jit(solution)/shard_map/reduce_scatter | solution.py:584
  1796.0 266.9 %all-gather.34.cloned.1.call-start = ((), (), s32[]{:S(2)}) async-start(), calls=%async_computation.31 | async-start | bytes 1638400 | tf_op jit(solution)/shard_map/all_gather | solution.py:585
  1796.3 130.4 %collective-permute-start.43 = (bf16[1,256,3072]{2,1,0:T(8,128)(2,1)}, bf16[1,256,3072]{2,1,0:T(8,128)(2,1)}, u32[]{:S(2)}, u32[]{:S(2)}) collective-permute-start(bf16[1,256,3072]{2,1,0:T(8,128)(2,1)} %get-tuple-element.227), channel_id=1, source_target_pairs={{0,4},{1,5},{2,6},{3,7},{4,0},{5,1},{6,2},{7,3},{8,12},{9,13},{10,... | collective-permute-start | bytes 4718600 | tf_op jit(solution)/shard_map/ppermute | solution.py:21
  1798.8 160.6 %collective-permute-start.44 = (bf16[1,256,3072]{2,1,0:T(8,128)(2,1)}, bf16[1,256,3072]{2,1,0:T(8,128)(2,1)}, u32[]{:S(2)}, u32[]{:S(2)}) collective-permute-start(bf16[1,256,3072]{2,1,0:T(8,128)(2,1)} %get-tuple-element.229), channel_id=1, source_target_pairs={{0,4},{1,5},{2,6},{3,7},{4,0},{5,1},{6,2},{7,3},{8,12},{9,13},{10,... | collective-permute-start | bytes 4718600 | tf_op jit(solution)/shard_map/ppermute | solution.py:21
  (97 other events, 3882.8 us)
Sparse Core Ops, SparseCore 0:
  17.9 124.6 all-gather.15
  186.8 137.9 all-gather.17
  421.0 69.4 all-gather.27
  491.9 20.4 all-gather.19
  514.1 69.1 all-gather.29
  589.1 16.7 all-gather.21
  719.8 16.7 all-gather.23
  738.9 22.6 reduce-scatter.10
  801.3 21.3 reduce-scatter.12
  923.6 15.4 all-gather.25
  1136.2 68.7 reduce-scatter.18
  1207.1 21.4 reduce-scatter.14
  1231.5 22.6 reduce-scatter.16
  1257.0 71.3 reduce-scatter.20
  1396.9 85.9 reduce-scatter.24
  1578.6 149.6 reduce-scatter.26
  1745.0 44.5 all-gather.31
  1792.5 70.2 reduce-scatter.22
  1865.0 55.2 reduce-scatter.28
  1994.6 61.1 all-gather.33

commit v6 on v5

--- a/solution.py
+++ b/solution.py
@@ -196,7 +196,7 @@
 def both_cores(pieces, *start):
     size = lax.axis_size("fsdp")
     return lax.all_gather(
-        after(jnp.concatenate(pieces), *start),
+        jnp.concatenate([after(piece, *start) for piece in pieces]),
         "fsdp",
         axis=0,
         tiled=True,
@@ -373,7 +373,9 @@
     def add(self, *others):
         many = self.terms[0].shape[0] // 2
         if many:
-            self.terms[0] = after(self.terms[0], *others)
+            if others:
+                count = len(self.terms)
+                self.terms = list(lax.optimization_barrier((*self.terms, *others))[:count])
             self.send = sum(t[many:].astype(f32) for t in self.terms).astype(bf16)
             self.terms = [t[:many] for t in self.terms]
         return self.send
@@ -407,7 +409,6 @@
     own_part = lax.dynamic_slice_in_dim(packed, half * per_half, per_half, 0)
     other_part = lax.dynamic_slice_in_dim(packed, (1 - half) * per_half, per_half, 0)
     cot_other = swap(cotangent[0], "fsdp", n_fsdp // 2)
-    begun = [start_expert(own_part[:1], other_part[:1], later=(cot_other,))]
     x_parts = send_rows(tokens[0], "seq")
     cot_own = join_rows(send_rows(cotangent[0], "seq", *x_parts), "seq")
 
@@ -446,8 +447,9 @@
         return (values * inverse * gain).astype(bf16), inverse
 
     x_all = join_rows(
-        x_parts, "seq", own_part, other_part, picks, share, cot_own, begun[0][n_fsdp // 2]
-    )
+        x_parts, "seq", own_part, other_part, picks, share, cot_own, cot_other
+    )
+    begun = [start_expert(own_part[:1], other_part[:1], x_all)]
     out_full = lax.all_gather(after(w_out, x_all), "fsdp", axis=0, tiled=True)
     normed_a, _ = normed_rows(x_all.astype(f32), gain_a)
     qkv = dot(normed_a, qkv_own, ((1,), (0,))).astype(bf16)
@@ -475,39 +477,47 @@
             part = part * share[at, i, :, None]
         return part.astype(bf16).reshape(-1, D)
 
-    def begin(i, *start):
-        if i < per_half:
-            begun.append(start_expert(own_part[i : i + 1], other_part[i : i + 1], *start))
+    sets = [[0], [1], list(range(2, per_half))]
+
+    def begin(k, *start):
+        cut = slice(sets[k][0], sets[k][-1] + 1)
+        begun.append(start_expert(own_part[cut], other_part[cut], *start))
 
     begin(1, moe_all[2])
     begin(2, moe_all[1])
     beside = swap(after(own_part, normed_m), "fsdp", 1)
-    near = [both_cores(list(begun[0].values()))]
+    near, last = [both_cores(list(begun[0].values()))], {}
     for i in range(per_half):
-        first, later = begun[i], experts[i]
-        ready = [near[i], *later.values()]
-        last = jnp.concatenate(list(later.values()))
-        last = swap(after(last, *(backward_parts[-1][:1] if i else [])), "fsdp", 1)
-        if i:
-            ready.extend(backward_parts[-1])
-        cots = [after(cot_all[g], *ready) for g in range(2)]
-        if i + 1 < per_half:
-            ready.extend(begun[i + 1].values())
+        k = [n for n, members in enumerate(sets) if i in members][0]
+        first, later, many = begun[k], experts[k], len(sets[k])
+        back = backward_parts[-1] if i else []
+        ready = [near[k], *later.values(), *back]
+        if k not in last:
+            last[k] = swap(
+                jnp.concatenate([after(p, *back[:1]) for p in later.values()]), "fsdp", 1
+            )
+        if i == 0:
+            ready.extend(begun[1].values())
+        if i == 2:
+            ready.extend(begun[2].values())
+        cots = [after(cot_all[g], *back) for g in range(2)]
         if i >= 2:
             ready.append(chains[i - 2].sums())
-        if i >= 3:
-            ready.append(chains[i - 3].sums())
         slots = [dispatch(i, g, after(moe_all[g], *ready), False) for g in range(2)]
         grad_slots = [dispatch(i, g, cots[g], True) for g in range(2)]
-        if i + 1 < per_half:
-            experts.append(finish_expert(begun[i + 1], slots[1]))
-            near.append(both_cores(list(begun[i + 1].values()), slots[1]))
+        if i == 0:
+            experts.append(finish_expert(begun[1], slots[1]))
+            near.append(both_cores(list(begun[1].values()), slots[1]))
         even = [*first, *later]
-        pieces = [own_part, beside, near[i], last, *first.values(), *later.values()]
+        pieces = [own_part, beside, near[k], last[k], *first.values(), *later.values()]
+        at = i - sets[k][0]
         parts = {0: (0, i, 0), 1: (1, i, 0)}
         for n, j in enumerate(even):
-            parts[j] = (4 + n, 0, 0)
-            parts[j + 1] = (2, n, len(first)) if j in first else (3, n - len(first), 0)
+            parts[j] = (4 + n, at, 0)
+            if j in first:
+                parts[j + 1] = (2, n * many + at, len(first) * many)
+            else:
+                parts[j + 1] = (3, (n - len(first)) * many + at, 0)
         parts = [parts[j] for j in range(n_fsdp)]
         *made, grad = run_expert(
             place, share[:, i].reshape(-1, 1), slots, grad_slots, pieces, parts
@@ -515,12 +525,16 @@
         forward_parts.append([part.reshape(n_seq, capacity, D) for part in made[:2]])
         backward_parts.append([part.reshape(n_seq, capacity, D) for part in made[2:]])
         chains.append(GradChain(grad))
-        begin(i + 3, backward_parts[-1][0])
+        if i == 1:
+            experts.append(finish_expert(begun[2], made[2]))
+            near.append(both_cores(list(begun[2].values()), made[2]))
 
     every_pick = picks.reshape(2, n_seq, per_half * capacity, rows)
 
     def combine(parts, g, *others):
-        together = after(jnp.concatenate([part[g] for part in parts], axis=1), *others)
+        together = jnp.concatenate([part[g] for part in parts], axis=1)
+        if others:
+            together = after(together, *others)
         total = dot(every_pick[g], together, ((1,), (1,)), ((0,), (0,)))
         return total.astype(bf16).reshape(span_len, D)
 
@@ -532,11 +546,13 @@
     swapped_back = scatter(back_other)
     grad_normed_m = scatter(back_own, swapped_back)
     swapped_back = swap(swapped_back, "fsdp", n_fsdp // 2)
-    ready = [chain.arrive() for chain in chains]
-    ready.extend(chain.add(back_own) for chain in chains[1:-1])
+    for chain in chains[-2:]:
+        chain.arrive()
+    ready = [chain.add(back_own) for chain in chains[-2:]]
     made_other = combine(forward_parts, 1, back_own)
     made_own = combine(forward_parts, 0, made_other, *ready)
-    grad_normed_m = after(grad_normed_m, made_own).astype(f32) + swapped_back.astype(f32)
+    ready = [made_own, *[chain.arrive() for chain in chains[:-2]]]
+    grad_normed_m = after(grad_normed_m, *ready).astype(f32) + swapped_back.astype(f32)
 
     scaled_m = grad_normed_m * gain_m
     grad_resid = (
@@ -552,18 +568,15 @@
     grad_heads = lax.all_to_all(
         grad_heads_rows, "seq", split_axis=1, concat_axis=0, tiled=True
     )
-    ready = [chains[-1].add(grad_heads_rows)]
-    chains[-2].arrive()
-    ready.append(chains[-2].add(grad_heads_rows))
-    grad_heads = after(grad_heads, *ready)
+    for chain in chains[:-2]:
+        chain.add(grad_heads_rows)
     out_sum = []
     for k in range(n_seq):
         columns = lax.dynamic_slice_in_dim(grad_attn, (at_seq ^ k) * width, width, 1)
         part = dot(heads_rows, columns, ((0,), (0,))).astype(bf16)
         out_sum.append(part)
     grad_qkv = attend(qkv, segment, grad_heads)
-    ready = [chain.arrive() for chain in chains[1:-2]]
-    grad_qkv = after(grad_qkv, mixed_other, *ready)
+    grad_qkv = after(grad_qkv, mixed_other, chains[0].arrive(), chains[-2].arrive())
     mixed_other = swap(mixed_other, "fsdp", n_fsdp // 2)
     mixed = (resid + mixed_own.astype(f32) + mixed_other.astype(f32)).astype(bf16)
 
@@ -571,13 +584,14 @@
     reduced_qkv = lax.psum_scatter(grad_qkv_w, "fsdp", scatter_dimension=0, tiled=True)
     part_normed_a = dot(after(grad_qkv, grad_qkv_w), qkv_own, ((1,), (1,)))
     part_sent = part_normed_a.astype(bf16)
-    chains[-1].arrive()
-    ready = [chains[-1].add(part_sent)]
+    chains[-2].add(grad_qkv_w)
+    ready = [part_sent, *[chain.arrive() for chain in chains[1:]]]
+    ready.append(chains[-1].add(grad_qkv_w))
     out_sum = [swap(after(p, grad_qkv_w), "seq", k) if k else p for k, p in enumerate(out_sum)]
     grad_normed_a = scatter_rows(after(part_sent, *out_sum), "seq")
     qkv_sum = after(reduced_qkv, mixed_other, *ready, *out_sum[1:])
     qkv_sum = lax.all_gather(qkv_sum, "seq", axis=0, tiled=False)
-    out_sum[0] = after(out_sum[0], qkv_sum)
+    out_sum[0] = after(out_sum[0], qkv_sum, grad_normed_a)
     out_sum = sum(part.astype(f32) for part in out_sum).astype(bf16)
     gain_column = jnp.zeros((D, 128), bf16).at[:, 0].set(grad_gain_m.astype(bf16))
     out_sum = jnp.concatenate([out_sum, gain_column], axis=1)

time: 2080 us -> 2080 us (level)
  waiting for transfers between devices: 1210 us -> 1150 us
  blocking collectives: 8.68 us -> 65.8 us
    ppermute x45 -> x41, waiting for transfers between devices: 1100 us -> 957 us  [swap(): return lax.ppermute(value, axis, [(i, i ^ bit) for i in range(size)])]
    reduce_scatter x4, waiting for transfers between devices: 54.7 us -> 113 us  [scatter(): lax.psum_scatter(after(sums, *others), 'seq', scatter_dimension=0, tiled=...]
    all_gather x1, blocking collectives: 8.68 us -> 65.8 us  [body(): lax.all_gather(routing, 'seq', axis=0, tiled=False)]
    all_gather x1, waiting for transfers between devices: 38.3 us -> 0.01 us  [body(): qkv_sum = lax.all_gather(qkv_sum, 'seq', axis=0, tiled=False)]
    all_to_all x1, waiting for transfers between devices: 0.01 us -> 26.7 us  [body(): lax.all_to_all(grad_heads_rows, 'seq', split_axis=1, concat_axis=0, tiled...]
    reduce_scatter x4, waiting for transfers between devices: 0.01 us -> 21.9 us  [__init__(): lax.psum_scatter(grad.reshape(-1, columns), 'fsdp', scatter_dimension=0,...]
    ppermute x45 -> x41, starting transfers between devices: 56.2 us -> 54.8 us  [swap(): return lax.ppermute(value, axis, [(i, i ^ bit) for i in range(size)])]
  transfers between devices with their start and end apart: 67 -> 62, of which waited for: 26 -> 26; matrix products, arithmetic and copies ran while one was open for 17% -> 16% of each run, Pallas kernels for 13% -> 13%
where the time goes in v6:
time: 2080 us; the launch traced here: 2070 us
  waiting for transfers between devices  1150 us (55%)
  Pallas kernels  341 us (16%)
  matrix products  185 us (9%)
  local copies, waits for them, and re-layouts  133 us (6%)
  other arithmetic  111 us (5%)
  blocking collectives  65.8 us (3%)
  starting transfers between devices  65.3 us (3%)
    ppermute x41, waiting for transfers between devices, swap(): return lax.ppermute(value, axis, [(i, i ^ bit) for i in range(size)])  957 us
    pallas_call x4, Pallas kernels, run_expert(): pl.pallas_call(lambda *refs: expert_kernel(size, tiles, parts, *refs), ou...  238 us
    dot_general x29, matrix products, dot(): return lax.dot_general(a, b, (contract, batch), preferred_element_type=f32)  184 us
    reduce_scatter x4, waiting for transfers between devices, scatter(): lax.psum_scatter(after(sums, *others), 'seq', scatter_dimension=0, tiled=...  113 us
    pallas_call x2, Pallas kernels, attend(): pl.pallas_call(lambda *refs: (attend_backward_kernel if backward else att...  76.2 us
    all_gather x1, blocking collectives, body(): lax.all_gather(routing, 'seq', axis=0, tiled=False)  65.8 us
    ppermute x41, starting transfers between devices, swap(): return lax.ppermute(value, axis, [(i, i ^ bit) for i in range(size)])  54.8 us
  transfers between devices with their start and end apart: 62, of which 26 were waited for; matrix products, arithmetic and copies ran while one was open for 16% of the time, Pallas kernels for 13%

profile of v6, /device:TPU:0, one launch (start us, length us, event | category | flops | bytes accessed | tf_op | source)
XLA Modules:
  0.0 2066.0 jit_solution(12589319862139933538)
XLA Ops:
  36.9 14.5 reshape.375
  62.0 32.8 %collective-permute-done.2 = bf16[384,2048]{1,0:T(8,128)(2,1)} collective-permute-done((bf16[384,2048]{1,0:T(8,128)(2,1)S(1)}, bf16[384,2048]{1,0:T(8,128)(2,1)}, u32[]{:S(2)}, u32[]{:S(2)}) %collective-permute-start.2) | collective-permute-done | bytes 1572896 | tf_op jit(solution)/shard_map/ppermute | solution.py:21
  103.4 65.8 %all-gather = f32[8,384,16]{1,2,0:T(8,128)S(1)} all-gather(f32[2,384,16]{1,2,0:T(8,128)S(1)} %pad_maximum_fusion.9), channel_id=2, replica_groups=mesh['seq'=4,'fsdp'=8] {'seq'}, dimensions={0}, use_global_device_ids=true | all-gather | bytes 245760 | tf_op jit(solution)/shard_map/all_gather | solution.py:428
  209.9 122.7 %collective-permute-done.11.refs_10_ = bf16[1,256,3072]{2,1,0:T(8,128)(2,1)} collective-permute-done((bf16[1,256,3072]{2,1,0:T(8,128)(2,1)S(1)}, bf16[1,256,3072]{2,1,0:T(8,128)(2,1)}, u32[]{:S(2)}, u32[]{:S(2)}) %collective-permute-start.11) | collective-permute-done | bytes 1572896 | tf_op jit(solution)/shard_map/ppermute | solution.py:21
  333.9 16.1 convolution_convert_fusion.2.refs_0_
  350.0 25.2 %attend_forward.1 = bf16[1536,512]{1,0:T(8,128)(2,1)} custom-call(bf16[1536,1536]{1,0:T(8,128)(2,1)} %convolution_convert_fusion.2.refs_0_, s32[1536,1]{1,0:T(8,128)} %reshape.439.refs_1_.refs_2_, s32[1,1536]{1,0:T(1,128)} %reshape.384.refs_2_.refs_3_), custom_call_target="tpu_custom_call" | custom-call | flops 24159191040 | bytes 9437184 | tf_op jit(solution)/shard_map/attend_forward/pallas_call | solution.py:97
  419.0 67.2 %collective-permute-done.14 = bf16[384,2048]{1,0:T(8,128)(2,1)} collective-permute-done((bf16[384,2048]{1,0:T(8,128)(2,1)S(1)}, bf16[384,2048]{1,0:T(8,128)(2,1)}, u32[]{:S(2)}, u32[]{:S(2)}) %collective-permute-start.14) | collective-permute-done | bytes 1572896 | tf_op jit(solution)/shard_map/ppermute | solution.py:21
  501.2 57.0 %collective-permute-done.15.refs_10_ = bf16[1,256,3072]{2,1,0:T(8,128)(2,1)} collective-permute-done((bf16[1,256,3072]{2,1,0:T(8,128)(2,1)}, bf16[1,256,3072]{2,1,0:T(8,128)(2,1)}, u32[]{:S(2)}, u32[]{:S(2)}) %collective-permute-start.15) | collective-permute-done | bytes 1572896 | tf_op jit(solution)/shard_map/ppermute | solution.py:21
  558.2 14.1 all-gather.27.cloned.1.call-done
  599.9 59.1 %expert.4 = (bf16[544,2048]{1,0:T(8,128)(2,1)}, bf16[544,2048]{1,0:T(8,128)(2,1)}, bf16[544,2048]{1,0:T(8,128)(2,1)}, bf16[544,2048]{1,0:T(8,128)(2,1)}, bf16[8,256,3072]{2,1,0:T(8,128)(2,1)}) custom-call(s32[1]{0:T(128)} %bitcast.23.refs_0_, f32[1088,1]{1,0:T(8,128)} %reshape_squeeze.16.refs_1_, bf16[544,2048]{1,0:T(8,128)(2,1)} %bitcast.257, ...), custom_call_target="tpu_custom_call" | custom-call | flops 41070624768 | bytes 42991616 | tf_op jit(solution)/shard_map/expert/pallas_call | solution.py:316
  673.2 47.6 %collective-permute-done.19.refs_12_ = bf16[1,256,3072]{2,1,0:T(8,128)(2,1)S(1)} collective-permute-done((bf16[1,256,3072]{2,1,0:T(8,128)(2,1)}, bf16[1,256,3072]{2,1,0:T(8,128)(2,1)S(1)}, u32[]{:S(2)}, u32[]{:S(2)}) %collective-permute-start.19) | collective-permute-done | bytes 1572896 | tf_op jit(solution)/shard_map/ppermute | solution.py:21
  743.3 59.4 %expert.5 = (bf16[544,2048]{1,0:T(8,128)(2,1)}, bf16[544,2048]{1,0:T(8,128)(2,1)}, bf16[544,2048]{1,0:T(8,128)(2,1)}, bf16[544,2048]{1,0:T(8,128)(2,1)}, bf16[8,256,3072]{2,1,0:T(8,128)(2,1)}) custom-call(s32[1]{0:T(128)} %bitcast.23.refs_0_, f32[1088,1]{1,0:T(8,128)} %reshape_squeeze.17.refs_1_, bf16[544,2048]{1,0:T(8,128)(2,1)} %bitcast.260, ...), custom_call_target="tpu_custom_call" | custom-call | flops 41070624768 | bytes 42991616 | tf_op jit(solution)/shard_map/expert/pallas_call | solution.py:316
  802.7 28.9 %collective-permute-done.22.refs_11_ = bf16[2,256,3072]{2,1,0:T(8,128)(2,1)} collective-permute-done((bf16[2,256,3072]{2,1,0:T(8,128)(2,1)}, bf16[2,256,3072]{2,1,0:T(8,128)(2,1)}, u32[]{:S(2)}, u32[]{:S(2)}) %collective-permute-start.22) | collective-permute-done | bytes 3145760 | tf_op jit(solution)/shard_map/ppermute | solution.py:21
  842.0 66.8 %collective-permute-done.23.refs_12_ = bf16[2,256,3072]{2,1,0:T(8,128)(2,1)} collective-permute-done((bf16[2,256,3072]{2,1,0:T(8,128)(2,1)}, bf16[2,256,3072]{2,1,0:T(8,128)(2,1)}, u32[]{:S(2)}, u32[]{:S(2)}) %collective-permute-start.23) | collective-permute-done | bytes 3145760 | tf_op jit(solution)/shard_map/ppermute | solution.py:21
  937.6 59.6 %expert.6 = (bf16[544,2048]{1,0:T(8,128)(2,1)}, bf16[544,2048]{1,0:T(8,128)(2,1)}, bf16[544,2048]{1,0:T(8,128)(2,1)}, bf16[544,2048]{1,0:T(8,128)(2,1)}, bf16[8,256,3072]{2,1,0:T(8,128)(2,1)}) custom-call(s32[1]{0:T(128)} %bitcast.23.refs_0_, f32[1088,1]{1,0:T(8,128)} %reshape_squeeze.18.refs_1_, bf16[544,2048]{1,0:T(8,128)(2,1)} %bitcast.262, ...), custom_call_target="tpu_custom_call" | custom-call | flops 41070624768 | bytes 42991616 | tf_op jit(solution)/shard_map/expert/pallas_call | solution.py:316
  1025.0 59.5 %expert.7 = (bf16[544,2048]{1,0:T(8,128)(2,1)}, bf16[544,2048]{1,0:T(8,128)(2,1)}, bf16[544,2048]{1,0:T(8,128)(2,1)}, bf16[544,2048]{1,0:T(8,128)(2,1)}, bf16[8,256,3072]{2,1,0:T(8,128)(2,1)}) custom-call(s32[1]{0:T(128)} %bitcast.23.refs_0_, f32[1088,1]{1,0:T(8,128)} %reshape_squeeze.19.refs_1_, bf16[544,2048]{1,0:T(8,128)(2,1)} %bitcast.259, ...), custom_call_target="tpu_custom_call" | custom-call | flops 41070624768 | bytes 42991616 | tf_op jit(solution)/shard_map/expert/pallas_call | solution.py:316
  1106.9 57.0 %reduce-scatter.19.cloned.1.call-done = bf16[384,2048]{1,0:T(8,128)(2,1)} async-done(((bf16[1536,2048]{1,0:T(8,128)(2,1)}), bf16[384,2048]{1,0:T(8,128)(2,1)}) %reduce-scatter.19.cloned.1.call-update) | async-done | bytes 1572880 | tf_op jit(solution)/shard_map/reduce_scatter | solution.py:542
  1193.6 19.5 reduce-scatter.17.cloned.1.call-done
  1228.8 40.5 %collective-permute-done.25 = bf16[2,256,3072]{2,1,0:T(8,128)(2,1)} collective-permute-done((bf16[2,256,3072]{2,1,0:T(8,128)(2,1)}, bf16[2,256,3072]{2,1,0:T(8,128)(2,1)}, u32[]{:S(2)}, u32[]{:S(2)}) %collective-permute-start.25) | collective-permute-done | bytes 3145760 | tf_op jit(solution)/shard_map/ppermute | solution.py:21
  1269.2 66.3 %collective-permute-done.26 = bf16[2,256,3072]{2,1,0:T(8,128)(2,1)} collective-permute-done((bf16[2,256,3072]{2,1,0:T(8,128)(2,1)}, bf16[2,256,3072]{2,1,0:T(8,128)(2,1)}, u32[]{:S(2)}, u32[]{:S(2)}) %collective-permute-start.26) | collective-permute-done | bytes 3145760 | tf_op jit(solution)/shard_map/ppermute | solution.py:21
  1366.1 26.7 %all-to-all-done.1 = bf16[384,4,512]{2,0,1:T(8,128)(2,1)} async-done(((bf16[384,4,512]{2,0,1:T(8,128)(2,1)}), bf16[384,4,512]{2,0,1:T(8,128)(2,1)}, u32[]{:S(2)}, u32[]{:S(2)}) %all-to-all-start.1) | async-done | bytes 1572896 | tf_op jit(solution)/shard_map/all_to_all | solution.py:568
  1392.8 51.0 %attend_backward.1 = bf16[1536,1536]{1,0:T(8,128)(2,1)} custom-call(bf16[1536,1536]{1,0:T(8,128)(2,1)} %convolution_convert_fusion.2.refs_0_, bf16[1536,512]{1,0:T(8,128)(2,1)} %bitcast.90.refs_1_, s32[1536,1]{1,0:T(8,128)} %reshape.439.refs_1_.refs_2_, s32[1,1536]{1,0:T(1,128)} %reshape.384.refs_2_.refs_3_), custom_call_target="tpu_custom_call" | custom-call | flops 48318382080 | bytes 9437184 | tf_op jit(solution)/shard_map/attend_backward/pallas_call | solution.py:97
  1443.8 16.3 collective-permute-done.30
  1460.2 15.8 convolution_convert_fusion.1
  1497.9 173.3 %collective-permute-done.39 = bf16[2,256,3072]{2,1,0:T(8,128)(2,1)} collective-permute-done((bf16[2,256,3072]{2,1,0:T(8,128)(2,1)}, bf16[2,256,3072]{2,1,0:T(8,128)(2,1)}, u32[]{:S(2)}, u32[]{:S(2)}) %collective-permute-start.39) | collective-permute-done | bytes 3145760 | tf_op jit(solution)/shard_map/ppermute | solution.py:21
  1679.0 13.6 convolution_convert_fusion
  1692.5 53.2 %collective-permute-done.28 = bf16[384,2048]{1,0:T(8,128)(2,1)S(1)} collective-permute-done((bf16[384,2048]{1,0:T(8,128)(2,1)S(1)}, bf16[384,2048]{1,0:T(8,128)(2,1)S(1)}, u32[]{:S(2)}, u32[]{:S(2)}) %collective-permute-start.28) | collective-permute-done | bytes 1572896 | tf_op jit(solution)/shard_map/ppermute | solution.py:21
  1757.9 56.0 %collective-permute-done.34 = bf16[384,2048]{1,0:T(8,128)(2,1)S(1)} collective-permute-done((bf16[384,2048]{1,0:T(8,128)(2,1)S(1)}, bf16[384,2048]{1,0:T(8,128)(2,1)S(1)}, u32[]{:S(2)}, u32[]{:S(2)}) %collective-permute-start.34) | collective-permute-done | bytes 1572896 | tf_op jit(solution)/shard_map/ppermute | solution.py:21
  1813.9 34.9 %collective-permute-done.36 = bf16[384,2048]{1,0:T(8,128)(2,1)S(1)} collective-permute-done((bf16[384,2048]{1,0:T(8,128)(2,1)S(1)}, bf16[384,2048]{1,0:T(8,128)(2,1)S(1)}, u32[]{:S(2)}, u32[]{:S(2)}) %collective-permute-start.36) | collective-permute-done | bytes 1572896 | tf_op jit(solution)/shard_map/ppermute | solution.py:21
  1863.0 90.7 %collective-permute-done.40 = bf16[1,256,3072]{2,1,0:T(8,128)(2,1)} collective-permute-done((bf16[1,256,3072]{2,1,0:T(8,128)(2,1)}, bf16[1,256,3072]{2,1,0:T(8,128)(2,1)}, u32[]{:S(2)}, u32[]{:S(2)}) %collective-permute-start.40) | collective-permute-done | bytes 1572896 | tf_op jit(solution)/shard_map/ppermute | solution.py:21
  1962.3 55.6 %reduce-scatter.23.cloned.1.call-done = bf16[384,2048]{1,0:T(8,128)(2,1)} async-done(((bf16[1536,2048]{1,0:T(8,128)(2,1)}), bf16[384,2048]{1,0:T(8,128)(2,1)}) %reduce-scatter.23.cloned.1.call-update) | async-done | bytes 1572880 | tf_op jit(solution)/shard_map/reduce_scatter | solution.py:542
  2021.8 14.7 finish.1
  (372 shorter events, 469.5 us)
Async XLA Ops:
  7.2 325.9 %all-gather.15.cloned.1.call-start = ((), (), s32[]{:S(2)}) async-start(), calls=%async_computation.12 | async-start | bytes 7667712 | tf_op jit(solution)/shard_map/all_gather | solution.py:419
  22.6 377.9 %all-gather.17.cloned.1.call-start = ((), (), s32[]{:S(2)}) async-start(), calls=%async_computation.13 | async-start | bytes 9437184 | tf_op jit(solution)/shard_map/all_gather | solution.py:453
  30.4 147.4 %collective-permute-start.7 = (bf16[384,2048]{1,0:T(8,128)(2,1)S(1)}, bf16[384,2048]{1,0:T(8,128)(2,1)}, u32[]{:S(2)}, u32[]{:S(2)}) collective-permute-start(bf16[384,2048]{1,0:T(8,128)(2,1)S(1)} %bitcast.229), channel_id=1, source_target_pairs={{0,4},{1,5},{2,6},{3,7},{4,0},{5,1},{6,2},{7,3},{8,12},{9,13},{10,... | collective-permute-start | bytes 4718600 | tf_op jit(solution)/shard_map/ppermute | solution.py:21
  195.8 136.7 %collective-permute-start.11 = (bf16[1,256,3072]{2,1,0:T(8,128)(2,1)S(1)}, bf16[1,256,3072]{2,1,0:T(8,128)(2,1)}, u32[]{:S(2)}, u32[]{:S(2)}) collective-permute-start(bf16[1,256,3072]{2,1,0:T(8,128)(2,1)S(1)} %get-tuple-element.128), channel_id=1, source_target_pairs={{0,4},{1,5},{2,6},{3,7},{4,0},{5,1},{6,2},{7,3},{8,12},{9,13},{10,... | collective-permute-start | bytes 4718600 | tf_op jit(solution)/shard_map/ppermute | solution.py:21
  200.7 192.4 %collective-permute-start.10 = (bf16[384,2048]{1,0:T(8,128)(2,1)}, bf16[384,2048]{1,0:T(8,128)(2,1)}, u32[]{:S(2)}, u32[]{:S(2)}) collective-permute-start(bf16[384,2048]{1,0:T(8,128)(2,1)} %collective-permute-done.7), channel_id=1, source_target_pairs={{0,24},{8,16},{16,8},{24,0},{1,25},{9,17},{17,9},{25,1},{2,26},{10... | collective-permute-start | bytes 4718600 | tf_op jit(solution)/shard_map/ppermute | solution.py:21
  202.1 188.2 %collective-permute-start.9 = (bf16[384,2048]{1,0:T(8,128)(2,1)}, bf16[384,2048]{1,0:T(8,128)(2,1)}, u32[]{:S(2)}, u32[]{:S(2)}) collective-permute-start(bf16[384,2048]{1,0:T(8,128)(2,1)} %collective-permute-done.7), channel_id=1, source_target_pairs={{0,16},{8,24},{16,0},{24,8},{1,17},{9,25},{17,1},{25,9},{2,18},{10... | collective-permute-start | bytes 4718600 | tf_op jit(solution)/shard_map/ppermute | solution.py:21
  204.1 183.4 %collective-permute-start.8 = (bf16[384,2048]{1,0:T(8,128)(2,1)}, bf16[384,2048]{1,0:T(8,128)(2,1)}, u32[]{:S(2)}, u32[]{:S(2)}) collective-permute-start(bf16[384,2048]{1,0:T(8,128)(2,1)} %collective-permute-done.7), channel_id=1, source_target_pairs={{0,8},{8,0},{16,24},{24,16},{1,9},{9,1},{17,25},{25,17},{2,10},{10... | collective-permute-start | bytes 4718600 | tf_op jit(solution)/shard_map/ppermute | solution.py:21
  204.2 191.7 %collective-permute-start.13 = (bf16[1,256,3072]{2,1,0:T(8,128)(2,1)}, bf16[1,256,3072]{2,1,0:T(8,128)(2,1)}, u32[]{:S(2)}, u32[]{:S(2)}) collective-permute-start(bf16[1,256,3072]{2,1,0:T(8,128)(2,1)} %get-tuple-element.130), channel_id=1, source_target_pairs={{0,2},{1,3},{2,0},{3,1},{4,6},{5,7},{6,4},{7,5},{8,10},{9,11},{10,... | collective-permute-start | bytes 4718600 | tf_op jit(solution)/shard_map/ppermute | solution.py:21
  414.3 158.0 %all-gather.27.cloned.1.call-start = ((), (), s32[]{:S(2)}) async-start(), calls=%async_computation.28 | async-start | bytes 7864320 | tf_op jit(solution)/shard_map/all_gather | solution.py:468
  486.3 246.0 %all-gather.21.cloned.1.call-start = ((), (), s32[]{:S(2)}) async-start(), calls=%async_computation.15 | async-start | bytes 9437184 | tf_op jit(solution)/shard_map/all_gather | solution.py:198
  486.3 112.4 %collective-permute-start.17 = (bf16[4,256,3072]{2,1,0:T(8,128)(2,1)}, bf16[4,256,3072]{2,1,0:T(8,128)(2,1)}, u32[]{:S(2)}, u32[]{:S(2)}) collective-permute-start(bf16[4,256,3072]{2,1,0:T(8,128)(2,1)} %get-tuple-element.138.refs_6_), channel_id=1, source_target_pairs={{0,1},{1,0},{2,3},{3,2},{4,5},{5,4},{6,7},{7,6},{8,9},{9,8},{10,11... | collective-permute-start | bytes 18874376 | tf_op jit(solution)/shard_map/ppermute | solution.py:21
  581.8 338.9 %reduce-scatter.11.cloned.1.call-start = ((), (), s32[]{:S(2)}) async-start(), calls=%async_computation.17 | async-start | bytes 18874368 | tf_op jit(solution)/shard_map/reduce_scatter | solution.py:358
  659.0 267.6 %all-gather.23.cloned.1.call-start = ((), (), s32[]{:S(2)}) async-start(), calls=%async_computation.16 | async-start | bytes 18874368 | tf_op jit(solution)/shard_map/all_gather | solution.py:198
  670.5 161.0 %collective-permute-start.21 = (bf16[2,256,3072]{2,1,0:T(8,128)(2,1)}, bf16[2,256,3072]{2,1,0:T(8,128)(2,1)}, u32[]{:S(2)}, u32[]{:S(2)}) collective-permute-start(bf16[2,256,3072]{2,1,0:T(8,128)(2,1)} %slice.325), channel_id=1, source_target_pairs={{0,4},{1,5},{2,6},{3,7},{4,0},{5,1},{6,2},{7,3},{8,12},{9,13},{10,... | collective-permute-start | bytes 9437192 | tf_op jit(solution)/shard_map/ppermute | solution.py:21
  673.2 158.4 %collective-permute-start.22 = (bf16[2,256,3072]{2,1,0:T(8,128)(2,1)}, bf16[2,256,3072]{2,1,0:T(8,128)(2,1)}, u32[]{:S(2)}, u32[]{:S(2)}) collective-permute-start(bf16[2,256,3072]{2,1,0:T(8,128)(2,1)} %slice.326), channel_id=1, source_target_pairs={{0,2},{1,3},{2,0},{3,1},{4,6},{5,7},{6,4},{7,5},{8,10},{9,11},{10,... | collective-permute-start | bytes 9437192 | tf_op jit(solution)/shard_map/ppermute | solution.py:21
  837.6 170.6 %reduce-scatter.13.cloned.1.call-start = ((), (), s32[]{:S(2)}) async-start(), calls=%async_computation.18 | async-start | bytes 18874368 | tf_op jit(solution)/shard_map/reduce_scatter | solution.py:358
  838.3 325.6 %reduce-scatter.19.cloned.1.call-start = ((), (), s32[]{:S(2)}) async-start(), calls=%async_computation.21 | async-start | bytes 7864320 | tf_op jit(solution)/shard_map/reduce_scatter | solution.py:542
  1094.3 118.9 %reduce-scatter.17.cloned.1.call-start = ((), (), s32[]{:S(2)}) async-start(), calls=%async_computation.20 | async-start | bytes 18874368 | tf_op jit(solution)/shard_map/reduce_scatter | solution.py:358
  1094.9 240.7 %reduce-scatter.21.cloned.1.call-start = ((), (), s32[]{:S(2)}) async-start(), calls=%async_computation.22 | async-start | bytes 7864320 | tf_op jit(solution)/shard_map/reduce_scatter | solution.py:542
  1163.9 296.2 %reduce-scatter.25.cloned.1.call-start = ((), (), s32[]{:S(2)}) async-start(), calls=%async_computation.24 | async-start | bytes 7864320 | tf_op jit(solution)/shard_map/reduce_scatter | solution.py:542
  1165.7 169.8 %collective-permute-start.26 = (bf16[2,256,3072]{2,1,0:T(8,128)(2,1)}, bf16[2,256,3072]{2,1,0:T(8,128)(2,1)}, u32[]{:S(2)}, u32[]{:S(2)}) collective-permute-start(bf16[2,256,3072]{2,1,0:T(8,128)(2,1)} %bitcast.64), channel_id=1, source_target_pairs={{0,2},{1,3},{2,0},{3,1},{4,6},{5,7},{6,4},{7,5},{8,10},{9,11},{10,... | collective-permute-start | bytes 9437192 | tf_op jit(solution)/shard_map/ppermute | solution.py:21
  1182.9 152.7 %collective-permute-start.27 = (bf16[384,2048]{1,0:T(8,128)(2,1)}, bf16[384,2048]{1,0:T(8,128)(2,1)}, u32[]{:S(2)}, u32[]{:S(2)}) collective-permute-start(bf16[384,2048]{1,0:T(8,128)(2,1)} %reduce-scatter.19.cloned.1.call-done), channel_id=1, source_target_pairs={{0,4},{1,5},{2,6},{3,7},{4,0},{5,1},{6,2},{7,3},{8,12},{9,13},{10,... | collective-permute-start | bytes 4718600 | tf_op jit(solution)/shard_map/ppermute | solution.py:21
  1356.0 391.4 %reduce-scatter.27.cloned.1.call-start = ((), (), s32[]{:S(2)}) async-start(), calls=%async_computation.25 | async-start | bytes 7077888 | tf_op jit(solution)/shard_map/reduce_scatter | solution.py:584
  1475.9 377.4 %all-gather.29.cloned.1.call-start = ((), (), s32[]{:S(2)}) async-start(), calls=%async_computation.29 | async-start | bytes 3932160 | tf_op jit(solution)/shard_map/all_gather | solution.py:593
  1476.2 195.1 %collective-permute-start.39 = (bf16[2,256,3072]{2,1,0:T(8,128)(2,1)}, bf16[2,256,3072]{2,1,0:T(8,128)(2,1)}, u32[]{:S(2)}, u32[]{:S(2)}) collective-permute-start(bf16[2,256,3072]{2,1,0:T(8,128)(2,1)} %get-tuple-element.228), channel_id=1, source_target_pairs={{0,2},{1,3},{2,0},{3,1},{4,6},{5,7},{6,4},{7,5},{8,10},{9,11},{10,... | collective-permute-start | bytes 9437192 | tf_op jit(solution)/shard_map/ppermute | solution.py:21
  1483.1 195.2 %collective-permute-start.37 = (bf16[1,256,3072]{2,1,0:T(8,128)(2,1)S(1)}, bf16[1,256,3072]{2,1,0:T(8,128)(2,1)S(1)}, u32[]{:S(2)}, u32[]{:S(2)}) collective-permute-start(bf16[1,256,3072]{2,1,0:T(8,128)(2,1)S(1)} %get-tuple-element.222), channel_id=1, source_target_pairs={{0,4},{1,5},{2,6},{3,7},{4,0},{5,1},{6,2},{7,3},{8,12},{9,13},{10,... | collective-permute-start | bytes 4718600 | tf_op jit(solution)/shard_map/ppermute | solution.py:21
  1493.4 252.4 %collective-permute-start.38 = (bf16[1,256,3072]{2,1,0:T(8,128)(2,1)S(1)}, bf16[1,256,3072]{2,1,0:T(8,128)(2,1)S(1)}, u32[]{:S(2)}, u32[]{:S(2)}) collective-permute-start(bf16[1,256,3072]{2,1,0:T(8,128)(2,1)S(1)} %get-tuple-element.224), channel_id=1, source_target_pairs={{0,4},{1,5},{2,6},{3,7},{4,0},{5,1},{6,2},{7,3},{8,12},{9,13},{10,... | collective-permute-start | bytes 4718600 | tf_op jit(solution)/shard_map/ppermute | solution.py:21
  1494.8 252.2 %collective-permute-start.31 = (bf16[2048,512]{1,0:T(8,128)(2,1)S(1)}, bf16[2048,512]{1,0:T(8,128)(2,1)}, u32[]{:S(2)}, u32[]{:S(2)}) collective-permute-start(bf16[2048,512]{1,0:T(8,128)(2,1)S(1)} %convolution_convert_fusion.16), channel_id=1, source_target_pairs={{0,8},{8,0},{16,24},{24,16},{1,9},{9,1},{17,25},{25,17},{2,10},{10... | collective-permute-start | bytes 6291464 | tf_op jit(solution)/shard_map/ppermute | solution.py:21
  1496.5 251.0 %collective-permute-start.32 = (bf16[2048,512]{1,0:T(8,128)(2,1)S(1)}, bf16[2048,512]{1,0:T(8,128)(2,1)}, u32[]{:S(2)}, u32[]{:S(2)}) collective-permute-start(bf16[2048,512]{1,0:T(8,128)(2,1)S(1)} %convolution_convert_fusion.15), channel_id=1, source_target_pairs={{0,16},{8,24},{16,0},{24,8},{1,17},{9,25},{17,1},{25,9},{2,18},{10... | collective-permute-start | bytes 6291464 | tf_op jit(solution)/shard_map/ppermute | solution.py:21
  1747.4 214.9 %reduce-scatter.29.cloned.1.call-start = ((), (), s32[]{:S(2)}) async-start(), calls=%async_computation.26 | async-start | bytes 2949120 | tf_op jit(solution)/shard_map/reduce_scatter | solution.py:598
  1859.8 158.2 %reduce-scatter.23.cloned.1.call-start = ((), (), s32[]{:S(2)}) async-start(), calls=%async_computation.23 | async-start | bytes 7864320 | tf_op jit(solution)/shard_map/reduce_scatter | solution.py:542
  1860.4 193.7 %all-gather.31.cloned.1.call-start = ((), (), s32[]{:S(2)}) async-start(), calls=%async_computation.30 | async-start | bytes 1638400 | tf_op jit(solution)/shard_map/all_gather | solution.py:599
  (89 other events, 4272.7 us)
Sparse Core Ops, SparseCore 0:
  22.7 128.8 all-gather.14
  190.8 145.5 all-gather.16
  410.5 70.2 all-gather.24
  482.1 19.0 all-gather.18
  502.9 69.3 all-gather.26
  581.9 16.7 all-gather.20
  659.1 21.6 reduce-scatter.10
  837.7 24.8 all-gather.22
  865.5 22.6 reduce-scatter.12
  1093.7 70.1 reduce-scatter.18
  1166.2 21.4 reduce-scatter.14
  1190.4 22.6 reduce-scatter.16
  1216.1 71.3 reduce-scatter.20
  1349.1 87.0 reduce-scatter.24
  1476.1 183.6 reduce-scatter.26
  1747.6 102.5 all-gather.28
  1859.9 75.1 reduce-scatter.28
  1938.5 79.4 reduce-scatter.22
  2019.8 28.7 all-gather.30

commit v7 on v6

--- a/solution.py
+++ b/solution.py
@@ -231,7 +231,7 @@
     arrays = 1 + max(part[0] for part in parts)
     slots, pieces, rest = rest[:4], rest[4 : 4 + arrays], rest[4 + arrays :]
     made_refs, back_refs, rest = rest[:2], rest[2:4], rest[4:]
-    grad_ref, weights, x_ref, g_ref, act, grad_proj, sems = rest
+    send_ref, keep_ref, weights, x_ref, g_ref, act, grad_proj, sems = rest
     step = pl.program_id(0)
     place = place_ref[0]
     rows = weights.shape[0] // size
@@ -293,8 +293,17 @@
             made_refs[g][...] = made[g * count : (g + 1) * count]
             back_refs[g][...] = back[g * count : (g + 1) * count]
 
-        grad_ref[0, :, : 2 * ffe] = dot(x_ref[:, at], grad_proj[...], tn).astype(bf16)
-        grad_ref[0, :, 2 * ffe :] = dot(g_ref[:, at], act[...], tn).astype(bf16)
+        def grads(out_ref):
+            out_ref[0, :, : 2 * ffe] = dot(x_ref[:, at], grad_proj[...], tn).astype(bf16)
+            out_ref[0, :, 2 * ffe :] = dot(g_ref[:, at], act[...], tn).astype(bf16)
+
+        @pl.when(turn < size // 2)
+        def _():
+            grads(send_ref)
+
+        @pl.when(turn >= size // 2)
+        def _():
+            grads(keep_ref)
 
 
 def run_expert(place, share, slots, grad_slots, pieces, parts):
@@ -308,16 +317,12 @@
         turn = jnp.maximum(step - tiles, 0)
         return 0, place[0] ^ reversed_bits((turn + half) % size, size)
 
-    def stands(step, place):
-        turn = jnp.maximum(step - tiles, 0)
-        core = (whose(step, place)[1]) & 1
-        return core * half + turn % half, 0, 0
-
     return pl.pallas_call(
         lambda *refs: expert_kernel(size, tiles, parts, *refs),
         out_shape=[
             *[jax.ShapeDtypeStruct((count // 2, D), bf16)] * 4,
-            jax.ShapeDtypeStruct((size, rows, columns), bf16),
+            jax.ShapeDtypeStruct((half, rows, columns), bf16),
+            jax.ShapeDtypeStruct((half, rows, columns), bf16),
         ],
         grid_spec=pltpu.PrefetchScalarGridSpec(
             num_scalar_prefetch=1,
@@ -328,7 +333,13 @@
             ],
             out_specs=[
                 *[pl.BlockSpec((count // 2, rows), whose)] * 4,
-                pl.BlockSpec((1, rows, columns), stands),
+                pl.BlockSpec(
+                    (1, rows, columns), lambda t, place: (jnp.clip(t - tiles, 0, half - 1), 0, 0)
+                ),
+                pl.BlockSpec(
+                    (1, rows, columns),
+                    lambda t, place: (jnp.clip(t - tiles - half, 0, half - 1), 0, 0),
+                ),
             ],
             scratch_shapes=[
                 pltpu.VMEM((size * rows, columns), bf16),
@@ -352,22 +363,14 @@
 
 
 class GradChain:
-    def __init__(self, grad):
+    def __init__(self, send, keep):
         self.bit, self.size = 1, lax.axis_size("fsdp")
-        rows, columns = grad.shape[1:]
-        core_sums = lax.psum_scatter(
-            grad.reshape(-1, columns),
-            "fsdp",
-            scatter_dimension=0,
-            tiled=True,
-            axis_index_groups=[[i, i + 1] for i in range(0, self.size, 2)],
-        )
-        self.terms = [core_sums.reshape(-1, rows, columns)]
+        self.terms, self.send = [keep], send
 
     def arrive(self):
-        if 1 < self.bit < self.size:
+        if self.bit < self.size:
             self.terms.append(swap(self.send, "fsdp", self.bit))
-        self.bit = min(2 * self.bit, self.size)
+            self.bit *= 2
         return self.terms[-1]
 
     def add(self, *others):
@@ -449,7 +452,6 @@
     x_all = join_rows(
         x_parts, "seq", own_part, other_part, picks, share, cot_own, cot_other
     )
-    begun = [start_expert(own_part[:1], other_part[:1], x_all)]
     out_full = lax.all_gather(after(w_out, x_all), "fsdp", axis=0, tiled=True)
     normed_a, _ = normed_rows(x_all.astype(f32), gain_a)
     qkv = dot(normed_a, qkv_own, ((1,), (0,))).astype(bf16)
@@ -458,8 +460,9 @@
     heads_rows = lax.all_to_all(attended, "seq", split_axis=0, concat_axis=1, tiled=True)
     cot_all = [cot_own, join_rows(send_rows(cot_other, "seq", cot_own), "seq")]
     cot_all = [rows_of.reshape(n_seq, rows, D) for rows_of in cot_all]
-    experts = [finish_expert(begun[0], x_all)]
-    heads_rows = after(heads_rows, *cot_all, *experts[0].values(), *begun[0].values())
+    begun = [start_expert(own_part[:1], other_part[:1], attended)]
+    heads_rows = after(heads_rows, *cot_all, *begun[0].values())
+    experts = [finish_expert(begun[0], heads_rows)]
     x_float = tokens[0].astype(f32)
     resid = x_float + dot(heads_rows, out_full, ((1,), (0,)))
     normed_m, inv_m = normed_rows(resid, gain_m)
@@ -477,7 +480,7 @@
             part = part * share[at, i, :, None]
         return part.astype(bf16).reshape(-1, D)
 
-    sets = [[0], [1], list(range(2, per_half))]
+    sets = [[i] for i in range(per_half)]
 
     def begin(k, *start):
         cut = slice(sets[k][0], sets[k][-1] + 1)
@@ -496,18 +499,18 @@
             last[k] = swap(
                 jnp.concatenate([after(p, *back[:1]) for p in later.values()]), "fsdp", 1
             )
-        if i == 0:
-            ready.extend(begun[1].values())
-        if i == 2:
-            ready.extend(begun[2].values())
+        if i + 1 < per_half:
+            ready.extend(begun[i + 1].values())
         cots = [after(cot_all[g], *back) for g in range(2)]
-        if i >= 2:
-            ready.append(chains[i - 2].sums())
+        for chain in chains[max(i - 3, 0) : max(i - 1, 0)]:
+            ready.append(chain.arrive())
         slots = [dispatch(i, g, after(moe_all[g], *ready), False) for g in range(2)]
+        ready = [chain.add(back[0]) for chain in chains[max(i - 3, 0) : max(i - 1, 0)]]
+        slots[1] = after(slots[1], *ready)
         grad_slots = [dispatch(i, g, cots[g], True) for g in range(2)]
-        if i == 0:
-            experts.append(finish_expert(begun[1], slots[1]))
-            near.append(both_cores(list(begun[1].values()), slots[1]))
+        if i + 1 < per_half:
+            experts.append(finish_expert(begun[i + 1], slots[1]))
+            near.append(both_cores(list(begun[i + 1].values()), slots[1]))
         even = [*first, *later]
         pieces = [own_part, beside, near[k], last[k], *first.values(), *later.values()]
         at = i - sets[k][0]
@@ -519,15 +522,14 @@
             else:
                 parts[j + 1] = (3, (n - len(first)) * many + at, 0)
         parts = [parts[j] for j in range(n_fsdp)]
-        *made, grad = run_expert(
+        *made, send, keep = run_expert(
             place, share[:, i].reshape(-1, 1), slots, grad_slots, pieces, parts
         )
         forward_parts.append([part.reshape(n_seq, capacity, D) for part in made[:2]])
         backward_parts.append([part.reshape(n_seq, capacity, D) for part in made[2:]])
-        chains.append(GradChain(grad))
-        if i == 1:
-            experts.append(finish_expert(begun[2], made[2]))
-            near.append(both_cores(list(begun[2].values()), made[2]))
+        chains.append(GradChain(send, keep))
+        if i + 3 < per_half:
+            begin(i + 3, made[2])
 
     every_pick = picks.reshape(2, n_seq, per_half * capacity, rows)
 
@@ -541,17 +543,16 @@
     def scatter(sums, *others):
         return lax.psum_scatter(after(sums, *others), "seq", scatter_dimension=0, tiled=True)
 
-    back_other = combine(backward_parts, 1)
+    back_other = combine(backward_parts, 1, chains[-3].arrive())
     back_own = combine(backward_parts, 0, back_other)
     swapped_back = scatter(back_other)
     grad_normed_m = scatter(back_own, swapped_back)
     swapped_back = swap(swapped_back, "fsdp", n_fsdp // 2)
-    for chain in chains[-2:]:
-        chain.arrive()
-    ready = [chain.add(back_own) for chain in chains[-2:]]
+    ready = [chain.arrive() for chain in chains[-2:]]
+    ready.extend(chain.add(back_own) for chain in chains[-3:])
     made_other = combine(forward_parts, 1, back_own)
     made_own = combine(forward_parts, 0, made_other, *ready)
-    ready = [made_own, *[chain.arrive() for chain in chains[:-2]]]
+    ready = [made_own, *[chain.arrive() for chain in (*chains[:-3], chains[-2])]]
     grad_normed_m = after(grad_normed_m, *ready).astype(f32) + swapped_back.astype(f32)
 
     scaled_m = grad_normed_m * gain_m
@@ -568,30 +569,29 @@
     grad_heads = lax.all_to_all(
         grad_heads_rows, "seq", split_axis=1, concat_axis=0, tiled=True
     )
-    for chain in chains[:-2]:
-        chain.add(grad_heads_rows)
+    chains[-2].add(grad_heads_rows)
     out_sum = []
     for k in range(n_seq):
         columns = lax.dynamic_slice_in_dim(grad_attn, (at_seq ^ k) * width, width, 1)
         part = dot(heads_rows, columns, ((0,), (0,))).astype(bf16)
         out_sum.append(part)
     grad_qkv = attend(qkv, segment, grad_heads)
-    grad_qkv = after(grad_qkv, mixed_other, chains[0].arrive(), chains[-2].arrive())
+    ready = [chain.arrive() for chain in (chains[-3], chains[-1])]
+    grad_qkv = after(grad_qkv, mixed_other, *ready)
     mixed_other = swap(mixed_other, "fsdp", n_fsdp // 2)
     mixed = (resid + mixed_own.astype(f32) + mixed_other.astype(f32)).astype(bf16)
 
     grad_qkv_w = dot(normed_a, grad_qkv, ((0,), (0,))).astype(bf16)
-    reduced_qkv = lax.psum_scatter(grad_qkv_w, "fsdp", scatter_dimension=0, tiled=True)
+    reduced_qkv = after(grad_qkv_w, mixed_own)
+    reduced_qkv = lax.psum_scatter(reduced_qkv, "fsdp", scatter_dimension=0, tiled=True)
     part_normed_a = dot(after(grad_qkv, grad_qkv_w), qkv_own, ((1,), (1,)))
     part_sent = part_normed_a.astype(bf16)
-    chains[-2].add(grad_qkv_w)
-    ready = [part_sent, *[chain.arrive() for chain in chains[1:]]]
-    ready.append(chains[-1].add(grad_qkv_w))
+    ready = [part_sent, chains[-1].add(grad_qkv_w)]
     out_sum = [swap(after(p, grad_qkv_w), "seq", k) if k else p for k, p in enumerate(out_sum)]
     grad_normed_a = scatter_rows(after(part_sent, *out_sum), "seq")
-    qkv_sum = after(reduced_qkv, mixed_other, *ready, *out_sum[1:])
+    qkv_sum = after(reduced_qkv, mixed_other, *ready)
     qkv_sum = lax.all_gather(qkv_sum, "seq", axis=0, tiled=False)
-    out_sum[0] = after(out_sum[0], qkv_sum, grad_normed_a)
+    out_sum[0] = after(out_sum[0], qkv_sum, grad_normed_a, *[c.arrive() for c in chains[-2:]])
     out_sum = sum(part.astype(f32) for part in out_sum).astype(bf16)
     gain_column = jnp.zeros((D, 128), bf16).at[:, 0].set(grad_gain_m.astype(bf16))
     out_sum = jnp.concatenate([out_sum, gain_column], axis=1)

time: 2080 us -> 1760 us (0.85)
  waiting for transfers between devices: 1150 us -> 815 us
    ppermute x41 -> x49, waiting for transfers between devices: 957 us -> 660 us  [swap(): return lax.ppermute(value, axis, [(i, i ^ bit) for i in range(size)])]
    reduce_scatter x1, waiting for transfers between devices: 0.01 us -> 25.4 us  [body(): out_sum = lax.psum_scatter(out_sum, 'fsdp', scatter_dimension=0, tiled=True)]
    reduce_scatter x4, waiting for transfers between devices: 113 us -> 89.6 us  [scatter(): lax.psum_scatter(after(sums, *others), 'seq', scatter_dimension=0, tiled=...]
    reduce_scatter x5 -> x1, waiting for transfers between devices: 21.9 us -> 0.01 us  [body(): lax.psum_scatter(reduced_qkv, 'fsdp', scatter_dimension=0, tiled=True)]
    ppermute x41 -> x49, starting transfers between devices: 54.8 us -> 60.5 us  [swap(): return lax.ppermute(value, axis, [(i, i ^ bit) for i in range(size)])]
  transfers between devices with their start and end apart: 62 -> 67, of which waited for: 26 -> 23; matrix products, arithmetic and copies ran while one was open for 16% -> 21% of each run, Pallas kernels for 13% -> 20%
where the time goes in v7:
time: 1760 us
  waiting for transfers between devices  815 us (46%)
  Pallas kernels  352 us (20%)
  matrix products  183 us (10%)
  local copies, waits for them, and re-layouts  128 us (7%)
  other arithmetic  126 us (7%)
  starting transfers between devices  69.9 us (4%)
  blocking collectives  65.8 us (4%)
    ppermute x49, waiting for transfers between devices, swap(): return lax.ppermute(value, axis, [(i, i ^ bit) for i in range(size)])  660 us
    pallas_call x4, Pallas kernels, run_expert(): pl.pallas_call(lambda *refs: expert_kernel(size, tiles, parts, *refs), ou...  249 us
    dot_general x29, matrix products, dot(): return lax.dot_general(a, b, (contract, batch), preferred_element_type=f32)  183 us
    reduce_scatter x4, waiting for transfers between devices, scatter(): lax.psum_scatter(after(sums, *others), 'seq', scatter_dimension=0, tiled=...  89.6 us
    pallas_call x2, Pallas kernels, attend(): pl.pallas_call(lambda *refs: (attend_backward_kernel if backward else att...  76.5 us
    all_gather x1, blocking collectives, body(): lax.all_gather(routing, 'seq', axis=0, tiled=False)  65.8 us
    ppermute x49, starting transfers between devices, swap(): return lax.ppermute(value, axis, [(i, i ^ bit) for i in range(size)])  60.5 us
  transfers between devices with their start and end apart: 67, of which 23 were waited for; matrix products, arithmetic and copies ran while one was open for 21% of the time, Pallas kernels for 20%

profile of v7, /device:TPU:0, one launch (start us, length us, event | category | flops | bytes accessed | tf_op | source)
XLA Modules:
  0.0 1755.1 jit_solution(1072219378772047146)
XLA Ops:
  36.9 14.5 reshape.351
  62.0 32.8 %collective-permute-done.2 = bf16[384,2048]{1,0:T(8,128)(2,1)} collective-permute-done((bf16[384,2048]{1,0:T(8,128)(2,1)S(1)}, bf16[384,2048]{1,0:T(8,128)(2,1)}, u32[]{:S(2)}, u32[]{:S(2)}) %collective-permute-start.2) | collective-permute-done | bytes 1572896 | tf_op jit(solution)/shard_map/ppermute | solution.py:21
  103.4 65.8 %all-gather = f32[8,384,16]{1,2,0:T(8,128)S(1)} all-gather(f32[2,384,16]{1,2,0:T(8,128)S(1)} %pad_maximum_fusion.11), channel_id=2, replica_groups=mesh['seq'=4,'fsdp'=8] {'seq'}, dimensions={0}, use_global_device_ids=true | all-gather | bytes 245760 | tf_op jit(solution)/shard_map/all_gather | solution.py:431
  210.6 16.1 convolution_convert_fusion.2.refs_0_
  226.7 25.3 %attend_forward.1 = bf16[1536,512]{1,0:T(8,128)(2,1)} custom-call(bf16[1536,1536]{1,0:T(8,128)(2,1)} %convolution_convert_fusion.2.refs_0_, s32[1536,1]{1,0:T(8,128)} %reshape.409.refs_1_.refs_2_, s32[1,1536]{1,0:T(1,128)} %reshape.360.refs_2_.refs_3_), custom_call_target="tpu_custom_call" | custom-call | flops 24159191040 | bytes 9437184 | tf_op jit(solution)/shard_map/attend_forward/pallas_call | solution.py:97
  287.8 51.9 %collective-permute-done.11.refs_10_ = bf16[1,256,3072]{2,1,0:T(8,128)(2,1)} collective-permute-done((bf16[1,256,3072]{2,1,0:T(8,128)(2,1)}, bf16[1,256,3072]{2,1,0:T(8,128)(2,1)}, u32[]{:S(2)}, u32[]{:S(2)}) %collective-permute-start.11) | collective-permute-done | bytes 1572896 | tf_op jit(solution)/shard_map/ppermute | solution.py:21
  355.0 68.2 %collective-permute-done.14 = bf16[384,2048]{1,0:T(8,128)(2,1)} collective-permute-done((bf16[384,2048]{1,0:T(8,128)(2,1)S(1)}, bf16[384,2048]{1,0:T(8,128)(2,1)}, u32[]{:S(2)}, u32[]{:S(2)}) %collective-permute-start.14) | collective-permute-done | bytes 1572896 | tf_op jit(solution)/shard_map/ppermute | solution.py:21
  428.5 66.1 %collective-permute-done.13.refs_12_ = bf16[1,256,3072]{2,1,0:T(8,128)(2,1)} collective-permute-done((bf16[1,256,3072]{2,1,0:T(8,128)(2,1)}, bf16[1,256,3072]{2,1,0:T(8,128)(2,1)}, u32[]{:S(2)}, u32[]{:S(2)}) %collective-permute-start.13) | collective-permute-done | bytes 1572896 | tf_op jit(solution)/shard_map/ppermute | solution.py:21
  494.9 33.0 %collective-permute-done.16.refs_11_ = bf16[1,256,3072]{2,1,0:T(8,128)(2,1)} collective-permute-done((bf16[1,256,3072]{2,1,0:T(8,128)(2,1)}, bf16[1,256,3072]{2,1,0:T(8,128)(2,1)}, u32[]{:S(2)}, u32[]{:S(2)}) %collective-permute-start.16) | collective-permute-done | bytes 1572896 | tf_op jit(solution)/shard_map/ppermute | solution.py:21
  556.6 61.5 %expert.4 = (bf16[544,2048]{1,0:T(8,128)(2,1)}, bf16[544,2048]{1,0:T(8,128)(2,1)}, bf16[544,2048]{1,0:T(8,128)(2,1)}, bf16[544,2048]{1,0:T(8,128)(2,1)}, bf16[4,...) custom-call(s32[1]{0:T(128)} %bitcast.23.refs_0_, f32[1088,1]{1,0:T(8,128)} %reshape_squeeze.16.refs_1_, ...), custom_call_target="tpu_custom_call" | custom-call | flops 41070624768 | bytes 42991616 | tf_op jit(solution)/shard_map/expert/pallas_call | solution.py:320
  631.4 56.4 %collective-permute-done.21.refs_11_ = bf16[1,256,3072]{2,1,0:T(8,128)(2,1)} collective-permute-done((bf16[1,256,3072]{2,1,0:T(8,128)(2,1)}, bf16[1,256,3072]{2,1,0:T(8,128)(2,1)}, u32[]{:S(2)}, u32[]{:S(2)}) %collective-permute-start.21) | collective-permute-done | bytes 1572896 | tf_op jit(solution)/shard_map/ppermute | solution.py:21
  706.7 62.6 %expert.5 = (bf16[544,2048]{1,0:T(8,128)(2,1)}, bf16[544,2048]{1,0:T(8,128)(2,1)}, bf16[544,2048]{1,0:T(8,128)(2,1)}, bf16[544,2048]{1,0:T(8,128)(2,1)}, bf16[4,...) custom-call(s32[1]{0:T(128)} %bitcast.23.refs_0_, f32[1088,1]{1,0:T(8,128)} %reshape_squeeze.17.refs_1_, ...), custom_call_target="tpu_custom_call" | custom-call | flops 41070624768 | bytes 42991616 | tf_op jit(solution)/shard_map/expert/pallas_call | solution.py:320
  811.3 63.9 %expert.6 = (bf16[544,2048]{1,0:T(8,128)(2,1)}, bf16[544,2048]{1,0:T(8,128)(2,1)}, bf16[544,2048]{1,0:T(8,128)(2,1)}, bf16[544,2048]{1,0:T(8,128)(2,1)}, bf16[4,...) custom-call(s32[1]{0:T(128)} %bitcast.23.refs_0_, f32[1088,1]{1,0:T(8,128)} %reshape_squeeze.18.refs_1_, ...), custom_call_target="tpu_custom_call" | custom-call | flops 41070624768 | bytes 42991616 | tf_op jit(solution)/shard_map/expert/pallas_call | solution.py:320
  909.5 61.1 %expert.7 = (bf16[544,2048]{1,0:T(8,128)(2,1)}, bf16[544,2048]{1,0:T(8,128)(2,1)}, bf16[544,2048]{1,0:T(8,128)(2,1)}, bf16[544,2048]{1,0:T(8,128)(2,1)}, bf16[4,...) custom-call(s32[1]{0:T(128)} %bitcast.23.refs_0_, f32[1088,1]{1,0:T(8,128)} %reshape_squeeze.19.refs_1_, ...), custom_call_target="tpu_custom_call" | custom-call | flops 41070624768 | bytes 42991616 | tf_op jit(solution)/shard_map/expert/pallas_call | solution.py:320
  994.6 57.5 %reduce-scatter.7.cloned.1.call-done = bf16[384,2048]{1,0:T(8,128)(2,1)} async-done(((bf16[1536,2048]{1,0:T(8,128)(2,1)}), bf16[384,2048]{1,0:T(8,128)(2,1)}) %reduce-scatter.7.cloned.1.call-update) | async-done | bytes 1572880 | tf_op jit(solution)/shard_map/reduce_scatter | solution.py:544
  1088.1 10.1 convolution_convert_fusion.3
  1098.2 31.1 %collective-permute-done.35 = bf16[1,256,3072]{2,1,0:T(8,128)(2,1)} collective-permute-done((bf16[1,256,3072]{2,1,0:T(8,128)(2,1)}, bf16[1,256,3072]{2,1,0:T(8,128)(2,1)}, u32[]{:S(2)}, u32[]{:S(2)}) %collective-permute-start.35) | collective-permute-done | bytes 1572896 | tf_op jit(solution)/shard_map/ppermute | solution.py:21
  1129.3 71.9 %collective-permute-done.36 = bf16[2,256,3072]{2,1,0:T(8,128)(2,1)} collective-permute-done((bf16[2,256,3072]{2,1,0:T(8,128)(2,1)}, bf16[2,256,3072]{2,1,0:T(8,128)(2,1)}, u32[]{:S(2)}, u32[]{:S(2)}) %collective-permute-start.36) | collective-permute-done | bytes 3145760 | tf_op jit(solution)/shard_map/ppermute | solution.py:21
  1223.1 33.6 %all-to-all-done.1 = bf16[384,4,512]{2,0,1:T(8,128)(2,1)} async-done(((bf16[384,4,512]{2,0,1:T(8,128)(2,1)}), bf16[384,4,512]{2,0,1:T(8,128)(2,1)}, u32[]{:S(2)}, u32[]{:S(2)}) %all-to-all-start.1) | async-done | bytes 1572896 | tf_op jit(solution)/shard_map/all_to_all | solution.py:569
  1256.6 51.2 %attend_backward.1 = bf16[1536,1536]{1,0:T(8,128)(2,1)} custom-call(bf16[1536,1536]{1,0:T(8,128)(2,1)} %convolution_convert_fusion.2.refs_0_, bf16[1536,512]{1,0:T(8,128)(2,1)} %bitcast.82.refs_1_, s32[1536,1]{1,0:T(8,128)} %reshape.409.refs_1_.refs_2_, s32[1,1536]{1,0:T(1,128)} %reshape.360.refs_2_.refs_3_), custom_call_target="tpu_custom_call" | custom-call | flops 48318382080 | bytes 9437184 | tf_op jit(solution)/shard_map/attend_backward/pallas_call | solution.py:97
  1307.8 16.2 collective-permute-done.40
  1324.0 17.2 convolution_convert_fusion.1
  1341.2 32.0 %reduce-scatter.11.cloned.1.call-done = bf16[384,2048]{1,0:T(8,128)(2,1)} async-done(((bf16[1536,2048]{1,0:T(8,128)(2,1)}), bf16[384,2048]{1,0:T(8,128)(2,1)}) %reduce-scatter.11.cloned.1.call-update) | async-done | bytes 1572880 | tf_op jit(solution)/shard_map/reduce_scatter | solution.py:544
  1391.3 11.6 convolution_convert_fusion
  1405.3 97.4 %collective-permute-done.38 = bf16[384,2048]{1,0:T(8,128)(2,1)} collective-permute-done((bf16[384,2048]{1,0:T(8,128)(2,1)S(1)}, bf16[384,2048]{1,0:T(8,128)(2,1)}, u32[]{:S(2)}, u32[]{:S(2)}) %collective-permute-start.38) | collective-permute-done | bytes 1572896 | tf_op jit(solution)/shard_map/ppermute | solution.py:21
  1518.7 10.4 collective-permute-start.47
  1531.0 26.0 %collective-permute-done.44 = bf16[384,2048]{1,0:T(8,128)(2,1)S(1)} collective-permute-done((bf16[384,2048]{1,0:T(8,128)(2,1)S(1)}, bf16[384,2048]{1,0:T(8,128)(2,1)S(1)}, u32[]{:S(2)}, u32[]{:S(2)}) %collective-permute-start.44) | collective-permute-done | bytes 1572896 | tf_op jit(solution)/shard_map/ppermute | solution.py:21
  1557.0 46.7 %collective-permute-done.46 = bf16[384,2048]{1,0:T(8,128)(2,1)S(1)} collective-permute-done((bf16[384,2048]{1,0:T(8,128)(2,1)S(1)}, bf16[384,2048]{1,0:T(8,128)(2,1)S(1)}, u32[]{:S(2)}, u32[]{:S(2)}) %collective-permute-start.46) | collective-permute-done | bytes 1572896 | tf_op jit(solution)/shard_map/ppermute | solution.py:21
  1606.8 24.9 %collective-permute-done.47 = bf16[1,256,3072]{2,1,0:T(8,128)(2,1)S(1)} collective-permute-done((bf16[1,256,3072]{2,1,0:T(8,128)(2,1)S(1)}, bf16[1,256,3072]{2,1,0:T(8,128)(2,1)S(1)}, u32[]{:S(2)}, u32[]{:S(2)}) %collective-permute-start.47) | collective-permute-done | bytes 1572896 | tf_op jit(solution)/shard_map/ppermute | solution.py:21
  1632.8 29.7 %collective-permute-done.48 = bf16[1,256,3072]{2,1,0:T(8,128)(2,1)} collective-permute-done((bf16[1,256,3072]{2,1,0:T(8,128)(2,1)S(1)}, bf16[1,256,3072]{2,1,0:T(8,128)(2,1)}, u32[]{:S(2)}, u32[]{:S(2)}) %collective-permute-start.48) | collective-permute-done | bytes 1572896 | tf_op jit(solution)/shard_map/ppermute | solution.py:21
  1681.2 25.4 %reduce-scatter.17.cloned.1.call-done = bf16[256,640]{1,0:T(8,128)(2,1)} async-done(((bf16[2048,640]{1,0:T(8,128)(2,1)}), bf16[256,640]{1,0:T(8,128)(2,1)}) %reduce-scatter.17.cloned.1.call-update) | async-done | bytes 327696 | tf_op jit(solution)/shard_map/reduce_scatter | solution.py:598
  1710.4 14.8 finish.1
  (433 shorter events, 452.9 us)
Async XLA Ops:
  7.2 202.5 %all-gather.16.cloned.1.call-start = ((), (), s32[]{:S(2)}) async-start(), calls=%async_computation.8 | async-start | bytes 7667712 | tf_op jit(solution)/shard_map/all_gather | solution.py:422
  22.6 317.1 %all-gather.18.cloned.1.call-start = ((), (), s32[]{:S(2)}) async-start(), calls=%async_computation.9 | async-start | bytes 9437184 | tf_op jit(solution)/shard_map/all_gather | solution.py:455
  30.4 147.4 %collective-permute-start.7 = (bf16[384,2048]{1,0:T(8,128)(2,1)S(1)}, bf16[384,2048]{1,0:T(8,128)(2,1)}, u32[]{:S(2)}, u32[]{:S(2)}) collective-permute-start(bf16[384,2048]{1,0:T(8,128)(2,1)S(1)} %bitcast.221), channel_id=1, source_target_pairs={{0,4},{1,5},{2,6},{3,7},{4,0},{5,1},{6,2},{7,3},{8,12},{9,13},{10,... | collective-permute-start | bytes 4718600 | tf_op jit(solution)/shard_map/ppermute | solution.py:21
  262.1 161.1 %all-gather.28.cloned.1.call-start = ((), (), s32[]{:S(2)}) async-start(), calls=%async_computation.20 | async-start | bytes 7864320 | tf_op jit(solution)/shard_map/all_gather | solution.py:469
  348.9 145.7 %all-gather.20.cloned.1.call-start = ((), (), s32[]{:S(2)}) async-start(), calls=%async_computation.10 | async-start | bytes 9437184 | tf_op jit(solution)/shard_map/all_gather | solution.py:198
  352.7 175.2 %all-gather.30.cloned.1.call-start = ((), (), s32[]{:S(2)}) async-start(), calls=%async_computation.21 | async-start | bytes 7864320 | tf_op jit(solution)/shard_map/all_gather | solution.py:471
  423.2 264.6 %all-gather.22.cloned.1.call-start = ((), (), s32[]{:S(2)}) async-start(), calls=%async_computation.11 | async-start | bytes 9437184 | tf_op jit(solution)/shard_map/all_gather | solution.py:198
  423.3 133.3 %collective-permute-start.17 = (bf16[4,256,3072]{2,1,0:T(8,128)(2,1)}, bf16[4,256,3072]{2,1,0:T(8,128)(2,1)}, u32[]{:S(2)}, u32[]{:S(2)}) collective-permute-start(bf16[4,256,3072]{2,1,0:T(8,128)(2,1)} %get-tuple-element.161.refs_6_), channel_id=1, source_target_pairs={{0,1},{1,0},{2,3},{3,2},{4,5},{5,4},{6,7},{7,6},{8,9},{9,8},{10,11... | collective-permute-start | bytes 18874376 | tf_op jit(solution)/shard_map/ppermute | solution.py:21
  426.5 101.4 %collective-permute-start.16 = (bf16[1,256,3072]{2,1,0:T(8,128)(2,1)}, bf16[1,256,3072]{2,1,0:T(8,128)(2,1)}, u32[]{:S(2)}, u32[]{:S(2)}) collective-permute-start(bf16[1,256,3072]{2,1,0:T(8,128)(2,1)} %get-tuple-element.158), channel_id=1, source_target_pairs={{0,2},{1,3},{2,0},{3,1},{4,6},{5,7},{6,4},{7,5},{8,10},{9,11},{10,... | collective-permute-start | bytes 4718600 | tf_op jit(solution)/shard_map/ppermute | solution.py:21
  537.2 258.9 %all-gather.24.cloned.1.call-start = ((), (), s32[]{:S(2)}) async-start(), calls=%async_computation.12 | async-start | bytes 9437184 | tf_op jit(solution)/shard_map/all_gather | solution.py:198
  556.3 131.6 %collective-permute-start.21 = (bf16[1,256,3072]{2,1,0:T(8,128)(2,1)}, bf16[1,256,3072]{2,1,0:T(8,128)(2,1)}, u32[]{:S(2)}, u32[]{:S(2)}) collective-permute-start(bf16[1,256,3072]{2,1,0:T(8,128)(2,1)} %get-tuple-element.168), channel_id=1, source_target_pairs={{0,2},{1,3},{2,0},{3,1},{4,6},{5,7},{6,4},{7,5},{8,10},{9,11},{10,... | collective-permute-start | bytes 4718600 | tf_op jit(solution)/shard_map/ppermute | solution.py:21
  618.1 151.3 %collective-permute-start.26 = (bf16[4,256,3072]{2,1,0:T(8,128)(2,1)}, bf16[4,256,3072]{2,1,0:T(8,128)(2,1)}, u32[]{:S(2)}, u32[]{:S(2)}) collective-permute-start(bf16[4,256,3072]{2,1,0:T(8,128)(2,1)} %get-tuple-element.181), channel_id=1, source_target_pairs={{0,1},{1,0},{2,3},{3,2},{4,5},{5,4},{6,7},{7,6},{8,9},{9,8},{10,11... | collective-permute-start | bytes 18874376 | tf_op jit(solution)/shard_map/ppermute | solution.py:21
  623.9 172.2 %collective-permute-start.24 = (bf16[1,256,3072]{2,1,0:T(8,128)(2,1)}, bf16[1,256,3072]{2,1,0:T(8,128)(2,1)}, u32[]{:S(2)}, u32[]{:S(2)}) collective-permute-start(bf16[1,256,3072]{2,1,0:T(8,128)(2,1)} %get-tuple-element.179), channel_id=1, source_target_pairs={{0,4},{1,5},{2,6},{3,7},{4,0},{5,1},{6,2},{7,3},{8,12},{9,13},{10,... | collective-permute-start | bytes 4718600 | tf_op jit(solution)/shard_map/ppermute | solution.py:21
  631.1 164.9 %collective-permute-start.25 = (bf16[1,256,3072]{2,1,0:T(8,128)(2,1)}, bf16[1,256,3072]{2,1,0:T(8,128)(2,1)}, u32[]{:S(2)}, u32[]{:S(2)}) collective-permute-start(bf16[1,256,3072]{2,1,0:T(8,128)(2,1)} %get-tuple-element.180), channel_id=1, source_target_pairs={{0,2},{1,3},{2,0},{3,1},{4,6},{5,7},{6,4},{7,5},{8,10},{9,11},{10,... | collective-permute-start | bytes 4718600 | tf_op jit(solution)/shard_map/ppermute | solution.py:21
  697.2 201.3 %all-gather.26.cloned.1.call-start = ((), (), s32[]{:S(2)}) async-start(), calls=%async_computation.13 | async-start | bytes 9437184 | tf_op jit(solution)/shard_map/all_gather | solution.py:198
  769.3 106.0 %collective-permute-start.30 = (bf16[4,256,3072]{2,1,0:T(8,128)(2,1)}, bf16[4,256,3072]{2,1,0:T(8,128)(2,1)}, u32[]{:S(2)}, u32[]{:S(2)}) collective-permute-start(bf16[4,256,3072]{2,1,0:T(8,128)(2,1)} %get-tuple-element.196), channel_id=1, source_target_pairs={{0,1},{1,0},{2,3},{3,2},{4,5},{5,4},{6,7},{7,6},{8,9},{9,8},{10,11... | collective-permute-start | bytes 18874376 | tf_op jit(solution)/shard_map/ppermute | solution.py:21
  805.8 246.3 %reduce-scatter.7.cloned.1.call-start = ((), (), s32[]{:S(2)}) async-start(), calls=%async_computation.14 | async-start | bytes 7864320 | tf_op jit(solution)/shard_map/reduce_scatter | solution.py:544
  981.8 219.3 %reduce-scatter.9.cloned.1.call-start = ((), (), s32[]{:S(2)}) async-start(), calls=%async_computation.15 | async-start | bytes 7864320 | tf_op jit(solution)/shard_map/reduce_scatter | solution.py:544
  1052.2 271.9 %reduce-scatter.13.cloned.1.call-start = ((), (), s32[]{:S(2)}) async-start(), calls=%async_computation.17 | async-start | bytes 7864320 | tf_op jit(solution)/shard_map/reduce_scatter | solution.py:544
  1064.6 136.6 %collective-permute-start.36 = (bf16[2,256,3072]{2,1,0:T(8,128)(2,1)}, bf16[2,256,3072]{2,1,0:T(8,128)(2,1)}, u32[]{:S(2)}, u32[]{:S(2)}) collective-permute-start(bf16[2,256,3072]{2,1,0:T(8,128)(2,1)} %add_convert_fusion.1), channel_id=1, source_target_pairs={{0,2},{1,3},{2,0},{3,1},{4,6},{5,7},{6,4},{7,5},{8,10},{9,11},{10,... | collective-permute-start | bytes 9437192 | tf_op jit(solution)/shard_map/ppermute | solution.py:21
  1084.4 116.8 %collective-permute-start.37 = (bf16[384,2048]{1,0:T(8,128)(2,1)}, bf16[384,2048]{1,0:T(8,128)(2,1)}, u32[]{:S(2)}, u32[]{:S(2)}) collective-permute-start(bf16[384,2048]{1,0:T(8,128)(2,1)} %reduce-scatter.7.cloned.1.call-done), channel_id=1, source_target_pairs={{0,4},{1,5},{2,6},{3,7},{4,0},{5,1},{6,2},{7,3},{8,12},{9,13},{10,... | collective-permute-start | bytes 4718600 | tf_op jit(solution)/shard_map/ppermute | solution.py:21
  1213.6 159.6 %reduce-scatter.11.cloned.1.call-start = ((), (), s32[]{:S(2)}) async-start(), calls=%async_computation.16 | async-start | bytes 7864320 | tf_op jit(solution)/shard_map/reduce_scatter | solution.py:544
  1219.8 282.9 %reduce-scatter.15.cloned.1.call-start = ((), (), s32[]{:S(2)}) async-start(), calls=%async_computation.18 | async-start | bytes 7077888 | tf_op jit(solution)/shard_map/reduce_scatter | solution.py:586
  1220.6 103.4 %collective-permute-start.40 = (bf16[2,256,3072]{2,1,0:T(8,128)(2,1)}, bf16[2,256,3072]{2,1,0:T(8,128)(2,1)S(1)}, u32[]{:S(2)}, u32[]{:S(2)}) collective-permute-start(bf16[2,256,3072]{2,1,0:T(8,128)(2,1)} %add_convert_fusion), channel_id=1, source_target_pairs={{0,2},{1,3},{2,0},{3,1},{4,6},{5,7},{6,4},{7,5},{8,10},{9,11},{10,... | collective-permute-start | bytes 9437192 | tf_op jit(solution)/shard_map/ppermute | solution.py:21
  1373.3 289.2 %all-gather.32.cloned.1.call-start = ((), (), s32[]{:S(2)}) async-start(), calls=%async_computation.22 | async-start | bytes 3932160 | tf_op jit(solution)/shard_map/all_gather | solution.py:593
  1385.4 125.8 %collective-permute-start.42 = (bf16[2048,512]{1,0:T(8,128)(2,1)}, bf16[2048,512]{1,0:T(8,128)(2,1)}, u32[]{:S(2)}, u32[]{:S(2)}) collective-permute-start(bf16[2048,512]{1,0:T(8,128)(2,1)} %convolution_convert_fusion.16), channel_id=1, source_target_pairs={{0,16},{8,24},{16,0},{24,8},{1,17},{9,25},{17,1},{25,9},{2,18},{10... | collective-permute-start | bytes 6291464 | tf_op jit(solution)/shard_map/ppermute | solution.py:21
  1386.6 124.6 %collective-permute-start.41 = (bf16[2048,512]{1,0:T(8,128)(2,1)}, bf16[2048,512]{1,0:T(8,128)(2,1)}, u32[]{:S(2)}, u32[]{:S(2)}) collective-permute-start(bf16[2048,512]{1,0:T(8,128)(2,1)} %convolution_convert_fusion.17), channel_id=1, source_target_pairs={{0,8},{8,0},{16,24},{24,16},{1,9},{9,1},{17,25},{25,17},{2,10},{10... | collective-permute-start | bytes 6291464 | tf_op jit(solution)/shard_map/ppermute | solution.py:21
  1387.4 123.8 %collective-permute-start.43 = (bf16[2048,512]{1,0:T(8,128)(2,1)}, bf16[2048,512]{1,0:T(8,128)(2,1)}, u32[]{:S(2)}, u32[]{:S(2)}) collective-permute-start(bf16[2048,512]{1,0:T(8,128)(2,1)} %convolution_convert_fusion.15), channel_id=1, source_target_pairs={{0,24},{8,16},{16,8},{24,0},{1,25},{9,17},{17,9},{25,1},{2,26},{10... | collective-permute-start | bytes 6291464 | tf_op jit(solution)/shard_map/ppermute | solution.py:21
  1388.8 113.9 %collective-permute-start.38 = (bf16[384,2048]{1,0:T(8,128)(2,1)S(1)}, bf16[384,2048]{1,0:T(8,128)(2,1)}, u32[]{:S(2)}, u32[]{:S(2)}) collective-permute-start(bf16[384,2048]{1,0:T(8,128)(2,1)S(1)} %copy-done.57), channel_id=1, source_target_pairs={{0,4},{1,5},{2,6},{3,7},{4,0},{5,1},{6,2},{7,3},{8,12},{9,13},{10,... | collective-permute-start | bytes 4718600 | tf_op jit(solution)/shard_map/ppermute | solution.py:21
  1502.8 203.7 %reduce-scatter.17.cloned.1.call-start = ((), (), s32[]{:S(2)}) async-start(), calls=%async_computation.19 | async-start | bytes 2949120 | tf_op jit(solution)/shard_map/reduce_scatter | solution.py:598
  1518.7 113.0 %collective-permute-start.47 = (bf16[1,256,3072]{2,1,0:T(8,128)(2,1)S(1)}, bf16[1,256,3072]{2,1,0:T(8,128)(2,1)S(1)}, u32[]{:S(2)}, u32[]{:S(2)}) collective-permute-start(bf16[1,256,3072]{2,1,0:T(8,128)(2,1)S(1)} %get-tuple-element.268), channel_id=1, source_target_pairs={{0,4},{1,5},{2,6},{3,7},{4,0},{5,1},{6,2},{7,3},{8,12},{9,13},{10,... | collective-permute-start | bytes 4718600 | tf_op jit(solution)/shard_map/ppermute | solution.py:21
  1529.1 133.3 %collective-permute-start.48 = (bf16[1,256,3072]{2,1,0:T(8,128)(2,1)S(1)}, bf16[1,256,3072]{2,1,0:T(8,128)(2,1)}, u32[]{:S(2)}, u32[]{:S(2)}) collective-permute-start(bf16[1,256,3072]{2,1,0:T(8,128)(2,1)S(1)} %copy-done.35), channel_id=1, source_target_pairs={{0,4},{1,5},{2,6},{3,7},{4,0},{5,1},{6,2},{7,3},{8,12},{9,13},{10,... | collective-permute-start | bytes 4718600 | tf_op jit(solution)/shard_map/ppermute | solution.py:21
  (114 other events, 4072.2 us)
Sparse Core Ops, SparseCore 0:
  22.7 128.8 all-gather.15
  190.8 126.8 all-gather.17
  349.0 68.6 all-gather.27
  419.1 19.0 all-gather.19
  439.9 70.2 all-gather.29
  537.4 16.8 all-gather.21
  697.3 16.5 all-gather.23
  805.9 16.8 all-gather.25
  982.0 70.1 reduce-scatter.6
  1055.0 70.1 reduce-scatter.8
  1213.7 85.8 reduce-scatter.12
  1303.1 70.1 reduce-scatter.10
  1376.1 125.6 reduce-scatter.14
  1503.5 107.5 all-gather.31
  1669.0 37.5 reduce-scatter.16
  1708.2 27.7 all-gather.33

commit v8 on v7

--- a/solution.py
+++ b/solution.py
@@ -504,6 +504,8 @@
         cots = [after(cot_all[g], *back) for g in range(2)]
         for chain in chains[max(i - 3, 0) : max(i - 1, 0)]:
             ready.append(chain.arrive())
+        if i == 0:
+            ready = [dispatch(i, g, cots[g], True) for g in range(2)]
         slots = [dispatch(i, g, after(moe_all[g], *ready), False) for g in range(2)]
         ready = [chain.add(back[0]) for chain in chains[max(i - 3, 0) : max(i - 1, 0)]]
         slots[1] = after(slots[1], *ready)
@@ -543,16 +545,19 @@
     def scatter(sums, *others):
         return lax.psum_scatter(after(sums, *others), "seq", scatter_dimension=0, tiled=True)
 
-    back_other = combine(backward_parts, 1, chains[-3].arrive())
+    back_other = combine(backward_parts, 1, *[chain.arrive() for chain in chains[:-2]])
     back_own = combine(backward_parts, 0, back_other)
     swapped_back = scatter(back_other)
-    grad_normed_m = scatter(back_own, swapped_back)
-    swapped_back = swap(swapped_back, "fsdp", n_fsdp // 2)
     ready = [chain.arrive() for chain in chains[-2:]]
     ready.extend(chain.add(back_own) for chain in chains[-3:])
+    ready.append(chains[-3].arrive())
+    grad_normed_m = scatter(back_own, swapped_back, *ready)
+    swapped_back = swap(swapped_back, "fsdp", n_fsdp // 2)
+    ready = [swapped_back, chains[-2].arrive()]
     made_other = combine(forward_parts, 1, back_own)
     made_own = combine(forward_parts, 0, made_other, *ready)
-    ready = [made_own, *[chain.arrive() for chain in (*chains[:-3], chains[-2])]]
+    mixed_other, mixed_own = scatter(made_other, grad_normed_m), scatter(made_own, grad_normed_m)
+    ready = [made_own]
     grad_normed_m = after(grad_normed_m, *ready).astype(f32) + swapped_back.astype(f32)
 
     scaled_m = grad_normed_m * gain_m
@@ -564,8 +569,6 @@
     grad_gain_m = jnp.sum(grad_normed_m * resid * inv_m, axis=0)
     grad_attn = grad_resid.astype(bf16)
     grad_heads_rows = dot(grad_attn, out_full, ((1,), (1,))).astype(bf16)
-    mixed_other = scatter(made_other, grad_heads_rows)
-    mixed_own = scatter(made_own, grad_heads_rows)
     grad_heads = lax.all_to_all(
         grad_heads_rows, "seq", split_axis=1, concat_axis=0, tiled=True
     )
@@ -576,22 +579,21 @@
         part = dot(heads_rows, columns, ((0,), (0,))).astype(bf16)
         out_sum.append(part)
     grad_qkv = attend(qkv, segment, grad_heads)
-    ready = [chain.arrive() for chain in (chains[-3], chains[-1])]
-    grad_qkv = after(grad_qkv, mixed_other, *ready)
-    mixed_other = swap(mixed_other, "fsdp", n_fsdp // 2)
+    ready = [chain.arrive() for chain in chains[-2:]]
+    grad_qkv = after(grad_qkv, mixed_own, *ready)
+    mixed_other = swap(after(mixed_other, grad_qkv), "fsdp", n_fsdp // 2)
     mixed = (resid + mixed_own.astype(f32) + mixed_other.astype(f32)).astype(bf16)
 
     grad_qkv_w = dot(normed_a, grad_qkv, ((0,), (0,))).astype(bf16)
-    reduced_qkv = after(grad_qkv_w, mixed_own)
-    reduced_qkv = lax.psum_scatter(reduced_qkv, "fsdp", scatter_dimension=0, tiled=True)
+    reduced_qkv = lax.psum_scatter(grad_qkv_w, "fsdp", scatter_dimension=0, tiled=True)
     part_normed_a = dot(after(grad_qkv, grad_qkv_w), qkv_own, ((1,), (1,)))
     part_sent = part_normed_a.astype(bf16)
     ready = [part_sent, chains[-1].add(grad_qkv_w)]
     out_sum = [swap(after(p, grad_qkv_w), "seq", k) if k else p for k, p in enumerate(out_sum)]
     grad_normed_a = scatter_rows(after(part_sent, *out_sum), "seq")
-    qkv_sum = after(reduced_qkv, mixed_other, *ready)
+    qkv_sum = after(reduced_qkv, mixed_other, *ready, *out_sum[1:])
     qkv_sum = lax.all_gather(qkv_sum, "seq", axis=0, tiled=False)
-    out_sum[0] = after(out_sum[0], qkv_sum, grad_normed_a, *[c.arrive() for c in chains[-2:]])
+    out_sum[0] = after(out_sum[0], qkv_sum, grad_normed_a, chains[-1].arrive())
     out_sum = sum(part.astype(f32) for part in out_sum).astype(bf16)
     gain_column = jnp.zeros((D, 128), bf16).at[:, 0].set(grad_gain_m.astype(bf16))
     out_sum = jnp.concatenate([out_sum, gain_column], axis=1)

time: 1760 us -> 1680 us (0.955)
  waiting for transfers between devices: 815 us -> 713 us
    reduce_scatter x4, waiting for transfers between devices: 89.6 us -> 2.69 us  [scatter(): lax.psum_scatter(after(sums, *others), 'seq', scatter_dimension=0, tiled=...]
    ppermute x49, waiting for transfers between devices: 660 us -> 641 us  [swap(): return lax.ppermute(value, axis, [(i, i ^ bit) for i in range(size)])]
  transfers between devices with their start and end apart: 67 -> 67, of which waited for: 23 -> 23; matrix products, arithmetic and copies ran while one was open for 21% -> 25% of each run, Pallas kernels for 20% -> 21%
where the time goes in v8:
time: 1680 us; the launch traced here: 1670 us
  waiting for transfers between devices  713 us (42%)
  Pallas kernels  352 us (21%)
  matrix products  186 us (11%)
  other arithmetic  135 us (8%)
  local copies, waits for them, and re-layouts  132 us (8%)
  starting transfers between devices  71.1 us (4%)
  blocking collectives  65.8 us (4%)
    ppermute x49, waiting for transfers between devices, swap(): return lax.ppermute(value, axis, [(i, i ^ bit) for i in range(size)])  641 us
    pallas_call x4, Pallas kernels, run_expert(): pl.pallas_call(lambda *refs: expert_kernel(size, tiles, parts, *refs), ou...  249 us
    dot_general x29, matrix products, dot(): return lax.dot_general(a, b, (contract, batch), preferred_element_type=f32)  186 us
    pallas_call x2, Pallas kernels, attend(): pl.pallas_call(lambda *refs: (attend_backward_kernel if backward else att...  76.2 us
    all_gather x1, blocking collectives, body(): lax.all_gather(routing, 'seq', axis=0, tiled=False)  65.8 us
    ppermute x49, starting transfers between devices, swap(): return lax.ppermute(value, axis, [(i, i ^ bit) for i in range(size)])  61.2 us
  transfers between devices with their start and end apart: 67, of which 23 were waited for; matrix products, arithmetic and copies ran while one was open for 25% of the time, Pallas kernels for 21%

profile of v8, /device:TPU:0, one launch (start us, length us, event | category | flops | bytes accessed | tf_op | source)
XLA Modules:
  0.0 1671.5 jit_solution(2038500788563826088)
XLA Ops:
  36.9 14.5 reshape.353
  51.4 9.3 fusion.3
  62.0 32.8 %collective-permute-done.2 = bf16[384,2048]{1,0:T(8,128)(2,1)} collective-permute-done((bf16[384,2048]{1,0:T(8,128)(2,1)S(1)}, bf16[384,2048]{1,0:T(8,128)(2,1)}, u32[]{:S(2)}, u32[]{:S(2)}) %collective-permute-start.2) | collective-permute-done | bytes 1572896 | tf_op jit(solution)/shard_map/ppermute | solution.py:21
  103.4 65.8 %all-gather = f32[8,384,16]{1,2,0:T(8,128)S(1)} all-gather(f32[2,384,16]{1,2,0:T(8,128)S(1)} %pad_maximum_fusion.11), channel_id=2, replica_groups=mesh['seq'=4,'fsdp'=8] {'seq'}, dimensions={0}, use_global_device_ids=true | all-gather | bytes 245760 | tf_op jit(solution)/shard_map/all_gather | solution.py:431
  210.6 16.1 convolution_convert_fusion.2.refs_0_
  226.7 25.3 %attend_forward.1 = bf16[1536,512]{1,0:T(8,128)(2,1)} custom-call(bf16[1536,1536]{1,0:T(8,128)(2,1)} %convolution_convert_fusion.2.refs_0_, s32[1536,1]{1,0:T(8,128)} %reshape.411.refs_1_.refs_2_, s32[1,1536]{1,0:T(1,128)} %reshape.362.refs_2_.refs_3_), custom_call_target="tpu_custom_call" | custom-call | flops 24159191040 | bytes 9437184 | tf_op jit(solution)/shard_map/attend_forward/pallas_call | solution.py:97
  287.8 51.9 %collective-permute-done.11.refs_10_ = bf16[1,256,3072]{2,1,0:T(8,128)(2,1)} collective-permute-done((bf16[1,256,3072]{2,1,0:T(8,128)(2,1)}, bf16[1,256,3072]{2,1,0:T(8,128)(2,1)}, u32[]{:S(2)}, u32[]{:S(2)}) %collective-permute-start.11) | collective-permute-done | bytes 1572896 | tf_op jit(solution)/shard_map/ppermute | solution.py:21
  349.9 68.3 %collective-permute-done.13 = bf16[384,2048]{1,0:T(8,128)(2,1)S(1)} collective-permute-done((bf16[384,2048]{1,0:T(8,128)(2,1)}, bf16[384,2048]{1,0:T(8,128)(2,1)S(1)}, u32[]{:S(2)}, u32[]{:S(2)}) %collective-permute-start.13) | collective-permute-done | bytes 1572896 | tf_op jit(solution)/shard_map/ppermute | solution.py:21
  439.9 53.9 %collective-permute-done.15.refs_12_ = bf16[1,256,3072]{2,1,0:T(8,128)(2,1)} collective-permute-done((bf16[1,256,3072]{2,1,0:T(8,128)(2,1)}, bf16[1,256,3072]{2,1,0:T(8,128)(2,1)}, u32[]{:S(2)}, u32[]{:S(2)}) %collective-permute-start.15) | collective-permute-done | bytes 1572896 | tf_op jit(solution)/shard_map/ppermute | solution.py:21
  499.3 28.8 %collective-permute-done.18.refs_11_ = bf16[1,256,3072]{2,1,0:T(8,128)(2,1)} collective-permute-done((bf16[1,256,3072]{2,1,0:T(8,128)(2,1)}, bf16[1,256,3072]{2,1,0:T(8,128)(2,1)}, u32[]{:S(2)}, u32[]{:S(2)}) %collective-permute-start.18) | collective-permute-done | bytes 1572896 | tf_op jit(solution)/shard_map/ppermute | solution.py:21
  542.4 62.2 %expert.4 = (bf16[544,2048]{1,0:T(8,128)(2,1)}, bf16[544,2048]{1,0:T(8,128)(2,1)}, bf16[544,2048]{1,0:T(8,128)(2,1)}, bf16[544,2048]{1,0:T(8,128)(2,1)}, bf16[4,...) custom-call(s32[1]{0:T(128)} %bitcast.23.refs_0_, f32[1088,1]{1,0:T(8,128)} %reshape_squeeze.16.refs_1_, ...), custom_call_target="tpu_custom_call" | custom-call | flops 41070624768 | bytes 42991616 | tf_op jit(solution)/shard_map/expert/pallas_call | solution.py:320
  618.7 54.3 %collective-permute-done.21.refs_11_ = bf16[1,256,3072]{2,1,0:T(8,128)(2,1)} collective-permute-done((bf16[1,256,3072]{2,1,0:T(8,128)(2,1)}, bf16[1,256,3072]{2,1,0:T(8,128)(2,1)}, u32[]{:S(2)}, u32[]{:S(2)}) %collective-permute-start.21) | collective-permute-done | bytes 1572896 | tf_op jit(solution)/shard_map/ppermute | solution.py:21
  691.8 62.5 %expert.5 = (bf16[544,2048]{1,0:T(8,128)(2,1)}, bf16[544,2048]{1,0:T(8,128)(2,1)}, bf16[544,2048]{1,0:T(8,128)(2,1)}, bf16[544,2048]{1,0:T(8,128)(2,1)}, bf16[4,...) custom-call(s32[1]{0:T(128)} %bitcast.23.refs_0_, f32[1088,1]{1,0:T(8,128)} %reshape_squeeze.17.refs_1_, ...), custom_call_target="tpu_custom_call" | custom-call | flops 41070624768 | bytes 42991616 | tf_op jit(solution)/shard_map/expert/pallas_call | solution.py:320
  797.4 63.4 %expert.6 = (bf16[544,2048]{1,0:T(8,128)(2,1)}, bf16[544,2048]{1,0:T(8,128)(2,1)}, bf16[544,2048]{1,0:T(8,128)(2,1)}, bf16[544,2048]{1,0:T(8,128)(2,1)}, bf16[4,...) custom-call(s32[1]{0:T(128)} %bitcast.23.refs_0_, f32[1088,1]{1,0:T(8,128)} %reshape_squeeze.18.refs_1_, ...), custom_call_target="tpu_custom_call" | custom-call | flops 41070624768 | bytes 42991616 | tf_op jit(solution)/shard_map/expert/pallas_call | solution.py:320
  895.9 61.1 %expert.7 = (bf16[544,2048]{1,0:T(8,128)(2,1)}, bf16[544,2048]{1,0:T(8,128)(2,1)}, bf16[544,2048]{1,0:T(8,128)(2,1)}, bf16[544,2048]{1,0:T(8,128)(2,1)}, bf16[4,...) custom-call(s32[1]{0:T(128)} %bitcast.23.refs_0_, f32[1088,1]{1,0:T(8,128)} %reshape_squeeze.19.refs_1_, ...), custom_call_target="tpu_custom_call" | custom-call | flops 41070624768 | bytes 42991616 | tf_op jit(solution)/shard_map/expert/pallas_call | solution.py:320
  960.9 12.0 collective-permute-done.32
  990.2 7.2 convolution_convert_fusion.5
  1014.2 58.5 %collective-permute-done.38 = bf16[1,256,3072]{2,1,0:T(8,128)(2,1)} collective-permute-done((bf16[1,256,3072]{2,1,0:T(8,128)(2,1)S(1)}, bf16[1,256,3072]{2,1,0:T(8,128)(2,1)}, u32[]{:S(2)}, u32[]{:S(2)}) %collective-permute-start.38) | collective-permute-done | bytes 1572896 | tf_op jit(solution)/shard_map/ppermute | solution.py:21
  1091.4 84.3 %collective-permute-done.36 = bf16[2,256,3072]{2,1,0:T(8,128)(2,1)} collective-permute-done((bf16[2,256,3072]{2,1,0:T(8,128)(2,1)S(1)}, bf16[2,256,3072]{2,1,0:T(8,128)(2,1)}, u32[]{:S(2)}, u32[]{:S(2)}) %collective-permute-start.36) | collective-permute-done | bytes 3145760 | tf_op jit(solution)/shard_map/ppermute | solution.py:21
  1175.8 9.5 convolution_convert_fusion.3
  1215.6 26.0 %all-to-all-done.1 = bf16[384,4,512]{2,0,1:T(8,128)(2,1)} async-done(((bf16[384,4,512]{2,0,1:T(8,128)(2,1)}), bf16[384,4,512]{2,0,1:T(8,128)(2,1)}, u32[]{:S(2)}, u32[]{:S(2)}) %all-to-all-start.1) | async-done | bytes 1572896 | tf_op jit(solution)/shard_map/all_to_all | solution.py:572
  1241.6 50.9 %attend_backward.1 = bf16[1536,1536]{1,0:T(8,128)(2,1)} custom-call(bf16[1536,1536]{1,0:T(8,128)(2,1)} %convolution_convert_fusion.2.refs_0_, bf16[1536,512]{1,0:T(8,128)(2,1)} %bitcast.81.refs_1_, s32[1536,1]{1,0:T(8,128)} %reshape.411.refs_1_.refs_2_, s32[1,1536]{1,0:T(1,128)} %reshape.362.refs_2_.refs_3_), custom_call_target="tpu_custom_call" | custom-call | flops 48318382080 | bytes 9437184 | tf_op jit(solution)/shard_map/attend_backward/pallas_call | solution.py:97
  1292.5 18.7 %collective-permute-done.40 = bf16[2,256,3072]{2,1,0:T(8,128)(2,1)} collective-permute-done((bf16[2,256,3072]{2,1,0:T(8,128)(2,1)}, bf16[2,256,3072]{2,1,0:T(8,128)(2,1)}, u32[]{:S(2)}, u32[]{:S(2)}) %collective-permute-start.40) | collective-permute-done | bytes 3145760 | tf_op jit(solution)/shard_map/ppermute | solution.py:21
  1311.2 15.8 convolution_convert_fusion.1
  1358.0 15.1 convolution_convert_fusion
  1373.1 89.7 %collective-permute-done.41 = bf16[384,2048]{1,0:T(8,128)(2,1)} collective-permute-done((bf16[384,2048]{1,0:T(8,128)(2,1)}, bf16[384,2048]{1,0:T(8,128)(2,1)}, u32[]{:S(2)}, u32[]{:S(2)}) %collective-permute-start.41) | collective-permute-done | bytes 1572896 | tf_op jit(solution)/shard_map/ppermute | solution.py:21
  1478.2 9.5 collective-permute-start.48
  1489.5 32.2 %collective-permute-done.45 = bf16[384,2048]{1,0:T(8,128)(2,1)S(1)} collective-permute-done((bf16[384,2048]{1,0:T(8,128)(2,1)S(1)}, bf16[384,2048]{1,0:T(8,128)(2,1)S(1)}, u32[]{:S(2)}, u32[]{:S(2)}) %collective-permute-start.45) | collective-permute-done | bytes 1572896 | tf_op jit(solution)/shard_map/ppermute | solution.py:21
  1521.7 47.1 %collective-permute-done.47 = bf16[384,2048]{1,0:T(8,128)(2,1)S(1)} collective-permute-done((bf16[384,2048]{1,0:T(8,128)(2,1)S(1)}, bf16[384,2048]{1,0:T(8,128)(2,1)S(1)}, u32[]{:S(2)}, u32[]{:S(2)}) %collective-permute-start.47) | collective-permute-done | bytes 1572896 | tf_op jit(solution)/shard_map/ppermute | solution.py:21
  1594.1 28.8 %reduce-scatter.17.cloned.1.call-done = bf16[256,640]{1,0:T(8,128)(2,1)} async-done(((bf16[2048,640]{1,0:T(8,128)(2,1)}), bf16[256,640]{1,0:T(8,128)(2,1)}) %reduce-scatter.17.cloned.1.call-update) | async-done | bytes 327696 | tf_op jit(solution)/shard_map/reduce_scatter | solution.py:600
  1626.7 14.8 finish.1
  1646.6 8.6 unpack.2
  (392 shorter events, 457.1 us)
Async XLA Ops:
  7.2 202.5 %all-gather.16.cloned.1.call-start = ((), (), s32[]{:S(2)}) async-start(), calls=%async_computation.8 | async-start | bytes 7667712 | tf_op jit(solution)/shard_map/all_gather | solution.py:422
  22.6 317.1 %all-gather.18.cloned.1.call-start = ((), (), s32[]{:S(2)}) async-start(), calls=%async_computation.9 | async-start | bytes 9437184 | tf_op jit(solution)/shard_map/all_gather | solution.py:455
  30.4 147.4 %collective-permute-start.7 = (bf16[384,2048]{1,0:T(8,128)(2,1)S(1)}, bf16[384,2048]{1,0:T(8,128)(2,1)}, u32[]{:S(2)}, u32[]{:S(2)}) collective-permute-start(bf16[384,2048]{1,0:T(8,128)(2,1)S(1)} %bitcast.214), channel_id=1, source_target_pairs={{0,4},{1,5},{2,6},{3,7},{4,0},{5,1},{6,2},{7,3},{8,12},{9,13},{10,... | collective-permute-start | bytes 4718600 | tf_op jit(solution)/shard_map/ppermute | solution.py:21
  262.2 156.0 %all-gather.28.cloned.1.call-start = ((), (), s32[]{:S(2)}) async-start(), calls=%async_computation.20 | async-start | bytes 7864320 | tf_op jit(solution)/shard_map/all_gather | solution.py:469
  348.9 144.9 %all-gather.30.cloned.1.call-start = ((), (), s32[]{:S(2)}) async-start(), calls=%async_computation.21 | async-start | bytes 7864320 | tf_op jit(solution)/shard_map/all_gather | solution.py:471
  419.4 123.0 %all-gather.20.cloned.1.call-start = ((), (), s32[]{:S(2)}) async-start(), calls=%async_computation.10 | async-start | bytes 9437184 | tf_op jit(solution)/shard_map/all_gather | solution.py:198
  423.2 249.8 %all-gather.22.cloned.1.call-start = ((), (), s32[]{:S(2)}) async-start(), calls=%async_computation.11 | async-start | bytes 9437184 | tf_op jit(solution)/shard_map/all_gather | solution.py:198
  423.5 118.9 %collective-permute-start.14 = (bf16[4,256,3072]{2,1,0:T(8,128)(2,1)}, bf16[4,256,3072]{2,1,0:T(8,128)(2,1)}, u32[]{:S(2)}, u32[]{:S(2)}) collective-permute-start(bf16[4,256,3072]{2,1,0:T(8,128)(2,1)} %get-tuple-element.158.refs_6_), channel_id=1, source_target_pairs={{0,1},{1,0},{2,3},{3,2},{4,5},{5,4},{6,7},{7,6},{8,9},{9,8},{10,11... | collective-permute-start | bytes 18874376 | tf_op jit(solution)/shard_map/ppermute | solution.py:21
  424.6 103.5 %collective-permute-start.17 = (bf16[1,256,3072]{2,1,0:T(8,128)(2,1)S(1)}, bf16[1,256,3072]{2,1,0:T(8,128)(2,1)}, u32[]{:S(2)}, u32[]{:S(2)}) collective-permute-start(bf16[1,256,3072]{2,1,0:T(8,128)(2,1)S(1)} %copy-done.30), channel_id=1, source_target_pairs={{0,4},{1,5},{2,6},{3,7},{4,0},{5,1},{6,2},{7,3},{8,12},{9,13},{10,... | collective-permute-start | bytes 4718600 | tf_op jit(solution)/shard_map/ppermute | solution.py:21
  427.7 100.4 %collective-permute-start.18 = (bf16[1,256,3072]{2,1,0:T(8,128)(2,1)}, bf16[1,256,3072]{2,1,0:T(8,128)(2,1)}, u32[]{:S(2)}, u32[]{:S(2)}) collective-permute-start(bf16[1,256,3072]{2,1,0:T(8,128)(2,1)} %get-tuple-element.163), channel_id=1, source_target_pairs={{0,2},{1,3},{2,0},{3,1},{4,6},{5,7},{6,4},{7,5},{8,10},{9,11},{10,... | collective-permute-start | bytes 4718600 | tf_op jit(solution)/shard_map/ppermute | solution.py:21
  532.0 249.1 %all-gather.24.cloned.1.call-start = ((), (), s32[]{:S(2)}) async-start(), calls=%async_computation.12 | async-start | bytes 9437184 | tf_op jit(solution)/shard_map/all_gather | solution.py:198
  542.1 130.9 %collective-permute-start.21 = (bf16[1,256,3072]{2,1,0:T(8,128)(2,1)}, bf16[1,256,3072]{2,1,0:T(8,128)(2,1)}, u32[]{:S(2)}, u32[]{:S(2)}) collective-permute-start(bf16[1,256,3072]{2,1,0:T(8,128)(2,1)} %get-tuple-element.168), channel_id=1, source_target_pairs={{0,2},{1,3},{2,0},{3,1},{4,6},{5,7},{6,4},{7,5},{8,10},{9,11},{10,... | collective-permute-start | bytes 4718600 | tf_op jit(solution)/shard_map/ppermute | solution.py:21
  604.6 149.8 %collective-permute-start.26 = (bf16[4,256,3072]{2,1,0:T(8,128)(2,1)}, bf16[4,256,3072]{2,1,0:T(8,128)(2,1)}, u32[]{:S(2)}, u32[]{:S(2)}) collective-permute-start(bf16[4,256,3072]{2,1,0:T(8,128)(2,1)} %get-tuple-element.181), channel_id=1, source_target_pairs={{0,1},{1,0},{2,3},{3,2},{4,5},{5,4},{6,7},{7,6},{8,9},{9,8},{10,11... | collective-permute-start | bytes 18874376 | tf_op jit(solution)/shard_map/ppermute | solution.py:21
  610.5 170.6 %collective-permute-start.24 = (bf16[1,256,3072]{2,1,0:T(8,128)(2,1)}, bf16[1,256,3072]{2,1,0:T(8,128)(2,1)}, u32[]{:S(2)}, u32[]{:S(2)}) collective-permute-start(bf16[1,256,3072]{2,1,0:T(8,128)(2,1)} %get-tuple-element.179), channel_id=1, source_target_pairs={{0,4},{1,5},{2,6},{3,7},{4,0},{5,1},{6,2},{7,3},{8,12},{9,13},{10,... | collective-permute-start | bytes 4718600 | tf_op jit(solution)/shard_map/ppermute | solution.py:21
  618.0 163.1 %collective-permute-start.25 = (bf16[1,256,3072]{2,1,0:T(8,128)(2,1)}, bf16[1,256,3072]{2,1,0:T(8,128)(2,1)}, u32[]{:S(2)}, u32[]{:S(2)}) collective-permute-start(bf16[1,256,3072]{2,1,0:T(8,128)(2,1)} %get-tuple-element.180), channel_id=1, source_target_pairs={{0,2},{1,3},{2,0},{3,1},{4,6},{5,7},{6,4},{7,5},{8,10},{9,11},{10,... | collective-permute-start | bytes 4718600 | tf_op jit(solution)/shard_map/ppermute | solution.py:21
  682.4 202.6 %all-gather.26.cloned.1.call-start = ((), (), s32[]{:S(2)}) async-start(), calls=%async_computation.13 | async-start | bytes 9437184 | tf_op jit(solution)/shard_map/all_gather | solution.py:198
  754.4 106.4 %collective-permute-start.30 = (bf16[4,256,3072]{2,1,0:T(8,128)(2,1)}, bf16[4,256,3072]{2,1,0:T(8,128)(2,1)}, u32[]{:S(2)}, u32[]{:S(2)}) collective-permute-start(bf16[4,256,3072]{2,1,0:T(8,128)(2,1)} %get-tuple-element.196), channel_id=1, source_target_pairs={{0,1},{1,0},{2,3},{3,2},{4,5},{5,4},{6,7},{7,6},{8,9},{9,8},{10,11... | collective-permute-start | bytes 18874376 | tf_op jit(solution)/shard_map/ppermute | solution.py:21
  767.8 100.6 %collective-permute-start.29 = (bf16[2,256,3072]{2,1,0:T(8,128)(2,1)}, bf16[2,256,3072]{2,1,0:T(8,128)(2,1)}, u32[]{:S(2)}, u32[]{:S(2)}) collective-permute-start(bf16[2,256,3072]{2,1,0:T(8,128)(2,1)} %add_convert_fusion.3), channel_id=1, source_target_pairs={{0,2},{1,3},{2,0},{3,1},{4,6},{5,7},{6,4},{7,5},{8,10},{9,11},{10,... | collective-permute-start | bytes 9437192 | tf_op jit(solution)/shard_map/ppermute | solution.py:21
  790.7 282.0 %reduce-scatter.7.cloned.1.call-start = ((), (), s32[]{:S(2)}) async-start(), calls=%async_computation.14 | async-start | bytes 7864320 | tf_op jit(solution)/shard_map/reduce_scatter | solution.py:546
  866.6 107.1 %collective-permute-start.33 = (bf16[2,256,3072]{2,1,0:T(8,128)(2,1)}, bf16[2,256,3072]{2,1,0:T(8,128)(2,1)}, u32[]{:S(2)}, u32[]{:S(2)}) collective-permute-start(bf16[2,256,3072]{2,1,0:T(8,128)(2,1)} %add_convert_fusion.2), channel_id=1, source_target_pairs={{0,2},{1,3},{2,0},{3,1},{4,6},{5,7},{6,4},{7,5},{8,10},{9,11},{10,... | collective-permute-start | bytes 9437192 | tf_op jit(solution)/shard_map/ppermute | solution.py:21
  980.8 204.5 %reduce-scatter.9.cloned.1.call-start = ((), (), s32[]{:S(2)}) async-start(), calls=%async_computation.15 | async-start | bytes 7864320 | tf_op jit(solution)/shard_map/reduce_scatter | solution.py:546
  1072.8 238.4 %reduce-scatter.11.cloned.1.call-start = ((), (), s32[]{:S(2)}) async-start(), calls=%async_computation.16 | async-start | bytes 7864320 | tf_op jit(solution)/shard_map/reduce_scatter | solution.py:546
  1072.8 103.0 %collective-permute-start.36 = (bf16[2,256,3072]{2,1,0:T(8,128)(2,1)S(1)}, bf16[2,256,3072]{2,1,0:T(8,128)(2,1)}, u32[]{:S(2)}, u32[]{:S(2)}) collective-permute-start(bf16[2,256,3072]{2,1,0:T(8,128)(2,1)S(1)} %add_convert_fusion.1), channel_id=1, source_target_pairs={{0,2},{1,3},{2,0},{3,1},{4,6},{5,7},{6,4},{7,5},{8,10},{9,11},{10,... | collective-permute-start | bytes 9437192 | tf_op jit(solution)/shard_map/ppermute | solution.py:21
  1185.4 160.0 %reduce-scatter.13.cloned.1.call-start = ((), (), s32[]{:S(2)}) async-start(), calls=%async_computation.17 | async-start | bytes 7864320 | tf_op jit(solution)/shard_map/reduce_scatter | solution.py:546
  1205.3 264.2 %reduce-scatter.15.cloned.1.call-start = ((), (), s32[]{:S(2)}) async-start(), calls=%async_computation.18 | async-start | bytes 7077888 | tf_op jit(solution)/shard_map/reduce_scatter | solution.py:588
  1210.0 101.2 %collective-permute-start.40 = (bf16[2,256,3072]{2,1,0:T(8,128)(2,1)}, bf16[2,256,3072]{2,1,0:T(8,128)(2,1)}, u32[]{:S(2)}, u32[]{:S(2)}) collective-permute-start(bf16[2,256,3072]{2,1,0:T(8,128)(2,1)} %add_convert_fusion), channel_id=1, source_target_pairs={{0,2},{1,3},{2,0},{3,1},{4,6},{5,7},{6,4},{7,5},{8,10},{9,11},{10,... | collective-permute-start | bytes 9437192 | tf_op jit(solution)/shard_map/ppermute | solution.py:21
  1327.0 247.1 %all-gather.32.cloned.1.call-start = ((), (), s32[]{:S(2)}) async-start(), calls=%async_computation.22 | async-start | bytes 3932160 | tf_op jit(solution)/shard_map/all_gather | solution.py:595
  1345.4 117.4 %collective-permute-start.41 = (bf16[384,2048]{1,0:T(8,128)(2,1)}, bf16[384,2048]{1,0:T(8,128)(2,1)}, u32[]{:S(2)}, u32[]{:S(2)}) collective-permute-start(bf16[384,2048]{1,0:T(8,128)(2,1)} %reduce-scatter.13.cloned.1.call-done), channel_id=1, source_target_pairs={{0,4},{1,5},{2,6},{3,7},{4,0},{5,1},{6,2},{7,3},{8,12},{9,13},{10,... | collective-permute-start | bytes 4718600 | tf_op jit(solution)/shard_map/ppermute | solution.py:21
  1347.9 115.0 %collective-permute-start.43 = (bf16[2048,512]{1,0:T(8,128)(2,1)}, bf16[2048,512]{1,0:T(8,128)(2,1)}, u32[]{:S(2)}, u32[]{:S(2)}) collective-permute-start(bf16[2048,512]{1,0:T(8,128)(2,1)} %convolution_convert_fusion.16), channel_id=1, source_target_pairs={{0,16},{8,24},{16,0},{24,8},{1,17},{9,25},{17,1},{25,9},{2,18},{10... | collective-permute-start | bytes 6291464 | tf_op jit(solution)/shard_map/ppermute | solution.py:21
  1349.1 113.7 %collective-permute-start.42 = (bf16[2048,512]{1,0:T(8,128)(2,1)}, bf16[2048,512]{1,0:T(8,128)(2,1)}, u32[]{:S(2)}, u32[]{:S(2)}) collective-permute-start(bf16[2048,512]{1,0:T(8,128)(2,1)} %convolution_convert_fusion.17), channel_id=1, source_target_pairs={{0,8},{8,0},{16,24},{24,16},{1,9},{9,1},{17,25},{25,17},{2,10},{10... | collective-permute-start | bytes 6291464 | tf_op jit(solution)/shard_map/ppermute | solution.py:21
  1349.9 113.0 %collective-permute-start.44 = (bf16[2048,512]{1,0:T(8,128)(2,1)}, bf16[2048,512]{1,0:T(8,128)(2,1)}, u32[]{:S(2)}, u32[]{:S(2)}) collective-permute-start(bf16[2048,512]{1,0:T(8,128)(2,1)} %convolution_convert_fusion.15), channel_id=1, source_target_pairs={{0,24},{8,16},{16,8},{24,0},{1,25},{9,17},{17,9},{25,1},{2,26},{10... | collective-permute-start | bytes 6291464 | tf_op jit(solution)/shard_map/ppermute | solution.py:21
  1469.5 153.4 %reduce-scatter.17.cloned.1.call-start = ((), (), s32[]{:S(2)}) async-start(), calls=%async_computation.19 | async-start | bytes 2949120 | tf_op jit(solution)/shard_map/reduce_scatter | solution.py:600
  (96 other events, 3470.6 us)
Sparse Core Ops, SparseCore 0:
  22.7 128.8 all-gather.15
  190.8 126.8 all-gather.17
  349.0 68.6 all-gather.27
  419.9 70.1 all-gather.29
  491.5 16.7 all-gather.19
  532.1 16.8 all-gather.21
  682.5 16.1 all-gather.23
  790.8 16.4 all-gather.25
  981.0 70.4 reduce-scatter.6
  1072.9 69.7 reduce-scatter.8
  1185.5 86.2 reduce-scatter.10
  1275.2 70.2 reduce-scatter.12
  1348.3 121.1 reduce-scatter.14
  1471.2 102.8 all-gather.31
  1580.6 42.2 reduce-scatter.16
  1624.6 27.9 all-gather.33

commit v9 on v8

--- a/solution.py
+++ b/solution.py
@@ -419,9 +419,8 @@
         w_qkv.reshape(shard, 3, HEADS, HEAD), at_seq * heads_here, heads_here, 2
     ).reshape(shard, 3 * width)
     gains = jnp.zeros((shard, 128), bf16).at[:, 0].set(gain_attn).at[:, 1].set(gain_moe)
-    gathered = lax.all_gather(
-        jnp.concatenate([part, gains], axis=1), "fsdp", axis=0, tiled=True
-    )
+    part = jnp.concatenate([part, gains], axis=1)
+    gathered = lax.all_gather(part, "fsdp", axis=0, tiled=True)
     qkv_own = gathered[:, : 3 * width]
     gain_a = gathered[:, 3 * width].astype(f32)
     gain_m = gathered[:, 3 * width + 1].astype(f32)
@@ -450,9 +449,9 @@
         return (values * inverse * gain).astype(bf16), inverse
 
     x_all = join_rows(
-        x_parts, "seq", own_part, other_part, picks, share, cot_own, cot_other
-    )
-    out_full = lax.all_gather(after(w_out, x_all), "fsdp", axis=0, tiled=True)
+        x_parts, "seq", own_part, other_part
+    )
+    out_full = lax.all_gather(after(w_out, part, *x_parts[1:]), "fsdp", axis=0, tiled=True)
     normed_a, _ = normed_rows(x_all.astype(f32), gain_a)
     qkv = dot(normed_a, qkv_own, ((1,), (0,))).astype(bf16)
     segment = segment_ids(lengths[0], span_len)
@@ -461,7 +460,7 @@
     cot_all = [cot_own, join_rows(send_rows(cot_other, "seq", cot_own), "seq")]
     cot_all = [rows_of.reshape(n_seq, rows, D) for rows_of in cot_all]
     begun = [start_expert(own_part[:1], other_part[:1], attended)]
-    heads_rows = after(heads_rows, *cot_all, *begun[0].values())
+    heads_rows = after(heads_rows, picks, share, *cot_all, *begun[0].values())
     experts = [finish_expert(begun[0], heads_rows)]
     x_float = tokens[0].astype(f32)
     resid = x_float + dot(heads_rows, out_full, ((1,), (0,)))
@@ -556,7 +555,7 @@
     ready = [swapped_back, chains[-2].arrive()]
     made_other = combine(forward_parts, 1, back_own)
     made_own = combine(forward_parts, 0, made_other, *ready)
-    mixed_other, mixed_own = scatter(made_other, grad_normed_m), scatter(made_own, grad_normed_m)
+    mixed_other = scatter(made_other, grad_normed_m, made_own)
     ready = [made_own]
     grad_normed_m = after(grad_normed_m, *ready).astype(f32) + swapped_back.astype(f32)
 
@@ -569,6 +568,7 @@
     grad_gain_m = jnp.sum(grad_normed_m * resid * inv_m, axis=0)
     grad_attn = grad_resid.astype(bf16)
     grad_heads_rows = dot(grad_attn, out_full, ((1,), (1,))).astype(bf16)
+    mixed_own = scatter(made_own, grad_heads_rows)
     grad_heads = lax.all_to_all(
         grad_heads_rows, "seq", split_axis=1, concat_axis=0, tiled=True
     )
@@ -580,20 +580,21 @@
         out_sum.append(part)
     grad_qkv = attend(qkv, segment, grad_heads)
     ready = [chain.arrive() for chain in chains[-2:]]
-    grad_qkv = after(grad_qkv, mixed_own, *ready)
+    grad_qkv = after(grad_qkv, mixed_other, *ready)
     mixed_other = swap(after(mixed_other, grad_qkv), "fsdp", n_fsdp // 2)
     mixed = (resid + mixed_own.astype(f32) + mixed_other.astype(f32)).astype(bf16)
 
     grad_qkv_w = dot(normed_a, grad_qkv, ((0,), (0,))).astype(bf16)
-    reduced_qkv = lax.psum_scatter(grad_qkv_w, "fsdp", scatter_dimension=0, tiled=True)
+    reduced_qkv = after(grad_qkv_w, mixed_own)
+    reduced_qkv = lax.psum_scatter(reduced_qkv, "fsdp", scatter_dimension=0, tiled=True)
     part_normed_a = dot(after(grad_qkv, grad_qkv_w), qkv_own, ((1,), (1,)))
     part_sent = part_normed_a.astype(bf16)
     ready = [part_sent, chains[-1].add(grad_qkv_w)]
     out_sum = [swap(after(p, grad_qkv_w), "seq", k) if k else p for k, p in enumerate(out_sum)]
-    grad_normed_a = scatter_rows(after(part_sent, *out_sum), "seq")
     qkv_sum = after(reduced_qkv, mixed_other, *ready, *out_sum[1:])
     qkv_sum = lax.all_gather(qkv_sum, "seq", axis=0, tiled=False)
-    out_sum[0] = after(out_sum[0], qkv_sum, grad_normed_a, chains[-1].arrive())
+    grad_normed_a = scatter_rows(after(part_sent, qkv_sum), "seq")
+    out_sum[0] = after(out_sum[0], qkv_sum, chains[-1].arrive())
     out_sum = sum(part.astype(f32) for part in out_sum).astype(bf16)
     gain_column = jnp.zeros((D, 128), bf16).at[:, 0].set(grad_gain_m.astype(bf16))
     out_sum = jnp.concatenate([out_sum, gain_column], axis=1)

time: 1680 us -> 1690 us (level)
  waiting for transfers between devices: 713 us -> 795 us
  blocking collectives: 65.8 us -> 9.22 us
    ppermute x49, waiting for transfers between devices: 641 us -> 735 us  [swap(): return lax.ppermute(value, axis, [(i, i ^ bit) for i in range(size)])]
    all_gather x1, blocking collectives: 65.8 us -> 9.22 us  [body(): lax.all_gather(routing, 'seq', axis=0, tiled=False)]
    reduce_scatter x1, waiting for transfers between devices: 28.8 us -> 0.01 us  [body(): out_sum = lax.psum_scatter(out_sum, 'fsdp', scatter_dimension=0, tiled=True)]
  transfers between devices with their start and end apart: 67 -> 67, of which waited for: 23 -> 27; matrix products, arithmetic and copies ran while one was open for 25% -> 23% of each run, Pallas kernels for 21% -> 21%
where the time goes in v9:
time: 1690 us; the launch traced here: 1680 us
  waiting for transfers between devices  795 us (47%)
  Pallas kernels  351 us (21%)
  matrix products  178 us (11%)
  other arithmetic  134 us (8%)
  local copies, waits for them, and re-layouts  126 us (7%)
  starting transfers between devices  75.1 us (4%)
    ppermute x49, waiting for transfers between devices, swap(): return lax.ppermute(value, axis, [(i, i ^ bit) for i in range(size)])  735 us
    pallas_call x4, Pallas kernels, run_expert(): pl.pallas_call(lambda *refs: expert_kernel(size, tiles, parts, *refs), ou...  248 us
    dot_general x29, matrix products, dot(): return lax.dot_general(a, b, (contract, batch), preferred_element_type=f32)  178 us
    pallas_call x2, Pallas kernels, attend(): pl.pallas_call(lambda *refs: (attend_backward_kernel if backward else att...  76.2 us
    ppermute x49, starting transfers between devices, swap(): return lax.ppermute(value, axis, [(i, i ^ bit) for i in range(size)])  65.1 us
  transfers between devices with their start and end apart: 67, of which 27 were waited for; matrix products, arithmetic and copies ran while one was open for 23% of the time, Pallas kernels for 21%

profile of v9, /device:TPU:0, one launch (start us, length us, event | category | flops | bytes accessed | tf_op | source)
XLA Modules:
  0.0 1684.0 jit_solution(4366883027869474380)
XLA Ops:
  27.3 34.6 %collective-permute-done.2 = bf16[384,2048]{1,0:T(8,128)(2,1)S(1)} collective-permute-done((bf16[384,2048]{1,0:T(8,128)(2,1)S(1)}, bf16[384,2048]{1,0:T(8,128)(2,1)S(1)}, u32[]{:S(2)}, u32[]{:S(2)}) %collective-permute-start.2) | collective-permute-done | bytes 1572896 | tf_op jit(solution)/shard_map/ppermute | solution.py:21
  61.9 32.8 %collective-permute-done.1 = bf16[384,2048]{1,0:T(8,128)(2,1)S(1)} collective-permute-done((bf16[384,2048]{1,0:T(8,128)(2,1)S(1)}, bf16[384,2048]{1,0:T(8,128)(2,1)S(1)}, u32[]{:S(2)}, u32[]{:S(2)}) %collective-permute-start.1) | collective-permute-done | bytes 1572896 | tf_op jit(solution)/shard_map/ppermute | solution.py:21
  105.6 14.6 reshape.353
  120.2 9.3 fusion.3
  169.4 24.2 %collective-permute-done.4 = bf16[384,2048]{1,0:T(8,128)(2,1)S(1)} collective-permute-done((bf16[384,2048]{1,0:T(8,128)(2,1)S(1)}, bf16[384,2048]{1,0:T(8,128)(2,1)S(1)}, u32[]{:S(2)}, u32[]{:S(2)}) %collective-permute-start.4) | collective-permute-done | bytes 1572896 | tf_op jit(solution)/shard_map/ppermute | solution.py:21
  195.0 31.4 %collective-permute-done.5 = bf16[384,2048]{1,0:T(8,128)(2,1)S(1)} collective-permute-done((bf16[384,2048]{1,0:T(8,128)(2,1)S(1)}, bf16[384,2048]{1,0:T(8,128)(2,1)S(1)}, u32[]{:S(2)}, u32[]{:S(2)}) %collective-permute-start.5) | collective-permute-done | bytes 1572896 | tf_op jit(solution)/shard_map/ppermute | solution.py:21
  241.5 15.7 convolution_convert_fusion.2.refs_0_
  257.2 25.2 %attend_forward.1 = bf16[1536,512]{1,0:T(8,128)(2,1)} custom-call(bf16[1536,1536]{1,0:T(8,128)(2,1)} %convolution_convert_fusion.2.refs_0_, s32[1536,1]{1,0:T(8,128)} %reshape.411.refs_1_.refs_2_, s32[1,1536]{1,0:T(1,128)} %reshape.361.refs_2_.refs_3_), custom_call_target="tpu_custom_call" | custom-call | flops 24159191040 | bytes 9437184 | tf_op jit(solution)/shard_map/attend_forward/pallas_call | solution.py:97
  299.6 9.8 collective-permute-done.8
  321.8 27.9 %collective-permute-done.11.refs_10_ = bf16[1,256,3072]{2,1,0:T(8,128)(2,1)} collective-permute-done((bf16[1,256,3072]{2,1,0:T(8,128)(2,1)}, bf16[1,256,3072]{2,1,0:T(8,128)(2,1)}, u32[]{:S(2)}, u32[]{:S(2)}) %collective-permute-start.11) | collective-permute-done | bytes 1572896 | tf_op jit(solution)/shard_map/ppermute | solution.py:21
  362.4 67.1 %collective-permute-done.13 = bf16[384,2048]{1,0:T(8,128)(2,1)S(1)} collective-permute-done((bf16[384,2048]{1,0:T(8,128)(2,1)}, bf16[384,2048]{1,0:T(8,128)(2,1)S(1)}, u32[]{:S(2)}, u32[]{:S(2)}) %collective-permute-start.13) | collective-permute-done | bytes 1572896 | tf_op jit(solution)/shard_map/ppermute | solution.py:21
  452.3 52.5 %collective-permute-done.15.refs_12_ = bf16[1,256,3072]{2,1,0:T(8,128)(2,1)} collective-permute-done((bf16[1,256,3072]{2,1,0:T(8,128)(2,1)}, bf16[1,256,3072]{2,1,0:T(8,128)(2,1)}, u32[]{:S(2)}, u32[]{:S(2)}) %collective-permute-start.15) | collective-permute-done | bytes 1572896 | tf_op jit(solution)/shard_map/ppermute | solution.py:21
  510.4 28.8 %collective-permute-done.18.refs_11_ = bf16[1,256,3072]{2,1,0:T(8,128)(2,1)} collective-permute-done((bf16[1,256,3072]{2,1,0:T(8,128)(2,1)}, bf16[1,256,3072]{2,1,0:T(8,128)(2,1)}, u32[]{:S(2)}, u32[]{:S(2)}) %collective-permute-start.18) | collective-permute-done | bytes 1572896 | tf_op jit(solution)/shard_map/ppermute | solution.py:21
  554.4 61.5 %expert.4 = (bf16[544,2048]{1,0:T(8,128)(2,1)}, bf16[544,2048]{1,0:T(8,128)(2,1)}, bf16[544,2048]{1,0:T(8,128)(2,1)}, bf16[544,2048]{1,0:T(8,128)(2,1)}, bf16[4,...) custom-call(s32[1]{0:T(128)} %bitcast.23.refs_0_, f32[1088,1]{1,0:T(8,128)} %reshape_squeeze.16.refs_1_, ...), custom_call_target="tpu_custom_call" | custom-call | flops 41070624768 | bytes 42991616 | tf_op jit(solution)/shard_map/expert/pallas_call | solution.py:320
  630.4 54.3 %collective-permute-done.21.refs_11_ = bf16[1,256,3072]{2,1,0:T(8,128)(2,1)} collective-permute-done((bf16[1,256,3072]{2,1,0:T(8,128)(2,1)}, bf16[1,256,3072]{2,1,0:T(8,128)(2,1)}, u32[]{:S(2)}, u32[]{:S(2)}) %collective-permute-start.21) | collective-permute-done | bytes 1572896 | tf_op jit(solution)/shard_map/ppermute | solution.py:21
  703.6 62.2 %expert.5 = (bf16[544,2048]{1,0:T(8,128)(2,1)}, bf16[544,2048]{1,0:T(8,128)(2,1)}, bf16[544,2048]{1,0:T(8,128)(2,1)}, bf16[544,2048]{1,0:T(8,128)(2,1)}, bf16[4,...) custom-call(s32[1]{0:T(128)} %bitcast.23.refs_0_, f32[1088,1]{1,0:T(8,128)} %reshape_squeeze.17.refs_1_, ...), custom_call_target="tpu_custom_call" | custom-call | flops 41070624768 | bytes 42991616 | tf_op jit(solution)/shard_map/expert/pallas_call | solution.py:320
  808.8 63.3 %expert.6 = (bf16[544,2048]{1,0:T(8,128)(2,1)}, bf16[544,2048]{1,0:T(8,128)(2,1)}, bf16[544,2048]{1,0:T(8,128)(2,1)}, bf16[544,2048]{1,0:T(8,128)(2,1)}, bf16[4,...) custom-call(s32[1]{0:T(128)} %bitcast.23.refs_0_, f32[1088,1]{1,0:T(8,128)} %reshape_squeeze.18.refs_1_, ...), custom_call_target="tpu_custom_call" | custom-call | flops 41070624768 | bytes 42991616 | tf_op jit(solution)/shard_map/expert/pallas_call | solution.py:320
  907.6 61.1 %expert.7 = (bf16[544,2048]{1,0:T(8,128)(2,1)}, bf16[544,2048]{1,0:T(8,128)(2,1)}, bf16[544,2048]{1,0:T(8,128)(2,1)}, bf16[544,2048]{1,0:T(8,128)(2,1)}, bf16[4,...) custom-call(s32[1]{0:T(128)} %bitcast.23.refs_0_, f32[1088,1]{1,0:T(8,128)} %reshape_squeeze.19.refs_1_, ...), custom_call_target="tpu_custom_call" | custom-call | flops 41070624768 | bytes 42991616 | tf_op jit(solution)/shard_map/expert/pallas_call | solution.py:320
  972.6 11.7 collective-permute-done.32
  1027.4 57.7 %collective-permute-done.38 = bf16[1,256,3072]{2,1,0:T(8,128)(2,1)} collective-permute-done((bf16[1,256,3072]{2,1,0:T(8,128)(2,1)S(1)}, bf16[1,256,3072]{2,1,0:T(8,128)(2,1)}, u32[]{:S(2)}, u32[]{:S(2)}) %collective-permute-start.38) | collective-permute-done | bytes 1572896 | tf_op jit(solution)/shard_map/ppermute | solution.py:21
  1104.3 83.3 %collective-permute-done.36 = bf16[2,256,3072]{2,1,0:T(8,128)(2,1)} collective-permute-done((bf16[2,256,3072]{2,1,0:T(8,128)(2,1)S(1)}, bf16[2,256,3072]{2,1,0:T(8,128)(2,1)}, u32[]{:S(2)}, u32[]{:S(2)}) %collective-permute-start.36) | collective-permute-done | bytes 3145760 | tf_op jit(solution)/shard_map/ppermute | solution.py:21
  1187.5 9.6 convolution_convert_fusion.3
  1228.4 25.6 %all-to-all-done.1 = bf16[384,4,512]{2,0,1:T(8,128)(2,1)} async-done(((bf16[384,4,512]{2,0,1:T(8,128)(2,1)}), bf16[384,4,512]{2,0,1:T(8,128)(2,1)}, u32[]{:S(2)}, u32[]{:S(2)}) %all-to-all-start.1) | async-done | bytes 1572896 | tf_op jit(solution)/shard_map/all_to_all | solution.py:572
  1254.1 51.0 %attend_backward.1 = bf16[1536,1536]{1,0:T(8,128)(2,1)} custom-call(bf16[1536,1536]{1,0:T(8,128)(2,1)} %convolution_convert_fusion.2.refs_0_, bf16[1536,512]{1,0:T(8,128)(2,1)} %bitcast.81.refs_1_, s32[1536,1]{1,0:T(8,128)} %reshape.411.refs_1_.refs_2_, s32[1,1536]{1,0:T(1,128)} %reshape.361.refs_2_.refs_3_), custom_call_target="tpu_custom_call" | custom-call | flops 48318382080 | bytes 9437184 | tf_op jit(solution)/shard_map/attend_backward/pallas_call | solution.py:97
  1305.0 19.1 %collective-permute-done.40 = bf16[2,256,3072]{2,1,0:T(8,128)(2,1)} collective-permute-done((bf16[2,256,3072]{2,1,0:T(8,128)(2,1)}, bf16[2,256,3072]{2,1,0:T(8,128)(2,1)}, u32[]{:S(2)}, u32[]{:S(2)}) %collective-permute-start.40) | collective-permute-done | bytes 3145760 | tf_op jit(solution)/shard_map/ppermute | solution.py:21
  1324.2 15.8 convolution_convert_fusion.1
  1340.0 17.3 %reduce-scatter.11.cloned.1.call-done = bf16[384,2048]{1,0:T(8,128)(2,1)} async-done(((bf16[1536,2048]{1,0:T(8,128)(2,1)}), bf16[384,2048]{1,0:T(8,128)(2,1)}) %reduce-scatter.11.cloned.1.call-update) | async-done | bytes 1572880 | tf_op jit(solution)/shard_map/reduce_scatter | solution.py:545
  1376.6 11.6 convolution_convert_fusion
  1388.2 95.7 %collective-permute-done.41 = bf16[384,2048]{1,0:T(8,128)(2,1)} collective-permute-done((bf16[384,2048]{1,0:T(8,128)(2,1)S(1)}, bf16[384,2048]{1,0:T(8,128)(2,1)}, u32[]{:S(2)}, u32[]{:S(2)}) %collective-permute-start.41) | collective-permute-done | bytes 1572896 | tf_op jit(solution)/shard_map/ppermute | solution.py:21
  1502.8 61.8 %collective-permute-done.48 = bf16[1,256,3072]{2,1,0:T(8,128)(2,1)} collective-permute-done((bf16[1,256,3072]{2,1,0:T(8,128)(2,1)}, bf16[1,256,3072]{2,1,0:T(8,128)(2,1)}, u32[]{:S(2)}, u32[]{:S(2)}) %collective-permute-start.48) | collective-permute-done | bytes 1572896 | tf_op jit(solution)/shard_map/ppermute | solution.py:21
  1591.4 14.9 finish.1
  1622.9 32.7 %collective-permute-done.47 = bf16[384,2048]{1,0:T(8,128)(2,1)} collective-permute-done((bf16[384,2048]{1,0:T(8,128)(2,1)}, bf16[384,2048]{1,0:T(8,128)(2,1)}, u32[]{:S(2)}, u32[]{:S(2)}) %collective-permute-start.47) | collective-permute-done | bytes 1572896 | tf_op jit(solution)/shard_map/ppermute | solution.py:21
  (420 shorter events, 484.6 us)
Async XLA Ops:
  7.2 233.5 %all-gather.16.cloned.1.call-start = ((), (), s32[]{:S(2)}) async-start(), calls=%async_computation.8 | async-start | bytes 7667712 | tf_op jit(solution)/shard_map/all_gather | solution.py:423
  22.6 327.1 %all-gather.18.cloned.1.call-start = ((), (), s32[]{:S(2)}) async-start(), calls=%async_computation.9 | async-start | bytes 9437184 | tf_op jit(solution)/shard_map/all_gather | solution.py:454
  98.8 138.3 %collective-permute-start.7 = (bf16[384,2048]{1,0:T(8,128)(2,1)S(1)}, bf16[384,2048]{1,0:T(8,128)(2,1)}, u32[]{:S(2)}, u32[]{:S(2)}) collective-permute-start(bf16[384,2048]{1,0:T(8,128)(2,1)S(1)} %bitcast.217), channel_id=1, source_target_pairs={{0,4},{1,5},{2,6},{3,7},{4,0},{5,1},{6,2},{7,3},{8,12},{9,13},{10,... | collective-permute-start | bytes 4718600 | tf_op jit(solution)/shard_map/ppermute | solution.py:21
  291.9 138.6 %all-gather.28.cloned.1.call-start = ((), (), s32[]{:S(2)}) async-start(), calls=%async_computation.20 | async-start | bytes 7864320 | tf_op jit(solution)/shard_map/all_gather | solution.py:468
  359.0 145.9 %all-gather.30.cloned.1.call-start = ((), (), s32[]{:S(2)}) async-start(), calls=%async_computation.21 | async-start | bytes 7864320 | tf_op jit(solution)/shard_map/all_gather | solution.py:470
  430.7 123.8 %all-gather.20.cloned.1.call-start = ((), (), s32[]{:S(2)}) async-start(), calls=%async_computation.10 | async-start | bytes 9437184 | tf_op jit(solution)/shard_map/all_gather | solution.py:198
  434.5 250.2 %all-gather.22.cloned.1.call-start = ((), (), s32[]{:S(2)}) async-start(), calls=%async_computation.11 | async-start | bytes 9437184 | tf_op jit(solution)/shard_map/all_gather | solution.py:198
  434.6 119.9 %collective-permute-start.14 = (bf16[4,256,3072]{2,1,0:T(8,128)(2,1)}, bf16[4,256,3072]{2,1,0:T(8,128)(2,1)}, u32[]{:S(2)}, u32[]{:S(2)}) collective-permute-start(bf16[4,256,3072]{2,1,0:T(8,128)(2,1)} %get-tuple-element.159.refs_6_), channel_id=1, source_target_pairs={{0,1},{1,0},{2,3},{3,2},{4,5},{5,4},{6,7},{7,6},{8,9},{9,8},{10,11... | collective-permute-start | bytes 18874376 | tf_op jit(solution)/shard_map/ppermute | solution.py:21
  437.0 102.2 %collective-permute-start.17 = (bf16[1,256,3072]{2,1,0:T(8,128)(2,1)S(1)}, bf16[1,256,3072]{2,1,0:T(8,128)(2,1)}, u32[]{:S(2)}, u32[]{:S(2)}) collective-permute-start(bf16[1,256,3072]{2,1,0:T(8,128)(2,1)S(1)} %copy-done.30), channel_id=1, source_target_pairs={{0,4},{1,5},{2,6},{3,7},{4,0},{5,1},{6,2},{7,3},{8,12},{9,13},{10,... | collective-permute-start | bytes 4718600 | tf_op jit(solution)/shard_map/ppermute | solution.py:21
  543.0 249.4 %all-gather.24.cloned.1.call-start = ((), (), s32[]{:S(2)}) async-start(), calls=%async_computation.12 | async-start | bytes 9437184 | tf_op jit(solution)/shard_map/all_gather | solution.py:198
  554.1 130.6 %collective-permute-start.21 = (bf16[1,256,3072]{2,1,0:T(8,128)(2,1)}, bf16[1,256,3072]{2,1,0:T(8,128)(2,1)}, u32[]{:S(2)}, u32[]{:S(2)}) collective-permute-start(bf16[1,256,3072]{2,1,0:T(8,128)(2,1)} %get-tuple-element.169), channel_id=1, source_target_pairs={{0,2},{1,3},{2,0},{3,1},{4,6},{5,7},{6,4},{7,5},{8,10},{9,11},{10,... | collective-permute-start | bytes 4718600 | tf_op jit(solution)/shard_map/ppermute | solution.py:21
  615.9 149.9 %collective-permute-start.26 = (bf16[4,256,3072]{2,1,0:T(8,128)(2,1)}, bf16[4,256,3072]{2,1,0:T(8,128)(2,1)}, u32[]{:S(2)}, u32[]{:S(2)}) collective-permute-start(bf16[4,256,3072]{2,1,0:T(8,128)(2,1)} %get-tuple-element.182), channel_id=1, source_target_pairs={{0,1},{1,0},{2,3},{3,2},{4,5},{5,4},{6,7},{7,6},{8,9},{9,8},{10,11... | collective-permute-start | bytes 18874376 | tf_op jit(solution)/shard_map/ppermute | solution.py:21
  621.8 170.6 %collective-permute-start.24 = (bf16[1,256,3072]{2,1,0:T(8,128)(2,1)}, bf16[1,256,3072]{2,1,0:T(8,128)(2,1)}, u32[]{:S(2)}, u32[]{:S(2)}) collective-permute-start(bf16[1,256,3072]{2,1,0:T(8,128)(2,1)} %get-tuple-element.180), channel_id=1, source_target_pairs={{0,4},{1,5},{2,6},{3,7},{4,0},{5,1},{6,2},{7,3},{8,12},{9,13},{10,... | collective-permute-start | bytes 4718600 | tf_op jit(solution)/shard_map/ppermute | solution.py:21
  629.0 163.5 %collective-permute-start.25 = (bf16[1,256,3072]{2,1,0:T(8,128)(2,1)}, bf16[1,256,3072]{2,1,0:T(8,128)(2,1)}, u32[]{:S(2)}, u32[]{:S(2)}) collective-permute-start(bf16[1,256,3072]{2,1,0:T(8,128)(2,1)} %get-tuple-element.181), channel_id=1, source_target_pairs={{0,2},{1,3},{2,0},{3,1},{4,6},{5,7},{6,4},{7,5},{8,10},{9,11},{10,... | collective-permute-start | bytes 4718600 | tf_op jit(solution)/shard_map/ppermute | solution.py:21
  694.1 202.6 %all-gather.26.cloned.1.call-start = ((), (), s32[]{:S(2)}) async-start(), calls=%async_computation.13 | async-start | bytes 9437184 | tf_op jit(solution)/shard_map/all_gather | solution.py:198
  765.8 106.3 %collective-permute-start.30 = (bf16[4,256,3072]{2,1,0:T(8,128)(2,1)}, bf16[4,256,3072]{2,1,0:T(8,128)(2,1)}, u32[]{:S(2)}, u32[]{:S(2)}) collective-permute-start(bf16[4,256,3072]{2,1,0:T(8,128)(2,1)} %get-tuple-element.197), channel_id=1, source_target_pairs={{0,1},{1,0},{2,3},{3,2},{4,5},{5,4},{6,7},{7,6},{8,9},{9,8},{10,11... | collective-permute-start | bytes 18874376 | tf_op jit(solution)/shard_map/ppermute | solution.py:21
  779.3 100.4 %collective-permute-start.29 = (bf16[2,256,3072]{2,1,0:T(8,128)(2,1)}, bf16[2,256,3072]{2,1,0:T(8,128)(2,1)}, u32[]{:S(2)}, u32[]{:S(2)}) collective-permute-start(bf16[2,256,3072]{2,1,0:T(8,128)(2,1)} %add_convert_fusion.3), channel_id=1, source_target_pairs={{0,2},{1,3},{2,0},{3,1},{4,6},{5,7},{6,4},{7,5},{8,10},{9,11},{10,... | collective-permute-start | bytes 9437192 | tf_op jit(solution)/shard_map/ppermute | solution.py:21
  802.2 282.9 %reduce-scatter.7.cloned.1.call-start = ((), (), s32[]{:S(2)}) async-start(), calls=%async_computation.14 | async-start | bytes 7864320 | tf_op jit(solution)/shard_map/reduce_scatter | solution.py:545
  877.9 107.1 %collective-permute-start.33 = (bf16[2,256,3072]{2,1,0:T(8,128)(2,1)}, bf16[2,256,3072]{2,1,0:T(8,128)(2,1)}, u32[]{:S(2)}, u32[]{:S(2)}) collective-permute-start(bf16[2,256,3072]{2,1,0:T(8,128)(2,1)} %add_convert_fusion.2), channel_id=1, source_target_pairs={{0,2},{1,3},{2,0},{3,1},{4,6},{5,7},{6,4},{7,5},{8,10},{9,11},{10,... | collective-permute-start | bytes 9437192 | tf_op jit(solution)/shard_map/ppermute | solution.py:21
  992.2 204.9 %reduce-scatter.9.cloned.1.call-start = ((), (), s32[]{:S(2)}) async-start(), calls=%async_computation.15 | async-start | bytes 7864320 | tf_op jit(solution)/shard_map/reduce_scatter | solution.py:545
  1085.1 239.1 %reduce-scatter.13.cloned.1.call-start = ((), (), s32[]{:S(2)}) async-start(), calls=%async_computation.17 | async-start | bytes 7864320 | tf_op jit(solution)/shard_map/reduce_scatter | solution.py:545
  1085.1 102.4 %collective-permute-start.36 = (bf16[2,256,3072]{2,1,0:T(8,128)(2,1)S(1)}, bf16[2,256,3072]{2,1,0:T(8,128)(2,1)}, u32[]{:S(2)}, u32[]{:S(2)}) collective-permute-start(bf16[2,256,3072]{2,1,0:T(8,128)(2,1)S(1)} %add_convert_fusion.1), channel_id=1, source_target_pairs={{0,2},{1,3},{2,0},{3,1},{4,6},{5,7},{6,4},{7,5},{8,10},{9,11},{10,... | collective-permute-start | bytes 9437192 | tf_op jit(solution)/shard_map/ppermute | solution.py:21
  1197.1 160.2 %reduce-scatter.11.cloned.1.call-start = ((), (), s32[]{:S(2)}) async-start(), calls=%async_computation.16 | async-start | bytes 7864320 | tf_op jit(solution)/shard_map/reduce_scatter | solution.py:545
  1217.7 271.7 %reduce-scatter.15.cloned.1.call-start = ((), (), s32[]{:S(2)}) async-start(), calls=%async_computation.18 | async-start | bytes 7077888 | tf_op jit(solution)/shard_map/reduce_scatter | solution.py:589
  1222.3 101.8 %collective-permute-start.40 = (bf16[2,256,3072]{2,1,0:T(8,128)(2,1)}, bf16[2,256,3072]{2,1,0:T(8,128)(2,1)}, u32[]{:S(2)}, u32[]{:S(2)}) collective-permute-start(bf16[2,256,3072]{2,1,0:T(8,128)(2,1)} %add_convert_fusion), channel_id=1, source_target_pairs={{0,2},{1,3},{2,0},{3,1},{4,6},{5,7},{6,4},{7,5},{8,10},{9,11},{10,... | collective-permute-start | bytes 9437192 | tf_op jit(solution)/shard_map/ppermute | solution.py:21
  1357.4 207.3 %all-gather.32.cloned.1.call-start = ((), (), s32[]{:S(2)}) async-start(), calls=%async_computation.22 | async-start | bytes 3932160 | tf_op jit(solution)/shard_map/all_gather | solution.py:595
  1366.8 117.0 %collective-permute-start.41 = (bf16[384,2048]{1,0:T(8,128)(2,1)S(1)}, bf16[384,2048]{1,0:T(8,128)(2,1)}, u32[]{:S(2)}, u32[]{:S(2)}) collective-permute-start(bf16[384,2048]{1,0:T(8,128)(2,1)S(1)} %copy-done.55), channel_id=1, source_target_pairs={{0,4},{1,5},{2,6},{3,7},{4,0},{5,1},{6,2},{7,3},{8,12},{9,13},{10,... | collective-permute-start | bytes 4718600 | tf_op jit(solution)/shard_map/ppermute | solution.py:21
  1368.9 114.9 %collective-permute-start.43 = (bf16[2048,512]{1,0:T(8,128)(2,1)S(1)}, bf16[2048,512]{1,0:T(8,128)(2,1)}, u32[]{:S(2)}, u32[]{:S(2)}) collective-permute-start(bf16[2048,512]{1,0:T(8,128)(2,1)S(1)} %convolution_convert_fusion.17), channel_id=1, source_target_pairs={{0,16},{8,24},{16,0},{24,8},{1,17},{9,25},{17,1},{25,9},{2,18},{10... | collective-permute-start | bytes 6291464 | tf_op jit(solution)/shard_map/ppermute | solution.py:21
  1370.2 113.7 %collective-permute-start.42 = (bf16[2048,512]{1,0:T(8,128)(2,1)S(1)}, bf16[2048,512]{1,0:T(8,128)(2,1)}, u32[]{:S(2)}, u32[]{:S(2)}) collective-permute-start(bf16[2048,512]{1,0:T(8,128)(2,1)S(1)} %convolution_convert_fusion.18), channel_id=1, source_target_pairs={{0,8},{8,0},{16,24},{24,16},{1,9},{9,1},{17,25},{25,17},{2,10},{10... | collective-permute-start | bytes 6291464 | tf_op jit(solution)/shard_map/ppermute | solution.py:21
  1370.9 112.9 %collective-permute-start.44 = (bf16[2048,512]{1,0:T(8,128)(2,1)S(1)}, bf16[2048,512]{1,0:T(8,128)(2,1)}, u32[]{:S(2)}, u32[]{:S(2)}) collective-permute-start(bf16[2048,512]{1,0:T(8,128)(2,1)S(1)} %convolution_convert_fusion.16), channel_id=1, source_target_pairs={{0,24},{8,16},{16,8},{24,0},{1,25},{9,17},{17,9},{25,1},{2,26},{10... | collective-permute-start | bytes 6291464 | tf_op jit(solution)/shard_map/ppermute | solution.py:21
  1489.5 129.2 %reduce-scatter.17.cloned.1.call-start = ((), (), s32[]{:S(2)}) async-start(), calls=%async_computation.19 | async-start | bytes 2949120 | tf_op jit(solution)/shard_map/reduce_scatter | solution.py:601
  1571.1 100.7 %all-gather.34.cloned.1.call-start = ((), (), s32[]{:S(2)}) async-start(), calls=%async_computation.23 | async-start | bytes 1638400 | tf_op jit(solution)/shard_map/all_gather | solution.py:602
  (108 other events, 3702.1 us)
Sparse Core Ops, SparseCore 0:
  22.8 72.1 all-gather.15
  96.6 142.0 all-gather.17
  359.1 71.2 all-gather.27
  432.7 70.1 all-gather.29
  504.3 16.7 all-gather.19
  543.1 16.9 all-gather.21
  694.2 15.5 all-gather.23
  802.3 16.0 all-gather.25
  992.3 69.5 reduce-scatter.6
  1085.2 69.2 reduce-scatter.8
  1197.2 86.9 reduce-scatter.12
  1287.1 70.1 reduce-scatter.10
  1360.2 129.1 reduce-scatter.14
  1491.1 49.4 all-gather.31
  1571.2 36.3 reduce-scatter.16
  1618.8 52.9 all-gather.33

commit v10 on v8

--- a/solution.py
+++ b/solution.py
@@ -490,6 +490,7 @@
     begin(2, moe_all[1])
     beside = swap(after(own_part, normed_m), "fsdp", 1)
     near, last = [both_cores(list(begun[0].values()))], {}
+    every_grad_slots = []
     for i in range(per_half):
         k = [n for n, members in enumerate(sets) if i in members][0]
         first, later, many = begun[k], experts[k], len(sets[k])
@@ -501,15 +502,22 @@
             )
         if i + 1 < per_half:
             ready.extend(begun[i + 1].values())
-        cots = [after(cot_all[g], *back) for g in range(2)]
+        if i < 2:
+            cots = [after(cot_all[g], *back) for g in range(2)]
+            every_grad_slots.extend(
+                [dispatch(j, g, cots[g], True) for g in range(2)]
+                for j in (range(1, per_half) if i else (0,))
+            )
         for chain in chains[max(i - 3, 0) : max(i - 1, 0)]:
             ready.append(chain.arrive())
         if i == 0:
-            ready = [dispatch(i, g, cots[g], True) for g in range(2)]
+            ready = every_grad_slots[0]
         slots = [dispatch(i, g, after(moe_all[g], *ready), False) for g in range(2)]
         ready = [chain.add(back[0]) for chain in chains[max(i - 3, 0) : max(i - 1, 0)]]
         slots[1] = after(slots[1], *ready)
-        grad_slots = [dispatch(i, g, cots[g], True) for g in range(2)]
+        grad_slots = every_grad_slots[i]
+        if i == 1:
+            slots[1] = after(slots[1], *[part for parts in every_grad_slots[1:] for part in parts])
         if i + 1 < per_half:
             experts.append(finish_expert(begun[i + 1], slots[1]))
             near.append(both_cores(list(begun[i + 1].values()), slots[1]))

time: 1680 us -> 1710 us (1.018)
  waiting for transfers between devices: 713 us -> 746 us
    ppermute x49, waiting for transfers between devices: 641 us -> 674 us  [swap(): return lax.ppermute(value, axis, [(i, i ^ bit) for i in range(size)])]
  transfers between devices with their start and end apart: 67 -> 67, of which waited for: 23 -> 24; matrix products, arithmetic and copies ran while one was open for 25% -> 24% of each run, Pallas kernels for 21% -> 20%
where the time goes in v10:
time: 1710 us; the launch traced here: 1700 us
  waiting for transfers between devices  746 us (44%)
  Pallas kernels  350 us (20%)
  matrix products  185 us (11%)
  other arithmetic  136 us (8%)
  local copies, waits for them, and re-layouts  135 us (8%)
  starting transfers between devices  66.5 us (4%)
  blocking collectives  65.8 us (4%)
    ppermute x49, waiting for transfers between devices, swap(): return lax.ppermute(value, axis, [(i, i ^ bit) for i in range(size)])  674 us
    pallas_call x4, Pallas kernels, run_expert(): pl.pallas_call(lambda *refs: expert_kernel(size, tiles, parts, *refs), ou...  247 us
    dot_general x29, matrix products, dot(): return lax.dot_general(a, b, (contract, batch), preferred_element_type=f32)  185 us
    pallas_call x2, Pallas kernels, attend(): pl.pallas_call(lambda *refs: (attend_backward_kernel if backward else att...  76.2 us
    all_gather x1, blocking collectives, body(): lax.all_gather(routing, 'seq', axis=0, tiled=False)  65.8 us
    ppermute x49, starting transfers between devices, swap(): return lax.ppermute(value, axis, [(i, i ^ bit) for i in range(size)])  56.2 us
  transfers between devices with their start and end apart: 67, of which 24 were waited for; matrix products, arithmetic and copies ran while one was open for 24% of the time, Pallas kernels for 20%

profile of v10, /device:TPU:0, one launch (start us, length us, event | category | flops | bytes accessed | tf_op | source)
XLA Modules:
  0.0 1699.9 jit_solution(12843014124727962915)
XLA Ops:
  36.9 14.5 reshape.351
  51.4 9.3 fusion.3
  62.0 32.8 %collective-permute-done.2 = bf16[384,2048]{1,0:T(8,128)(2,1)} collective-permute-done((bf16[384,2048]{1,0:T(8,128)(2,1)S(1)}, bf16[384,2048]{1,0:T(8,128)(2,1)}, u32[]{:S(2)}, u32[]{:S(2)}) %collective-permute-start.2) | collective-permute-done | bytes 1572896 | tf_op jit(solution)/shard_map/ppermute | solution.py:21
  103.4 65.8 %all-gather = f32[8,384,16]{1,2,0:T(8,128)S(1)} all-gather(f32[2,384,16]{1,2,0:T(8,128)S(1)} %pad_maximum_fusion.11), channel_id=2, replica_groups=mesh['seq'=4,'fsdp'=8] {'seq'}, dimensions={0}, use_global_device_ids=true | all-gather | bytes 245760 | tf_op jit(solution)/shard_map/all_gather | solution.py:431
  210.5 16.2 convolution_convert_fusion.2.refs_0_
  226.7 25.3 %attend_forward.1 = bf16[1536,512]{1,0:T(8,128)(2,1)} custom-call(bf16[1536,1536]{1,0:T(8,128)(2,1)} %convolution_convert_fusion.2.refs_0_, s32[1536,1]{1,0:T(8,128)} %reshape.409.refs_1_.refs_2_, s32[1,1536]{1,0:T(1,128)} %reshape.360.refs_2_.refs_3_), custom_call_target="tpu_custom_call" | custom-call | flops 24159191040 | bytes 9437184 | tf_op jit(solution)/shard_map/attend_forward/pallas_call | solution.py:97
  287.9 51.8 %collective-permute-done.11.refs_10_ = bf16[1,256,3072]{2,1,0:T(8,128)(2,1)} collective-permute-done((bf16[1,256,3072]{2,1,0:T(8,128)(2,1)}, bf16[1,256,3072]{2,1,0:T(8,128)(2,1)}, u32[]{:S(2)}, u32[]{:S(2)}) %collective-permute-start.11) | collective-permute-done | bytes 1572896 | tf_op jit(solution)/shard_map/ppermute | solution.py:21
  349.9 68.3 %collective-permute-done.13 = bf16[384,2048]{1,0:T(8,128)(2,1)S(1)} collective-permute-done((bf16[384,2048]{1,0:T(8,128)(2,1)}, bf16[384,2048]{1,0:T(8,128)(2,1)S(1)}, u32[]{:S(2)}, u32[]{:S(2)}) %collective-permute-start.13) | collective-permute-done | bytes 1572896 | tf_op jit(solution)/shard_map/ppermute | solution.py:21
  434.8 57.7 %collective-permute-done.15.refs_12_ = bf16[1,256,3072]{2,1,0:T(8,128)(2,1)} collective-permute-done((bf16[1,256,3072]{2,1,0:T(8,128)(2,1)}, bf16[1,256,3072]{2,1,0:T(8,128)(2,1)}, u32[]{:S(2)}, u32[]{:S(2)}) %collective-permute-start.15) | collective-permute-done | bytes 1572896 | tf_op jit(solution)/shard_map/ppermute | solution.py:21
  507.3 44.7 %collective-permute-done.18.refs_11_ = bf16[1,256,3072]{2,1,0:T(8,128)(2,1)} collective-permute-done((bf16[1,256,3072]{2,1,0:T(8,128)(2,1)}, bf16[1,256,3072]{2,1,0:T(8,128)(2,1)}, u32[]{:S(2)}, u32[]{:S(2)}) %collective-permute-start.18) | collective-permute-done | bytes 1572896 | tf_op jit(solution)/shard_map/ppermute | solution.py:21
  558.4 62.8 %expert.4 = (bf16[544,2048]{1,0:T(8,128)(2,1)}, bf16[544,2048]{1,0:T(8,128)(2,1)}, bf16[544,2048]{1,0:T(8,128)(2,1)}, bf16[544,2048]{1,0:T(8,128)(2,1)}, bf16[4,...) custom-call(s32[1]{0:T(128)} %bitcast.23.refs_0_, f32[1088,1]{1,0:T(8,128)} %reshape_squeeze.16.refs_1_, ...), custom_call_target="tpu_custom_call" | custom-call | flops 41070624768 | bytes 42991616 | tf_op jit(solution)/shard_map/expert/pallas_call | solution.py:320
  673.9 62.0 %expert.5 = (bf16[544,2048]{1,0:T(8,128)(2,1)}, bf16[544,2048]{1,0:T(8,128)(2,1)}, bf16[544,2048]{1,0:T(8,128)(2,1)}, bf16[544,2048]{1,0:T(8,128)(2,1)}, bf16[4,...) custom-call(s32[1]{0:T(128)} %bitcast.23.refs_0_, f32[1088,1]{1,0:T(8,128)} %reshape_squeeze.17.refs_1_, ...), custom_call_target="tpu_custom_call" | custom-call | flops 41070624768 | bytes 42991616 | tf_op jit(solution)/shard_map/expert/pallas_call | solution.py:320
  741.6 28.1 %collective-permute-done.23.refs_12_ = bf16[1,256,3072]{2,1,0:T(8,128)(2,1)} collective-permute-done((bf16[1,256,3072]{2,1,0:T(8,128)(2,1)}, bf16[1,256,3072]{2,1,0:T(8,128)(2,1)}, u32[]{:S(2)}, u32[]{:S(2)}) %collective-permute-start.23) | collective-permute-done | bytes 1572896 | tf_op jit(solution)/shard_map/ppermute | solution.py:21
  801.5 61.0 %expert.6 = (bf16[544,2048]{1,0:T(8,128)(2,1)}, bf16[544,2048]{1,0:T(8,128)(2,1)}, bf16[544,2048]{1,0:T(8,128)(2,1)}, bf16[544,2048]{1,0:T(8,128)(2,1)}, bf16[4,...) custom-call(s32[1]{0:T(128)} %bitcast.23.refs_0_, f32[1088,1]{1,0:T(8,128)} %reshape_squeeze.18.refs_1_, ...), custom_call_target="tpu_custom_call" | custom-call | flops 41070624768 | bytes 42991616 | tf_op jit(solution)/shard_map/expert/pallas_call | solution.py:320
  868.4 32.4 %collective-permute-done.28.refs_12_ = bf16[1,256,3072]{2,1,0:T(8,128)(2,1)} collective-permute-done((bf16[1,256,3072]{2,1,0:T(8,128)(2,1)}, bf16[1,256,3072]{2,1,0:T(8,128)(2,1)}, u32[]{:S(2)}, u32[]{:S(2)}) %collective-permute-start.28) | collective-permute-done | bytes 1572896 | tf_op jit(solution)/shard_map/ppermute | solution.py:21
  918.2 61.0 %expert.7 = (bf16[544,2048]{1,0:T(8,128)(2,1)}, bf16[544,2048]{1,0:T(8,128)(2,1)}, bf16[544,2048]{1,0:T(8,128)(2,1)}, bf16[544,2048]{1,0:T(8,128)(2,1)}, bf16[4,...) custom-call(s32[1]{0:T(128)} %bitcast.23.refs_0_, f32[1088,1]{1,0:T(8,128)} %reshape_squeeze.19.refs_1_, ...), custom_call_target="tpu_custom_call" | custom-call | flops 41070624768 | bytes 42991616 | tf_op jit(solution)/shard_map/expert/pallas_call | solution.py:320
  983.1 16.1 collective-permute-done.32
  1040.5 59.4 %collective-permute-done.38 = bf16[1,256,3072]{2,1,0:T(8,128)(2,1)} collective-permute-done((bf16[1,256,3072]{2,1,0:T(8,128)(2,1)S(1)}, bf16[1,256,3072]{2,1,0:T(8,128)(2,1)}, u32[]{:S(2)}, u32[]{:S(2)}) %collective-permute-start.38) | collective-permute-done | bytes 1572896 | tf_op jit(solution)/shard_map/ppermute | solution.py:21
  1119.1 84.5 %collective-permute-done.36 = bf16[2,256,3072]{2,1,0:T(8,128)(2,1)} collective-permute-done((bf16[2,256,3072]{2,1,0:T(8,128)(2,1)S(1)}, bf16[2,256,3072]{2,1,0:T(8,128)(2,1)}, u32[]{:S(2)}, u32[]{:S(2)}) %collective-permute-start.36) | collective-permute-done | bytes 3145760 | tf_op jit(solution)/shard_map/ppermute | solution.py:21
  1203.6 9.5 convolution_convert_fusion.3
  1244.0 25.7 %all-to-all-done.1 = bf16[384,4,512]{2,0,1:T(8,128)(2,1)} async-done(((bf16[384,4,512]{2,0,1:T(8,128)(2,1)}), bf16[384,4,512]{2,0,1:T(8,128)(2,1)}, u32[]{:S(2)}, u32[]{:S(2)}) %all-to-all-start.1) | async-done | bytes 1572896 | tf_op jit(solution)/shard_map/all_to_all | solution.py:580
  1269.6 50.9 %attend_backward.1 = bf16[1536,1536]{1,0:T(8,128)(2,1)} custom-call(bf16[1536,1536]{1,0:T(8,128)(2,1)} %convolution_convert_fusion.2.refs_0_, bf16[1536,512]{1,0:T(8,128)(2,1)} %bitcast.81.refs_1_, s32[1536,1]{1,0:T(8,128)} %reshape.409.refs_1_.refs_2_, s32[1,1536]{1,0:T(1,128)} %reshape.360.refs_2_.refs_3_), custom_call_target="tpu_custom_call" | custom-call | flops 48318382080 | bytes 9437184 | tf_op jit(solution)/shard_map/attend_backward/pallas_call | solution.py:97
  1320.6 19.0 %collective-permute-done.40 = bf16[2,256,3072]{2,1,0:T(8,128)(2,1)} collective-permute-done((bf16[2,256,3072]{2,1,0:T(8,128)(2,1)}, bf16[2,256,3072]{2,1,0:T(8,128)(2,1)}, u32[]{:S(2)}, u32[]{:S(2)}) %collective-permute-start.40) | collective-permute-done | bytes 3145760 | tf_op jit(solution)/shard_map/ppermute | solution.py:21
  1339.6 15.8 convolution_convert_fusion.1
  1386.3 15.1 convolution_convert_fusion
  1401.4 89.8 %collective-permute-done.41 = bf16[384,2048]{1,0:T(8,128)(2,1)} collective-permute-done((bf16[384,2048]{1,0:T(8,128)(2,1)}, bf16[384,2048]{1,0:T(8,128)(2,1)}, u32[]{:S(2)}, u32[]{:S(2)}) %collective-permute-start.41) | collective-permute-done | bytes 1572896 | tf_op jit(solution)/shard_map/ppermute | solution.py:21
  1506.5 9.5 collective-permute-start.48
  1517.8 32.2 %collective-permute-done.45 = bf16[384,2048]{1,0:T(8,128)(2,1)S(1)} collective-permute-done((bf16[384,2048]{1,0:T(8,128)(2,1)S(1)}, bf16[384,2048]{1,0:T(8,128)(2,1)S(1)}, u32[]{:S(2)}, u32[]{:S(2)}) %collective-permute-start.45) | collective-permute-done | bytes 1572896 | tf_op jit(solution)/shard_map/ppermute | solution.py:21
  1550.0 47.0 %collective-permute-done.47 = bf16[384,2048]{1,0:T(8,128)(2,1)S(1)} collective-permute-done((bf16[384,2048]{1,0:T(8,128)(2,1)S(1)}, bf16[384,2048]{1,0:T(8,128)(2,1)S(1)}, u32[]{:S(2)}, u32[]{:S(2)}) %collective-permute-start.47) | collective-permute-done | bytes 1572896 | tf_op jit(solution)/shard_map/ppermute | solution.py:21
  1622.5 28.8 %reduce-scatter.17.cloned.1.call-done = bf16[256,640]{1,0:T(8,128)(2,1)} async-done(((bf16[2048,640]{1,0:T(8,128)(2,1)}), bf16[256,640]{1,0:T(8,128)(2,1)}) %reduce-scatter.17.cloned.1.call-update) | async-done | bytes 327696 | tf_op jit(solution)/shard_map/reduce_scatter | solution.py:608
  1655.1 14.8 finish.1
  1675.0 8.6 unpack.2
  (391 shorter events, 464.1 us)
Async XLA Ops:
  7.2 202.5 %all-gather.16.cloned.1.call-start = ((), (), s32[]{:S(2)}) async-start(), calls=%async_computation.8 | async-start | bytes 7667712 | tf_op jit(solution)/shard_map/all_gather | solution.py:422
  22.6 317.1 %all-gather.18.cloned.1.call-start = ((), (), s32[]{:S(2)}) async-start(), calls=%async_computation.9 | async-start | bytes 9437184 | tf_op jit(solution)/shard_map/all_gather | solution.py:455
  30.4 147.4 %collective-permute-start.7 = (bf16[384,2048]{1,0:T(8,128)(2,1)S(1)}, bf16[384,2048]{1,0:T(8,128)(2,1)}, u32[]{:S(2)}, u32[]{:S(2)}) collective-permute-start(bf16[384,2048]{1,0:T(8,128)(2,1)S(1)} %bitcast.216), channel_id=1, source_target_pairs={{0,4},{1,5},{2,6},{3,7},{4,0},{5,1},{6,2},{7,3},{8,12},{9,13},{10,... | collective-permute-start | bytes 4718600 | tf_op jit(solution)/shard_map/ppermute | solution.py:21
  262.2 156.0 %all-gather.28.cloned.1.call-start = ((), (), s32[]{:S(2)}) async-start(), calls=%async_computation.20 | async-start | bytes 7864320 | tf_op jit(solution)/shard_map/all_gather | solution.py:469
  348.9 152.1 %all-gather.30.cloned.1.call-start = ((), (), s32[]{:S(2)}) async-start(), calls=%async_computation.21 | async-start | bytes 7864320 | tf_op jit(solution)/shard_map/all_gather | solution.py:471
  419.3 139.1 %all-gather.20.cloned.1.call-start = ((), (), s32[]{:S(2)}) async-start(), calls=%async_computation.10 | async-start | bytes 9437184 | tf_op jit(solution)/shard_map/all_gather | solution.py:198
  423.2 231.4 %all-gather.22.cloned.1.call-start = ((), (), s32[]{:S(2)}) async-start(), calls=%async_computation.11 | async-start | bytes 9437184 | tf_op jit(solution)/shard_map/all_gather | solution.py:198
  423.5 134.9 %collective-permute-start.14 = (bf16[4,256,3072]{2,1,0:T(8,128)(2,1)}, bf16[4,256,3072]{2,1,0:T(8,128)(2,1)}, u32[]{:S(2)}, u32[]{:S(2)}) collective-permute-start(bf16[4,256,3072]{2,1,0:T(8,128)(2,1)} %get-tuple-element.155.refs_6_), channel_id=1, source_target_pairs={{0,1},{1,0},{2,3},{3,2},{4,5},{5,4},{6,7},{7,6},{8,9},{9,8},{10,11... | collective-permute-start | bytes 18874376 | tf_op jit(solution)/shard_map/ppermute | solution.py:21
  425.6 126.4 %collective-permute-start.17 = (bf16[1,256,3072]{2,1,0:T(8,128)(2,1)}, bf16[1,256,3072]{2,1,0:T(8,128)(2,1)}, u32[]{:S(2)}, u32[]{:S(2)}) collective-permute-start(bf16[1,256,3072]{2,1,0:T(8,128)(2,1)} %get-tuple-element.158), channel_id=1, source_target_pairs={{0,4},{1,5},{2,6},{3,7},{4,0},{5,1},{6,2},{7,3},{8,12},{9,13},{10,... | collective-permute-start | bytes 4718600 | tf_op jit(solution)/shard_map/ppermute | solution.py:21
  428.7 123.3 %collective-permute-start.18 = (bf16[1,256,3072]{2,1,0:T(8,128)(2,1)}, bf16[1,256,3072]{2,1,0:T(8,128)(2,1)}, u32[]{:S(2)}, u32[]{:S(2)}) collective-permute-start(bf16[1,256,3072]{2,1,0:T(8,128)(2,1)} %get-tuple-element.160), channel_id=1, source_target_pairs={{0,2},{1,3},{2,0},{3,1},{4,6},{5,7},{6,4},{7,5},{8,10},{9,11},{10,... | collective-permute-start | bytes 4718600 | tf_op jit(solution)/shard_map/ppermute | solution.py:21
  501.0 153.6 %collective-permute-start.20 = (bf16[1,256,3072]{2,1,0:T(8,128)(2,1)S(1)}, bf16[1,256,3072]{2,1,0:T(8,128)(2,1)}, u32[]{:S(2)}, u32[]{:S(2)}) collective-permute-start(bf16[1,256,3072]{2,1,0:T(8,128)(2,1)S(1)} %copy-done.29), channel_id=1, source_target_pairs={{0,4},{1,5},{2,6},{3,7},{4,0},{5,1},{6,2},{7,3},{8,12},{9,13},{10,... | collective-permute-start | bytes 4718600 | tf_op jit(solution)/shard_map/ppermute | solution.py:21
  552.0 102.6 %collective-permute-start.21 = (bf16[1,256,3072]{2,1,0:T(8,128)(2,1)}, bf16[1,256,3072]{2,1,0:T(8,128)(2,1)}, u32[]{:S(2)}, u32[]{:S(2)}) collective-permute-start(bf16[1,256,3072]{2,1,0:T(8,128)(2,1)} %get-tuple-element.165), channel_id=1, source_target_pairs={{0,2},{1,3},{2,0},{3,1},{4,6},{5,7},{6,4},{7,5},{8,10},{9,11},{10,... | collective-permute-start | bytes 4718600 | tf_op jit(solution)/shard_map/ppermute | solution.py:21
  552.0 102.1 %collective-permute-start.19 = (bf16[1,256,3072]{2,1,0:T(8,128)(2,1)}, bf16[1,256,3072]{2,1,0:T(8,128)(2,1)}, u32[]{:S(2)}, u32[]{:S(2)}) collective-permute-start(bf16[1,256,3072]{2,1,0:T(8,128)(2,1)} %collective-permute-done.17.refs_10_), channel_id=1, source_target_pairs={{0,2},{1,3},{2,0},{3,1},{4,6},{5,7},{6,4},{7,5},{8,10},{9,11},{10,... | collective-permute-start | bytes 4718600 | tf_op jit(solution)/shard_map/ppermute | solution.py:21
  557.9 211.9 %all-gather.24.cloned.1.call-start = ((), (), s32[]{:S(2)}) async-start(), calls=%async_computation.12 | async-start | bytes 9437184 | tf_op jit(solution)/shard_map/all_gather | solution.py:198
  664.0 241.9 %all-gather.26.cloned.1.call-start = ((), (), s32[]{:S(2)}) async-start(), calls=%async_computation.13 | async-start | bytes 9437184 | tf_op jit(solution)/shard_map/all_gather | solution.py:198
  665.5 104.2 %collective-permute-start.24 = (bf16[1,256,3072]{2,1,0:T(8,128)(2,1)S(1)}, bf16[1,256,3072]{2,1,0:T(8,128)(2,1)}, u32[]{:S(2)}, u32[]{:S(2)}) collective-permute-start(bf16[1,256,3072]{2,1,0:T(8,128)(2,1)S(1)} %copy-done.28), channel_id=1, source_target_pairs={{0,4},{1,5},{2,6},{3,7},{4,0},{5,1},{6,2},{7,3},{8,12},{9,13},{10,... | collective-permute-start | bytes 4718600 | tf_op jit(solution)/shard_map/ppermute | solution.py:21
  665.5 104.2 %collective-permute-start.25 = (bf16[1,256,3072]{2,1,0:T(8,128)(2,1)}, bf16[1,256,3072]{2,1,0:T(8,128)(2,1)}, u32[]{:S(2)}, u32[]{:S(2)}) collective-permute-start(bf16[1,256,3072]{2,1,0:T(8,128)(2,1)} %get-tuple-element.178), channel_id=1, source_target_pairs={{0,2},{1,3},{2,0},{3,1},{4,6},{5,7},{6,4},{7,5},{8,10},{9,11},{10,... | collective-permute-start | bytes 4718600 | tf_op jit(solution)/shard_map/ppermute | solution.py:21
  735.8 126.7 %collective-permute-start.30 = (bf16[4,256,3072]{2,1,0:T(8,128)(2,1)}, bf16[4,256,3072]{2,1,0:T(8,128)(2,1)}, u32[]{:S(2)}, u32[]{:S(2)}) collective-permute-start(bf16[4,256,3072]{2,1,0:T(8,128)(2,1)} %get-tuple-element.192), channel_id=1, source_target_pairs={{0,1},{1,0},{2,3},{3,2},{4,5},{5,4},{6,7},{7,6},{8,9},{9,8},{10,11... | collective-permute-start | bytes 18874376 | tf_op jit(solution)/shard_map/ppermute | solution.py:21
  779.1 320.8 %reduce-scatter.7.cloned.1.call-start = ((), (), s32[]{:S(2)}) async-start(), calls=%async_computation.14 | async-start | bytes 7864320 | tf_op jit(solution)/shard_map/reduce_scatter | solution.py:554
  795.8 105.0 %collective-permute-start.28 = (bf16[1,256,3072]{2,1,0:T(8,128)(2,1)}, bf16[1,256,3072]{2,1,0:T(8,128)(2,1)}, u32[]{:S(2)}, u32[]{:S(2)}) collective-permute-start(bf16[1,256,3072]{2,1,0:T(8,128)(2,1)} %collective-permute-done.24.refs_10_), channel_id=1, source_target_pairs={{0,2},{1,3},{2,0},{3,1},{4,6},{5,7},{6,4},{7,5},{8,10},{9,11},{10,... | collective-permute-start | bytes 4718600 | tf_op jit(solution)/shard_map/ppermute | solution.py:21
  868.4 133.0 %collective-permute-start.33 = (bf16[2,256,3072]{2,1,0:T(8,128)(2,1)}, bf16[2,256,3072]{2,1,0:T(8,128)(2,1)}, u32[]{:S(2)}, u32[]{:S(2)}) collective-permute-start(bf16[2,256,3072]{2,1,0:T(8,128)(2,1)} %add_convert_fusion.2), channel_id=1, source_target_pairs={{0,2},{1,3},{2,0},{3,1},{4,6},{5,7},{6,4},{7,5},{8,10},{9,11},{10,... | collective-permute-start | bytes 9437192 | tf_op jit(solution)/shard_map/ppermute | solution.py:21
  1008.7 204.4 %reduce-scatter.9.cloned.1.call-start = ((), (), s32[]{:S(2)}) async-start(), calls=%async_computation.15 | async-start | bytes 7864320 | tf_op jit(solution)/shard_map/reduce_scatter | solution.py:554
  1099.9 239.6 %reduce-scatter.11.cloned.1.call-start = ((), (), s32[]{:S(2)}) async-start(), calls=%async_computation.16 | async-start | bytes 7864320 | tf_op jit(solution)/shard_map/reduce_scatter | solution.py:554
  1100.0 103.6 %collective-permute-start.36 = (bf16[2,256,3072]{2,1,0:T(8,128)(2,1)S(1)}, bf16[2,256,3072]{2,1,0:T(8,128)(2,1)}, u32[]{:S(2)}, u32[]{:S(2)}) collective-permute-start(bf16[2,256,3072]{2,1,0:T(8,128)(2,1)S(1)} %add_convert_fusion.1), channel_id=1, source_target_pairs={{0,2},{1,3},{2,0},{3,1},{4,6},{5,7},{6,4},{7,5},{8,10},{9,11},{10,... | collective-permute-start | bytes 9437192 | tf_op jit(solution)/shard_map/ppermute | solution.py:21
  1213.2 160.6 %reduce-scatter.13.cloned.1.call-start = ((), (), s32[]{:S(2)}) async-start(), calls=%async_computation.17 | async-start | bytes 7864320 | tf_op jit(solution)/shard_map/reduce_scatter | solution.py:554
  1233.0 264.8 %reduce-scatter.15.cloned.1.call-start = ((), (), s32[]{:S(2)}) async-start(), calls=%async_computation.18 | async-start | bytes 7077888 | tf_op jit(solution)/shard_map/reduce_scatter | solution.py:596
  1355.4 247.0 %all-gather.32.cloned.1.call-start = ((), (), s32[]{:S(2)}) async-start(), calls=%async_computation.22 | async-start | bytes 3932160 | tf_op jit(solution)/shard_map/all_gather | solution.py:603
  1373.8 117.4 %collective-permute-start.41 = (bf16[384,2048]{1,0:T(8,128)(2,1)}, bf16[384,2048]{1,0:T(8,128)(2,1)}, u32[]{:S(2)}, u32[]{:S(2)}) collective-permute-start(bf16[384,2048]{1,0:T(8,128)(2,1)} %reduce-scatter.13.cloned.1.call-done), channel_id=1, source_target_pairs={{0,4},{1,5},{2,6},{3,7},{4,0},{5,1},{6,2},{7,3},{8,12},{9,13},{10,... | collective-permute-start | bytes 4718600 | tf_op jit(solution)/shard_map/ppermute | solution.py:21
  1376.2 115.0 %collective-permute-start.43 = (bf16[2048,512]{1,0:T(8,128)(2,1)}, bf16[2048,512]{1,0:T(8,128)(2,1)}, u32[]{:S(2)}, u32[]{:S(2)}) collective-permute-start(bf16[2048,512]{1,0:T(8,128)(2,1)} %convolution_convert_fusion.16), channel_id=1, source_target_pairs={{0,16},{8,24},{16,0},{24,8},{1,17},{9,25},{17,1},{25,9},{2,18},{10... | collective-permute-start | bytes 6291464 | tf_op jit(solution)/shard_map/ppermute | solution.py:21
  1377.5 113.7 %collective-permute-start.42 = (bf16[2048,512]{1,0:T(8,128)(2,1)}, bf16[2048,512]{1,0:T(8,128)(2,1)}, u32[]{:S(2)}, u32[]{:S(2)}) collective-permute-start(bf16[2048,512]{1,0:T(8,128)(2,1)} %convolution_convert_fusion.17), channel_id=1, source_target_pairs={{0,8},{8,0},{16,24},{24,16},{1,9},{9,1},{17,25},{25,17},{2,10},{10... | collective-permute-start | bytes 6291464 | tf_op jit(solution)/shard_map/ppermute | solution.py:21
  1378.2 113.0 %collective-permute-start.44 = (bf16[2048,512]{1,0:T(8,128)(2,1)}, bf16[2048,512]{1,0:T(8,128)(2,1)}, u32[]{:S(2)}, u32[]{:S(2)}) collective-permute-start(bf16[2048,512]{1,0:T(8,128)(2,1)} %convolution_convert_fusion.15), channel_id=1, source_target_pairs={{0,24},{8,16},{16,8},{24,0},{1,25},{9,17},{17,9},{25,1},{2,26},{10... | collective-permute-start | bytes 6291464 | tf_op jit(solution)/shard_map/ppermute | solution.py:21
  1497.8 153.5 %reduce-scatter.17.cloned.1.call-start = ((), (), s32[]{:S(2)}) async-start(), calls=%async_computation.19 | async-start | bytes 2949120 | tf_op jit(solution)/shard_map/reduce_scatter | solution.py:608
  (95 other events, 3710.0 us)
Sparse Core Ops, SparseCore 0:
  22.7 128.8 all-gather.15
  190.8 126.8 all-gather.17
  349.0 68.6 all-gather.27
  420.0 70.1 all-gather.29
  491.5 16.7 all-gather.19
  558.0 16.7 all-gather.21
  664.1 16.0 all-gather.23
  779.2 16.6 all-gather.25
  1008.8 69.9 reduce-scatter.6
  1100.1 69.7 reduce-scatter.8
  1213.3 86.7 reduce-scatter.10
  1303.5 70.2 reduce-scatter.12
  1376.6 121.1 reduce-scatter.14
  1499.5 102.8 all-gather.31
  1608.9 42.3 reduce-scatter.16
  1653.0 27.8 all-gather.33

commit v11 on v8

--- a/solution.py
+++ b/solution.py
@@ -556,7 +556,7 @@
     ready = [swapped_back, chains[-2].arrive()]
     made_other = combine(forward_parts, 1, back_own)
     made_own = combine(forward_parts, 0, made_other, *ready)
-    mixed_other, mixed_own = scatter(made_other, grad_normed_m), scatter(made_own, grad_normed_m)
+    mixed_other = scatter(made_other, grad_normed_m, made_own)
     ready = [made_own]
     grad_normed_m = after(grad_normed_m, *ready).astype(f32) + swapped_back.astype(f32)
 
@@ -569,6 +569,7 @@
     grad_gain_m = jnp.sum(grad_normed_m * resid * inv_m, axis=0)
     grad_attn = grad_resid.astype(bf16)
     grad_heads_rows = dot(grad_attn, out_full, ((1,), (1,))).astype(bf16)
+    mixed_own = scatter(made_own, grad_heads_rows)
     grad_heads = lax.all_to_all(
         grad_heads_rows, "seq", split_axis=1, concat_axis=0, tiled=True
     )
@@ -580,20 +581,21 @@
         out_sum.append(part)
     grad_qkv = attend(qkv, segment, grad_heads)
     ready = [chain.arrive() for chain in chains[-2:]]
-    grad_qkv = after(grad_qkv, mixed_own, *ready)
+    grad_qkv = after(grad_qkv, mixed_other, *ready)
     mixed_other = swap(after(mixed_other, grad_qkv), "fsdp", n_fsdp // 2)
     mixed = (resid + mixed_own.astype(f32) + mixed_other.astype(f32)).astype(bf16)
 
     grad_qkv_w = dot(normed_a, grad_qkv, ((0,), (0,))).astype(bf16)
-    reduced_qkv = lax.psum_scatter(grad_qkv_w, "fsdp", scatter_dimension=0, tiled=True)
+    reduced_qkv = after(grad_qkv_w, mixed_own)
+    reduced_qkv = lax.psum_scatter(reduced_qkv, "fsdp", scatter_dimension=0, tiled=True)
     part_normed_a = dot(after(grad_qkv, grad_qkv_w), qkv_own, ((1,), (1,)))
     part_sent = part_normed_a.astype(bf16)
     ready = [part_sent, chains[-1].add(grad_qkv_w)]
     out_sum = [swap(after(p, grad_qkv_w), "seq", k) if k else p for k, p in enumerate(out_sum)]
-    grad_normed_a = scatter_rows(after(part_sent, *out_sum), "seq")
-    qkv_sum = after(reduced_qkv, mixed_other, *ready, *out_sum[1:])
+    qkv_sum = after(reduced_qkv, mixed_other, *ready, *out_sum[1:], chains[-1].arrive())
     qkv_sum = lax.all_gather(qkv_sum, "seq", axis=0, tiled=False)
-    out_sum[0] = after(out_sum[0], qkv_sum, grad_normed_a, chains[-1].arrive())
+    grad_normed_a = scatter_rows(after(part_sent, qkv_sum), "seq")
+    out_sum[0] = after(out_sum[0], qkv_sum)
     out_sum = sum(part.astype(f32) for part in out_sum).astype(bf16)
     gain_column = jnp.zeros((D, 128), bf16).at[:, 0].set(grad_gain_m.astype(bf16))
     out_sum = jnp.concatenate([out_sum, gain_column], axis=1)

time: 1680 us -> 1730 us (1.030)
  waiting for transfers between devices: 713 us -> 774 us
    ppermute x49, waiting for transfers between devices: 641 us -> 682 us  [swap(): return lax.ppermute(value, axis, [(i, i ^ bit) for i in range(size)])]
    all_gather x1, waiting for transfers between devices: 2.21 us -> 37.3 us  [body(): qkv_sum = lax.all_gather(qkv_sum, 'seq', axis=0, tiled=False)]
    reduce_scatter x1, waiting for transfers between devices: 28.8 us -> 0.01 us  [body(): out_sum = lax.psum_scatter(out_sum, 'fsdp', scatter_dimension=0, tiled=True)]
  transfers between devices with their start and end apart: 67 -> 67, of which waited for: 23 -> 23; matrix products, arithmetic and copies ran while one was open for 25% -> 23% of each run, Pallas kernels for 21% -> 20%
where the time goes in v11:
time: 1730 us; the launch traced here: 1720 us
  waiting for transfers between devices  774 us (45%)
  Pallas kernels  353 us (20%)
  matrix products  179 us (10%)
  local copies, waits for them, and re-layouts  134 us (8%)
  other arithmetic  133 us (8%)
  blocking collectives  65.8 us (4%)
  starting transfers between devices  61.4 us (4%)
    ppermute x49, waiting for transfers between devices, swap(): return lax.ppermute(value, axis, [(i, i ^ bit) for i in range(size)])  682 us
    pallas_call x4, Pallas kernels, run_expert(): pl.pallas_call(lambda *refs: expert_kernel(size, tiles, parts, *refs), ou...  249 us
    dot_general x29, matrix products, dot(): return lax.dot_general(a, b, (contract, batch), preferred_element_type=f32)  178 us
    pallas_call x2, Pallas kernels, attend(): pl.pallas_call(lambda *refs: (attend_backward_kernel if backward else att...  76.3 us
    all_gather x1, blocking collectives, body(): lax.all_gather(routing, 'seq', axis=0, tiled=False)  65.8 us
    ppermute x49, starting transfers between devices, swap(): return lax.ppermute(value, axis, [(i, i ^ bit) for i in range(size)])  51.5 us
    all_gather x1, waiting for transfers between devices, body(): qkv_sum = lax.all_gather(qkv_sum, 'seq', axis=0, tiled=False)  37.3 us
  transfers between devices with their start and end apart: 67, of which 23 were waited for; matrix products, arithmetic and copies ran while one was open for 23% of the time, Pallas kernels for 20%

profile of v11, /device:TPU:0, one launch (start us, length us, event | category | flops | bytes accessed | tf_op | source)
XLA Modules:
  0.0 1715.5 jit_solution(2968507887749896439)
XLA Ops:
  36.9 14.5 reshape.353
  51.4 9.3 fusion.3
  62.0 32.8 %collective-permute-done.2 = bf16[384,2048]{1,0:T(8,128)(2,1)} collective-permute-done((bf16[384,2048]{1,0:T(8,128)(2,1)S(1)}, bf16[384,2048]{1,0:T(8,128)(2,1)}, u32[]{:S(2)}, u32[]{:S(2)}) %collective-permute-start.2) | collective-permute-done | bytes 1572896 | tf_op jit(solution)/shard_map/ppermute | solution.py:21
  103.4 65.8 %all-gather = f32[8,384,16]{1,2,0:T(8,128)S(1)} all-gather(f32[2,384,16]{1,2,0:T(8,128)S(1)} %pad_maximum_fusion.11), channel_id=2, replica_groups=mesh['seq'=4,'fsdp'=8] {'seq'}, dimensions={0}, use_global_device_ids=true | all-gather | bytes 245760 | tf_op jit(solution)/shard_map/all_gather | solution.py:431
  210.5 16.1 convolution_convert_fusion.2.refs_0_
  226.7 25.3 %attend_forward.1 = bf16[1536,512]{1,0:T(8,128)(2,1)} custom-call(bf16[1536,1536]{1,0:T(8,128)(2,1)} %convolution_convert_fusion.2.refs_0_, s32[1536,1]{1,0:T(8,128)} %reshape.411.refs_1_.refs_2_, s32[1,1536]{1,0:T(1,128)} %reshape.362.refs_2_.refs_3_), custom_call_target="tpu_custom_call" | custom-call | flops 24159191040 | bytes 9437184 | tf_op jit(solution)/shard_map/attend_forward/pallas_call | solution.py:97
  287.8 51.9 %collective-permute-done.11.refs_10_ = bf16[1,256,3072]{2,1,0:T(8,128)(2,1)} collective-permute-done((bf16[1,256,3072]{2,1,0:T(8,128)(2,1)}, bf16[1,256,3072]{2,1,0:T(8,128)(2,1)}, u32[]{:S(2)}, u32[]{:S(2)}) %collective-permute-start.11) | collective-permute-done | bytes 1572896 | tf_op jit(solution)/shard_map/ppermute | solution.py:21
  349.9 68.3 %collective-permute-done.13 = bf16[384,2048]{1,0:T(8,128)(2,1)S(1)} collective-permute-done((bf16[384,2048]{1,0:T(8,128)(2,1)}, bf16[384,2048]{1,0:T(8,128)(2,1)S(1)}, u32[]{:S(2)}, u32[]{:S(2)}) %collective-permute-start.13) | collective-permute-done | bytes 1572896 | tf_op jit(solution)/shard_map/ppermute | solution.py:21
  439.9 53.9 %collective-permute-done.15.refs_12_ = bf16[1,256,3072]{2,1,0:T(8,128)(2,1)} collective-permute-done((bf16[1,256,3072]{2,1,0:T(8,128)(2,1)}, bf16[1,256,3072]{2,1,0:T(8,128)(2,1)}, u32[]{:S(2)}, u32[]{:S(2)}) %collective-permute-start.15) | collective-permute-done | bytes 1572896 | tf_op jit(solution)/shard_map/ppermute | solution.py:21
  499.4 28.8 %collective-permute-done.18.refs_11_ = bf16[1,256,3072]{2,1,0:T(8,128)(2,1)} collective-permute-done((bf16[1,256,3072]{2,1,0:T(8,128)(2,1)}, bf16[1,256,3072]{2,1,0:T(8,128)(2,1)}, u32[]{:S(2)}, u32[]{:S(2)}) %collective-permute-start.18) | collective-permute-done | bytes 1572896 | tf_op jit(solution)/shard_map/ppermute | solution.py:21
  542.4 62.3 %expert.4 = (bf16[544,2048]{1,0:T(8,128)(2,1)}, bf16[544,2048]{1,0:T(8,128)(2,1)}, bf16[544,2048]{1,0:T(8,128)(2,1)}, bf16[544,2048]{1,0:T(8,128)(2,1)}, bf16[4,...) custom-call(s32[1]{0:T(128)} %bitcast.23.refs_0_, f32[1088,1]{1,0:T(8,128)} %reshape_squeeze.16.refs_1_, ...), custom_call_target="tpu_custom_call" | custom-call | flops 41070624768 | bytes 42991616 | tf_op jit(solution)/shard_map/expert/pallas_call | solution.py:320
  618.6 54.3 %collective-permute-done.21.refs_11_ = bf16[1,256,3072]{2,1,0:T(8,128)(2,1)} collective-permute-done((bf16[1,256,3072]{2,1,0:T(8,128)(2,1)}, bf16[1,256,3072]{2,1,0:T(8,128)(2,1)}, u32[]{:S(2)}, u32[]{:S(2)}) %collective-permute-start.21) | collective-permute-done | bytes 1572896 | tf_op jit(solution)/shard_map/ppermute | solution.py:21
  691.8 62.5 %expert.5 = (bf16[544,2048]{1,0:T(8,128)(2,1)}, bf16[544,2048]{1,0:T(8,128)(2,1)}, bf16[544,2048]{1,0:T(8,128)(2,1)}, bf16[544,2048]{1,0:T(8,128)(2,1)}, bf16[4,...) custom-call(s32[1]{0:T(128)} %bitcast.23.refs_0_, f32[1088,1]{1,0:T(8,128)} %reshape_squeeze.17.refs_1_, ...), custom_call_target="tpu_custom_call" | custom-call | flops 41070624768 | bytes 42991616 | tf_op jit(solution)/shard_map/expert/pallas_call | solution.py:320
  797.5 63.4 %expert.6 = (bf16[544,2048]{1,0:T(8,128)(2,1)}, bf16[544,2048]{1,0:T(8,128)(2,1)}, bf16[544,2048]{1,0:T(8,128)(2,1)}, bf16[544,2048]{1,0:T(8,128)(2,1)}, bf16[4,...) custom-call(s32[1]{0:T(128)} %bitcast.23.refs_0_, f32[1088,1]{1,0:T(8,128)} %reshape_squeeze.18.refs_1_, ...), custom_call_target="tpu_custom_call" | custom-call | flops 41070624768 | bytes 42991616 | tf_op jit(solution)/shard_map/expert/pallas_call | solution.py:320
  896.2 61.1 %expert.7 = (bf16[544,2048]{1,0:T(8,128)(2,1)}, bf16[544,2048]{1,0:T(8,128)(2,1)}, bf16[544,2048]{1,0:T(8,128)(2,1)}, bf16[544,2048]{1,0:T(8,128)(2,1)}, bf16[4,...) custom-call(s32[1]{0:T(128)} %bitcast.23.refs_0_, f32[1088,1]{1,0:T(8,128)} %reshape_squeeze.19.refs_1_, ...), custom_call_target="tpu_custom_call" | custom-call | flops 41070624768 | bytes 42991616 | tf_op jit(solution)/shard_map/expert/pallas_call | solution.py:320
  961.2 11.8 collective-permute-done.32
  990.3 7.2 convolution_convert_fusion.5
  1014.4 58.6 %collective-permute-done.38 = bf16[1,256,3072]{2,1,0:T(8,128)(2,1)} collective-permute-done((bf16[1,256,3072]{2,1,0:T(8,128)(2,1)S(1)}, bf16[1,256,3072]{2,1,0:T(8,128)(2,1)}, u32[]{:S(2)}, u32[]{:S(2)}) %collective-permute-start.38) | collective-permute-done | bytes 1572896 | tf_op jit(solution)/shard_map/ppermute | solution.py:21
  1091.6 84.6 %collective-permute-done.36 = bf16[2,256,3072]{2,1,0:T(8,128)(2,1)} collective-permute-done((bf16[2,256,3072]{2,1,0:T(8,128)(2,1)S(1)}, bf16[2,256,3072]{2,1,0:T(8,128)(2,1)}, u32[]{:S(2)}, u32[]{:S(2)}) %collective-permute-start.36) | collective-permute-done | bytes 3145760 | tf_op jit(solution)/shard_map/ppermute | solution.py:21
  1176.3 9.5 convolution_convert_fusion.3
  1215.2 27.9 %all-to-all-done.1 = bf16[384,4,512]{2,0,1:T(8,128)(2,1)} async-done(((bf16[384,4,512]{2,0,1:T(8,128)(2,1)}), bf16[384,4,512]{2,0,1:T(8,128)(2,1)}, u32[]{:S(2)}, u32[]{:S(2)}) %all-to-all-start.1) | async-done | bytes 1572896 | tf_op jit(solution)/shard_map/all_to_all | solution.py:573
  1243.1 51.0 %attend_backward.1 = bf16[1536,1536]{1,0:T(8,128)(2,1)} custom-call(bf16[1536,1536]{1,0:T(8,128)(2,1)} %convolution_convert_fusion.2.refs_0_, bf16[1536,512]{1,0:T(8,128)(2,1)} %bitcast.81.refs_1_, s32[1536,1]{1,0:T(8,128)} %reshape.411.refs_1_.refs_2_, s32[1,1536]{1,0:T(1,128)} %reshape.362.refs_2_.refs_3_), custom_call_target="tpu_custom_call" | custom-call | flops 48318382080 | bytes 9437184 | tf_op jit(solution)/shard_map/attend_backward/pallas_call | solution.py:97
  1294.1 18.9 %collective-permute-done.40 = bf16[2,256,3072]{2,1,0:T(8,128)(2,1)} collective-permute-done((bf16[2,256,3072]{2,1,0:T(8,128)(2,1)}, bf16[2,256,3072]{2,1,0:T(8,128)(2,1)}, u32[]{:S(2)}, u32[]{:S(2)}) %collective-permute-start.40) | collective-permute-done | bytes 3145760 | tf_op jit(solution)/shard_map/ppermute | solution.py:21
  1313.1 15.9 convolution_convert_fusion.1
  1329.0 16.1 reduce-scatter.11.cloned.1.call-done
  1364.8 11.6 convolution_convert_fusion
  1376.4 129.1 %collective-permute-done.41 = bf16[384,2048]{1,0:T(8,128)(2,1)S(1)} collective-permute-done((bf16[384,2048]{1,0:T(8,128)(2,1)S(1)}, bf16[384,2048]{1,0:T(8,128)(2,1)S(1)}, u32[]{:S(2)}, u32[]{:S(2)}) %collective-permute-start.41) | collective-permute-done | bytes 1572896 | tf_op jit(solution)/shard_map/ppermute | solution.py:21
  1505.6 45.5 %collective-permute-done.45 = bf16[1,256,3072]{2,1,0:T(8,128)(2,1)S(1)} collective-permute-done((bf16[1,256,3072]{2,1,0:T(8,128)(2,1)S(1)}, bf16[1,256,3072]{2,1,0:T(8,128)(2,1)S(1)}, u32[]{:S(2)}, u32[]{:S(2)}) %collective-permute-start.45) | collective-permute-done | bytes 1572896 | tf_op jit(solution)/shard_map/ppermute | solution.py:21
  1557.7 37.3 %all-gather.32.cloned.1.call-done = bf16[1024,1536]{1,0:T(8,128)(2,1)} async-done(((bf16[256,1536]{1,0:T(8,128)(2,1)}), bf16[1024,1536]{1,0:T(8,128)(2,1)}) %all-gather.32.cloned.1.call-update) | async-done | bytes 3145744 | tf_op jit(solution)/shard_map/all_gather | solution.py:596
  1621.4 14.9 finish.1
  1640.2 8.6 unpack.2
  1653.0 34.1 %collective-permute-done.48 = bf16[384,2048]{1,0:T(8,128)(2,1)} collective-permute-done((bf16[384,2048]{1,0:T(8,128)(2,1)}, bf16[384,2048]{1,0:T(8,128)(2,1)}, u32[]{:S(2)}, u32[]{:S(2)}) %collective-permute-start.48) | collective-permute-done | bytes 1572896 | tf_op jit(solution)/shard_map/ppermute | solution.py:21
  (411 shorter events, 447.0 us)
Async XLA Ops:
  7.2 202.5 %all-gather.16.cloned.1.call-start = ((), (), s32[]{:S(2)}) async-start(), calls=%async_computation.8 | async-start | bytes 7667712 | tf_op jit(solution)/shard_map/all_gather | solution.py:422
  22.6 317.1 %all-gather.18.cloned.1.call-start = ((), (), s32[]{:S(2)}) async-start(), calls=%async_computation.9 | async-start | bytes 9437184 | tf_op jit(solution)/shard_map/all_gather | solution.py:455
  30.4 147.4 %collective-permute-start.7 = (bf16[384,2048]{1,0:T(8,128)(2,1)S(1)}, bf16[384,2048]{1,0:T(8,128)(2,1)}, u32[]{:S(2)}, u32[]{:S(2)}) collective-permute-start(bf16[384,2048]{1,0:T(8,128)(2,1)S(1)} %bitcast.215), channel_id=1, source_target_pairs={{0,4},{1,5},{2,6},{3,7},{4,0},{5,1},{6,2},{7,3},{8,12},{9,13},{10,... | collective-permute-start | bytes 4718600 | tf_op jit(solution)/shard_map/ppermute | solution.py:21
  262.1 156.1 %all-gather.28.cloned.1.call-start = ((), (), s32[]{:S(2)}) async-start(), calls=%async_computation.20 | async-start | bytes 7864320 | tf_op jit(solution)/shard_map/all_gather | solution.py:469
  348.9 144.9 %all-gather.30.cloned.1.call-start = ((), (), s32[]{:S(2)}) async-start(), calls=%async_computation.21 | async-start | bytes 7864320 | tf_op jit(solution)/shard_map/all_gather | solution.py:471
  419.4 123.0 %all-gather.20.cloned.1.call-start = ((), (), s32[]{:S(2)}) async-start(), calls=%async_computation.10 | async-start | bytes 9437184 | tf_op jit(solution)/shard_map/all_gather | solution.py:198
  423.3 249.7 %all-gather.22.cloned.1.call-start = ((), (), s32[]{:S(2)}) async-start(), calls=%async_computation.11 | async-start | bytes 9437184 | tf_op jit(solution)/shard_map/all_gather | solution.py:198
  423.6 118.9 %collective-permute-start.14 = (bf16[4,256,3072]{2,1,0:T(8,128)(2,1)}, bf16[4,256,3072]{2,1,0:T(8,128)(2,1)}, u32[]{:S(2)}, u32[]{:S(2)}) collective-permute-start(bf16[4,256,3072]{2,1,0:T(8,128)(2,1)} %get-tuple-element.159.refs_6_), channel_id=1, source_target_pairs={{0,1},{1,0},{2,3},{3,2},{4,5},{5,4},{6,7},{7,6},{8,9},{9,8},{10,11... | collective-permute-start | bytes 18874376 | tf_op jit(solution)/shard_map/ppermute | solution.py:21
  424.7 103.5 %collective-permute-start.17 = (bf16[1,256,3072]{2,1,0:T(8,128)(2,1)S(1)}, bf16[1,256,3072]{2,1,0:T(8,128)(2,1)}, u32[]{:S(2)}, u32[]{:S(2)}) collective-permute-start(bf16[1,256,3072]{2,1,0:T(8,128)(2,1)S(1)} %copy-done.29), channel_id=1, source_target_pairs={{0,4},{1,5},{2,6},{3,7},{4,0},{5,1},{6,2},{7,3},{8,12},{9,13},{10,... | collective-permute-start | bytes 4718600 | tf_op jit(solution)/shard_map/ppermute | solution.py:21
  532.0 249.2 %all-gather.24.cloned.1.call-start = ((), (), s32[]{:S(2)}) async-start(), calls=%async_computation.12 | async-start | bytes 9437184 | tf_op jit(solution)/shard_map/all_gather | solution.py:198
  542.1 130.9 %collective-permute-start.21 = (bf16[1,256,3072]{2,1,0:T(8,128)(2,1)}, bf16[1,256,3072]{2,1,0:T(8,128)(2,1)}, u32[]{:S(2)}, u32[]{:S(2)}) collective-permute-start(bf16[1,256,3072]{2,1,0:T(8,128)(2,1)} %get-tuple-element.169), channel_id=1, source_target_pairs={{0,2},{1,3},{2,0},{3,1},{4,6},{5,7},{6,4},{7,5},{8,10},{9,11},{10,... | collective-permute-start | bytes 4718600 | tf_op jit(solution)/shard_map/ppermute | solution.py:21
  604.7 149.8 %collective-permute-start.26 = (bf16[4,256,3072]{2,1,0:T(8,128)(2,1)}, bf16[4,256,3072]{2,1,0:T(8,128)(2,1)}, u32[]{:S(2)}, u32[]{:S(2)}) collective-permute-start(bf16[4,256,3072]{2,1,0:T(8,128)(2,1)} %get-tuple-element.182), channel_id=1, source_target_pairs={{0,1},{1,0},{2,3},{3,2},{4,5},{5,4},{6,7},{7,6},{8,9},{9,8},{10,11... | collective-permute-start | bytes 18874376 | tf_op jit(solution)/shard_map/ppermute | solution.py:21
  610.5 170.6 %collective-permute-start.24 = (bf16[1,256,3072]{2,1,0:T(8,128)(2,1)}, bf16[1,256,3072]{2,1,0:T(8,128)(2,1)}, u32[]{:S(2)}, u32[]{:S(2)}) collective-permute-start(bf16[1,256,3072]{2,1,0:T(8,128)(2,1)} %get-tuple-element.180), channel_id=1, source_target_pairs={{0,4},{1,5},{2,6},{3,7},{4,0},{5,1},{6,2},{7,3},{8,12},{9,13},{10,... | collective-permute-start | bytes 4718600 | tf_op jit(solution)/shard_map/ppermute | solution.py:21
  617.9 163.2 %collective-permute-start.25 = (bf16[1,256,3072]{2,1,0:T(8,128)(2,1)}, bf16[1,256,3072]{2,1,0:T(8,128)(2,1)}, u32[]{:S(2)}, u32[]{:S(2)}) collective-permute-start(bf16[1,256,3072]{2,1,0:T(8,128)(2,1)} %get-tuple-element.181), channel_id=1, source_target_pairs={{0,2},{1,3},{2,0},{3,1},{4,6},{5,7},{6,4},{7,5},{8,10},{9,11},{10,... | collective-permute-start | bytes 4718600 | tf_op jit(solution)/shard_map/ppermute | solution.py:21
  682.3 202.9 %all-gather.26.cloned.1.call-start = ((), (), s32[]{:S(2)}) async-start(), calls=%async_computation.13 | async-start | bytes 9437184 | tf_op jit(solution)/shard_map/all_gather | solution.py:198
  754.3 106.6 %collective-permute-start.30 = (bf16[4,256,3072]{2,1,0:T(8,128)(2,1)}, bf16[4,256,3072]{2,1,0:T(8,128)(2,1)}, u32[]{:S(2)}, u32[]{:S(2)}) collective-permute-start(bf16[4,256,3072]{2,1,0:T(8,128)(2,1)} %get-tuple-element.197), channel_id=1, source_target_pairs={{0,1},{1,0},{2,3},{3,2},{4,5},{5,4},{6,7},{7,6},{8,9},{9,8},{10,11... | collective-permute-start | bytes 18874376 | tf_op jit(solution)/shard_map/ppermute | solution.py:21
  767.9 100.7 %collective-permute-start.29 = (bf16[2,256,3072]{2,1,0:T(8,128)(2,1)}, bf16[2,256,3072]{2,1,0:T(8,128)(2,1)}, u32[]{:S(2)}, u32[]{:S(2)}) collective-permute-start(bf16[2,256,3072]{2,1,0:T(8,128)(2,1)} %add_convert_fusion.3), channel_id=1, source_target_pairs={{0,2},{1,3},{2,0},{3,1},{4,6},{5,7},{6,4},{7,5},{8,10},{9,11},{10,... | collective-permute-start | bytes 9437192 | tf_op jit(solution)/shard_map/ppermute | solution.py:21
  790.9 282.2 %reduce-scatter.7.cloned.1.call-start = ((), (), s32[]{:S(2)}) async-start(), calls=%async_computation.14 | async-start | bytes 7864320 | tf_op jit(solution)/shard_map/reduce_scatter | solution.py:546
  866.8 107.0 %collective-permute-start.33 = (bf16[2,256,3072]{2,1,0:T(8,128)(2,1)}, bf16[2,256,3072]{2,1,0:T(8,128)(2,1)}, u32[]{:S(2)}, u32[]{:S(2)}) collective-permute-start(bf16[2,256,3072]{2,1,0:T(8,128)(2,1)} %add_convert_fusion.2), channel_id=1, source_target_pairs={{0,2},{1,3},{2,0},{3,1},{4,6},{5,7},{6,4},{7,5},{8,10},{9,11},{10,... | collective-permute-start | bytes 9437192 | tf_op jit(solution)/shard_map/ppermute | solution.py:21
  980.9 204.9 %reduce-scatter.9.cloned.1.call-start = ((), (), s32[]{:S(2)}) async-start(), calls=%async_computation.15 | async-start | bytes 7864320 | tf_op jit(solution)/shard_map/reduce_scatter | solution.py:546
  1073.1 240.0 %reduce-scatter.13.cloned.1.call-start = ((), (), s32[]{:S(2)}) async-start(), calls=%async_computation.17 | async-start | bytes 7864320 | tf_op jit(solution)/shard_map/reduce_scatter | solution.py:546
  1073.1 103.2 %collective-permute-start.36 = (bf16[2,256,3072]{2,1,0:T(8,128)(2,1)S(1)}, bf16[2,256,3072]{2,1,0:T(8,128)(2,1)}, u32[]{:S(2)}, u32[]{:S(2)}) collective-permute-start(bf16[2,256,3072]{2,1,0:T(8,128)(2,1)S(1)} %add_convert_fusion.1), channel_id=1, source_target_pairs={{0,2},{1,3},{2,0},{3,1},{4,6},{5,7},{6,4},{7,5},{8,10},{9,11},{10,... | collective-permute-start | bytes 9437192 | tf_op jit(solution)/shard_map/ppermute | solution.py:21
  1185.9 159.2 %reduce-scatter.11.cloned.1.call-start = ((), (), s32[]{:S(2)}) async-start(), calls=%async_computation.16 | async-start | bytes 7864320 | tf_op jit(solution)/shard_map/reduce_scatter | solution.py:546
  1206.7 345.5 %reduce-scatter.15.cloned.1.call-start = ((), (), s32[]{:S(2)}) async-start(), calls=%async_computation.18 | async-start | bytes 7077888 | tf_op jit(solution)/shard_map/reduce_scatter | solution.py:590
  1211.3 101.8 %collective-permute-start.40 = (bf16[2,256,3072]{2,1,0:T(8,128)(2,1)}, bf16[2,256,3072]{2,1,0:T(8,128)(2,1)}, u32[]{:S(2)}, u32[]{:S(2)}) collective-permute-start(bf16[2,256,3072]{2,1,0:T(8,128)(2,1)} %add_convert_fusion), channel_id=1, source_target_pairs={{0,2},{1,3},{2,0},{3,1},{4,6},{5,7},{6,4},{7,5},{8,10},{9,11},{10,... | collective-permute-start | bytes 9437192 | tf_op jit(solution)/shard_map/ppermute | solution.py:21
  1345.1 250.0 %all-gather.32.cloned.1.call-start = ((), (), s32[]{:S(2)}) async-start(), calls=%async_computation.22 | async-start | bytes 3932160 | tf_op jit(solution)/shard_map/all_gather | solution.py:596
  1354.5 151.0 %collective-permute-start.41 = (bf16[384,2048]{1,0:T(8,128)(2,1)S(1)}, bf16[384,2048]{1,0:T(8,128)(2,1)S(1)}, u32[]{:S(2)}, u32[]{:S(2)}) collective-permute-start(bf16[384,2048]{1,0:T(8,128)(2,1)S(1)} %copy-done.53), channel_id=1, source_target_pairs={{0,4},{1,5},{2,6},{3,7},{4,0},{5,1},{6,2},{7,3},{8,12},{9,13},{10,... | collective-permute-start | bytes 4718600 | tf_op jit(solution)/shard_map/ppermute | solution.py:21
  1356.6 195.6 %collective-permute-start.43 = (bf16[2048,512]{1,0:T(8,128)(2,1)S(1)}, bf16[2048,512]{1,0:T(8,128)(2,1)}, u32[]{:S(2)}, u32[]{:S(2)}) collective-permute-start(bf16[2048,512]{1,0:T(8,128)(2,1)S(1)} %convolution_convert_fusion.17), channel_id=1, source_target_pairs={{0,16},{8,24},{16,0},{24,8},{1,17},{9,25},{17,1},{25,9},{2,18},{10... | collective-permute-start | bytes 6291464 | tf_op jit(solution)/shard_map/ppermute | solution.py:21
  1357.9 194.3 %collective-permute-start.42 = (bf16[2048,512]{1,0:T(8,128)(2,1)S(1)}, bf16[2048,512]{1,0:T(8,128)(2,1)}, u32[]{:S(2)}, u32[]{:S(2)}) collective-permute-start(bf16[2048,512]{1,0:T(8,128)(2,1)S(1)} %convolution_convert_fusion.18), channel_id=1, source_target_pairs={{0,8},{8,0},{16,24},{24,16},{1,9},{9,1},{17,25},{25,17},{2,10},{10... | collective-permute-start | bytes 6291464 | tf_op jit(solution)/shard_map/ppermute | solution.py:21
  1358.6 193.6 %collective-permute-start.44 = (bf16[2048,512]{1,0:T(8,128)(2,1)S(1)}, bf16[2048,512]{1,0:T(8,128)(2,1)}, u32[]{:S(2)}, u32[]{:S(2)}) collective-permute-start(bf16[2048,512]{1,0:T(8,128)(2,1)S(1)} %convolution_convert_fusion.16), channel_id=1, source_target_pairs={{0,24},{8,16},{16,8},{24,0},{1,25},{9,17},{17,9},{25,1},{2,26},{10... | collective-permute-start | bytes 6291464 | tf_op jit(solution)/shard_map/ppermute | solution.py:21
  1364.0 187.1 %collective-permute-start.45 = (bf16[1,256,3072]{2,1,0:T(8,128)(2,1)S(1)}, bf16[1,256,3072]{2,1,0:T(8,128)(2,1)S(1)}, u32[]{:S(2)}, u32[]{:S(2)}) collective-permute-start(bf16[1,256,3072]{2,1,0:T(8,128)(2,1)S(1)} %get-tuple-element.271), channel_id=1, source_target_pairs={{0,4},{1,5},{2,6},{3,7},{4,0},{5,1},{6,2},{7,3},{8,12},{9,13},{10,... | collective-permute-start | bytes 4718600 | tf_op jit(solution)/shard_map/ppermute | solution.py:21
  1601.5 101.8 %all-gather.34.cloned.1.call-start = ((), (), s32[]{:S(2)}) async-start(), calls=%async_computation.23 | async-start | bytes 1638400 | tf_op jit(solution)/shard_map/all_gather | solution.py:603
  (104 other events, 3519.9 us)
Sparse Core Ops, SparseCore 0:
  22.7 128.8 all-gather.15
  190.8 126.8 all-gather.17
  349.0 68.6 all-gather.27
  420.0 70.1 all-gather.29
  491.6 16.7 all-gather.19
  532.1 16.8 all-gather.21
  682.4 16.1 all-gather.23
  791.0 16.3 all-gather.25
  981.1 70.4 reduce-scatter.6
  1073.2 69.6 reduce-scatter.8
  1186.0 85.9 reduce-scatter.12
  1274.8 70.1 reduce-scatter.10
  1347.9 165.2 reduce-scatter.14
  1552.4 42.5 all-gather.31
  1601.6 37.4 reduce-scatter.16
  1648.9 54.4 all-gather.33
